TPU v7x, 32 devices: a whole 2x2x4 slice. The times are simulated.
32 devices in a mesh: groups: 2 (over x), pairs: 8 (over z, y), aux: 2 (over core).
Axes of the slice: x: 2, y: 2, z: 4, core: 2. Of those that a mesh axis runs over, the one named last changes fastest.
Arguments:
- blocks: bfloat16 [256, 32, 10240], P(('groups', 'pairs'), None, 'aux'), parts along dimension 0, may hold values from -0.75 to 0.75
- wanted: int32 [256], P(('groups', 'pairs')), parts along dimension 0, may hold values from 0 to 127, as said below
- pair_slots: int32 [256, 16], P(('groups', 'pairs')), parts along dimension 0, may hold values from 0 to 15
- fock: bfloat16 [256, 256, 256], P(('groups', 'pairs', 'aux')), parts along dimension 0, may hold values from -0.375 to 0.375
- correlation: bfloat16 [256, 256, 256], P(('groups', 'pairs', 'aux')), parts along dimension 0, may hold values from -0.375 to 0.375
- amplitudes: bfloat16 [256, 256, 256], P(('groups', 'pairs', 'aux')), parts along dimension 0, may hold values from -6 to 6
Outputs:
- pair_residual: bfloat16 [256, 256, 256], P(('groups', 'pairs', 'aux')), parts along dimension 0
There are 2 independent parts, one for each index of `groups`. A program takes and returns all parts, laid end to end along the dimension named above; each array names one. Nothing has to cross between parts.
Inputs may be any that keep to these rules, and one draw needn't show every extreme that they name: `wanted`: block b is held by orbital owner b // 16 along pairs. Among the 16 entries of one pair owner at most 4 name blocks of the same orbital owner, and on every pair owner some orbital owner is named exactly 4 times.
All inputs are finite; a program needn't handle non-finite values.
Results may differ from a plain program's by a relative error of at most 0.012.
Values may be sent and summed in bfloat16 or wider, within the bound.
No kernel may reach another device: no remote copies, remote signals or barrier semaphores. Data moves between devices by JAX's collectives and lax.ppermute only.
A program may use at most 128 MiB of HBM per device.

v0:
```python
import jax
import jax.numpy as jnp
from jax import lax
from jax.sharding import PartitionSpec as P

DOM = 8
UNIQ = 16


def pick_tiles(gram, left_ids, right_ids):
    count = left_ids.shape[0]
    sides = left_ids.shape[1]
    width = gram.shape[2]
    tiles = gram[left_ids[:, :, None], right_ids[:, None, :]]
    return tiles.transpose(0, 1, 3, 2, 4).reshape(count, sides * width, sides * width)


def pair_integrals(held, left_ids, right_ids):
    units, width, depth = held.shape
    stacked = held.reshape(units * width, depth)
    gram = lax.dot_general(
        stacked, stacked, (((1,), (1,)), ((), ())), preferred_element_type=jnp.float32
    )
    gram = gram.reshape(units, width, units, width).transpose(0, 2, 1, 3)
    return pick_tiles(gram, left_ids, right_ids)


def on_device(blocks, wanted, pair_slots, fock, correlation, amplitudes):
    holders = lax.axis_size("pairs")
    owned = blocks.shape[0]
    width = blocks.shape[1]
    depth = blocks.shape[2]
    capacity = max(2, (2 * UNIQ + holders - 1) // holders)
    holder = wanted // owned
    local_ids = wanted - holder * owned
    order_ids = jnp.arange(wanted.shape[0])
    earlier = (holder[None, :] == holder[:, None]) & (order_ids[None, :] < order_ids[:, None])
    rank = jnp.sum(earlier.astype(jnp.int32), axis=1)
    slot = holder * capacity + rank
    places = jnp.arange(holders * capacity)
    table = jnp.sum(jnp.where(places[:, None] == slot[None, :], local_ids[None, :], 0), axis=1)
    table = table.reshape(holders, capacity)
    asked = lax.all_to_all(table, "pairs", split_axis=0, concat_axis=0, tiled=True)
    outgoing = jnp.take(blocks, asked.reshape(-1), axis=0).reshape(holders, capacity, width, depth)
    arrived = lax.all_to_all(outgoing, "pairs", split_axis=0, concat_axis=0, tiled=True)
    held = jnp.take(arrived.reshape(holders * capacity, width, depth), slot, axis=0)
    partial_value = pair_integrals(held, pair_slots[:, :DOM], pair_slots[:, DOM:])
    integrals = lax.psum_scatter(
        partial_value.astype(jnp.bfloat16), "aux", scatter_dimension=0, tiled=True
    ).astype(jnp.float32)
    fock_amp = jnp.einsum(
        "pab,pbc->pac", fock, amplitudes, preferred_element_type=jnp.float32
    ).astype(jnp.bfloat16)
    over_amp = jnp.einsum(
        "pab,pbc->pac", correlation, amplitudes, preferred_element_type=jnp.float32
    ).astype(jnp.bfloat16)
    first_term = jnp.einsum(
        "pab,pbc->pac", fock_amp, correlation, preferred_element_type=jnp.float32
    )
    second_term = jnp.einsum("pab,pbc->pac", over_amp, fock, preferred_element_type=jnp.float32)
    return (integrals + first_term + second_term).astype(jnp.bfloat16)


def solution(mesh):
    return jax.shard_map(
        on_device,
        mesh=mesh,
        in_specs=(
            P(("groups", "pairs"), None, "aux"),
            P(("groups", "pairs")),
            P(("groups", "pairs"), None),
            P(("groups", "pairs", "aux"), None, None),
            P(("groups", "pairs", "aux"), None, None),
            P(("groups", "pairs", "aux"), None, None),
        ),
        out_specs=P(("groups", "pairs", "aux"), None, None),
        check_vma=False,
    )
```

profile of v0, /device:TPU:0, one launch (start us, length us, event | category | flops | bytes accessed | tf_op | source)
XLA Modules:
  0.0 352.7 jit_solution(265725061350813884)
XLA Ops:
  6.5 0.0 copy-start
  6.5 0.8 multiply_subtract_fusion
  7.3 0.2 convert_reduce_fusion
  7.5 0.1 select_reduce_fusion
  7.6 0.1 all_to_all.9
  7.7 13.5 %all_to_all.14 = s32[8,1,4]{2,1,0:T(1,128)S(1)} all-to-all(s32[8,1,4]{2,1,0:T(1,128)S(1)} %bitcast.39), channel_id=1, replica_groups=mesh['groups'=2,'pairs'=8,'aux'=2] {'pairs'}, dimensions={0} | all-to-all | bytes 256 | tf_op jit(solution)/shard_map/all_to_all | solution.py:43
  21.2 0.5 broadcast.134
  21.7 0.7 reduce.3
  22.4 0.1 reshape.97
  22.5 0.1 copy.18
  22.6 0.1 copy.19
  22.7 8.4 %gather_fusion = bf16[32,32,5120]{2,1,0:T(8,128)(2,1)} fusion(bf16[16,32,5120]{2,1,0:T(8,128)(2,1)} %param.6, s32[1024]{0:T(1024)S(1)} %pad_clamp_fusion.1), kind=kCustom, calls=%fused_computation | custom fusion | bytes 20971648 | tf_op jit(solution)/shard_map/jit(_take)/gather | solution.py:44
  31.1 10.1 %broadcast_select_fusion = bf16[8,4,32,5120]{3,2,1,0:T(8,128)(2,1)} fusion(bf16[8,4,32,5120]{3,2,1,0:T(8,128)(2,1)} %bitcast.37, pred[8,4]{1,0:T(8,128)(4,1)S(1)} %copy.19), kind=kLoop, calls=%fused_computation.3 | loop fusion | flops 5242880 | bytes 20971552 | tf_op jit(solution)/shard_map/jit(_take)/select_n | solution.py:44
  41.2 0.0 copy-start.1
  41.2 5.3 %all-to-all-start.1 = ((bf16[8,4,32,5120]{3,2,1,0:T(8,128)(2,1)}), bf16[8,4,32,5120]{3,2,1,0:T(8,128)(2,1)}, u32[]{:S(2)}, u32[]{:S(2)}) async-start(bf16[8,4,32,5120]{3,2,1,0:T(8,128)(2,1)} %broadcast_select_fusion), calls=%async_computation.1 | async-start | bytes 20971520 | tf_op jit(solution)/shard_map/all_to_all | solution.py:45
  46.5 0.0 reduce-scatter.2.cloned.1.call-start
  46.5 0.0 copy-done.1
  46.5 0.1 fusion.13
  46.6 0.1 broadcast_or_fusion
  46.7 0.1 reshape.115
  46.8 226.5 %all-to-all-done.1 = bf16[8,4,32,5120]{3,2,1,0:T(8,128)(2,1)} async-done(((bf16[8,4,32,5120]{3,2,1,0:T(8,128)(2,1)}), bf16[8,4,32,5120]{3,2,1,0:T(8,128)(2,1)}, u32[]{:S(2)}, u32[]{:S(2)}) %all-to-all-start.1) | async-done | bytes 10485792 | tf_op jit(solution)/shard_map/all_to_all | solution.py:45
  273.3 7.2 %gather_fusion.1 = bf16[16,32,5120]{2,1,0:T(8,128)(2,1)} fusion(bf16[32,32,5120]{2,1,0:T(8,128)(2,1)} %bitcast.4, s32[1024]{0:T(1024)S(1)} %pad_clamp_fusion), kind=kCustom, calls=%fused_computation.1 | custom fusion | bytes 10485824 | tf_op jit(solution)/shard_map/jit(_take)/gather | solution.py:46
  280.6 15.4 %fusion.6 = bf16[16,16,32,32]{3,2,1,0:T(8,128)(2,1)S(1)} fusion(bf16[16,32,5120]{2,1,0:T(8,128)(2,1)} %gather_fusion.1, pred[16]{0:T(512)(128)(4,1)S(1)} %get-tuple-element.5), kind=kOutput, calls=%fused_computation.10 | convolution fusion | flops 2689597440 | bytes 5767184 | tf_op jit(solution)/shard_map/dot_general | solution.py:21
  295.9 11.7 %gather_fusion.2 = bf16[1024,32,32]{2,1,0:T(8,128)(2,1)} fusion(bf16[16,16,32,32]{3,2,1,0:T(8,128)(2,1)S(1)} %fusion.6, s32[1024]{0:T(1024)S(1)} %reshape.115), kind=kCustom, calls=%fused_computation.2 | custom fusion | bytes 4202496 | tf_op jit(solution)/shard_map/gather | solution.py:14
  307.7 15.1 %copy.20 = bf16[16,8,32,8,32]{4,3,2,1,0:T(8,128)(2,1)} copy(bf16[16,8,32,8,32]{4,2,3,1,0:T(8,128)(2,1)} %bitcast.38) | data formatting | bytes 4194304 | tf_op jit(solution)/shard_map/convert_element_type | solution.py:49
  322.7 10.8 %convert_element_type.27 = bf16[16,256,256]{2,1,0:T(8,128)(2,1)} reshape(bf16[16,8,32,8,32]{4,3,2,1,0:T(8,128)(2,1)} %copy.20) | data formatting | bytes 4194304 | tf_op jit(solution)/shard_map/convert_element_type | solution.py:49
  333.5 0.0 reduce-scatter.2.cloned.1.call-update
  333.5 0.0 copy-done
  333.5 2.3 fusion.11
  335.8 6.5 %reduce-scatter.2.cloned.1.call-done = bf16[8,256,256]{2,1,0:T(8,128)(2,1)} async-done(((bf16[16,256,256]{2,1,0:T(8,128)(2,1)}), bf16[8,256,256]{2,1,0:T(8,128)(2,1)}) %reduce-scatter.2.cloned.1.call-update) | async-done | bytes 1048592 | tf_op jit(solution)/shard_map/reduce_scatter | solution.py:48
  342.3 3.6 %add_convert_fusion = bf16[8,256,256]{2,1,0:T(8,128)(2,1)} fusion(f32[8,256,256]{2,1,0:T(8,128)S(1)} %fusion.11, bf16[8,256,256]{2,1,0:T(8,128)(2,1)} %reduce-scatter.2.cloned.1.call-done, bf16[8,256,256]{2,1,0:T(8,128)(2,1)} %param.9, bf16[8,256,256]{2,1,0:T(8,128)(2,1)S(1)} %copy-done, bf16[8,256,256]{2,1,0:T(8,128)(2,1)} %param.11), kind=kOutput, calls=%fused_computation.11 | convolution fusion | flops 539492352 | bytes 7340032 | tf_op jit(solution)/shard_map/pab,pbc->pac/dot_general | solution.py:60
  (6 shorter events, 0.0 us)
Async XLA Ops:
  6.5 327.0 %copy-start = (bf16[8,256,256]{2,1,0:T(8,128)(2,1)S(1)}, bf16[8,256,256]{2,1,0:T(8,128)(2,1)}, u32[]{:S(2)}) copy-start(bf16[8,256,256]{2,1,0:T(8,128)(2,1)} %param.10) | copy-start | bytes 3145732
  41.2 5.3 %copy-start.1 = (s32[16,16]{1,0:T(8,128)S(1)}, s32[16,16]{1,0:T(8,128)}, u32[]{:S(2)}) copy-start(s32[16,16]{1,0:T(8,128)} %param.8) | copy-start | bytes 3076
  41.2 232.1 %all-to-all-start.1 = ((bf16[8,4,32,5120]{3,2,1,0:T(8,128)(2,1)}), bf16[8,4,32,5120]{3,2,1,0:T(8,128)(2,1)}, u32[]{:S(2)}, u32[]{:S(2)}) async-start(bf16[8,4,32,5120]{3,2,1,0:T(8,128)(2,1)} %broadcast_select_fusion), calls=%async_computation.1 | async-start | bytes 20971520 | tf_op jit(solution)/shard_map/all_to_all | solution.py:45
  46.5 295.8 %reduce-scatter.2.cloned.1.call-start = ((), (), s32[]{:S(2)}) async-start(), calls=%async_computation.3 | async-start | bytes 3145728 | tf_op jit(solution)/shard_map/reduce_scatter | solution.py:48
Sparse Core Ops, SparseCore 0:
  333.6 8.5 reduce-scatter.1
where the time goes:
time: 353 us
  waiting for transfers between devices  233 us (66%)
  local copies, waits for them, and re-layouts  54.2 us (15%)
  matrix products  21.2 us (6%)
  blocking collectives  13.5 us (4%)
  between operations  13.5 us (4%)
  other arithmetic  12 us (3%)
  starting transfers between devices  5.31 us (2%)
    all_to_all x1, waiting for transfers between devices, on_device(): lax.all_to_all(outgoing, 'pairs', split_axis=0, concat_axis=0, tiled=True)  227 us
    convert_element_type x2, local copies, waits for them, and re-layouts, on_device(): partial_value.astype(jnp.bfloat16)  25.8 us
    dot_general x1, matrix products, pair_integrals(): lax.dot_general(stacked, stacked, (((1,), (1,)), ((), ())), preferred_ele...  15.4 us
    all_to_all x1, blocking collectives, on_device(): lax.all_to_all(table, 'pairs', split_axis=0, concat_axis=0, tiled=True)  13.5 us
    gather x1, local copies, waits for them, and re-layouts, pick_tiles(): tiles = gram[left_ids[:, :, None], right_ids[:, None, :]]  11.7 us
    select_n x2, other arithmetic, on_device(): jnp.take(blocks, asked.reshape(-1), axis=0)  10.1 us
    gather x1, local copies, waits for them, and re-layouts, on_device(): jnp.take(blocks, asked.reshape(-1), axis=0)  8.42 us
    gather x1, local copies, waits for them, and re-layouts, on_device(): jnp.take(arrived.reshape(holders * capacity, width, depth), slot, axis=0)  7.23 us
  transfers between devices with their start and end apart: 2, of which 2 were waited for; matrix products, arithmetic and copies ran while one was open for 1% of the time, Pallas kernels for 0%

commit v1 on v0

--- a/solution.py
+++ b/solution.py
@@ -1,10 +1,222 @@
+import functools
+
 import jax
 import jax.numpy as jnp
 from jax import lax
+from jax.experimental import pallas as pl
+from jax.experimental.pallas import tpu as pltpu
 from jax.sharding import PartitionSpec as P
 
 DOM = 8
 UNIQ = 16
+TILE = 128
+VMEM_BYTES = 48 * 1024 * 1024
+SMEM_SPEC = pl.BlockSpec(memory_space=pltpu.SMEM)
+VMEM_SPEC = pl.BlockSpec(memory_space=pltpu.VMEM)
+ANY_SPEC = pl.BlockSpec(memory_space=pl.ANY)
+
+
+def upper_tiles(side):
+    return [(i, j) for i in range(side) for j in range(i, side)]
+
+
+def terms_kernel(fock_ref, corr_ref, amp_ref, out_ref):
+    fock, corr, amp = fock_ref[0], corr_ref[0], amp_ref[0]
+    fock_amp = jnp.dot(fock, amp, preferred_element_type=jnp.float32).astype(jnp.bfloat16)
+    over_amp = jnp.dot(corr, amp, preferred_element_type=jnp.float32).astype(jnp.bfloat16)
+    first = jnp.dot(fock_amp, corr, preferred_element_type=jnp.float32)
+    out_ref[0] = first + jnp.dot(over_amp, fock, preferred_element_type=jnp.float32)
+
+
+def pair_terms(fock, correlation, amplitudes):
+    pairs, rows, cols = fock.shape
+    spec = pl.BlockSpec((1, rows, cols), lambda p: (p, 0, 0))
+    return pl.pallas_call(
+        terms_kernel,
+        grid=(pairs,),
+        in_specs=[spec] * 3,
+        out_specs=spec,
+        out_shape=jax.ShapeDtypeStruct(fock.shape, jnp.float32),
+        compiler_params=pltpu.CompilerParams(vmem_limit_bytes=VMEM_BYTES),
+        cost_estimate=pl.CostEstimate(
+            flops=8 * pairs * rows * rows * cols,
+            bytes_accessed=10 * pairs * rows * cols,
+            transcendentals=0,
+        ),
+    )(fock, correlation, amplitudes)
+
+
+def gram_kernel(holders, addr_ref, core_ref, place_ref, blocks_ref, *rest):
+    arrived_refs = rest[: holders - 1]
+    keep_ref, send_ref, pool, rows_ref, sems = rest[holders - 1 :]
+    owned, width, depth = blocks_ref.shape
+    columns = depth // holders
+    start = pl.multiple_of(place_ref[0] * columns, TILE)
+    copies = [
+        pltpu.make_async_copy(
+            blocks_ref.at[:, :, pl.ds(start, columns)], pool.at[pl.ds(0, owned)], sems.at[0]
+        )
+    ]
+    for k, ref in enumerate(arrived_refs, 1):
+        copies.append(
+            pltpu.make_async_copy(ref, pool.at[pl.ds(k * owned, owned)], sems.at[k])
+        )
+    for copy in copies:
+        copy.start()
+    for copy in copies:
+        copy.wait()
+    side = UNIQ * width // TILE
+    half = len(upper_tiles(side)) // 2
+    core = core_ref[0]
+
+    @pl.loop(0, holders)
+    def _(k):
+        for m in range(UNIQ):
+            rows_ref[m * width : (m + 1) * width, :] = pool[addr_ref[k, m]]
+        tiles = []
+        for i in range(side):
+            strip = lax.dot_general(
+                rows_ref[i * TILE : (i + 1) * TILE, :],
+                rows_ref[i * TILE :, :],
+                (((1,), (1,)), ((), ())),
+                preferred_element_type=jnp.float32,
+            ).astype(jnp.bfloat16)
+            for j in range(i, side):
+                tiles.append(strip[:, (j - i) * TILE : (j - i + 1) * TILE])
+
+        @pl.when(core == 0)
+        def _():
+            for t in range(half):
+                keep_ref[k, t * TILE : (t + 1) * TILE, :] = tiles[t]
+                send_ref[k, t * TILE : (t + 1) * TILE, :] = tiles[half + t]
+
+        @pl.when(core != 0)
+        def _():
+            for t in range(half):
+                send_ref[k, t * TILE : (t + 1) * TILE, :] = tiles[t]
+                keep_ref[k, t * TILE : (t + 1) * TILE, :] = tiles[half + t]
+
+
+def partial_grams(addr, core, place, blocks, arrived):
+    holders = len(arrived) + 1
+    owned, width, depth = blocks.shape
+    columns = depth // holders
+    side = UNIQ * width // TILE
+    half = len(upper_tiles(side)) // 2
+    out = jax.ShapeDtypeStruct((holders, half * TILE, TILE), jnp.bfloat16)
+    return pl.pallas_call(
+        functools.partial(gram_kernel, holders),
+        in_specs=[SMEM_SPEC] * 3 + [ANY_SPEC] * holders,
+        out_specs=[VMEM_SPEC] * 2,
+        out_shape=[out, out],
+        scratch_shapes=[
+            pltpu.VMEM((holders * owned, width, columns), jnp.bfloat16),
+            pltpu.VMEM((UNIQ * width, columns), jnp.bfloat16),
+            pltpu.SemaphoreType.DMA((holders,)),
+        ],
+        compiler_params=pltpu.CompilerParams(vmem_limit_bytes=VMEM_BYTES),
+        cost_estimate=pl.CostEstimate(
+            flops=2 * holders * (UNIQ * width) ** 2 * columns,
+            bytes_accessed=2 * holders * owned * width * columns,
+            transcendentals=0,
+        ),
+    )(addr, core, place, blocks, *arrived)
+
+
+def finish_kernel(slots_ref, core_ref, mine_ref, other_ref, right_ref, terms_ref, out_ref, gram):
+    core = core_ref[0]
+    side = gram.shape[0] // TILE
+    order = upper_tiles(side)
+    half = len(order) // 2
+    width = gram.shape[0] // UNIQ
+    pair = pl.program_id(0)
+
+    def place(t, value):
+        i, j = order[t]
+        gram[i * TILE : (i + 1) * TILE, j * TILE : (j + 1) * TILE] = value
+        if i != j:
+            flipped = value.astype(jnp.float32).T.astype(jnp.bfloat16)
+            gram[j * TILE : (j + 1) * TILE, i * TILE : (i + 1) * TILE] = flipped
+
+    @pl.when(pair == 0)
+    def _():
+        for t in range(half):
+            mine = mine_ref[t * TILE : (t + 1) * TILE, :]
+            other = other_ref[t * TILE : (t + 1) * TILE, :]
+            place(t, jnp.where(core == 0, mine, other))
+            place(half + t, jnp.where(core == 0, other, mine))
+
+    left = jnp.concatenate(
+        [gram[pl.ds(slots_ref[pair, m] * width, width), :] for m in range(DOM)], axis=0
+    )
+    rows = lax.broadcasted_iota(jnp.int32, (gram.shape[0], DOM * width), 0)
+    choose = (rows == right_ref[0]).astype(jnp.float32).astype(jnp.bfloat16)
+    integrals = jnp.dot(left, choose, preferred_element_type=jnp.float32)
+    out_ref[0] = (integrals + terms_ref[0]).astype(jnp.bfloat16)
+
+
+def finish(slots, core, mine, other, right_rows, terms):
+    pairs, rows, cols = terms.shape
+    tile = pl.BlockSpec((1, rows, cols), lambda p: (p, 0, 0))
+    whole = pl.BlockSpec(mine.shape, lambda p: (0, 0))
+    gram_side = UNIQ * rows // DOM
+    return pl.pallas_call(
+        finish_kernel,
+        grid=(pairs,),
+        in_specs=[
+            SMEM_SPEC,
+            SMEM_SPEC,
+            whole,
+            whole,
+            pl.BlockSpec((1, 1, cols), lambda p: (p, 0, 0)),
+            tile,
+        ],
+        out_specs=tile,
+        out_shape=jax.ShapeDtypeStruct(terms.shape, jnp.bfloat16),
+        scratch_shapes=[pltpu.VMEM((gram_side, gram_side), jnp.bfloat16)],
+        compiler_params=pltpu.CompilerParams(vmem_limit_bytes=VMEM_BYTES),
+        cost_estimate=pl.CostEstimate(
+            flops=2 * pairs * rows * cols * gram_side,
+            bytes_accessed=6 * pairs * rows * cols,
+            transcendentals=0,
+        ),
+    )(slots, core, mine, other, right_rows, terms)
+
+
+def swap(value, axis, bit):
+    size = lax.axis_size(axis)
+    return lax.ppermute(value, axis, [(i, i ^ bit) for i in range(size)])
+
+
+def split_by_columns(blocks, wanted, pair_slots, fock, correlation, amplitudes):
+    holders = lax.axis_size("pairs")
+    me = lax.axis_index("pairs")
+    core = lax.axis_index("aux")
+    owned, width, depth = blocks.shape
+    columns = depth // holders
+    everyone = lax.all_gather(wanted, "pairs", tiled=False)
+    arrived = []
+    for k in range(1, holders):
+        part = lax.dynamic_slice_in_dim(blocks, (me ^ k) * columns, columns, axis=2)
+        arrived.append(swap(part, "pairs", k))
+    owners = me ^ jnp.arange(holders, dtype=jnp.int32)
+    asked = jnp.take(everyone, owners, axis=0)
+    addr = ((asked // owned) ^ me) * owned + asked % owned
+    pairs_here = fock.shape[0]
+    slots = lax.dynamic_slice_in_dim(pair_slots, core * pairs_here, pairs_here, axis=0)
+    offsets = jnp.arange(width, dtype=jnp.int32)
+    right_rows = (slots[:, DOM:, None] * width + offsets).reshape(pairs_here, 1, DOM * width)
+    terms = pair_terms(fock, correlation, amplitudes)
+    core_id = core.reshape(1).astype(jnp.int32)
+    keep, send = partial_grams(addr, core_id, me.reshape(1).astype(jnp.int32), blocks, arrived)
+    both = keep.astype(jnp.float32) + swap(send, "aux", 1).astype(jnp.float32)
+    both = both.astype(jnp.bfloat16)
+    total = both[0].astype(jnp.float32)
+    for k in range(1, holders):
+        total = total + swap(both[k], "pairs", k).astype(jnp.float32)
+    mine = total.astype(jnp.bfloat16)
+    other = swap(mine, "aux", 1)
+    return finish(slots, core_id, mine, other, right_rows, terms)
 
 
 def pick_tiles(gram, left_ids, right_ids):
@@ -25,11 +237,9 @@
     return pick_tiles(gram, left_ids, right_ids)
 
 
-def on_device(blocks, wanted, pair_slots, fock, correlation, amplitudes):
+def by_request(blocks, wanted, pair_slots, fock, correlation, amplitudes):
     holders = lax.axis_size("pairs")
-    owned = blocks.shape[0]
-    width = blocks.shape[1]
-    depth = blocks.shape[2]
+    owned, width, depth = blocks.shape
     capacity = max(2, (2 * UNIQ + holders - 1) // holders)
     holder = wanted // owned
     local_ids = wanted - holder * owned
@@ -48,17 +258,15 @@
     integrals = lax.psum_scatter(
         partial_value.astype(jnp.bfloat16), "aux", scatter_dimension=0, tiled=True
     ).astype(jnp.float32)
-    fock_amp = jnp.einsum(
-        "pab,pbc->pac", fock, amplitudes, preferred_element_type=jnp.float32
-    ).astype(jnp.bfloat16)
-    over_amp = jnp.einsum(
-        "pab,pbc->pac", correlation, amplitudes, preferred_element_type=jnp.float32
-    ).astype(jnp.bfloat16)
-    first_term = jnp.einsum(
-        "pab,pbc->pac", fock_amp, correlation, preferred_element_type=jnp.float32
-    )
-    second_term = jnp.einsum("pab,pbc->pac", over_amp, fock, preferred_element_type=jnp.float32)
-    return (integrals + first_term + second_term).astype(jnp.bfloat16)
+    terms = pair_terms(fock, correlation, amplitudes)
+    return (integrals + terms).astype(jnp.bfloat16)
+
+
+def on_device(blocks, *others):
+    holders = lax.axis_size("pairs")
+    even = holders & (holders - 1) == 0 and blocks.shape[2] % (TILE * holders) == 0
+    body = split_by_columns if even and holders <= UNIQ else by_request
+    return body(blocks, *others)
 
 
 def solution(mesh):

time: 353 us -> 180 us (0.51)
  waiting for transfers between devices: 233 us -> 54.9 us
  blocking collectives: 13.5 us -> 70.1 us
  local copies, waits for them, and re-layouts: 54.2 us -> 7.79 us
  matrix products: 21.2 us -> 0 us
  starting transfers between devices: 5.31 us -> 24.2 us
  Pallas kernels: 0 us -> 17.9 us
  between operations: 13.5 us -> 0.8 us
  other arithmetic: 12 us -> 2.09 us
    all_to_all x1 -> x0, waiting for transfers between devices: 227 us -> none  [on_device(): lax.all_to_all(outgoing, 'pairs', split_axis=0, concat_axis=0, tiled=True)]
    unnamed x0 -> x1, blocking collectives: none -> 70.1 us
    ppermute x0 -> x16, waiting for transfers between devices: none -> 54.9 us  [swap(): return lax.ppermute(value, axis, [(i, i ^ bit) for i in range(size)])]
    gather x3 -> x1, local copies, waits for them, and re-layouts: 27.4 us -> 0.56 us  [split_by_columns(): asked = jnp.take(everyone, owners, axis=0)]
    convert_element_type x2 -> x0, local copies, waits for them, and re-layouts: 25.8 us -> none  [on_device(): partial_value.astype(jnp.bfloat16)]
    ppermute x0 -> x16, starting transfers between devices: none -> 24.2 us  [swap(): return lax.ppermute(value, axis, [(i, i ^ bit) for i in range(size)])]
    dot_general x3 -> x0, matrix products: 21.2 us -> none  [the longest x1 15.4 us: pair_integrals(): lax.dot_general(stacked, stacked, (((1,), (1,)), ((), ())), preferred_ele...]
    pallas_call x0 -> x3, Pallas kernels: none -> 17.9 us  [the longest x1 9.49 us: partial_grams(): pl.pallas_call(functools.partial(gram_kernel, holders), in_specs=[SMEM_SP...]
  transfers between devices with their start and end apart: 2 -> 16, of which waited for: 2 -> 7; matrix products, arithmetic and copies ran while one was open for 1% -> 1% of each run, Pallas kernels for 0% -> 2%
where the time goes in v1:
time: 180 us; the launch traced here: 178 us
  blocking collectives  70.1 us (39%)
  waiting for transfers between devices  54.9 us (30%)
  starting transfers between devices  24.2 us (13%)
  Pallas kernels  17.9 us (10%)
  local copies, waits for them, and re-layouts  7.79 us (4%)
  other arithmetic  2.09 us (1%)
    unnamed x1, blocking collectives  70.1 us
    ppermute x16, waiting for transfers between devices, swap(): return lax.ppermute(value, axis, [(i, i ^ bit) for i in range(size)])  54.9 us
    ppermute x16, starting transfers between devices, swap(): return lax.ppermute(value, axis, [(i, i ^ bit) for i in range(size)])  24.2 us
    pallas_call x1, Pallas kernels, partial_grams(): pl.pallas_call(functools.partial(gram_kernel, holders), in_specs=[SMEM_SP...  9.49 us
    pallas_call x1, Pallas kernels, finish(): pl.pallas_call(finish_kernel, grid=(pairs,), in_specs=[SMEM_SPEC, SMEM_SP...  4.6 us
    dynamic_slice x1, local copies, waits for them, and re-layouts, split_by_columns(): part = lax.dynamic_slice_in_dim(blocks, (me ^ k) * columns, columns, axis=2)  4.09 us
    pallas_call x1, Pallas kernels, pair_terms(): pl.pallas_call(terms_kernel, grid=(pairs,), in_specs=[spec] * 3, out_spec...  3.84 us
  transfers between devices with their start and end apart: 16, of which 7 were waited for; matrix products, arithmetic and copies ran while one was open for 1% of the time, Pallas kernels for 2%

profile of v1, /device:TPU:0, one launch (start us, length us, event | category | flops | bytes accessed | tf_op | source)
XLA Modules:
  0.0 177.8 jit_solution(10340619196066129054)
XLA Ops:
  0.0 4.1 %constant_dynamic-slice_fusion = (bf16[16,32,640]{2,1,0:T(8,128)(2,1)}, bf16[16,32,640]{2,1,0:T(8,128)(2,1)}, bf16[16,32,640]{2,1,0:T(8,128)(2,1)}, bf16[16,32,6...) fusion(bf16[16,32,5120]{2,1,0:T(8,128)(2,1)} %blocks_ref.1, ...), kind=kLoop, calls=%fused_computation.36 | loop fusion | bytes 9175068 | tf_op jit(solution)/shard_map/dynamic_slice | solution.py:200
  4.1 3.0 %collective-permute-start = (bf16[16,32,640]{2,1,0:T(8,128)(2,1)S(1)}, bf16[16,32,640]{2,1,0:T(8,128)(2,1)S(1)}, u32[]{:S(2)}, u32[]{:S(2)}) collective-permute-start(bf16[16,32,640]{2,1,0:T(8,128)(2,1)S(1)} %get-tuple-element.15), channel_id=1, source_target_pairs={{0,2},{2,0},{4,6},{6,4},{8,10},{10,8},{12,14},{14,12},{1,3},{3,1},... | collective-permute-start | bytes 1966088 | tf_op jit(solution)/shard_map/ppermute | solution.py:188
  7.1 1.6 collective-permute-start.1
  8.6 0.0 collective-permute-start.2
  8.6 3.0 %collective-permute-start.3 = (bf16[16,32,640]{2,1,0:T(8,128)(2,1)}, bf16[16,32,640]{2,1,0:T(8,128)(2,1)S(1)}, u32[]{:S(2)}, u32[]{:S(2)}) collective-permute-start(bf16[16,32,640]{2,1,0:T(8,128)(2,1)} %get-tuple-element.12), channel_id=1, source_target_pairs={{0,8},{2,10},{4,12},{6,14},{8,0},{10,2},{12,4},{14,6},{1,9},{3,11}... | collective-permute-start | bytes 1966088 | tf_op jit(solution)/shard_map/ppermute | solution.py:188
  11.6 1.3 collective-permute-start.4
  12.9 8.9 %collective-permute-done.rest_0_ = bf16[16,32,640]{2,1,0:T(8,128)(2,1)S(1)} collective-permute-done((bf16[16,32,640]{2,1,0:T(8,128)(2,1)S(1)}, bf16[16,32,640]{2,1,0:T(8,128)(2,1)S(1)}, u32[]{:S(2)}, u32[]{:S(2)}) %collective-permute-start) | collective-permute-done | bytes 655392 | tf_op jit(solution)/shard_map/ppermute | solution.py:188
  21.8 3.8 %collective-permute-start.5 = (bf16[16,32,640]{2,1,0:T(8,128)(2,1)}, bf16[16,32,640]{2,1,0:T(8,128)(2,1)}, u32[]{:S(2)}, u32[]{:S(2)}) collective-permute-start(bf16[16,32,640]{2,1,0:T(8,128)(2,1)} %get-tuple-element.10), channel_id=1, source_target_pairs={{0,12},{2,14},{4,8},{6,10},{8,4},{10,6},{12,0},{14,2},{1,13},{3,15... | collective-permute-start | bytes 1966088 | tf_op jit(solution)/shard_map/ppermute | solution.py:188
  25.6 26.1 %collective-permute-done.1.rest_1_ = bf16[16,32,640]{2,1,0:T(8,128)(2,1)S(1)} collective-permute-done((bf16[16,32,640]{2,1,0:T(8,128)(2,1)S(1)}, bf16[16,32,640]{2,1,0:T(8,128)(2,1)S(1)}, u32[]{:S(2)}, u32[]{:S(2)}) %collective-permute-start.1) | collective-permute-done | bytes 655392 | tf_op jit(solution)/shard_map/ppermute | solution.py:188
  51.8 0.9 collective-permute-start.6
  52.7 0.6 dynamic-slice
  53.9 0.2 dynamic-update-slice
  54.1 70.1 %all-reduce = s32[128]{0:T(128)S(1)} all-reduce(s32[128]{0:T(128)S(1)} %dynamic-update-slice), channel_id=2, replica_groups=mesh['groups'=2,'pairs'=8,'aux'=2] {'pairs'}, use_global_device_ids=true, to_apply=%add | all-reduce | flops 128 | bytes 1024
  124.3 0.1 reshape.77
  124.4 0.6 gather_fusion
  124.9 0.1 fusion.9.addr_ref
  125.0 0.0 collective-permute-done.2.rest_2_
  125.0 0.0 collective-permute-done.3.rest_3_
  125.0 0.0 collective-permute-done.4.rest_4_
  125.0 0.0 collective-permute-done.5.rest_5_
  125.1 0.0 collective-permute-done.6.rest_6_
  125.1 9.5 %shard_map.64 = (bf16[8,640,128]{2,1,0:T(8,128)(2,1)S(1)}, bf16[8,640,128]{2,1,0:T(8,128)(2,1)}) custom-call(s32[8,16]{1,0:T(8,128)S(1)} %fusion.9.addr_ref, s32[1]{0:T(128)} %bitcast.core_ref, s32[1]{0:T(128)} %bitcast.3.place_ref, bf16[16,32,5120]{2,1,0:T(8,128)(2,1)} %blocks_ref.1, bf16[16,32,640]{2,1,0:T(8,128)(2,1)S(1)} %collective-permute-done.rest_0_, ...), custom_call_target="tpu_custom_call" | custom-call | flops 2684354560 | bytes 5242880 | tf_op jit(solution)/shard_map/pallas_call | solution.py:107
  134.6 0.1 collective-permute-start.7
  134.6 3.2 %collective-permute-done.7 = bf16[8,640,128]{2,1,0:T(8,128)(2,1)S(1)} collective-permute-done((bf16[8,640,128]{2,1,0:T(8,128)(2,1)}, bf16[8,640,128]{2,1,0:T(8,128)(2,1)S(1)}, u32[]{:S(2)}, u32[]{:S(2)}) %collective-permute-start.7) | collective-permute-done | bytes 1310752 | tf_op jit(solution)/shard_map/ppermute | solution.py:188
  137.9 0.3 add_convert_fusion
  138.2 1.1 copy-done.4
  139.3 0.9 slice_bitcast_fusion.6
  140.2 1.8 %collective-permute-start.10 = (bf16[640,128]{1,0:T(8,128)(2,1)}, bf16[640,128]{1,0:T(8,128)(2,1)}, u32[]{:S(2)}, u32[]{:S(2)}) collective-permute-start(bf16[640,128]{1,0:T(8,128)(2,1)} %get-tuple-element.21), channel_id=1, source_target_pairs={{0,6},{2,4},{4,2},{6,0},{8,14},{10,12},{12,10},{14,8},{1,7},{3,5},... | collective-permute-start | bytes 491528 | tf_op jit(solution)/shard_map/ppermute | solution.py:188
  142.0 3.3 %collective-permute-start.11 = (bf16[640,128]{1,0:T(8,128)(2,1)}, bf16[640,128]{1,0:T(8,128)(2,1)}, u32[]{:S(2)}, u32[]{:S(2)}) collective-permute-start(bf16[640,128]{1,0:T(8,128)(2,1)} %get-tuple-element.20), channel_id=1, source_target_pairs={{0,8},{2,10},{4,12},{6,14},{8,0},{10,2},{12,4},{14,6},{1,9},{3,11}... | collective-permute-start | bytes 491528 | tf_op jit(solution)/shard_map/ppermute | solution.py:188
  145.3 0.0 collective-permute-start.12
  145.4 3.1 %collective-permute-start.13 = (bf16[640,128]{1,0:T(8,128)(2,1)}, bf16[640,128]{1,0:T(8,128)(2,1)}, u32[]{:S(2)}, u32[]{:S(2)}) collective-permute-start(bf16[640,128]{1,0:T(8,128)(2,1)} %get-tuple-element.18), channel_id=1, source_target_pairs={{0,12},{2,14},{4,8},{6,10},{8,4},{10,6},{12,0},{14,2},{1,13},{3,15... | collective-permute-start | bytes 491528 | tf_op jit(solution)/shard_map/ppermute | solution.py:188
  148.4 1.7 collective-permute-start.14
  150.1 1.3 collective-permute-done.10
  151.4 0.5 collective-permute-start.8
  151.9 12.8 %collective-permute-done.11 = bf16[640,128]{1,0:T(8,128)(2,1)} collective-permute-done((bf16[640,128]{1,0:T(8,128)(2,1)}, bf16[640,128]{1,0:T(8,128)(2,1)}, u32[]{:S(2)}, u32[]{:S(2)}) %collective-permute-start.11) | collective-permute-done | bytes 163872 | tf_op jit(solution)/shard_map/ppermute | solution.py:188
  164.8 0.0 collective-permute-start.9
  164.8 0.1 slice_multiply_fusion
  164.8 0.1 add.119
  164.9 0.1 add.120
  165.0 0.1 add.122
  165.1 3.8 %shard_map.65.terms_ref = f32[8,256,256]{2,1,0:T(8,128)S(1)} custom-call(bf16[8,256,256]{2,1,0:T(8,128)(2,1)S(1)} %copy-done.1, bf16[8,256,256]{2,1,0:T(8,128)(2,1)S(1)} %copy-done.2, bf16[8,256,256]{2,1,0:T(8,128)(2,1)S(1)} %copy-done.3), custom_call_target="tpu_custom_call" | custom-call | flops 1073741824 | bytes 5242880 | tf_op jit(solution)/shard_map/pallas_call | solution.py:34
  169.0 0.0 collective-permute-done.13
  169.0 0.0 collective-permute-done.14
  169.0 1.2 collective-permute-done.9
  170.2 1.6 fusion.6.mine_ref
  171.8 0.1 collective-permute-start.15
  171.8 1.4 collective-permute-done.15.other_ref
  173.2 4.6 %shard_map.66 = bf16[8,256,256]{2,1,0:T(8,128)(2,1)} custom-call(s32[8,16]{1,0:T(8,128)S(1)} %constant_dynamic-slice_fusion.7.slots_ref, s32[1]{0:T(128)} %bitcast.core_ref, bf16[640,128]{1,0:T(8,128)(2,1)S(1)} %fusion.6.mine_ref, bf16[640,128]{1,0:T(8,128)(2,1)S(1)} %collective-permute-done.15.other_ref, s32[8,1,256]{2,1,0:T(1,128)S(1)} %broadcast_add_fusion.right_ref, ...), custom_call_target="tpu_custom_call" | custom-call | flops 536870912 | bytes 3145728 | tf_op jit(solution)/shard_map/pallas_call | solution.py:163
  (22 shorter events, 0.1 us)
Async XLA Ops:
  0.0 145.3 %copy-start = (s32[16,16]{1,0:T(8,128)S(1)}, s32[16,16]{1,0:T(8,128)}, u32[]{:S(2)}) copy-start(s32[16,16]{1,0:T(8,128)} %param.8) | copy-start | bytes 3076
  0.0 52.6 %copy-start.6 = (u32[32]{0:T(128)S(1)}, u32[32]{0:T(128)}, u32[]{:S(2)}) copy-start(u32[32]{0:T(128)} %constant.76) | copy-start | bytes 388
  0.0 53.9 %copy-start.5 = (s32[16]{0:T(128)S(1)}, s32[16]{0:T(128)}, u32[]{:S(2)}) copy-start(s32[16]{0:T(128)} %param.7) | copy-start | bytes 196
  4.1 17.7 %collective-permute-start = (bf16[16,32,640]{2,1,0:T(8,128)(2,1)S(1)}, bf16[16,32,640]{2,1,0:T(8,128)(2,1)S(1)}, u32[]{:S(2)}, u32[]{:S(2)}) collective-permute-start(bf16[16,32,640]{2,1,0:T(8,128)(2,1)S(1)} %get-tuple-element.15), channel_id=1, source_target_pairs={{0,2},{2,0},{4,6},{6,4},{8,10},{10,8},{12,14},{14,12},{1,3},{3,1},... | collective-permute-start | bytes 1966088 | tf_op jit(solution)/shard_map/ppermute | solution.py:188
  7.1 44.7 %collective-permute-start.1 = (bf16[16,32,640]{2,1,0:T(8,128)(2,1)S(1)}, bf16[16,32,640]{2,1,0:T(8,128)(2,1)S(1)}, u32[]{:S(2)}, u32[]{:S(2)}) collective-permute-start(bf16[16,32,640]{2,1,0:T(8,128)(2,1)S(1)} %get-tuple-element.14), channel_id=1, source_target_pairs={{0,4},{2,6},{4,0},{6,2},{8,12},{10,14},{12,8},{14,10},{1,5},{3,7},... | collective-permute-start | bytes 1966088 | tf_op jit(solution)/shard_map/ppermute | solution.py:188
  8.6 116.4 %collective-permute-start.2 = (bf16[16,32,640]{2,1,0:T(8,128)(2,1)}, bf16[16,32,640]{2,1,0:T(8,128)(2,1)S(1)}, u32[]{:S(2)}, u32[]{:S(2)}) collective-permute-start(bf16[16,32,640]{2,1,0:T(8,128)(2,1)} %get-tuple-element.13), channel_id=1, source_target_pairs={{0,6},{2,4},{4,2},{6,0},{8,14},{10,12},{12,10},{14,8},{1,7},{3,5},... | collective-permute-start | bytes 1966088 | tf_op jit(solution)/shard_map/ppermute | solution.py:188
  8.6 116.4 %collective-permute-start.3 = (bf16[16,32,640]{2,1,0:T(8,128)(2,1)}, bf16[16,32,640]{2,1,0:T(8,128)(2,1)S(1)}, u32[]{:S(2)}, u32[]{:S(2)}) collective-permute-start(bf16[16,32,640]{2,1,0:T(8,128)(2,1)} %get-tuple-element.12), channel_id=1, source_target_pairs={{0,8},{2,10},{4,12},{6,14},{8,0},{10,2},{12,4},{14,6},{1,9},{3,11}... | collective-permute-start | bytes 1966088 | tf_op jit(solution)/shard_map/ppermute | solution.py:188
  11.6 113.4 %collective-permute-start.4 = (bf16[16,32,640]{2,1,0:T(8,128)(2,1)}, bf16[16,32,640]{2,1,0:T(8,128)(2,1)S(1)}, u32[]{:S(2)}, u32[]{:S(2)}) collective-permute-start(bf16[16,32,640]{2,1,0:T(8,128)(2,1)} %get-tuple-element.11), channel_id=1, source_target_pairs={{0,10},{2,8},{4,14},{6,12},{8,2},{10,0},{12,6},{14,4},{1,11},{3,9}... | collective-permute-start | bytes 1966088 | tf_op jit(solution)/shard_map/ppermute | solution.py:188
  21.8 103.3 %collective-permute-start.5 = (bf16[16,32,640]{2,1,0:T(8,128)(2,1)}, bf16[16,32,640]{2,1,0:T(8,128)(2,1)}, u32[]{:S(2)}, u32[]{:S(2)}) collective-permute-start(bf16[16,32,640]{2,1,0:T(8,128)(2,1)} %get-tuple-element.10), channel_id=1, source_target_pairs={{0,12},{2,14},{4,8},{6,10},{8,4},{10,6},{12,0},{14,2},{1,13},{3,15... | collective-permute-start | bytes 1966088 | tf_op jit(solution)/shard_map/ppermute | solution.py:188
  51.8 73.3 %collective-permute-start.6 = (bf16[16,32,640]{2,1,0:T(8,128)(2,1)}, bf16[16,32,640]{2,1,0:T(8,128)(2,1)}, u32[]{:S(2)}, u32[]{:S(2)}) collective-permute-start(bf16[16,32,640]{2,1,0:T(8,128)(2,1)} %get-tuple-element.9), channel_id=1, source_target_pairs={{0,14},{2,12},{4,10},{6,8},{8,6},{10,4},{12,2},{14,0},{1,15},{3,13... | collective-permute-start | bytes 1966088 | tf_op jit(solution)/shard_map/ppermute | solution.py:188
  134.6 3.3 %collective-permute-start.7 = (bf16[8,640,128]{2,1,0:T(8,128)(2,1)}, bf16[8,640,128]{2,1,0:T(8,128)(2,1)S(1)}, u32[]{:S(2)}, u32[]{:S(2)}) collective-permute-start(bf16[8,640,128]{2,1,0:T(8,128)(2,1)} %get-tuple-element.8), channel_id=1, source_target_pairs={{0,1},{1,0},{2,3},{3,2},{4,5},{5,4},{6,7},{7,6},{8,9},{9,8},{10,11... | collective-permute-start | bytes 3932168 | tf_op jit(solution)/shard_map/ppermute | solution.py:188
  137.9 27.2 %copy-start.3 = (bf16[8,256,256]{2,1,0:T(8,128)(2,1)S(1)}, bf16[8,256,256]{2,1,0:T(8,128)(2,1)}, u32[]{:S(2)}) copy-start(bf16[8,256,256]{2,1,0:T(8,128)(2,1)} %amp_ref.1) | copy-start | bytes 3145732
  138.2 1.1 copy-start.4
  139.3 25.8 %copy-start.1 = (bf16[8,256,256]{2,1,0:T(8,128)(2,1)S(1)}, bf16[8,256,256]{2,1,0:T(8,128)(2,1)}, u32[]{:S(2)}) copy-start(bf16[8,256,256]{2,1,0:T(8,128)(2,1)} %fock_ref.1) | copy-start | bytes 3145732
  139.3 25.8 %copy-start.2 = (bf16[8,256,256]{2,1,0:T(8,128)(2,1)S(1)}, bf16[8,256,256]{2,1,0:T(8,128)(2,1)}, u32[]{:S(2)}) copy-start(bf16[8,256,256]{2,1,0:T(8,128)(2,1)} %corr_ref.1) | copy-start | bytes 3145732
  140.2 11.2 %collective-permute-start.10 = (bf16[640,128]{1,0:T(8,128)(2,1)}, bf16[640,128]{1,0:T(8,128)(2,1)}, u32[]{:S(2)}, u32[]{:S(2)}) collective-permute-start(bf16[640,128]{1,0:T(8,128)(2,1)} %get-tuple-element.21), channel_id=1, source_target_pairs={{0,6},{2,4},{4,2},{6,0},{8,14},{10,12},{12,10},{14,8},{1,7},{3,5},... | collective-permute-start | bytes 491528 | tf_op jit(solution)/shard_map/ppermute | solution.py:188
  142.0 22.7 %collective-permute-start.11 = (bf16[640,128]{1,0:T(8,128)(2,1)}, bf16[640,128]{1,0:T(8,128)(2,1)}, u32[]{:S(2)}, u32[]{:S(2)}) collective-permute-start(bf16[640,128]{1,0:T(8,128)(2,1)} %get-tuple-element.20), channel_id=1, source_target_pairs={{0,8},{2,10},{4,12},{6,14},{8,0},{10,2},{12,4},{14,6},{1,9},{3,11}... | collective-permute-start | bytes 491528 | tf_op jit(solution)/shard_map/ppermute | solution.py:188
  145.3 23.6 %collective-permute-start.12 = (bf16[640,128]{1,0:T(8,128)(2,1)}, bf16[640,128]{1,0:T(8,128)(2,1)}, u32[]{:S(2)}, u32[]{:S(2)}) collective-permute-start(bf16[640,128]{1,0:T(8,128)(2,1)} %get-tuple-element.19), channel_id=1, source_target_pairs={{0,10},{2,8},{4,14},{6,12},{8,2},{10,0},{12,6},{14,4},{1,11},{3,9}... | collective-permute-start | bytes 491528 | tf_op jit(solution)/shard_map/ppermute | solution.py:188
  145.4 23.6 %collective-permute-start.13 = (bf16[640,128]{1,0:T(8,128)(2,1)}, bf16[640,128]{1,0:T(8,128)(2,1)}, u32[]{:S(2)}, u32[]{:S(2)}) collective-permute-start(bf16[640,128]{1,0:T(8,128)(2,1)} %get-tuple-element.18), channel_id=1, source_target_pairs={{0,12},{2,14},{4,8},{6,10},{8,4},{10,6},{12,0},{14,2},{1,13},{3,15... | collective-permute-start | bytes 491528 | tf_op jit(solution)/shard_map/ppermute | solution.py:188
  148.4 20.6 %collective-permute-start.14 = (bf16[640,128]{1,0:T(8,128)(2,1)}, bf16[640,128]{1,0:T(8,128)(2,1)}, u32[]{:S(2)}, u32[]{:S(2)}) collective-permute-start(bf16[640,128]{1,0:T(8,128)(2,1)} %get-tuple-element.17), channel_id=1, source_target_pairs={{0,14},{2,12},{4,10},{6,8},{8,6},{10,4},{12,2},{14,0},{1,15},{3,13... | collective-permute-start | bytes 491528 | tf_op jit(solution)/shard_map/ppermute | solution.py:188
  151.4 17.6 %collective-permute-start.8 = (bf16[640,128]{1,0:T(8,128)(2,1)S(1)}, bf16[640,128]{1,0:T(8,128)(2,1)}, u32[]{:S(2)}, u32[]{:S(2)}) collective-permute-start(bf16[640,128]{1,0:T(8,128)(2,1)S(1)} %get-tuple-element.16), channel_id=1, source_target_pairs={{0,2},{2,0},{4,6},{6,4},{8,10},{10,8},{12,14},{14,12},{1,3},{3,1},... | collective-permute-start | bytes 491528 | tf_op jit(solution)/shard_map/ppermute | solution.py:188
  164.8 5.4 %collective-permute-start.9 = (bf16[640,128]{1,0:T(8,128)(2,1)S(1)}, bf16[640,128]{1,0:T(8,128)(2,1)}, u32[]{:S(2)}, u32[]{:S(2)}) collective-permute-start(bf16[640,128]{1,0:T(8,128)(2,1)S(1)} %get-tuple-element.22), channel_id=1, source_target_pairs={{0,4},{2,6},{4,0},{6,2},{8,12},{10,14},{12,8},{14,10},{1,5},{3,7},... | collective-permute-start | bytes 491528 | tf_op jit(solution)/shard_map/ppermute | solution.py:188
  171.8 1.5 collective-permute-start.15

commit v2 on v1

--- a/solution.py
+++ b/solution.py
@@ -10,10 +10,14 @@
 DOM = 8
 UNIQ = 16
 TILE = 128
-VMEM_BYTES = 48 * 1024 * 1024
+STRIP = 256
+LIST_ROWS = 16
+VMEM_BYTES = 60 * 1024 * 1024
+LAST_VMEM = 24 * 1024 * 1024
+FIRST = 448
 SMEM_SPEC = pl.BlockSpec(memory_space=pltpu.SMEM)
 VMEM_SPEC = pl.BlockSpec(memory_space=pltpu.VMEM)
-ANY_SPEC = pl.BlockSpec(memory_space=pl.ANY)
+HBM_SPEC = pl.BlockSpec(memory_space=pltpu.HBM)
 
 
 def upper_tiles(side):
@@ -46,81 +50,185 @@
     )(fock, correlation, amplitudes)
 
 
-def gram_kernel(holders, addr_ref, core_ref, place_ref, blocks_ref, *rest):
+def split_kernel(offsets, wanted_ref, place_ref, core_ref, blocks_ref, *rest):
+    count = (len(rest) - 3) // 2
+    outs, bufs, (tail, in_sems, out_sems) = rest[:count], rest[count : 2 * count], rest[-3:]
+    rows, depth = blocks_ref.shape
+    chunks = (outs[0].shape[0] - LIST_ROWS) // rows
+    lane = lax.broadcasted_iota(jnp.int32, tail.shape, 1)
+
+    def fetch(n, c):
+        offset = jnp.where(core_ref[0] % 2 == 0, offsets[0][n], offsets[1][n])
+        start = pl.multiple_of(((place_ref[0] ^ offset) * chunks + c) * TILE, TILE)
+        return pltpu.make_async_copy(
+            blocks_ref.at[:, pl.ds(start, TILE)],
+            bufs[n].at[pl.ds(c * rows, rows)],
+            in_sems.at[n, c],
+        )
+
+    fetches = [[fetch(n, c) for c in range(chunks)] for n in range(count)]
+    for some in fetches:
+        for copy in some:
+            copy.start()
+    ids = jnp.zeros(tail.shape, jnp.int32)
+    for m in range(UNIQ):
+        ids = jnp.where(lane == m, wanted_ref[m], ids)
+    tail[...] = ids.astype(jnp.float32).astype(jnp.bfloat16)
+    for buf in bufs:
+        buf[chunks * rows :, :] = tail[...]
+    stores = []
+    for n, (buf, out) in enumerate(zip(bufs, outs)):
+        for copy in fetches[n]:
+            copy.wait()
+        stores.append(pltpu.make_async_copy(buf, out, out_sems.at[n]))
+        stores[-1].start()
+    for copy in stores:
+        copy.wait()
+
+
+def column_parts(offsets, holders, wanted, place, core, blocks):
+    rows, depth = blocks.shape
+    chunks = depth // holders // TILE
+    shape = (chunks * rows + LIST_ROWS, TILE)
+    count = len(offsets[0])
+    return pl.pallas_call(
+        functools.partial(split_kernel, offsets),
+        in_specs=[SMEM_SPEC] * 3 + [HBM_SPEC],
+        out_specs=[HBM_SPEC] * count,
+        out_shape=[jax.ShapeDtypeStruct(shape, blocks.dtype)] * count,
+        scratch_shapes=[
+            *([pltpu.VMEM(shape, blocks.dtype)] * count),
+            pltpu.VMEM((LIST_ROWS, TILE), blocks.dtype),
+            pltpu.SemaphoreType.DMA((count, chunks)),
+            pltpu.SemaphoreType.DMA((count,)),
+        ],
+        compiler_params=pltpu.CompilerParams(vmem_limit_bytes=VMEM_BYTES),
+    )(wanted, place, core, blocks)
+
+
+def gram_kernel(ks, owned, wanted_ref, core_ref, place_ref, slot_ref, blocks_ref, *rest):
+    holders = 1 + len(rest) - 8
     arrived_refs = rest[: holders - 1]
-    keep_ref, send_ref, pool, rows_ref, sems = rest[holders - 1 :]
-    owned, width, depth = blocks_ref.shape
-    columns = depth // holders
-    start = pl.multiple_of(place_ref[0] * columns, TILE)
-    copies = [
-        pltpu.make_async_copy(
-            blocks_ref.at[:, :, pl.ds(start, columns)], pool.at[pl.ds(0, owned)], sems.at[0]
+    keep_ref, send_ref, pool, lists, ids_vmem, ids, sems, list_sems = rest[holders - 1 :]
+    rows, depth = blocks_ref.shape
+    width = rows // owned
+    chunks = depth // holders // TILE
+    part = chunks * rows
+    me = place_ref[0]
+    tails = [
+        pltpu.make_async_copy(ref.at[pl.ds(part, LIST_ROWS)], lists.at[k], list_sems.at[k])
+        for k, ref in enumerate(arrived_refs, 1)
+    ]
+    for copy in tails:
+        copy.start()
+    copies = []
+    for c in range(chunks):
+        start = pl.multiple_of((me * chunks + c) * TILE, TILE)
+        copies.append(
+            pltpu.make_async_copy(
+                blocks_ref.at[:, pl.ds(start, TILE)], pool.at[pl.ds(c * rows, rows)], sems.at[0, c]
+            )
         )
-    ]
     for k, ref in enumerate(arrived_refs, 1):
         copies.append(
-            pltpu.make_async_copy(ref, pool.at[pl.ds(k * owned, owned)], sems.at[k])
+            pltpu.make_async_copy(
+                ref.at[pl.ds(0, part)], pool.at[pl.ds(k * part, part)], sems.at[k, 0]
+            )
         )
     for copy in copies:
         copy.start()
+    for copy in tails:
+        copy.wait()
+    for n, k in enumerate(ks):
+        if k > 0:
+            ids_vmem[n, :] = lists[slot_ref[k]].astype(jnp.float32).astype(jnp.int32)[0]
+    to_scalars = pltpu.make_async_copy(ids_vmem, ids, list_sems.at[0])
+    to_scalars.start()
+    to_scalars.wait()
+    for n, k in enumerate(ks):
+        if k == 0:
+            for m in range(UNIQ):
+                ids[n, m] = wanted_ref[m]
     for copy in copies:
         copy.wait()
     side = UNIQ * width // TILE
     half = len(upper_tiles(side)) // 2
     core = core_ref[0]
 
-    @pl.loop(0, holders)
-    def _(k):
+    @pl.loop(0, len(ks))
+    def _(n):
+        places = []
         for m in range(UNIQ):
-            rows_ref[m * width : (m + 1) * width, :] = pool[addr_ref[k, m]]
-        tiles = []
-        for i in range(side):
+            holder = lax.div(ids[n, m], owned)
+            local = ids[n, m] - holder * owned
+            places.append(slot_ref[holder ^ me] * part + local * width)
+        held = jnp.concatenate(
+            [
+                jnp.concatenate(
+                    [
+                        pool[pl.ds(pl.multiple_of(place + c * rows, width), width), :]
+                        for place in places
+                    ],
+                    axis=0,
+                )
+                for c in range(chunks)
+            ],
+            axis=1,
+        )
+        found = {}
+        for top in range(0, side * TILE, STRIP):
             strip = lax.dot_general(
-                rows_ref[i * TILE : (i + 1) * TILE, :],
-                rows_ref[i * TILE :, :],
+                held[top : top + STRIP],
+                held[top:],
                 (((1,), (1,)), ((), ())),
                 preferred_element_type=jnp.float32,
             ).astype(jnp.bfloat16)
-            for j in range(i, side):
-                tiles.append(strip[:, (j - i) * TILE : (j - i + 1) * TILE])
+            for i in range(top // TILE, min(top + STRIP, side * TILE) // TILE):
+                for j in range(i, side):
+                    r, c = i * TILE - top, j * TILE - top
+                    found[i, j] = strip[r : r + TILE, c : c + TILE]
+        tiles = [found[t] for t in upper_tiles(side)]
 
         @pl.when(core == 0)
         def _():
             for t in range(half):
-                keep_ref[k, t * TILE : (t + 1) * TILE, :] = tiles[t]
-                send_ref[k, t * TILE : (t + 1) * TILE, :] = tiles[half + t]
+                keep_ref[n, t * TILE : (t + 1) * TILE, :] = tiles[t]
+                send_ref[n, t * TILE : (t + 1) * TILE, :] = tiles[half + t]
 
         @pl.when(core != 0)
         def _():
             for t in range(half):
-                send_ref[k, t * TILE : (t + 1) * TILE, :] = tiles[t]
-                keep_ref[k, t * TILE : (t + 1) * TILE, :] = tiles[half + t]
-
-
-def partial_grams(addr, core, place, blocks, arrived):
+                send_ref[n, t * TILE : (t + 1) * TILE, :] = tiles[t]
+                keep_ref[n, t * TILE : (t + 1) * TILE, :] = tiles[half + t]
+
+
+def partial_grams(ks, owned, wanted, core, place, slot, blocks, arrived):
     holders = len(arrived) + 1
-    owned, width, depth = blocks.shape
+    rows, depth = blocks.shape
     columns = depth // holders
-    side = UNIQ * width // TILE
+    side = UNIQ * rows // owned // TILE
     half = len(upper_tiles(side)) // 2
-    out = jax.ShapeDtypeStruct((holders, half * TILE, TILE), jnp.bfloat16)
+    out = jax.ShapeDtypeStruct((len(ks), half * TILE, TILE), jnp.bfloat16)
     return pl.pallas_call(
-        functools.partial(gram_kernel, holders),
-        in_specs=[SMEM_SPEC] * 3 + [ANY_SPEC] * holders,
+        functools.partial(gram_kernel, ks, owned),
+        in_specs=[SMEM_SPEC] * 4 + [HBM_SPEC] * holders,
         out_specs=[VMEM_SPEC] * 2,
         out_shape=[out, out],
         scratch_shapes=[
-            pltpu.VMEM((holders * owned, width, columns), jnp.bfloat16),
-            pltpu.VMEM((UNIQ * width, columns), jnp.bfloat16),
+            pltpu.VMEM((holders * rows * columns // TILE, TILE), jnp.bfloat16),
+            pltpu.VMEM((holders, LIST_ROWS, TILE), jnp.bfloat16),
+            pltpu.VMEM((len(ks), TILE), jnp.int32),
+            pltpu.SMEM((len(ks), TILE), jnp.int32),
+            pltpu.SemaphoreType.DMA((holders, max(2, columns // TILE))),
             pltpu.SemaphoreType.DMA((holders,)),
         ],
         compiler_params=pltpu.CompilerParams(vmem_limit_bytes=VMEM_BYTES),
         cost_estimate=pl.CostEstimate(
-            flops=2 * holders * (UNIQ * width) ** 2 * columns,
-            bytes_accessed=2 * holders * owned * width * columns,
+            flops=2 * len(ks) * (side * TILE) ** 2 * columns,
+            bytes_accessed=2 * holders * rows * columns,
             transcendentals=0,
         ),
-    )(addr, core, place, blocks, *arrived)
+    )(wanted, core, place, slot, blocks, *arrived)
 
 
 def finish_kernel(slots_ref, core_ref, mine_ref, other_ref, right_ref, terms_ref, out_ref, gram):
@@ -174,7 +282,7 @@
         out_specs=tile,
         out_shape=jax.ShapeDtypeStruct(terms.shape, jnp.bfloat16),
         scratch_shapes=[pltpu.VMEM((gram_side, gram_side), jnp.bfloat16)],
-        compiler_params=pltpu.CompilerParams(vmem_limit_bytes=VMEM_BYTES),
+        compiler_params=pltpu.CompilerParams(vmem_limit_bytes=LAST_VMEM),
         cost_estimate=pl.CostEstimate(
             flops=2 * pairs * rows * cols * gram_side,
             bytes_accessed=6 * pairs * rows * cols,
@@ -188,33 +296,80 @@
     return lax.ppermute(value, axis, [(i, i ^ bit) for i in range(size)])
 
 
+def add(*values):
+    return sum(value.astype(jnp.float32) for value in values)
+
+
+def to_owner(keep, came):
+    half = keep.shape[0] // 2
+    keep, came = (v.reshape(2, half, *v.shape[1:]) for v in (keep, came))
+
+    def both(bits, offsets, rows):
+        return add(keep[bits, offsets, rows], came[bits, offsets, rows]).astype(jnp.bfloat16)
+
+    every, top, rest = slice(None), slice(0, FIRST), slice(FIRST, None)
+    top_near = swap(both(1, every, top), "pairs", 1)
+    rest_far = [swap(both(every, j, rest), "pairs", 2 * j) for j in range(1, half)]
+    top_sums = [
+        add(keep[0, j, top], came[0, j, top], top_near[j]).astype(jnp.bfloat16)
+        for j in range(half)
+    ]
+    top_far = [swap(top_sums[j], "pairs", 2 * j) for j in range(1, half)]
+    rest_sums = [
+        add(keep[b, 0, rest], came[b, 0, rest], *(v[b] for v in rest_far)).astype(jnp.bfloat16)
+        for b in range(2)
+    ]
+    rest_near = swap(rest_sums[1], "pairs", 1)
+    top_total = add(top_sums[0], *top_far).astype(jnp.bfloat16)
+    rest_total = add(rest_sums[0], rest_near).astype(jnp.bfloat16)
+    return jnp.concatenate([top_total, rest_total], axis=0)
+
+
+def exchange_orders(holders):
+    light, heavy = [*range(1, holders // 2)], [*range(holders // 2, holders)]
+    first = heavy[:1]
+    for pair in zip(heavy[1:], light):
+        first += pair
+    second = [k for pair in zip(light, heavy) for k in pair] + heavy[-1:]
+    return [first, second]
+
+
 def split_by_columns(blocks, wanted, pair_slots, fock, correlation, amplitudes):
     holders = lax.axis_size("pairs")
-    me = lax.axis_index("pairs")
     core = lax.axis_index("aux")
     owned, width, depth = blocks.shape
-    columns = depth // holders
-    everyone = lax.all_gather(wanted, "pairs", tiled=False)
+    stacked = blocks.reshape(owned * width, depth)
+    place = lax.axis_index("pairs").reshape(1).astype(jnp.int32)
+    core_id = core.reshape(1).astype(jnp.int32)
+    orders = exchange_orders(holders)
+    slot_tables = [[0] * holders for _ in orders]
+    for table, ks in zip(slot_tables, orders):
+        for n, k in enumerate(ks, 1):
+            table[k] = n
+    slot = jnp.asarray(slot_tables, jnp.int32)[core % 2]
+    early = 2
+    begun = column_parts([o[:early] for o in orders], holders, wanted, place, core_id, stacked)
+    begun, later = lax.optimization_barrier((begun, stacked))
+    parts = begun + column_parts([o[early:] for o in orders], holders, wanted, place, core_id, later)
     arrived = []
-    for k in range(1, holders):
-        part = lax.dynamic_slice_in_dim(blocks, (me ^ k) * columns, columns, axis=2)
-        arrived.append(swap(part, "pairs", k))
-    owners = me ^ jnp.arange(holders, dtype=jnp.int32)
-    asked = jnp.take(everyone, owners, axis=0)
-    addr = ((asked // owned) ^ me) * owned + asked % owned
+    cores = lax.axis_size("aux")
+    for n, part in enumerate(parts):
+        moves = [
+            (p * cores + c, (p ^ orders[c % 2][n]) * cores + c)
+            for p in range(holders)
+            for c in range(cores)
+        ]
+        arrived.append(lax.ppermute(part, ("pairs", "aux"), moves))
     pairs_here = fock.shape[0]
     slots = lax.dynamic_slice_in_dim(pair_slots, core * pairs_here, pairs_here, axis=0)
     offsets = jnp.arange(width, dtype=jnp.int32)
     right_rows = (slots[:, DOM:, None] * width + offsets).reshape(pairs_here, 1, DOM * width)
     terms = pair_terms(fock, correlation, amplitudes)
-    core_id = core.reshape(1).astype(jnp.int32)
-    keep, send = partial_grams(addr, core_id, me.reshape(1).astype(jnp.int32), blocks, arrived)
-    both = keep.astype(jnp.float32) + swap(send, "aux", 1).astype(jnp.float32)
-    both = both.astype(jnp.bfloat16)
-    total = both[0].astype(jnp.float32)
-    for k in range(1, holders):
-        total = total + swap(both[k], "pairs", k).astype(jnp.float32)
-    mine = total.astype(jnp.bfloat16)
+    arrived, terms = lax.optimization_barrier((arrived, terms))
+    shared = (owned, wanted, core_id, place, slot, stacked, arrived)
+    order = (*range(0, holders, 2), *range(1, holders, 2))
+    keep, send = partial_grams(order, *shared)
+    mine = to_owner(keep, swap(send, "aux", 1))
     other = swap(mine, "aux", 1)
     return finish(slots, core_id, mine, other, right_rows, terms)
 
@@ -264,9 +419,9 @@
 
 def on_device(blocks, *others):
     holders = lax.axis_size("pairs")
-    even = holders & (holders - 1) == 0 and blocks.shape[2] % (TILE * holders) == 0
-    body = split_by_columns if even and holders <= UNIQ else by_request
-    return body(blocks, *others)
+    even = holders > 1 and holders & (holders - 1) == 0
+    even = even and blocks.shape[2] % (TILE * holders) == 0 and holders * blocks.shape[0] <= 256
+    return (split_by_columns if even else by_request)(blocks, *others)
 
 
 def solution(mesh):

time: 180 us -> 175 us (0.972)
  blocking collectives: 70.1 us -> 0 us
  waiting for transfers between devices: 54.9 us -> 102 us
  Pallas kernels: 17.9 us -> 29.4 us
  starting transfers between devices: 24.2 us -> 35.2 us
  local copies, waits for them, and re-layouts: 7.79 us -> 3.38 us
  other arithmetic: 2.09 us -> 4.05 us
    ppermute x0 -> x7, waiting for transfers between devices: none -> 87.8 us  [split_by_columns(): arrived.append(lax.ppermute(part, ('pairs', 'aux'), moves))]
    unnamed x1 -> x0, blocking collectives: 70.1 us -> none
    ppermute x16 -> x10, waiting for transfers between devices: 54.9 us -> 14.5 us  [swap(): return lax.ppermute(value, axis, [(i, i ^ bit) for i in range(size)])]
    ppermute x0 -> x7, starting transfers between devices: none -> 24.4 us  [split_by_columns(): arrived.append(lax.ppermute(part, ('pairs', 'aux'), moves))]
    ppermute x16 -> x10, starting transfers between devices: 24.2 us -> 10.8 us  [swap(): return lax.ppermute(value, axis, [(i, i ^ bit) for i in range(size)])]
    pallas_call x1 -> x3, Pallas kernels: 9.49 us -> 17.1 us  [the longest x1 10 us: partial_grams(): pl.pallas_call(functools.partial(gram_kernel, ks, owned), in_specs=[SMEM_...]
    dynamic_slice x1 -> x0, local copies, waits for them, and re-layouts: 4.09 us -> none  [split_by_columns(): part = lax.dynamic_slice_in_dim(blocks, (me ^ k) * columns, columns, axis=2)]
    pallas_call x1, Pallas kernels: 3.84 us -> 7.68 us  [pair_terms(): pl.pallas_call(terms_kernel, grid=(pairs,), in_specs=[spec] * 3, out_spec...]
  transfers between devices with their start and end apart: 16 -> 17, of which waited for: 7 -> 11; matrix products, arithmetic and copies ran while one was open for 1% -> 3% of each run, Pallas kernels for 2% -> 4%
where the time goes in v2:
time: 175 us; the launch traced here: 174 us
  waiting for transfers between devices  102 us (58%)
  starting transfers between devices  35.2 us (20%)
  Pallas kernels  29.4 us (17%)
  other arithmetic  4.05 us (2%)
  local copies, waits for them, and re-layouts  3.38 us (2%)
    ppermute x7, waiting for transfers between devices, split_by_columns(): arrived.append(lax.ppermute(part, ('pairs', 'aux'), moves))  87.8 us
    ppermute x7, starting transfers between devices, split_by_columns(): arrived.append(lax.ppermute(part, ('pairs', 'aux'), moves))  24.4 us
    ppermute x10, waiting for transfers between devices, swap(): return lax.ppermute(value, axis, [(i, i ^ bit) for i in range(size)])  14.5 us
    ppermute x10, starting transfers between devices, swap(): return lax.ppermute(value, axis, [(i, i ^ bit) for i in range(size)])  10.8 us
    pallas_call x1, Pallas kernels, partial_grams(): pl.pallas_call(functools.partial(gram_kernel, ks, owned), in_specs=[SMEM_...  10 us
    pallas_call x1, Pallas kernels, pair_terms(): pl.pallas_call(terms_kernel, grid=(pairs,), in_specs=[spec] * 3, out_spec...  7.68 us
    pallas_call x2, Pallas kernels, column_parts(): pl.pallas_call(functools.partial(split_kernel, offsets), in_specs=[SMEM_S...  7.12 us
    pallas_call x1, Pallas kernels, finish(): pl.pallas_call(finish_kernel, grid=(pairs,), in_specs=[SMEM_SPEC, SMEM_SP...  4.61 us
  transfers between devices with their start and end apart: 17, of which 11 were waited for; matrix products, arithmetic and copies ran while one was open for 3% of the time, Pallas kernels for 4%

profile of v2, /device:TPU:0, one launch (start us, length us, event | category | flops | bytes accessed | tf_op | source)
XLA Modules:
  0.0 174.5 jit_solution(4800293430645841836)
XLA Ops:
  0.0 3.1 %shard_map.73 = (bf16[2576,128]{1,0:T(8,128)(2,1)}, bf16[2576,128]{1,0:T(8,128)(2,1)}) custom-call(s32[16]{0:T(128)} %wanted_ref.5, s32[1]{0:T(128)} %bitcast.1.place_ref, s32[1]{0:T(128)} %bitcast.core_ref, bf16[512,5120]{1,0:T(8,128)(2,1)} %bitcast.81), custom_call_target="tpu_custom_call" | custom-call | tf_op jit(solution)/shard_map/pallas_call | solution.py:94
  3.2 0.0 copy-start.6
  3.2 4.0 %shard_map.74 = (bf16[2576,128]{1,0:T(8,128)(2,1)}, bf16[2576,128]{1,0:T(8,128)(2,1)}, bf16[2576,128]{1,0:T(8,128)(2,1)}, bf16[2576,128]{1,0:T(8,128)(2,1)}, bf16[2576,128]{1,0:T(8,128)(2,1)}) custom-call(s32[16]{0:T(128)} %wanted_ref.5, s32[1]{0:T(128)} %bitcast.1.place_ref, s32[1]{0:T(128)} %bitcast.core_ref, bf16[512,5120]{1,0:T(8,128)(2,1)} %bitcast.82), custom_call_target="tpu_custom_call" | custom-call | tf_op jit(solution)/shard_map/pallas_call | solution.py:94
  7.2 3.0 %collective-permute-start.2 = (bf16[2576,128]{1,0:T(8,128)(2,1)}, bf16[2576,128]{1,0:T(8,128)(2,1)S(1)}, u32[]{:S(2)}, u32[]{:S(2)}) collective-permute-start(bf16[2576,128]{1,0:T(8,128)(2,1)} %get-tuple-element.30), channel_id=1, source_target_pairs={{0,2},{1,5},{2,0},{3,7},{4,6},{5,1},{6,4},{7,3},{8,10},{9,13},{10,... | collective-permute-start | bytes 1978376 | tf_op jit(solution)/shard_map/ppermute | solution.py:362
  10.2 3.6 %collective-permute-start.3 = (bf16[2576,128]{1,0:T(8,128)(2,1)}, bf16[2576,128]{1,0:T(8,128)(2,1)S(1)}, u32[]{:S(2)}, u32[]{:S(2)}) collective-permute-start(bf16[2576,128]{1,0:T(8,128)(2,1)} %get-tuple-element.31), channel_id=1, source_target_pairs={{0,12},{1,11},{2,14},{3,9},{4,8},{5,15},{6,10},{7,13},{8,4},{9,3},... | collective-permute-start | bytes 1978376 | tf_op jit(solution)/shard_map/ppermute | solution.py:362
  13.8 0.0 collective-permute-start.4
  13.8 0.8 collective-permute-start.5
  14.6 1.4 collective-permute-start.6
  16.0 5.2 %collective-permute-done.2.rest_2_ = bf16[2576,128]{1,0:T(8,128)(2,1)S(1)} collective-permute-done((bf16[2576,128]{1,0:T(8,128)(2,1)}, bf16[2576,128]{1,0:T(8,128)(2,1)S(1)}, u32[]{:S(2)}, u32[]{:S(2)}) %collective-permute-start.2) | collective-permute-done | bytes 659488 | tf_op jit(solution)/shard_map/ppermute | solution.py:362
  21.2 0.9 collective-permute-start
  22.1 8.0 %collective-permute-done.3.rest_3_ = bf16[2576,128]{1,0:T(8,128)(2,1)S(1)} collective-permute-done((bf16[2576,128]{1,0:T(8,128)(2,1)}, bf16[2576,128]{1,0:T(8,128)(2,1)S(1)}, u32[]{:S(2)}, u32[]{:S(2)}) %collective-permute-start.3) | collective-permute-done | bytes 659488 | tf_op jit(solution)/shard_map/ppermute | solution.py:362
  30.1 14.6 %collective-permute-start.1 = (bf16[2576,128]{1,0:T(8,128)(2,1)S(1)}, bf16[2576,128]{1,0:T(8,128)(2,1)}, u32[]{:S(2)}, u32[]{:S(2)}) collective-permute-start(bf16[2576,128]{1,0:T(8,128)(2,1)S(1)} %copy-done.5), channel_id=1, source_target_pairs={{0,10},{1,9},{2,8},{3,11},{4,14},{5,13},{6,12},{7,15},{8,2},{9,1},... | collective-permute-start | bytes 1978376 | tf_op jit(solution)/shard_map/ppermute | solution.py:362
  44.7 7.7 %shard_map.75.terms_ref = f32[8,256,256]{2,1,0:T(8,128)} custom-call(bf16[8,256,256]{2,1,0:T(8,128)(2,1)} %fock_ref.1, bf16[8,256,256]{2,1,0:T(8,128)(2,1)} %corr_ref.1, bf16[8,256,256]{2,1,0:T(8,128)(2,1)} %amp_ref.1), custom_call_target="tpu_custom_call" | custom-call | flops 1073741824 | bytes 5242880 | tf_op jit(solution)/shard_map/pallas_call | solution.py:38
  52.4 0.5 dynamic-slice_bitcast_fusion.slot_ref
  52.9 0.0 collective-permute-done.4.rest_4_
  52.9 5.2 %collective-permute-done.5.rest_5_ = bf16[2576,128]{1,0:T(8,128)(2,1)} collective-permute-done((bf16[2576,128]{1,0:T(8,128)(2,1)}, bf16[2576,128]{1,0:T(8,128)(2,1)}, u32[]{:S(2)}, u32[]{:S(2)}) %collective-permute-start.5) | collective-permute-done | bytes 659488 | tf_op jit(solution)/shard_map/ppermute | solution.py:362
  58.2 13.7 %collective-permute-done.6.rest_6_ = bf16[2576,128]{1,0:T(8,128)(2,1)} collective-permute-done((bf16[2576,128]{1,0:T(8,128)(2,1)}, bf16[2576,128]{1,0:T(8,128)(2,1)}, u32[]{:S(2)}, u32[]{:S(2)}) %collective-permute-start.6) | collective-permute-done | bytes 659488 | tf_op jit(solution)/shard_map/ppermute | solution.py:362
  71.9 42.1 %collective-permute-done.rest_0_ = bf16[2576,128]{1,0:T(8,128)(2,1)} collective-permute-done((bf16[2576,128]{1,0:T(8,128)(2,1)S(1)}, bf16[2576,128]{1,0:T(8,128)(2,1)}, u32[]{:S(2)}, u32[]{:S(2)}) %collective-permute-start) | collective-permute-done | bytes 659488 | tf_op jit(solution)/shard_map/ppermute | solution.py:362
  113.9 13.6 %collective-permute-done.1.rest_1_ = bf16[2576,128]{1,0:T(8,128)(2,1)} collective-permute-done((bf16[2576,128]{1,0:T(8,128)(2,1)S(1)}, bf16[2576,128]{1,0:T(8,128)(2,1)}, u32[]{:S(2)}, u32[]{:S(2)}) %collective-permute-start.1) | collective-permute-done | bytes 659488 | tf_op jit(solution)/shard_map/ppermute | solution.py:362
  127.6 10.0 %shard_map.76 = (bf16[8,640,128]{2,1,0:T(8,128)(2,1)}, bf16[8,640,128]{2,1,0:T(8,128)(2,1)}) custom-call(s32[16]{0:T(128)} %wanted_ref.5, s32[1]{0:T(128)} %bitcast.core_ref, s32[1]{0:T(128)} %bitcast.1.place_ref, s32[8]{0:T(128)} %dynamic-slice_bitcast_fusion.slot_ref, bf16[512,5120]{1,0:T(8,128)(2,1)} %bitcast.83, ...), custom_call_target="tpu_custom_call" | custom-call | flops 2684354560 | bytes 5242880 | tf_op jit(solution)/shard_map/pallas_call | solution.py:212
  137.6 0.1 collective-permute-start.7
  137.7 3.2 %collective-permute-done.7 = bf16[8,640,128]{2,1,0:T(8,128)(2,1)S(1)} collective-permute-done((bf16[8,640,128]{2,1,0:T(8,128)(2,1)}, bf16[8,640,128]{2,1,0:T(8,128)(2,1)S(1)}, u32[]{:S(2)}, u32[]{:S(2)}) %collective-permute-start.7) | collective-permute-done | bytes 1310752 | tf_op jit(solution)/shard_map/ppermute | solution.py:296
  140.9 1.2 fusion
  142.1 1.6 collective-permute-start.8
  143.7 0.8 fusion.5
  144.4 3.0 %collective-permute-start.13 = (bf16[2,192,128]{2,1,0:T(8,128)(2,1)}, bf16[2,192,128]{2,1,0:T(8,128)(2,1)}, u32[]{:S(2)}, u32[]{:S(2)}) collective-permute-start(bf16[2,192,128]{2,1,0:T(8,128)(2,1)} %get-tuple-element.50), channel_id=1, source_target_pairs={{0,8},{2,10},{4,12},{6,14},{8,0},{10,2},{12,4},{14,6},{1,9},{3,11}... | collective-permute-start | bytes 294920 | tf_op jit(solution)/shard_map/ppermute | solution.py:296
  147.5 1.4 collective-permute-start.14
  148.8 0.1 slice_multiply_fusion
  148.9 0.7 add.163
  149.6 1.4 add.164
  151.0 0.7 add.166
  151.7 0.0 collective-permute-done.12
  151.7 3.9 %collective-permute-done.13 = bf16[2,192,128]{2,1,0:T(8,128)(2,1)} collective-permute-done((bf16[2,192,128]{2,1,0:T(8,128)(2,1)}, bf16[2,192,128]{2,1,0:T(8,128)(2,1)}, u32[]{:S(2)}, u32[]{:S(2)}) %collective-permute-start.13) | collective-permute-done | bytes 98336 | tf_op jit(solution)/shard_map/ppermute | solution.py:296
  155.6 0.9 fusion.8
  156.5 0.6 collective-permute-start.15
  157.1 0.0 collective-permute-done.8
  157.1 0.1 fusion.3
  157.2 2.6 %collective-permute-start.10 = (bf16[448,128]{1,0:T(8,128)(2,1)S(1)}, bf16[448,128]{1,0:T(8,128)(2,1)S(1)}, u32[]{:S(2)}, u32[]{:S(2)}) collective-permute-start(bf16[448,128]{1,0:T(8,128)(2,1)S(1)} %get-tuple-element.47), channel_id=1, source_target_pairs={{0,8},{2,10},{4,12},{6,14},{8,0},{10,2},{12,4},{14,6},{1,9},{3,11}... | collective-permute-start | bytes 344072 | tf_op jit(solution)/shard_map/ppermute | solution.py:296
  159.9 1.4 collective-permute-start.11
  161.3 0.0 collective-permute-start.9
  161.3 0.0 collective-permute-done.15
  161.3 0.9 add_convert_fusion.5
  162.2 5.6 %collective-permute-done.10 = bf16[448,128]{1,0:T(8,128)(2,1)S(1)} collective-permute-done((bf16[448,128]{1,0:T(8,128)(2,1)S(1)}, bf16[448,128]{1,0:T(8,128)(2,1)S(1)}, u32[]{:S(2)}, u32[]{:S(2)}) %collective-permute-start.10) | collective-permute-done | bytes 114720 | tf_op jit(solution)/shard_map/ppermute | solution.py:296
  167.8 0.5 collective-permute-done.9
  168.3 0.1 add_convert_fusion.1
  168.4 0.1 collective-permute-start.16
  168.5 1.3 collective-permute-done.16.other_ref
  169.9 4.6 %shard_map.77 = bf16[8,256,256]{2,1,0:T(8,128)(2,1)} custom-call(s32[8,16]{1,0:T(8,128)S(1)} %constant_dynamic-slice_fusion.slots_ref, s32[1]{0:T(128)} %bitcast.core_ref, bf16[640,128]{1,0:T(8,128)(2,1)S(1)} %pad_maximum_fusion.mine_ref, bf16[640,128]{1,0:T(8,128)(2,1)S(1)} %collective-permute-done.16.other_ref, ...), custom_call_target="tpu_custom_call" | custom-call | flops 536870912 | bytes 3145728 | tf_op jit(solution)/shard_map/pallas_call | solution.py:271
  (28 shorter events, 0.1 us)
Async XLA Ops:
  0.0 137.7 %copy-start = (s32[16,16]{1,0:T(8,128)S(1)}, s32[16,16]{1,0:T(8,128)}, u32[]{:S(2)}) copy-start(s32[16,16]{1,0:T(8,128)} %param.9) | copy-start | bytes 3076
  3.2 18.1 %copy-start.6 = (bf16[2576,128]{1,0:T(8,128)(2,1)S(1)}, bf16[2576,128]{1,0:T(8,128)(2,1)}, u32[]{:S(2)}) copy-start(bf16[2576,128]{1,0:T(8,128)(2,1)} %get-tuple-element.27) | copy-start | bytes 1978372
  3.2 26.9 %copy-start.5 = (bf16[2576,128]{1,0:T(8,128)(2,1)S(1)}, bf16[2576,128]{1,0:T(8,128)(2,1)}, u32[]{:S(2)}) copy-start(bf16[2576,128]{1,0:T(8,128)(2,1)} %get-tuple-element.28) | copy-start | bytes 1978372
  7.2 14.0 %collective-permute-start.2 = (bf16[2576,128]{1,0:T(8,128)(2,1)}, bf16[2576,128]{1,0:T(8,128)(2,1)S(1)}, u32[]{:S(2)}, u32[]{:S(2)}) collective-permute-start(bf16[2576,128]{1,0:T(8,128)(2,1)} %get-tuple-element.30), channel_id=1, source_target_pairs={{0,2},{1,5},{2,0},{3,7},{4,6},{5,1},{6,4},{7,3},{8,10},{9,13},{10,... | collective-permute-start | bytes 1978376 | tf_op jit(solution)/shard_map/ppermute | solution.py:362
  10.2 19.9 %collective-permute-start.3 = (bf16[2576,128]{1,0:T(8,128)(2,1)}, bf16[2576,128]{1,0:T(8,128)(2,1)S(1)}, u32[]{:S(2)}, u32[]{:S(2)}) collective-permute-start(bf16[2576,128]{1,0:T(8,128)(2,1)} %get-tuple-element.31), channel_id=1, source_target_pairs={{0,12},{1,11},{2,14},{3,9},{4,8},{5,15},{6,10},{7,13},{8,4},{9,3},... | collective-permute-start | bytes 1978376 | tf_op jit(solution)/shard_map/ppermute | solution.py:362
  13.8 39.1 %collective-permute-start.4 = (bf16[2576,128]{1,0:T(8,128)(2,1)}, bf16[2576,128]{1,0:T(8,128)(2,1)S(1)}, u32[]{:S(2)}, u32[]{:S(2)}) collective-permute-start(bf16[2576,128]{1,0:T(8,128)(2,1)} %get-tuple-element.32), channel_id=1, source_target_pairs={{0,4},{1,7},{2,6},{3,5},{4,0},{5,3},{6,2},{7,1},{8,12},{9,15},{10,... | collective-permute-start | bytes 1978376 | tf_op jit(solution)/shard_map/ppermute | solution.py:362
  13.8 44.4 %collective-permute-start.5 = (bf16[2576,128]{1,0:T(8,128)(2,1)}, bf16[2576,128]{1,0:T(8,128)(2,1)}, u32[]{:S(2)}, u32[]{:S(2)}) collective-permute-start(bf16[2576,128]{1,0:T(8,128)(2,1)} %get-tuple-element.33), channel_id=1, source_target_pairs={{0,14},{1,13},{2,12},{3,15},{4,10},{5,9},{6,8},{7,11},{8,6},{9,5},... | collective-permute-start | bytes 1978376 | tf_op jit(solution)/shard_map/ppermute | solution.py:362
  14.6 57.2 %collective-permute-start.6 = (bf16[2576,128]{1,0:T(8,128)(2,1)}, bf16[2576,128]{1,0:T(8,128)(2,1)}, u32[]{:S(2)}, u32[]{:S(2)}) collective-permute-start(bf16[2576,128]{1,0:T(8,128)(2,1)} %get-tuple-element.34), channel_id=1, source_target_pairs={{0,6},{1,15},{2,4},{3,13},{4,2},{5,11},{6,0},{7,9},{8,14},{9,7},{1... | collective-permute-start | bytes 1978376 | tf_op jit(solution)/shard_map/ppermute | solution.py:362
  21.2 31.2 %copy-start.7 = (bf16[2576,128]{1,0:T(8,128)(2,1)}, bf16[2576,128]{1,0:T(8,128)(2,1)S(1)}, u32[]{:S(2)}) copy-start(bf16[2576,128]{1,0:T(8,128)(2,1)S(1)} %collective-permute-done.2.rest_2_) | copy-start | bytes 1978372
  21.2 92.7 %collective-permute-start = (bf16[2576,128]{1,0:T(8,128)(2,1)S(1)}, bf16[2576,128]{1,0:T(8,128)(2,1)}, u32[]{:S(2)}, u32[]{:S(2)}) collective-permute-start(bf16[2576,128]{1,0:T(8,128)(2,1)S(1)} %copy-done.6), channel_id=1, source_target_pairs={{0,8},{1,3},{2,10},{3,1},{4,12},{5,7},{6,14},{7,5},{8,0},{9,11},{1... | collective-permute-start | bytes 1978376 | tf_op jit(solution)/shard_map/ppermute | solution.py:362
  30.1 22.3 %copy-start.8 = (bf16[2576,128]{1,0:T(8,128)(2,1)}, bf16[2576,128]{1,0:T(8,128)(2,1)S(1)}, u32[]{:S(2)}) copy-start(bf16[2576,128]{1,0:T(8,128)(2,1)S(1)} %collective-permute-done.3.rest_3_) | copy-start | bytes 1978372
  30.1 97.5 %collective-permute-start.1 = (bf16[2576,128]{1,0:T(8,128)(2,1)S(1)}, bf16[2576,128]{1,0:T(8,128)(2,1)}, u32[]{:S(2)}, u32[]{:S(2)}) collective-permute-start(bf16[2576,128]{1,0:T(8,128)(2,1)S(1)} %copy-done.5), channel_id=1, source_target_pairs={{0,10},{1,9},{2,8},{3,11},{4,14},{5,13},{6,12},{7,15},{8,2},{9,1},... | collective-permute-start | bytes 1978376 | tf_op jit(solution)/shard_map/ppermute | solution.py:362
  44.7 7.7 %copy-start.10 = (s32[2,8]{1,0:T(2,128)S(1)}, s32[2,8]{1,0:T(2,128)}, u32[]{:S(2)}) copy-start(s32[2,8]{1,0:T(2,128)} %constant.30.clone) | copy-start | bytes 196
  52.9 74.6 %copy-start.9 = (bf16[2576,128]{1,0:T(8,128)(2,1)}, bf16[2576,128]{1,0:T(8,128)(2,1)S(1)}, u32[]{:S(2)}) copy-start(bf16[2576,128]{1,0:T(8,128)(2,1)S(1)} %collective-permute-done.4.rest_4_) | copy-start | bytes 1978372
  137.6 6.1 %copy-start.2 = (bf16[8,640,128]{2,1,0:T(8,128)(2,1)S(1)}, bf16[8,640,128]{2,1,0:T(8,128)(2,1)}, u32[]{:S(2)}) copy-start(bf16[8,640,128]{2,1,0:T(8,128)(2,1)} %get-tuple-element.42) | copy-start | bytes 3932164
  137.6 3.3 %collective-permute-start.7 = (bf16[8,640,128]{2,1,0:T(8,128)(2,1)}, bf16[8,640,128]{2,1,0:T(8,128)(2,1)S(1)}, u32[]{:S(2)}, u32[]{:S(2)}) collective-permute-start(bf16[8,640,128]{2,1,0:T(8,128)(2,1)} %get-tuple-element.43), channel_id=1, source_target_pairs={{0,1},{1,0},{2,3},{3,2},{4,5},{5,4},{6,7},{7,6},{8,9},{9,8},{10,11... | collective-permute-start | bytes 3932168 | tf_op jit(solution)/shard_map/ppermute | solution.py:296
  142.1 15.0 %collective-permute-start.8 = (bf16[4,448,128]{2,1,0:T(8,128)(2,1)S(1)}, bf16[4,448,128]{2,1,0:T(8,128)(2,1)S(1)}, u32[]{:S(2)}, u32[]{:S(2)}) collective-permute-start(bf16[4,448,128]{2,1,0:T(8,128)(2,1)S(1)} %fusion), channel_id=1, source_target_pairs={{0,2},{2,0},{4,6},{6,4},{8,10},{10,8},{12,14},{14,12},{1,3},{3,1},... | collective-permute-start | bytes 1376264 | tf_op jit(solution)/shard_map/ppermute | solution.py:296
  144.4 7.3 %collective-permute-start.12 = (bf16[2,192,128]{2,1,0:T(8,128)(2,1)}, bf16[2,192,128]{2,1,0:T(8,128)(2,1)}, u32[]{:S(2)}, u32[]{:S(2)}) collective-permute-start(bf16[2,192,128]{2,1,0:T(8,128)(2,1)} %get-tuple-element.48), channel_id=1, source_target_pairs={{0,4},{2,6},{4,0},{6,2},{8,12},{10,14},{12,8},{14,10},{1,5},{3,7},... | collective-permute-start | bytes 294920 | tf_op jit(solution)/shard_map/ppermute | solution.py:296
  144.4 11.1 %collective-permute-start.13 = (bf16[2,192,128]{2,1,0:T(8,128)(2,1)}, bf16[2,192,128]{2,1,0:T(8,128)(2,1)}, u32[]{:S(2)}, u32[]{:S(2)}) collective-permute-start(bf16[2,192,128]{2,1,0:T(8,128)(2,1)} %get-tuple-element.50), channel_id=1, source_target_pairs={{0,8},{2,10},{4,12},{6,14},{8,0},{10,2},{12,4},{14,6},{1,9},{3,11}... | collective-permute-start | bytes 294920 | tf_op jit(solution)/shard_map/ppermute | solution.py:296
  147.5 8.1 %collective-permute-start.14 = (bf16[2,192,128]{2,1,0:T(8,128)(2,1)}, bf16[2,192,128]{2,1,0:T(8,128)(2,1)}, u32[]{:S(2)}, u32[]{:S(2)}) collective-permute-start(bf16[2,192,128]{2,1,0:T(8,128)(2,1)} %get-tuple-element.49), channel_id=1, source_target_pairs={{0,12},{2,14},{4,8},{6,10},{8,4},{10,6},{12,0},{14,2},{1,13},{3,15... | collective-permute-start | bytes 294920 | tf_op jit(solution)/shard_map/ppermute | solution.py:296
  156.5 12.0 %copy-start.3 = (s32[8,1,256]{2,1,0:T(1,128)S(1)}, s32[8,1,256]{2,1,0:T(1,128)}, u32[]{:S(2)}) copy-start(s32[8,1,256]{2,1,0:T(1,128)} %add.164) | copy-start | bytes 24580
  156.5 12.0 %copy-start.4 = (s32[256]{0:T(256)S(1)}, s32[256]{0:T(256)}, u32[]{:S(2)}) copy-start(s32[256]{0:T(256)} %add.166) | copy-start | bytes 3076
  156.5 13.4 %copy-start.1 = (f32[8,256,256]{2,1,0:T(8,128)S(1)}, f32[8,256,256]{2,1,0:T(8,128)}, u32[]{:S(2)}) copy-start(f32[8,256,256]{2,1,0:T(8,128)} %shard_map.75.terms_ref) | copy-start | bytes 6291460
  156.5 4.8 %collective-permute-start.15 = (bf16[192,128]{1,0:T(8,128)(2,1)S(1)}, bf16[192,128]{1,0:T(8,128)(2,1)S(1)}, u32[]{:S(2)}, u32[]{:S(2)}) collective-permute-start(bf16[192,128]{1,0:T(8,128)(2,1)S(1)} %fusion.8), channel_id=1, source_target_pairs={{0,2},{2,0},{4,6},{6,4},{8,10},{10,8},{12,14},{14,12},{1,3},{3,1},... | collective-permute-start | bytes 147464 | tf_op jit(solution)/shard_map/ppermute | solution.py:296
  157.2 10.6 %collective-permute-start.10 = (bf16[448,128]{1,0:T(8,128)(2,1)S(1)}, bf16[448,128]{1,0:T(8,128)(2,1)S(1)}, u32[]{:S(2)}, u32[]{:S(2)}) collective-permute-start(bf16[448,128]{1,0:T(8,128)(2,1)S(1)} %get-tuple-element.47), channel_id=1, source_target_pairs={{0,8},{2,10},{4,12},{6,14},{8,0},{10,2},{12,4},{14,6},{1,9},{3,11}... | collective-permute-start | bytes 344072 | tf_op jit(solution)/shard_map/ppermute | solution.py:296
  159.9 8.0 %collective-permute-start.11 = (bf16[448,128]{1,0:T(8,128)(2,1)S(1)}, bf16[448,128]{1,0:T(8,128)(2,1)S(1)}, u32[]{:S(2)}, u32[]{:S(2)}) collective-permute-start(bf16[448,128]{1,0:T(8,128)(2,1)S(1)} %get-tuple-element.46), channel_id=1, source_target_pairs={{0,12},{2,14},{4,8},{6,10},{8,4},{10,6},{12,0},{14,2},{1,13},{3,15... | collective-permute-start | bytes 344072 | tf_op jit(solution)/shard_map/ppermute | solution.py:296
  161.3 7.0 %collective-permute-start.9 = (bf16[448,128]{1,0:T(8,128)(2,1)S(1)}, bf16[448,128]{1,0:T(8,128)(2,1)S(1)}, u32[]{:S(2)}, u32[]{:S(2)}) collective-permute-start(bf16[448,128]{1,0:T(8,128)(2,1)S(1)} %get-tuple-element.45), channel_id=1, source_target_pairs={{0,4},{2,6},{4,0},{6,2},{8,12},{10,14},{12,8},{14,10},{1,5},{3,7},... | collective-permute-start | bytes 344072 | tf_op jit(solution)/shard_map/ppermute | solution.py:296
  168.4 1.5 collective-permute-start.16

commit v3 on v0

--- a/solution.py
+++ b/solution.py
@@ -1,10 +1,467 @@
+import functools
+
 import jax
 import jax.numpy as jnp
 from jax import lax
+from jax.experimental import pallas as pl
+from jax.experimental.pallas import tpu as pltpu
 from jax.sharding import PartitionSpec as P
 
 DOM = 8
 UNIQ = 16
+TILE = 128
+SIDE = 4
+LATE = 1
+STRIP = 256
+LIST_ROWS = 16
+VMEM_BYTES = 60 * 1024 * 1024
+LAST_VMEM = 24 * 1024 * 1024
+FIRST = 416
+SMEM_SPEC = pl.BlockSpec(memory_space=pltpu.SMEM)
+VMEM_SPEC = pl.BlockSpec(memory_space=pltpu.VMEM)
+HBM_SPEC = pl.BlockSpec(memory_space=pltpu.HBM)
+
+
+def terms_kernel(right_ref, fock_ref, corr_ref, amp_ref, out_ref, choose_ref):
+    fock, corr, amp = fock_ref[0], corr_ref[0], amp_ref[0]
+    fock_amp = jnp.dot(fock, amp, preferred_element_type=jnp.float32).astype(jnp.bfloat16)
+    over_amp = jnp.dot(corr, amp, preferred_element_type=jnp.float32).astype(jnp.bfloat16)
+    first = jnp.dot(fock_amp, corr, preferred_element_type=jnp.float32)
+    out_ref[0] = first + jnp.dot(over_amp, fock, preferred_element_type=jnp.float32)
+    rows = lax.broadcasted_iota(jnp.int32, choose_ref.shape[1:], 0)
+    choose_ref[0] = (rows == right_ref[0]).astype(jnp.float32).astype(jnp.bfloat16)
+
+
+def pair_terms(right_rows, fock, correlation, amplitudes):
+    pairs, rows, cols = fock.shape
+    spec = pl.BlockSpec((1, rows, cols), lambda p: (p, 0, 0))
+    side = UNIQ * rows // DOM
+    return pl.pallas_call(
+        terms_kernel,
+        grid=(pairs,),
+        in_specs=[pl.BlockSpec((1, 1, cols), lambda p: (p, 0, 0))] + [spec] * 3,
+        out_specs=[spec, pl.BlockSpec((1, side, cols), lambda p: (p, 0, 0))],
+        out_shape=[
+            jax.ShapeDtypeStruct(fock.shape, jnp.float32),
+            jax.ShapeDtypeStruct((pairs, side, cols), jnp.bfloat16),
+        ],
+        compiler_params=pltpu.CompilerParams(vmem_limit_bytes=VMEM_BYTES),
+        cost_estimate=pl.CostEstimate(
+            flops=8 * pairs * rows * rows * cols,
+            bytes_accessed=14 * pairs * rows * cols,
+            transcendentals=0,
+        ),
+    )(right_rows, fock, correlation, amplitudes)
+
+
+def split_kernel(orders, span, wanted_ref, place_ref, core_ref, blocks_ref, *rest):
+    outs, (bufs, tail, in_sems, out_sems) = rest[:-4], rest[-4:]
+    rows, depth = blocks_ref.shape
+    columns = depth // (len(outs) + 1)
+    chunks = bufs.shape[2] // TILE
+    with_list = outs[0].shape[0] > chunks * rows
+    fetches = []
+    for n, ks in enumerate(zip(*orders)):
+        offset = jnp.where(core_ref[0] % 2 == 0, *ks)
+        start = pl.multiple_of((place_ref[0] ^ offset) * columns + span[0] * TILE, TILE)
+        source = blocks_ref.at[:, pl.ds(start, chunks * TILE)]
+        fetches.append(pltpu.make_async_copy(source, bufs.at[n], in_sems.at[n]))
+        fetches[-1].start()
+    stores = []
+    if with_list:
+        lane = lax.broadcasted_iota(jnp.int32, tail.shape, 1)
+        ids = jnp.zeros(tail.shape, jnp.int32)
+        for m in range(UNIQ):
+            ids = jnp.where(lane == m, wanted_ref[m], ids)
+        tail[...] = ids.astype(jnp.float32).astype(jnp.bfloat16)
+        for n, out in enumerate(outs):
+            target = out.at[pl.ds(chunks * rows, LIST_ROWS)]
+            stores.append(pltpu.make_async_copy(tail, target, out_sems.at[n, chunks]))
+            stores[-1].start()
+    for n, out in enumerate(outs):
+        fetches[n].wait()
+        for c in range(chunks):
+            source = bufs.at[n, :, pl.ds(c * TILE, TILE)]
+            target = out.at[pl.ds(c * rows, rows)]
+            stores.append(pltpu.make_async_copy(source, target, out_sems.at[n, c]))
+            stores[-1].start()
+    for copy in stores:
+        copy.wait()
+
+
+def column_parts(orders, span, with_list, wanted, place, core, blocks):
+    rows, _ = blocks.shape
+    count = len(orders[0])
+    chunks = span[1] - span[0]
+    height = chunks * rows + LIST_ROWS * with_list
+    out = jax.ShapeDtypeStruct((height, TILE), blocks.dtype)
+    return pl.pallas_call(
+        functools.partial(split_kernel, orders, span),
+        in_specs=[SMEM_SPEC] * 3 + [HBM_SPEC],
+        out_specs=[HBM_SPEC] * count,
+        out_shape=[out] * count,
+        scratch_shapes=[
+            pltpu.VMEM((count, rows, chunks * TILE), blocks.dtype),
+            pltpu.VMEM((LIST_ROWS, TILE), blocks.dtype),
+            pltpu.SemaphoreType.DMA((count,)),
+            pltpu.SemaphoreType.DMA((count, chunks + 1)),
+        ],
+        compiler_params=pltpu.CompilerParams(vmem_limit_bytes=VMEM_BYTES),
+    )(wanted, place, core, blocks)
+
+
+def block_order(width):
+    bits = width.bit_length() - 1
+    row = lax.broadcasted_iota(jnp.int32, (TILE, TILE), 0) >> bits
+    col = lax.broadcasted_iota(jnp.int32, (TILE, TILE), 1) >> bits
+    return row, col
+
+
+def packed_gram(held, width):
+    tile = {}
+    for top in range(0, SIDE * TILE, STRIP):
+        strip = lax.dot_general(
+            held[top : top + STRIP],
+            held[top:],
+            (((1,), (1,)), ((), ())),
+            preferred_element_type=jnp.float32,
+        )
+        for i in range(top // TILE, (top + STRIP) // TILE):
+            for j in range(i, SIDE):
+                r, c = i * TILE - top, j * TILE - top
+                tile[i, j] = strip[r : r + TILE, c : c + TILE]
+    row, col = block_order(width)
+
+    def diagonal(value):
+        found = value[:width]
+        for r in range(1, TILE // width):
+            here = col[:width] == r
+            found = jnp.where(here, value[r * width : (r + 1) * width], found)
+        return found
+
+    both = [jnp.where(row <= col, tile[i, i], tile[i + 1, i + 1]) for i in (0, 2)]
+    first = [tile[0, 1], tile[0, 2], tile[0, 3], tile[1, 2], diagonal(tile[1, 1])]
+    second = [tile[1, 3], tile[2, 3], *both, diagonal(tile[3, 3])]
+    return first, second
+
+
+def gather_rows(pool, places, rows, width, chunks):
+    return jnp.concatenate(
+        [
+            jnp.concatenate(
+                [
+                    pool[pl.ds(pl.multiple_of(place + c * rows, width), width), :]
+                    for place in places
+                ],
+                axis=0,
+            )
+            for c in range(chunks)
+        ],
+        axis=1,
+    )
+
+
+def pool_copies(span, me, blocks_ref, arrived_refs, pool, sems):
+    rows, depth = blocks_ref.shape
+    holders = len(arrived_refs) + 1
+    part = (span[1] - span[0]) * rows
+    copies = []
+    for n, c in enumerate(range(*span)):
+        start = pl.multiple_of(me * (depth // holders) + c * TILE, TILE)
+        source = blocks_ref.at[:, pl.ds(start, TILE)]
+        copies.append(pltpu.make_async_copy(source, pool.at[pl.ds(n * rows, rows)], sems.at[0, n]))
+    for k, ref in enumerate(arrived_refs, 1):
+        target = pool.at[pl.ds(k * part, part)]
+        copies.append(pltpu.make_async_copy(ref.at[pl.ds(0, part)], target, sems.at[k, 0]))
+    return copies
+
+
+def early_kernel(ks, span, owned, wanted_ref, place_ref, slot_ref, blocks_ref, *rest):
+    arrived_refs, rest = rest[:-8], rest[-8:]
+    acc_ref, spots_ref, pool, lists, ids_vmem, ids, sems, list_sems = rest
+    rows = blocks_ref.shape[0]
+    width = rows // owned
+    chunks = span[1] - span[0]
+    part = chunks * rows
+    me = place_ref[0]
+    tails = [
+        pltpu.make_async_copy(ref.at[pl.ds(part, LIST_ROWS)], lists.at[k], list_sems.at[k])
+        for k, ref in enumerate(arrived_refs, 1)
+    ]
+    copies = pool_copies(span, me, blocks_ref, arrived_refs, pool, sems)
+    for copy in tails + copies:
+        copy.start()
+    for copy in tails:
+        copy.wait()
+    ids_vmem[...] = jnp.zeros_like(ids_vmem)
+    for n, k in enumerate(ks):
+        if k > 0:
+            ids_vmem[n, :] = lists[slot_ref[k]].astype(jnp.float32).astype(jnp.int32)[0]
+    to_scalars = pltpu.make_async_copy(ids_vmem, ids, list_sems.at[0])
+    to_scalars.start()
+    to_scalars.wait()
+    for n, k in enumerate(ks):
+        for m in range(UNIQ):
+            entry = wanted_ref[m] if k == 0 else ids[n, m]
+            holder = lax.div(entry, owned)
+            spots_ref[n, m] = slot_ref[holder ^ me] * owned + (entry - holder * owned)
+    for copy in copies:
+        copy.wait()
+
+    @pl.loop(0, len(ks))
+    def _(n):
+        places = []
+        for m in range(UNIQ):
+            where = lax.div(spots_ref[n, m], owned)
+            places.append(where * part + (spots_ref[n, m] - where * owned) * width)
+        held = gather_rows(pool, places, rows, width, chunks)
+        at = 0
+        for value in sum(packed_gram(held, width), []):
+            acc_ref[n, at : at + value.shape[0], :] = value
+            at += value.shape[0]
+
+
+def late_kernel(span, owned, spots_ref, core_ref, place_ref, blocks_ref, acc_ref, *rest):
+    arrived_refs, rest = rest[:-4], rest[-4:]
+    keep_ref, send_ref, pool, sems = rest
+    rows = blocks_ref.shape[0]
+    width = rows // owned
+    chunks = span[1] - span[0]
+    part = chunks * rows
+    owners = acc_ref.shape[0]
+    half = acc_ref.shape[1] // 2
+    core = core_ref[0]
+    copies = pool_copies(span, place_ref[0], blocks_ref, arrived_refs, pool, sems)
+    for copy in copies:
+        copy.start()
+    for copy in copies:
+        copy.wait()
+    for n in range(owners):
+        places = []
+        for m in range(UNIQ):
+            where = lax.div(spots_ref[n, m], owned)
+            places.append(where * part + (spots_ref[n, m] - where * owned) * width)
+        halves = packed_gram(gather_rows(pool, places, rows, width, chunks), width)
+        at = 0
+        for first, second in zip(*halves):
+            height = first.shape[0]
+            first += acc_ref[n, at : at + height, :]
+            second += acc_ref[n, half + at : half + at + height, :]
+            keep = jnp.where(core == 0, first, second)
+            send = jnp.where(core == 0, second, first)
+            keep_ref[n, at : at + height, :] = keep.astype(jnp.bfloat16)
+            send_ref[n, at : at + height, :] = send.astype(jnp.bfloat16)
+            at += height
+
+
+def half_rows(width):
+    return SIDE * TILE + width
+
+
+def early_grams(ks, span, owned, wanted, place, slot, blocks, arrived):
+    holders = len(arrived) + 1
+    rows, depth = blocks.shape
+    width = rows // owned
+    chunks = span[1] - span[0]
+    return pl.pallas_call(
+        functools.partial(early_kernel, ks, span, owned),
+        in_specs=[SMEM_SPEC] * 3 + [HBM_SPEC] * holders,
+        out_specs=[VMEM_SPEC, SMEM_SPEC],
+        out_shape=[
+            jax.ShapeDtypeStruct((len(ks), 2 * half_rows(width), TILE), jnp.float32),
+            jax.ShapeDtypeStruct((len(ks), UNIQ), jnp.int32),
+        ],
+        scratch_shapes=[
+            pltpu.VMEM((holders * rows * chunks, TILE), jnp.bfloat16),
+            pltpu.VMEM((holders, LIST_ROWS, TILE), jnp.bfloat16),
+            pltpu.VMEM((len(ks), TILE), jnp.int32),
+            pltpu.SMEM((len(ks), TILE), jnp.int32),
+            pltpu.SemaphoreType.DMA((holders, chunks)),
+            pltpu.SemaphoreType.DMA((holders,)),
+        ],
+        compiler_params=pltpu.CompilerParams(vmem_limit_bytes=24 * 1024 * 1024),
+        cost_estimate=pl.CostEstimate(
+            flops=2 * len(ks) * (SIDE * TILE) ** 2 * chunks * TILE,
+            bytes_accessed=2 * holders * rows * chunks * TILE,
+            transcendentals=0,
+        ),
+    )(wanted, place, slot, blocks, *arrived)
+
+
+def late_grams(span, owned, spots, core, place, blocks, acc, arrived):
+    holders = len(arrived) + 1
+    rows, depth = blocks.shape
+    width = rows // owned
+    chunks = span[1] - span[0]
+    half = half_rows(width)
+    out = jax.ShapeDtypeStruct((acc.shape[0], half, TILE), jnp.bfloat16)
+    owners = acc.shape[0]
+    return pl.pallas_call(
+        functools.partial(late_kernel, span, owned),
+        in_specs=[SMEM_SPEC] * 3 + [HBM_SPEC, VMEM_SPEC] + [HBM_SPEC] * len(arrived),
+        out_specs=[VMEM_SPEC] * 2,
+        out_shape=[out, out],
+        scratch_shapes=[
+            pltpu.VMEM((holders * rows * chunks, TILE), jnp.bfloat16),
+            pltpu.SemaphoreType.DMA((holders, chunks)),
+        ],
+        compiler_params=pltpu.CompilerParams(vmem_limit_bytes=16 * 1024 * 1024),
+        cost_estimate=pl.CostEstimate(
+            flops=2 * owners * (SIDE * TILE) ** 2 * chunks * TILE,
+            bytes_accessed=2 * holders * rows * chunks * TILE,
+            transcendentals=0,
+        ),
+    )(spots, core, place, blocks, acc, *arrived)
+
+
+def finish_kernel(slots_ref, core_ref, mine_ref, other_ref, choose_ref, terms_ref, out_ref, gram, stage, sems):
+    core = core_ref[0]
+    width = gram.shape[0] // UNIQ
+    pairs = out_ref.shape[0]
+
+    def put(i, j, value):
+        gram[i * TILE : (i + 1) * TILE, j * TILE : (j + 1) * TILE] = value.astype(jnp.bfloat16)
+
+    mine, other = mine_ref[...], other_ref[...]
+    first = jnp.where(core == 0, mine, other).astype(jnp.float32)
+    second = jnp.where(core == 0, other, mine).astype(jnp.float32)
+    pieces = [v[t * TILE : (t + 1) * TILE] for v in (first, second) for t in range(SIDE)]
+    places = [(0, 1), (0, 2), (0, 3), (1, 2), (1, 3), (2, 3)]
+    for (i, j), value in zip(places, pieces):
+        put(i, j, value)
+        put(j, i, value.T)
+    row, col = block_order(width)
+    for i, value, diagonal in zip((0, 2), pieces[6:], (first, second)):
+        flipped = value.T
+        squares = jnp.concatenate([diagonal[SIDE * TILE :]] * (TILE // width), axis=0)
+        put(i, i, jnp.where(row <= col, value, flipped))
+        lower = jnp.where(row > col, value, flipped)
+        put(i + 1, i + 1, jnp.where(row == col, squares, lower))
+
+    def result(pair):
+        return pltpu.make_async_copy(stage.at[pair], out_ref.at[pair], sems.at[pair])
+
+    for pair in range(pairs):
+        left = jnp.concatenate(
+            [gram[pl.ds(slots_ref[pair, m] * width, width), :] for m in range(DOM)], axis=0
+        )
+        integrals = jnp.dot(left, choose_ref[pair], preferred_element_type=jnp.float32)
+        stage[pair] = (integrals + terms_ref[pair]).astype(jnp.bfloat16)
+        result(pair).start()
+    for pair in range(pairs):
+        result(pair).wait()
+
+
+def finish(slots, core, mine, other, choose, terms):
+    pairs, rows, cols = terms.shape
+    gram_side = UNIQ * rows // DOM
+    return pl.pallas_call(
+        finish_kernel,
+        in_specs=[SMEM_SPEC] * 2 + [VMEM_SPEC] * 4,
+        out_specs=HBM_SPEC,
+        out_shape=jax.ShapeDtypeStruct(terms.shape, jnp.bfloat16),
+        scratch_shapes=[
+            pltpu.VMEM((gram_side, gram_side), jnp.bfloat16),
+            pltpu.VMEM(terms.shape, jnp.bfloat16),
+            pltpu.SemaphoreType.DMA((pairs,)),
+        ],
+        compiler_params=pltpu.CompilerParams(vmem_limit_bytes=LAST_VMEM),
+        cost_estimate=pl.CostEstimate(
+            flops=2 * pairs * rows * cols * gram_side,
+            bytes_accessed=10 * pairs * rows * cols,
+            transcendentals=0,
+        ),
+    )(slots, core, mine, other, choose, terms)
+
+
+def swap(value, axis, bit):
+    size = lax.axis_size(axis)
+    return lax.ppermute(value, axis, [(i, i ^ bit) for i in range(size)])
+
+
+def add(*values):
+    return sum(value.astype(jnp.float32) for value in values)
+
+
+def to_owner(keep, came):
+    half = keep.shape[0] // 2
+    keep, came = (v.reshape(2, half, *v.shape[1:]) for v in (keep, came))
+
+    def both(bits, offsets, rows):
+        return add(keep[bits, offsets, rows], came[bits, offsets, rows]).astype(jnp.bfloat16)
+
+    every, top, rest = slice(None), slice(0, FIRST), slice(FIRST, None)
+    top_near = swap(both(1, every, top), "pairs", 1)
+    rest_far = [swap(both(every, j, rest), "pairs", 2 * j) for j in range(1, half)]
+    top_sums = [
+        add(keep[0, j, top], came[0, j, top], top_near[j]).astype(jnp.bfloat16)
+        for j in range(half)
+    ]
+    top_far = [swap(top_sums[j], "pairs", 2 * j) for j in range(1, half)]
+    rest_sums = [
+        add(keep[b, 0, rest], came[b, 0, rest], *(v[b] for v in rest_far)).astype(jnp.bfloat16)
+        for b in range(2)
+    ]
+    rest_near = swap(rest_sums[1], "pairs", 1)
+    top_total = add(top_sums[0], *top_far).astype(jnp.bfloat16)
+    rest_total = add(rest_sums[0], rest_near).astype(jnp.bfloat16)
+    return jnp.concatenate([top_total, rest_total], axis=0)
+
+
+def exchange_orders(holders):
+    light, heavy = [*range(1, holders // 2)], [*range(holders // 2, holders)]
+    first = heavy[:1]
+    for pair in zip(heavy[1:], light):
+        first += pair
+    second = [k for pair in zip(light, heavy) for k in pair] + heavy[-1:]
+    return [first, second]
+
+
+def split_by_columns(blocks, wanted, pair_slots, fock, correlation, amplitudes):
+    holders = lax.axis_size("pairs")
+    core = lax.axis_index("aux")
+    owned, width, depth = blocks.shape
+    stacked = blocks.reshape(owned * width, depth)
+    place = lax.axis_index("pairs").reshape(1).astype(jnp.int32)
+    core_id = core.reshape(1).astype(jnp.int32)
+    orders = exchange_orders(holders)
+    slot_tables = [[0] * holders for _ in orders]
+    for table, ks in zip(slot_tables, orders):
+        for n, k in enumerate(ks, 1):
+            table[k] = n
+    slot = jnp.asarray(slot_tables, jnp.int32)[core % 2]
+    chunks = depth // holders // TILE
+    cores = lax.axis_size("aux")
+
+    def exchange(parts):
+        arrived = []
+        for n, part in enumerate(parts):
+            moves = [
+                (p * cores + c, (p ^ orders[c % 2][n]) * cores + c)
+                for p in range(holders)
+                for c in range(cores)
+            ]
+            arrived.append(lax.ppermute(part, ("pairs", "aux"), moves))
+        return arrived
+
+    cut = max(1, chunks - LATE)
+    first, second = (0, cut), (cut, chunks)
+    early = exchange(column_parts(orders, first, True, wanted, place, core_id, stacked))
+    tied = len(early) // 2
+    early[tied], later = lax.optimization_barrier((early[tied], stacked))
+    late = exchange(column_parts(orders, second, False, wanted, place, core_id, later))
+    pairs_here = fock.shape[0]
+    slots = lax.dynamic_slice_in_dim(pair_slots, core * pairs_here, pairs_here, axis=0)
+    offsets = jnp.arange(width, dtype=jnp.int32)
+    right_rows = (slots[:, DOM:, None] * width + offsets).reshape(pairs_here, 1, DOM * width)
+    terms, choose = pair_terms(right_rows, fock, correlation, amplitudes)
+    early, terms, choose, slots = lax.optimization_barrier((early, terms, choose, slots))
+    order = (*range(0, holders, 2), *range(1, holders, 2))
+    acc, spots = early_grams(order, first, owned, wanted, place, slot, stacked, early)
+    keep, send = late_grams(second, owned, spots, core_id, place, stacked, acc, late)
+    mine = to_owner(keep, swap(send, "aux", 1))
+    other = swap(mine, "aux", 1)
+    return finish(slots, core_id, mine, other, choose, terms)
 
 
 def pick_tiles(gram, left_ids, right_ids):
@@ -25,11 +482,9 @@
     return pick_tiles(gram, left_ids, right_ids)
 
 
-def on_device(blocks, wanted, pair_slots, fock, correlation, amplitudes):
+def by_request(blocks, wanted, pair_slots, fock, correlation, amplitudes):
     holders = lax.axis_size("pairs")
-    owned = blocks.shape[0]
-    width = blocks.shape[1]
-    depth = blocks.shape[2]
+    owned, width, depth = blocks.shape
     capacity = max(2, (2 * UNIQ + holders - 1) // holders)
     holder = wanted // owned
     local_ids = wanted - holder * owned
@@ -48,17 +503,22 @@
     integrals = lax.psum_scatter(
         partial_value.astype(jnp.bfloat16), "aux", scatter_dimension=0, tiled=True
     ).astype(jnp.float32)
-    fock_amp = jnp.einsum(
-        "pab,pbc->pac", fock, amplitudes, preferred_element_type=jnp.float32
-    ).astype(jnp.bfloat16)
-    over_amp = jnp.einsum(
-        "pab,pbc->pac", correlation, amplitudes, preferred_element_type=jnp.float32
-    ).astype(jnp.bfloat16)
-    first_term = jnp.einsum(
-        "pab,pbc->pac", fock_amp, correlation, preferred_element_type=jnp.float32
+    products = functools.partial(
+        jnp.einsum, "pab,pbc->pac", preferred_element_type=jnp.float32
     )
-    second_term = jnp.einsum("pab,pbc->pac", over_amp, fock, preferred_element_type=jnp.float32)
-    return (integrals + first_term + second_term).astype(jnp.bfloat16)
+    fock_amp = products(fock, amplitudes).astype(jnp.bfloat16)
+    over_amp = products(correlation, amplitudes).astype(jnp.bfloat16)
+    terms = products(fock_amp, correlation) + products(over_amp, fock)
+    return (integrals + terms).astype(jnp.bfloat16)
+
+
+def on_device(blocks, *others):
+    holders = lax.axis_size("pairs")
+    owned, width, depth = blocks.shape
+    fits = holders > 1 and holders & (holders - 1) == 0 and width & (width - 1) == 0
+    fits = fits and depth % (TILE * holders) == 0 and depth // holders >= 2 * TILE
+    fits = fits and holders * owned <= 256 and UNIQ * width == SIDE * TILE
+    return (split_by_columns if fits else by_request)(blocks, *others)
 
 
 def solution(mesh):

time: 353 us -> 158 us (0.45)
  waiting for transfers between devices: 233 us -> 85.3 us
  local copies, waits for them, and re-layouts: 54.2 us -> 2.76 us
  starting transfers between devices: 5.31 us -> 40.6 us
  Pallas kernels: 0 us -> 27.2 us
  matrix products: 21.2 us -> 0 us
  blocking collectives: 13.5 us -> 0 us
  between operations: 13.5 us -> 0.2 us
  other arithmetic: 12 us -> 1.13 us
    all_to_all x1 -> x0, waiting for transfers between devices: 227 us -> none  [on_device(): lax.all_to_all(outgoing, 'pairs', split_axis=0, concat_axis=0, tiled=True)]
    ppermute x0 -> x24, waiting for transfers between devices: none -> 85.3 us  [the longest x14 69.4 us: exchange(): arrived.append(lax.ppermute(part, ('pairs', 'aux'), moves))]
    ppermute x0 -> x24, starting transfers between devices: none -> 40.6 us  [the longest x14 29.4 us: exchange(): arrived.append(lax.ppermute(part, ('pairs', 'aux'), moves))]
    gather x3 -> x0, local copies, waits for them, and re-layouts: 27.4 us -> none  [the longest x1 11.7 us: pick_tiles(): tiles = gram[left_ids[:, :, None], right_ids[:, None, :]]]
    pallas_call x0 -> x6, Pallas kernels: none -> 27.2 us  [the longest x1 8.27 us: pair_terms(): pl.pallas_call(terms_kernel, grid=(pairs,), in_specs=[pl.BlockSpec((1, 1,...]
    convert_element_type x2 -> x0, local copies, waits for them, and re-layouts: 25.8 us -> none  [on_device(): partial_value.astype(jnp.bfloat16)]
    dot_general x3 -> x0, matrix products: 21.2 us -> none  [the longest x1 15.4 us: pair_integrals(): lax.dot_general(stacked, stacked, (((1,), (1,)), ((), ())), preferred_ele...]
    all_to_all x1 -> x0, blocking collectives: 13.5 us -> none  [on_device(): lax.all_to_all(table, 'pairs', split_axis=0, concat_axis=0, tiled=True)]
  transfers between devices with their start and end apart: 2 -> 24, of which waited for: 2 -> 12; matrix products, arithmetic and copies ran while one was open for 1% -> 1% of each run, Pallas kernels for 0% -> 11%
where the time goes in v3:
time: 158 us; the launch traced here: 157 us
  waiting for transfers between devices  85.3 us (54%)
  starting transfers between devices  40.6 us (26%)
  Pallas kernels  27.2 us (17%)
  local copies, waits for them, and re-layouts  2.76 us (2%)
    ppermute x14, waiting for transfers between devices, exchange(): arrived.append(lax.ppermute(part, ('pairs', 'aux'), moves))  69.4 us
    ppermute x14, starting transfers between devices, exchange(): arrived.append(lax.ppermute(part, ('pairs', 'aux'), moves))  29.4 us
    ppermute x10, waiting for transfers between devices, swap(): return lax.ppermute(value, axis, [(i, i ^ bit) for i in range(size)])  15.8 us
    ppermute x10, starting transfers between devices, swap(): return lax.ppermute(value, axis, [(i, i ^ bit) for i in range(size)])  11.2 us
    pallas_call x1, Pallas kernels, pair_terms(): pl.pallas_call(terms_kernel, grid=(pairs,), in_specs=[pl.BlockSpec((1, 1,...  8.27 us
    pallas_call x2, Pallas kernels, column_parts(): pl.pallas_call(functools.partial(split_kernel, orders, span), in_specs=[S...  6.96 us
    pallas_call x1, Pallas kernels, early_grams(): pl.pallas_call(functools.partial(early_kernel, ks, span, owned), in_specs...  6.76 us
  transfers between devices with their start and end apart: 24, of which 12 were waited for; matrix products, arithmetic and copies ran while one was open for 1% of the time, Pallas kernels for 11%

profile of v3, /device:TPU:0, one launch (start us, length us, event | category | flops | bytes accessed | tf_op | source)
XLA Modules:
  0.0 157.1 jit_solution(4875383107930053096)
XLA Ops:
  0.0 4.2 %shard_map.73 = (bf16[2064,128]{1,0:T(8,128)(2,1)}, bf16[2064,128]{1,0:T(8,128)(2,1)}, bf16[2064,128]{1,0:T(8,128)(2,1)}, bf16[2064,128]{1,0:T(8,128)(2,1)}, bf1...) custom-call(s32[16]{0:T(128)} %wanted_ref.5, s32[1]{0:T(128)} %bitcast.place_ref, ...), custom_call_target="tpu_custom_call" | custom-call | tf_op jit(solution)/shard_map/pallas_call | solution.py:98
  4.2 5.1 %collective-permute-start.3 = (bf16[2064,128]{1,0:T(8,128)(2,1)}, bf16[2064,128]{1,0:T(8,128)(2,1)S(1)}, u32[]{:S(2)}, u32[]{:S(2)}) collective-permute-start(bf16[2064,128]{1,0:T(8,128)(2,1)} %get-tuple-element.40), channel_id=1, source_target_pairs={{0,12},{1,11},{2,14},{3,9},{4,8},{5,15},{6,10},{7,13},{8,4},{9,3},... | collective-permute-start | bytes 1585160 | tf_op jit(solution)/shard_map/ppermute | solution.py:444
  9.3 3.9 %collective-permute-start.1 = (bf16[2064,128]{1,0:T(8,128)(2,1)}, bf16[2064,128]{1,0:T(8,128)(2,1)S(1)}, u32[]{:S(2)}, u32[]{:S(2)}) collective-permute-start(bf16[2064,128]{1,0:T(8,128)(2,1)} %get-tuple-element.38), channel_id=1, source_target_pairs={{0,10},{1,9},{2,8},{3,11},{4,14},{5,13},{6,12},{7,15},{8,2},{9,1},... | collective-permute-start | bytes 1585160 | tf_op jit(solution)/shard_map/ppermute | solution.py:444
  13.2 0.5 collective-permute-start.2
  13.7 8.6 %collective-permute-done.3.rest_3_ = bf16[2064,128]{1,0:T(8,128)(2,1)S(1)} collective-permute-done((bf16[2064,128]{1,0:T(8,128)(2,1)}, bf16[2064,128]{1,0:T(8,128)(2,1)S(1)}, u32[]{:S(2)}, u32[]{:S(2)}) %collective-permute-start.3) | collective-permute-done | bytes 528416 | tf_op jit(solution)/shard_map/ppermute | solution.py:444
  22.3 4.9 %collective-permute-start.5 = (bf16[2064,128]{1,0:T(8,128)(2,1)}, bf16[2064,128]{1,0:T(8,128)(2,1)S(1)}, u32[]{:S(2)}, u32[]{:S(2)}) collective-permute-start(bf16[2064,128]{1,0:T(8,128)(2,1)} %get-tuple-element.43), channel_id=1, source_target_pairs={{0,14},{1,13},{2,12},{3,15},{4,10},{5,9},{6,8},{7,11},{8,6},{9,5},... | collective-permute-start | bytes 1585160 | tf_op jit(solution)/shard_map/ppermute | solution.py:444
  27.3 51.1 %collective-permute-done.rest_0_ = bf16[2064,128]{1,0:T(8,128)(2,1)S(1)} collective-permute-done((bf16[2064,128]{1,0:T(8,128)(2,1)}, bf16[2064,128]{1,0:T(8,128)(2,1)S(1)}, u32[]{:S(2)}, u32[]{:S(2)}) %collective-permute-start) | collective-permute-done | bytes 528416 | tf_op jit(solution)/shard_map/ppermute | solution.py:444
  78.4 0.4 collective-permute-start.6
  78.9 0.1 slice_multiply_fusion
  78.9 0.1 add.131
  79.0 0.1 add.132
  79.1 0.1 add.134
  79.2 0.6 broadcast_add_fusion.right_ref
  79.8 2.8 %shard_map.76 = (bf16[512,128]{1,0:T(8,128)(2,1)}, bf16[512,128]{1,0:T(8,128)(2,1)}, bf16[512,128]{1,0:T(8,128)(2,1)}, bf16[512,128]{1,0:T(8,128)(2,1)}, bf16[51...) custom-call(s32[16]{0:T(128)} %wanted_ref.5, s32[1]{0:T(128)} %bitcast.place_ref, ...), custom_call_target="tpu_custom_call" | custom-call | tf_op jit(solution)/shard_map/pallas_call | solution.py:98
  82.6 9.4 %collective-permute-done.1.rest_1_ = bf16[2064,128]{1,0:T(8,128)(2,1)S(1)} collective-permute-done((bf16[2064,128]{1,0:T(8,128)(2,1)}, bf16[2064,128]{1,0:T(8,128)(2,1)S(1)}, u32[]{:S(2)}, u32[]{:S(2)}) %collective-permute-start.1) | collective-permute-done | bytes 528416 | tf_op jit(solution)/shard_map/ppermute | solution.py:444
  92.0 2.3 %collective-permute-start.10 = (bf16[512,128]{1,0:T(8,128)(2,1)}, bf16[512,128]{1,0:T(8,128)(2,1)S(1)}, u32[]{:S(2)}, u32[]{:S(2)}) collective-permute-start(bf16[512,128]{1,0:T(8,128)(2,1)} %get-tuple-element.61), channel_id=1, source_target_pairs={{0,12},{1,11},{2,14},{3,9},{4,8},{5,15},{6,10},{7,13},{8,4},{9,3},... | collective-permute-start | bytes 393224 | tf_op jit(solution)/shard_map/ppermute | solution.py:444
  94.3 8.3 %shard_map.74 = (f32[8,256,256]{2,1,0:T(8,128)}, bf16[8,512,256]{2,1,0:T(8,128)(2,1)}) custom-call(s32[8,1,256]{2,1,0:T(1,128)} %broadcast_add_fusion.right_ref, bf16[8,256,256]{2,1,0:T(8,128)(2,1)} %fock_ref.1, bf16[8,256,256]{2,1,0:T(8,128)(2,1)} %corr_ref.1, bf16[8,256,256]{2,1,0:T(8,128)(2,1)} %amp_ref.1), custom_call_target="tpu_custom_call" | custom-call | flops 1073741824 | bytes 7340032 | tf_op jit(solution)/shard_map/pallas_call | solution.py:39
  102.6 1.6 %collective-permute-start.12 = (bf16[512,128]{1,0:T(8,128)(2,1)}, bf16[512,128]{1,0:T(8,128)(2,1)S(1)}, u32[]{:S(2)}, u32[]{:S(2)}) collective-permute-start(bf16[512,128]{1,0:T(8,128)(2,1)} %get-tuple-element.63), channel_id=1, source_target_pairs={{0,14},{1,13},{2,12},{3,15},{4,10},{5,9},{6,8},{7,11},{8,6},{9,5},... | collective-permute-start | bytes 393224 | tf_op jit(solution)/shard_map/ppermute | solution.py:444
  104.3 6.1 %collective-permute-start.13 = (bf16[512,128]{1,0:T(8,128)(2,1)}, bf16[512,128]{1,0:T(8,128)(2,1)S(1)}, u32[]{:S(2)}, u32[]{:S(2)}) collective-permute-start(bf16[512,128]{1,0:T(8,128)(2,1)} %get-tuple-element.64), channel_id=1, source_target_pairs={{0,6},{1,15},{2,4},{3,13},{4,2},{5,11},{6,0},{7,9},{8,14},{9,7},{1... | collective-permute-start | bytes 393224 | tf_op jit(solution)/shard_map/ppermute | solution.py:444
  110.4 2.7 %collective-permute-start.8 = (bf16[512,128]{1,0:T(8,128)(2,1)}, bf16[512,128]{1,0:T(8,128)(2,1)S(1)}, u32[]{:S(2)}, u32[]{:S(2)}) collective-permute-start(bf16[512,128]{1,0:T(8,128)(2,1)} %get-tuple-element.59), channel_id=1, source_target_pairs={{0,10},{1,9},{2,8},{3,11},{4,14},{5,13},{6,12},{7,15},{8,2},{9,1},... | collective-permute-start | bytes 393224 | tf_op jit(solution)/shard_map/ppermute | solution.py:444
  113.2 1.6 %collective-permute-start.9 = (bf16[512,128]{1,0:T(8,128)(2,1)}, bf16[512,128]{1,0:T(8,128)(2,1)S(1)}, u32[]{:S(2)}, u32[]{:S(2)}) collective-permute-start(bf16[512,128]{1,0:T(8,128)(2,1)} %get-tuple-element.60), channel_id=1, source_target_pairs={{0,2},{1,5},{2,0},{3,7},{4,6},{5,1},{6,4},{7,3},{8,10},{9,13},{10,... | collective-permute-start | bytes 393224 | tf_op jit(solution)/shard_map/ppermute | solution.py:444
  114.8 2.5 %copy-done.1 = bf16[16,32,5120]{2,1,0:T(8,128)(2,1)S(1)} copy-done((bf16[16,32,5120]{2,1,0:T(8,128)(2,1)S(1)}, bf16[16,32,5120]{2,1,0:T(8,128)(2,1)}, u32[]{:S(2)}) %copy-start.1) | copy-done | bytes 5242904
  117.3 6.8 %shard_map.75 = (f32[8,1088,128]{2,1,0:T(8,128)S(1)}, s32[8,16]{1,0:T(8,128)S(1)}) custom-call(s32[16]{0:T(128)S(1)} %copy-done.5, s32[1]{0:T(128)} %bitcast.place_ref, s32[8]{0:T(128)S(1)} %dynamic-slice_bitcast_fusion.slot_ref, bf16[512,5120]{1,0:T(8,128)(2,1)S(1)} %bitcast.83, bf16[2064,128]{1,0:T(8,128)(2,1)S(1)} %collective-permute-done.rest_0_, ...), custom_call_target="tpu_custom_call" | custom-call | flops 2147483648 | bytes 4194304 | tf_op jit(solution)/shard_map/pallas_call | solution.py:266
  124.1 0.2 collective-permute-done.8.rest_1_
  124.3 3.0 %shard_map.77 = (bf16[8,544,128]{2,1,0:T(8,128)(2,1)S(1)}, bf16[8,544,128]{2,1,0:T(8,128)(2,1)S(1)}) custom-call(s32[8,16]{1,0:T(8,128)S(1)} %get-tuple-element.55.spots_ref, s32[1]{0:T(128)} %bitcast.1.core_ref, s32[1]{0:T(128)} %bitcast.place_ref, bf16[512,5120]{1,0:T(8,128)(2,1)S(1)} %bitcast.84, f32[8,1088,128]{2,1,0:T(8,128)S(1)} %get-tuple-element.56.acc_ref, ...), custom_call_target="tpu_custom_call" | custom-call | flops 536870912 | bytes 1048576 | tf_op jit(solution)/shard_map/pallas_call | solution.py:299
  127.3 0.1 collective-permute-start.14
  127.4 2.7 %collective-permute-done.14 = bf16[8,544,128]{2,1,0:T(8,128)(2,1)S(1)} collective-permute-done((bf16[8,544,128]{2,1,0:T(8,128)(2,1)S(1)}, bf16[8,544,128]{2,1,0:T(8,128)(2,1)S(1)}, u32[]{:S(2)}, u32[]{:S(2)}) %collective-permute-start.14) | collective-permute-done | bytes 1114144 | tf_op jit(solution)/shard_map/ppermute | solution.py:379
  130.1 0.1 fusion
  130.3 0.7 collective-permute-start.15
  130.9 0.1 fusion.5
  131.0 0.1 collective-permute-start.19
  131.1 3.1 %collective-permute-start.20 = (bf16[2,128,128]{2,1,0:T(8,128)(2,1)S(1)}, bf16[2,128,128]{2,1,0:T(8,128)(2,1)S(1)}, u32[]{:S(2)}, u32[]{:S(2)}) collective-permute-start(bf16[2,128,128]{2,1,0:T(8,128)(2,1)S(1)} %get-tuple-element.74), channel_id=1, source_target_pairs={{0,8},{2,10},{4,12},{6,14},{8,0},{10,2},{12,4},{14,6},{1,9},{3,11}... | collective-permute-start | bytes 196616 | tf_op jit(solution)/shard_map/ppermute | solution.py:379
  134.2 1.3 collective-permute-start.21
  135.4 0.7 collective-permute-done.19
  136.1 2.9 %collective-permute-done.20 = bf16[2,128,128]{2,1,0:T(8,128)(2,1)S(1)} collective-permute-done((bf16[2,128,128]{2,1,0:T(8,128)(2,1)S(1)}, bf16[2,128,128]{2,1,0:T(8,128)(2,1)S(1)}, u32[]{:S(2)}, u32[]{:S(2)}) %collective-permute-start.20) | collective-permute-done | bytes 65568 | tf_op jit(solution)/shard_map/ppermute | solution.py:379
  139.0 1.3 collective-permute-done.21
  140.4 1.5 collective-permute-start.22
  141.8 0.7 collective-permute-done.15
  142.5 0.1 fusion.3
  142.7 0.1 collective-permute-start.16
  142.8 3.0 %collective-permute-start.17 = (bf16[416,128]{1,0:T(8,128)(2,1)S(1)}, bf16[416,128]{1,0:T(8,128)(2,1)S(1)}, u32[]{:S(2)}, u32[]{:S(2)}) collective-permute-start(bf16[416,128]{1,0:T(8,128)(2,1)S(1)} %get-tuple-element.71), channel_id=1, source_target_pairs={{0,8},{2,10},{4,12},{6,14},{8,0},{10,2},{12,4},{14,6},{1,9},{3,11}... | collective-permute-start | bytes 319496 | tf_op jit(solution)/shard_map/ppermute | solution.py:379
  145.8 1.3 collective-permute-start.18
  147.2 0.6 collective-permute-done.16
  147.8 5.6 %collective-permute-done.17 = bf16[416,128]{1,0:T(8,128)(2,1)S(1)} collective-permute-done((bf16[416,128]{1,0:T(8,128)(2,1)S(1)}, bf16[416,128]{1,0:T(8,128)(2,1)S(1)}, u32[]{:S(2)}, u32[]{:S(2)}) %collective-permute-start.17) | collective-permute-done | bytes 106528 | tf_op jit(solution)/shard_map/ppermute | solution.py:379
  153.4 0.1 add_convert_fusion.1
  153.5 0.1 collective-permute-start.23
  153.5 1.3 collective-permute-done.23.other_ref
  154.9 2.2 %shard_map.78 = bf16[8,256,256]{2,1,0:T(8,128)(2,1)} custom-call(s32[8,16]{1,0:T(8,128)S(1)} %constant_dynamic-slice_fusion.slots_ref, s32[1]{0:T(128)} %bitcast.1.core_ref, bf16[544,128]{1,0:T(8,128)(2,1)S(1)} %pad_maximum_fusion.mine_ref, bf16[544,128]{1,0:T(8,128)(2,1)S(1)} %collective-permute-done.23.other_ref, bf16[8,512,256]{2,1,0:T(8,128)(2,1)S(1)} %copy-done.4, ...), custom_call_target="tpu_custom_call" | custom-call | flops 536870912 | bytes 5242880 | tf_op jit(solution)/shard_map/pallas_call | solution.py:358
  (35 shorter events, 0.1 us)
Async XLA Ops:
  0.0 13.7 %copy-start = (s32[16,16]{1,0:T(8,128)S(1)}, s32[16,16]{1,0:T(8,128)}, u32[]{:S(2)}) copy-start(s32[16,16]{1,0:T(8,128)} %param.9) | copy-start | bytes 3076
  4.2 18.1 %collective-permute-start.3 = (bf16[2064,128]{1,0:T(8,128)(2,1)}, bf16[2064,128]{1,0:T(8,128)(2,1)S(1)}, u32[]{:S(2)}, u32[]{:S(2)}) collective-permute-start(bf16[2064,128]{1,0:T(8,128)(2,1)} %get-tuple-element.40), channel_id=1, source_target_pairs={{0,12},{1,11},{2,14},{3,9},{4,8},{5,15},{6,10},{7,13},{8,4},{9,3},... | collective-permute-start | bytes 1585160 | tf_op jit(solution)/shard_map/ppermute | solution.py:444
  9.3 69.1 %collective-permute-start = (bf16[2064,128]{1,0:T(8,128)(2,1)}, bf16[2064,128]{1,0:T(8,128)(2,1)S(1)}, u32[]{:S(2)}, u32[]{:S(2)}) collective-permute-start(bf16[2064,128]{1,0:T(8,128)(2,1)} %get-tuple-element.37), channel_id=1, source_target_pairs={{0,8},{1,3},{2,10},{3,1},{4,12},{5,7},{6,14},{7,5},{8,0},{9,11},{1... | collective-permute-start | bytes 1585160 | tf_op jit(solution)/shard_map/ppermute | solution.py:444
  9.3 82.7 %collective-permute-start.1 = (bf16[2064,128]{1,0:T(8,128)(2,1)}, bf16[2064,128]{1,0:T(8,128)(2,1)S(1)}, u32[]{:S(2)}, u32[]{:S(2)}) collective-permute-start(bf16[2064,128]{1,0:T(8,128)(2,1)} %get-tuple-element.38), channel_id=1, source_target_pairs={{0,10},{1,9},{2,8},{3,11},{4,14},{5,13},{6,12},{7,15},{8,2},{9,1},... | collective-permute-start | bytes 1585160 | tf_op jit(solution)/shard_map/ppermute | solution.py:444
  13.2 81.1 %collective-permute-start.2 = (bf16[2064,128]{1,0:T(8,128)(2,1)}, bf16[2064,128]{1,0:T(8,128)(2,1)S(1)}, u32[]{:S(2)}, u32[]{:S(2)}) collective-permute-start(bf16[2064,128]{1,0:T(8,128)(2,1)} %get-tuple-element.39), channel_id=1, source_target_pairs={{0,2},{1,5},{2,0},{3,7},{4,6},{5,1},{6,4},{7,3},{8,10},{9,13},{10,... | collective-permute-start | bytes 1585160 | tf_op jit(solution)/shard_map/ppermute | solution.py:444
  13.7 88.9 %collective-permute-start.4 = (bf16[2064,128]{1,0:T(8,128)(2,1)}, bf16[2064,128]{1,0:T(8,128)(2,1)S(1)}, u32[]{:S(2)}, u32[]{:S(2)}) collective-permute-start(bf16[2064,128]{1,0:T(8,128)(2,1)} %get-tuple-element.42), channel_id=1, source_target_pairs={{0,4},{1,7},{2,6},{3,5},{4,0},{5,3},{6,2},{7,1},{8,12},{9,15},{10,... | collective-permute-start | bytes 1585160 | tf_op jit(solution)/shard_map/ppermute | solution.py:444
  22.3 80.3 %collective-permute-start.5 = (bf16[2064,128]{1,0:T(8,128)(2,1)}, bf16[2064,128]{1,0:T(8,128)(2,1)S(1)}, u32[]{:S(2)}, u32[]{:S(2)}) collective-permute-start(bf16[2064,128]{1,0:T(8,128)(2,1)} %get-tuple-element.43), channel_id=1, source_target_pairs={{0,14},{1,13},{2,12},{3,15},{4,10},{5,9},{6,8},{7,11},{8,6},{9,5},... | collective-permute-start | bytes 1585160 | tf_op jit(solution)/shard_map/ppermute | solution.py:444
  78.4 24.2 %collective-permute-start.6 = (bf16[2064,128]{1,0:T(8,128)(2,1)}, bf16[2064,128]{1,0:T(8,128)(2,1)}, u32[]{:S(2)}, u32[]{:S(2)}) collective-permute-start(bf16[2064,128]{1,0:T(8,128)(2,1)} %get-tuple-element.44), channel_id=1, source_target_pairs={{0,6},{1,15},{2,4},{3,13},{4,2},{5,11},{6,0},{7,9},{8,14},{9,7},{1... | collective-permute-start | bytes 1585160 | tf_op jit(solution)/shard_map/ppermute | solution.py:444
  92.0 18.5 %collective-permute-start.10 = (bf16[512,128]{1,0:T(8,128)(2,1)}, bf16[512,128]{1,0:T(8,128)(2,1)S(1)}, u32[]{:S(2)}, u32[]{:S(2)}) collective-permute-start(bf16[512,128]{1,0:T(8,128)(2,1)} %get-tuple-element.61), channel_id=1, source_target_pairs={{0,12},{1,11},{2,14},{3,9},{4,8},{5,15},{6,10},{7,13},{8,4},{9,3},... | collective-permute-start | bytes 393224 | tf_op jit(solution)/shard_map/ppermute | solution.py:444
  94.3 8.3 %copy-start.6 = (s32[2,8]{1,0:T(2,128)S(1)}, s32[2,8]{1,0:T(2,128)}, u32[]{:S(2)}) copy-start(s32[2,8]{1,0:T(2,128)} %constant.30.clone) | copy-start | bytes 196
  94.3 20.5 %copy-start.5 = (s32[16]{0:T(128)S(1)}, s32[16]{0:T(128)}, u32[]{:S(2)}) copy-start(s32[16]{0:T(128)} %wanted_ref.5) | copy-start | bytes 196
  94.3 18.8 %collective-permute-start.11 = (bf16[512,128]{1,0:T(8,128)(2,1)}, bf16[512,128]{1,0:T(8,128)(2,1)S(1)}, u32[]{:S(2)}, u32[]{:S(2)}) collective-permute-start(bf16[512,128]{1,0:T(8,128)(2,1)} %get-tuple-element.62), channel_id=1, source_target_pairs={{0,4},{1,7},{2,6},{3,5},{4,0},{5,3},{6,2},{7,1},{8,12},{9,15},{10,... | collective-permute-start | bytes 393224 | tf_op jit(solution)/shard_map/ppermute | solution.py:444
  102.6 21.4 %collective-permute-start.12 = (bf16[512,128]{1,0:T(8,128)(2,1)}, bf16[512,128]{1,0:T(8,128)(2,1)S(1)}, u32[]{:S(2)}, u32[]{:S(2)}) collective-permute-start(bf16[512,128]{1,0:T(8,128)(2,1)} %get-tuple-element.63), channel_id=1, source_target_pairs={{0,14},{1,13},{2,12},{3,15},{4,10},{5,9},{6,8},{7,11},{8,6},{9,5},... | collective-permute-start | bytes 393224 | tf_op jit(solution)/shard_map/ppermute | solution.py:444
  104.3 19.8 %collective-permute-start.13 = (bf16[512,128]{1,0:T(8,128)(2,1)}, bf16[512,128]{1,0:T(8,128)(2,1)S(1)}, u32[]{:S(2)}, u32[]{:S(2)}) collective-permute-start(bf16[512,128]{1,0:T(8,128)(2,1)} %get-tuple-element.64), channel_id=1, source_target_pairs={{0,6},{1,15},{2,4},{3,13},{4,2},{5,11},{6,0},{7,9},{8,14},{9,7},{1... | collective-permute-start | bytes 393224 | tf_op jit(solution)/shard_map/ppermute | solution.py:444
  110.4 13.7 %collective-permute-start.7 = (bf16[512,128]{1,0:T(8,128)(2,1)}, bf16[512,128]{1,0:T(8,128)(2,1)S(1)}, u32[]{:S(2)}, u32[]{:S(2)}) collective-permute-start(bf16[512,128]{1,0:T(8,128)(2,1)} %get-tuple-element.58), channel_id=1, source_target_pairs={{0,8},{1,3},{2,10},{3,1},{4,12},{5,7},{6,14},{7,5},{8,0},{9,11},{1... | collective-permute-start | bytes 393224 | tf_op jit(solution)/shard_map/ppermute | solution.py:444
  110.4 13.9 %collective-permute-start.8 = (bf16[512,128]{1,0:T(8,128)(2,1)}, bf16[512,128]{1,0:T(8,128)(2,1)S(1)}, u32[]{:S(2)}, u32[]{:S(2)}) collective-permute-start(bf16[512,128]{1,0:T(8,128)(2,1)} %get-tuple-element.59), channel_id=1, source_target_pairs={{0,10},{1,9},{2,8},{3,11},{4,14},{5,13},{6,12},{7,15},{8,2},{9,1},... | collective-permute-start | bytes 393224 | tf_op jit(solution)/shard_map/ppermute | solution.py:444
  113.2 11.2 %collective-permute-start.9 = (bf16[512,128]{1,0:T(8,128)(2,1)}, bf16[512,128]{1,0:T(8,128)(2,1)S(1)}, u32[]{:S(2)}, u32[]{:S(2)}) collective-permute-start(bf16[512,128]{1,0:T(8,128)(2,1)} %get-tuple-element.60), channel_id=1, source_target_pairs={{0,2},{1,5},{2,0},{3,7},{4,6},{5,1},{6,4},{7,3},{8,10},{9,13},{10,... | collective-permute-start | bytes 393224 | tf_op jit(solution)/shard_map/ppermute | solution.py:444
  114.8 2.5 %copy-start.1 = (bf16[16,32,5120]{2,1,0:T(8,128)(2,1)S(1)}, bf16[16,32,5120]{2,1,0:T(8,128)(2,1)}, u32[]{:S(2)}) copy-start(bf16[16,32,5120]{2,1,0:T(8,128)(2,1)} %param.7) | copy-start | bytes 15728644
  117.3 7.0 %copy-start.2 = (bf16[16,32,5120]{2,1,0:T(8,128)(2,1)S(1)}, bf16[16,32,5120]{2,1,0:T(8,128)(2,1)}, u32[]{:S(2)}) copy-start(bf16[16,32,5120]{2,1,0:T(8,128)(2,1)} %param.7) | copy-start | bytes 15728644
  127.3 2.8 %collective-permute-start.14 = (bf16[8,544,128]{2,1,0:T(8,128)(2,1)S(1)}, bf16[8,544,128]{2,1,0:T(8,128)(2,1)S(1)}, u32[]{:S(2)}, u32[]{:S(2)}) collective-permute-start(bf16[8,544,128]{2,1,0:T(8,128)(2,1)S(1)} %get-tuple-element.66), channel_id=1, source_target_pairs={{0,1},{1,0},{2,3},{3,2},{4,5},{5,4},{6,7},{7,6},{8,9},{9,8},{10,11... | collective-permute-start | bytes 3342344 | tf_op jit(solution)/shard_map/ppermute | solution.py:379
  130.1 24.8 %copy-start.4 = (bf16[8,512,256]{2,1,0:T(8,128)(2,1)S(1)}, bf16[8,512,256]{2,1,0:T(8,128)(2,1)}, u32[]{:S(2)}) copy-start(bf16[8,512,256]{2,1,0:T(8,128)(2,1)} %get-tuple-element.67.choose_ref) | copy-start | bytes 6291460
  130.3 12.3 %collective-permute-start.15 = (bf16[4,416,128]{2,1,0:T(8,128)(2,1)S(1)}, bf16[4,416,128]{2,1,0:T(8,128)(2,1)S(1)}, u32[]{:S(2)}, u32[]{:S(2)}) collective-permute-start(bf16[4,416,128]{2,1,0:T(8,128)(2,1)S(1)} %fusion), channel_id=1, source_target_pairs={{0,2},{2,0},{4,6},{6,4},{8,10},{10,8},{12,14},{14,12},{1,3},{3,1},... | collective-permute-start | bytes 1277960 | tf_op jit(solution)/shard_map/ppermute | solution.py:379
  131.0 5.1 %collective-permute-start.19 = (bf16[2,128,128]{2,1,0:T(8,128)(2,1)S(1)}, bf16[2,128,128]{2,1,0:T(8,128)(2,1)S(1)}, u32[]{:S(2)}, u32[]{:S(2)}) collective-permute-start(bf16[2,128,128]{2,1,0:T(8,128)(2,1)S(1)} %get-tuple-element.72), channel_id=1, source_target_pairs={{0,4},{2,6},{4,0},{6,2},{8,12},{10,14},{12,8},{14,10},{1,5},{3,7},... | collective-permute-start | bytes 196616 | tf_op jit(solution)/shard_map/ppermute | solution.py:379
  131.1 8.0 %collective-permute-start.20 = (bf16[2,128,128]{2,1,0:T(8,128)(2,1)S(1)}, bf16[2,128,128]{2,1,0:T(8,128)(2,1)S(1)}, u32[]{:S(2)}, u32[]{:S(2)}) collective-permute-start(bf16[2,128,128]{2,1,0:T(8,128)(2,1)S(1)} %get-tuple-element.74), channel_id=1, source_target_pairs={{0,8},{2,10},{4,12},{6,14},{8,0},{10,2},{12,4},{14,6},{1,9},{3,11}... | collective-permute-start | bytes 196616 | tf_op jit(solution)/shard_map/ppermute | solution.py:379
  134.2 6.2 %collective-permute-start.21 = (bf16[2,128,128]{2,1,0:T(8,128)(2,1)S(1)}, bf16[2,128,128]{2,1,0:T(8,128)(2,1)S(1)}, u32[]{:S(2)}, u32[]{:S(2)}) collective-permute-start(bf16[2,128,128]{2,1,0:T(8,128)(2,1)S(1)} %get-tuple-element.73), channel_id=1, source_target_pairs={{0,12},{2,14},{4,8},{6,10},{8,4},{10,6},{12,0},{14,2},{1,13},{3,15... | collective-permute-start | bytes 196616 | tf_op jit(solution)/shard_map/ppermute | solution.py:379
  140.4 14.5 %copy-start.3 = (f32[8,256,256]{2,1,0:T(8,128)S(1)}, f32[8,256,256]{2,1,0:T(8,128)}, u32[]{:S(2)}) copy-start(f32[8,256,256]{2,1,0:T(8,128)} %get-tuple-element.68.terms_ref) | copy-start | bytes 6291460
  140.4 6.8 %collective-permute-start.22 = (bf16[128,128]{1,0:T(8,128)(2,1)S(1)}, bf16[128,128]{1,0:T(8,128)(2,1)S(1)}, u32[]{:S(2)}, u32[]{:S(2)}) collective-permute-start(bf16[128,128]{1,0:T(8,128)(2,1)S(1)} %fusion.8), channel_id=1, source_target_pairs={{0,2},{2,0},{4,6},{6,4},{8,10},{10,8},{12,14},{14,12},{1,3},{3,1},... | collective-permute-start | bytes 98312 | tf_op jit(solution)/shard_map/ppermute | solution.py:379
  142.7 5.1 %collective-permute-start.16 = (bf16[416,128]{1,0:T(8,128)(2,1)S(1)}, bf16[416,128]{1,0:T(8,128)(2,1)S(1)}, u32[]{:S(2)}, u32[]{:S(2)}) collective-permute-start(bf16[416,128]{1,0:T(8,128)(2,1)S(1)} %get-tuple-element.69), channel_id=1, source_target_pairs={{0,4},{2,6},{4,0},{6,2},{8,12},{10,14},{12,8},{14,10},{1,5},{3,7},... | collective-permute-start | bytes 319496 | tf_op jit(solution)/shard_map/ppermute | solution.py:379
  142.8 10.5 %collective-permute-start.17 = (bf16[416,128]{1,0:T(8,128)(2,1)S(1)}, bf16[416,128]{1,0:T(8,128)(2,1)S(1)}, u32[]{:S(2)}, u32[]{:S(2)}) collective-permute-start(bf16[416,128]{1,0:T(8,128)(2,1)S(1)} %get-tuple-element.71), channel_id=1, source_target_pairs={{0,8},{2,10},{4,12},{6,14},{8,0},{10,2},{12,4},{14,6},{1,9},{3,11}... | collective-permute-start | bytes 319496 | tf_op jit(solution)/shard_map/ppermute | solution.py:379
  145.8 7.5 %collective-permute-start.18 = (bf16[416,128]{1,0:T(8,128)(2,1)S(1)}, bf16[416,128]{1,0:T(8,128)(2,1)S(1)}, u32[]{:S(2)}, u32[]{:S(2)}) collective-permute-start(bf16[416,128]{1,0:T(8,128)(2,1)S(1)} %get-tuple-element.70), channel_id=1, source_target_pairs={{0,12},{2,14},{4,8},{6,10},{8,4},{10,6},{12,0},{14,2},{1,13},{3,15... | collective-permute-start | bytes 319496 | tf_op jit(solution)/shard_map/ppermute | solution.py:379
  153.5 1.4 collective-permute-start.23

commit v4 on v3

--- a/solution.py
+++ b/solution.py
@@ -11,7 +11,7 @@
 UNIQ = 16
 TILE = 128
 SIDE = 4
-LATE = 1
+LATE = 2
 STRIP = 256
 LIST_ROWS = 16
 VMEM_BYTES = 60 * 1024 * 1024
@@ -54,57 +54,72 @@
     )(right_rows, fock, correlation, amplitudes)
 
 
-def split_kernel(orders, span, wanted_ref, place_ref, core_ref, blocks_ref, *rest):
-    outs, (bufs, tail, in_sems, out_sems) = rest[:-4], rest[-4:]
+def split_kernel(orders, span, own, wanted_ref, place_ref, core_ref, blocks_ref, *rest):
+    outs, (bufs, own_buf, tail, in_sems, out_sems) = rest[:-5], rest[-5:]
     rows, depth = blocks_ref.shape
-    columns = depth // (len(outs) + 1)
-    chunks = bufs.shape[2] // TILE
-    with_list = outs[0].shape[0] > chunks * rows
-    fetches = []
+    columns = own_buf.shape[1]
+    chunks = span[1] - span[0]
+    count = len(orders[0])
+    fetches, stores = [], []
+
+    def fetch(n, offset, first, buf):
+        start = pl.multiple_of((place_ref[0] ^ offset) * columns + first * TILE, TILE)
+        source = blocks_ref.at[:, pl.ds(start, buf.shape[1])]
+        fetches.append(pltpu.make_async_copy(source, buf, in_sems.at[n]))
+        fetches[-1].start()
+
+    def store(n, c, source, out, row):
+        target = out.at[pl.ds(row, source.shape[0])]
+        stores.append(pltpu.make_async_copy(source, target, out_sems.at[n, c]))
+        stores[-1].start()
+
     for n, ks in enumerate(zip(*orders)):
         offset = jnp.where(core_ref[0] % 2 == 0, *ks)
-        start = pl.multiple_of((place_ref[0] ^ offset) * columns + span[0] * TILE, TILE)
-        source = blocks_ref.at[:, pl.ds(start, chunks * TILE)]
-        fetches.append(pltpu.make_async_copy(source, bufs.at[n], in_sems.at[n]))
-        fetches[-1].start()
-    stores = []
-    if with_list:
+        fetch(n, offset, span[0], bufs.at[n])
+    if own:
+        fetch(count, 0, 0, own_buf)
+    else:
         lane = lax.broadcasted_iota(jnp.int32, tail.shape, 1)
         ids = jnp.zeros(tail.shape, jnp.int32)
         for m in range(UNIQ):
             ids = jnp.where(lane == m, wanted_ref[m], ids)
         tail[...] = ids.astype(jnp.float32).astype(jnp.bfloat16)
-        for n, out in enumerate(outs):
-            target = out.at[pl.ds(chunks * rows, LIST_ROWS)]
-            stores.append(pltpu.make_async_copy(tail, target, out_sems.at[n, chunks]))
-            stores[-1].start()
-    for n, out in enumerate(outs):
+        for n in range(count):
+            store(n, chunks, tail, outs[n], chunks * rows)
+    for n in range(count):
         fetches[n].wait()
         for c in range(chunks):
-            source = bufs.at[n, :, pl.ds(c * TILE, TILE)]
-            target = out.at[pl.ds(c * rows, rows)]
-            stores.append(pltpu.make_async_copy(source, target, out_sems.at[n, c]))
-            stores[-1].start()
+            store(n, c, bufs.at[n, :, pl.ds(c * TILE, TILE)], outs[n], c * rows)
+    if own:
+        fetches[count].wait()
+        for c in range(columns // TILE):
+            early = c < span[0]
+            out = outs[count] if early else outs[count + 1]
+            row = (c if early else c - span[0]) * rows
+            store(count, c, own_buf.at[:, pl.ds(c * TILE, TILE)], out, row)
     for copy in stores:
         copy.wait()
 
 
-def column_parts(orders, span, with_list, wanted, place, core, blocks):
-    rows, _ = blocks.shape
+def column_parts(orders, span, own, wanted, place, core, blocks):
+    rows, depth = blocks.shape
     count = len(orders[0])
+    columns = depth // (count + 1)
     chunks = span[1] - span[0]
-    height = chunks * rows + LIST_ROWS * with_list
-    out = jax.ShapeDtypeStruct((height, TILE), blocks.dtype)
+    heights = [chunks * rows + LIST_ROWS * (not own)] * count
+    if own:
+        heights += [span[0] * rows, chunks * rows]
     return pl.pallas_call(
-        functools.partial(split_kernel, orders, span),
+        functools.partial(split_kernel, orders, span, own),
         in_specs=[SMEM_SPEC] * 3 + [HBM_SPEC],
-        out_specs=[HBM_SPEC] * count,
-        out_shape=[out] * count,
+        out_specs=[HBM_SPEC] * len(heights),
+        out_shape=[jax.ShapeDtypeStruct((height, TILE), blocks.dtype) for height in heights],
         scratch_shapes=[
             pltpu.VMEM((count, rows, chunks * TILE), blocks.dtype),
+            pltpu.VMEM((rows, columns), blocks.dtype),
             pltpu.VMEM((LIST_ROWS, TILE), blocks.dtype),
-            pltpu.SemaphoreType.DMA((count,)),
-            pltpu.SemaphoreType.DMA((count, chunks + 1)),
+            pltpu.SemaphoreType.DMA((count + 1,)),
+            pltpu.SemaphoreType.DMA((count + 1, columns // TILE + 1)),
         ],
         compiler_params=pltpu.CompilerParams(vmem_limit_bytes=VMEM_BYTES),
     )(wanted, place, core, blocks)
@@ -161,34 +176,25 @@
     )
 
 
-def pool_copies(span, me, blocks_ref, arrived_refs, pool, sems):
-    rows, depth = blocks_ref.shape
-    holders = len(arrived_refs) + 1
-    part = (span[1] - span[0]) * rows
-    copies = []
-    for n, c in enumerate(range(*span)):
-        start = pl.multiple_of(me * (depth // holders) + c * TILE, TILE)
-        source = blocks_ref.at[:, pl.ds(start, TILE)]
-        copies.append(pltpu.make_async_copy(source, pool.at[pl.ds(n * rows, rows)], sems.at[0, n]))
-    for k, ref in enumerate(arrived_refs, 1):
-        target = pool.at[pl.ds(k * part, part)]
-        copies.append(pltpu.make_async_copy(ref.at[pl.ds(0, part)], target, sems.at[k, 0]))
-    return copies
-
-
-def early_kernel(ks, span, owned, wanted_ref, place_ref, slot_ref, blocks_ref, *rest):
-    arrived_refs, rest = rest[:-8], rest[-8:]
+def pool_copies(refs, part, pool, sems):
+    return [
+        pltpu.make_async_copy(ref.at[pl.ds(0, part)], pool.at[pl.ds(k * part, part)], sems.at[k])
+        for k, ref in enumerate(refs)
+    ]
+
+
+def early_kernel(ks, owned, width, wanted_ref, place_ref, slot_ref, *rest):
+    refs, rest = rest[:-8], rest[-8:]
     acc_ref, spots_ref, pool, lists, ids_vmem, ids, sems, list_sems = rest
-    rows = blocks_ref.shape[0]
-    width = rows // owned
-    chunks = span[1] - span[0]
-    part = chunks * rows
+    rows = owned * width
+    part = refs[0].shape[0]
+    chunks = part // rows
     me = place_ref[0]
     tails = [
         pltpu.make_async_copy(ref.at[pl.ds(part, LIST_ROWS)], lists.at[k], list_sems.at[k])
-        for k, ref in enumerate(arrived_refs, 1)
+        for k, ref in enumerate(refs[1:], 1)
     ]
-    copies = pool_copies(span, me, blocks_ref, arrived_refs, pool, sems)
+    copies = pool_copies(refs, part, pool, sems)
     for copy in tails + copies:
         copy.start()
     for copy in tails:
@@ -221,17 +227,16 @@
             at += value.shape[0]
 
 
-def late_kernel(span, owned, spots_ref, core_ref, place_ref, blocks_ref, acc_ref, *rest):
-    arrived_refs, rest = rest[:-4], rest[-4:]
+def late_kernel(owned, width, spots_ref, core_ref, acc_ref, *rest):
+    refs, rest = rest[:-4], rest[-4:]
     keep_ref, send_ref, pool, sems = rest
-    rows = blocks_ref.shape[0]
-    width = rows // owned
-    chunks = span[1] - span[0]
-    part = chunks * rows
+    rows = owned * width
+    part = refs[0].shape[0]
+    chunks = part // rows
     owners = acc_ref.shape[0]
     half = acc_ref.shape[1] // 2
     core = core_ref[0]
-    copies = pool_copies(span, place_ref[0], blocks_ref, arrived_refs, pool, sems)
+    copies = pool_copies(refs, part, pool, sems)
     for copy in copies:
         copy.start()
     for copy in copies:
@@ -258,13 +263,12 @@
     return SIDE * TILE + width
 
 
-def early_grams(ks, span, owned, wanted, place, slot, blocks, arrived):
-    holders = len(arrived) + 1
-    rows, depth = blocks.shape
-    width = rows // owned
-    chunks = span[1] - span[0]
+def early_grams(ks, owned, width, wanted, place, slot, parts):
+    holders = len(parts)
+    rows = owned * width
+    chunks = parts[0].shape[0] // rows
     return pl.pallas_call(
-        functools.partial(early_kernel, ks, span, owned),
+        functools.partial(early_kernel, ks, owned, width),
         in_specs=[SMEM_SPEC] * 3 + [HBM_SPEC] * holders,
         out_specs=[VMEM_SPEC, SMEM_SPEC],
         out_shape=[
@@ -276,7 +280,7 @@
             pltpu.VMEM((holders, LIST_ROWS, TILE), jnp.bfloat16),
             pltpu.VMEM((len(ks), TILE), jnp.int32),
             pltpu.SMEM((len(ks), TILE), jnp.int32),
-            pltpu.SemaphoreType.DMA((holders, chunks)),
+            pltpu.SemaphoreType.DMA((holders,)),
             pltpu.SemaphoreType.DMA((holders,)),
         ],
         compiler_params=pltpu.CompilerParams(vmem_limit_bytes=24 * 1024 * 1024),
@@ -285,25 +289,24 @@
             bytes_accessed=2 * holders * rows * chunks * TILE,
             transcendentals=0,
         ),
-    )(wanted, place, slot, blocks, *arrived)
-
-
-def late_grams(span, owned, spots, core, place, blocks, acc, arrived):
-    holders = len(arrived) + 1
-    rows, depth = blocks.shape
-    width = rows // owned
-    chunks = span[1] - span[0]
+    )(wanted, place, slot, *parts)
+
+
+def late_grams(owned, width, spots, core, acc, parts):
+    holders = len(parts)
+    rows = owned * width
+    chunks = parts[0].shape[0] // rows
     half = half_rows(width)
     out = jax.ShapeDtypeStruct((acc.shape[0], half, TILE), jnp.bfloat16)
     owners = acc.shape[0]
     return pl.pallas_call(
-        functools.partial(late_kernel, span, owned),
-        in_specs=[SMEM_SPEC] * 3 + [HBM_SPEC, VMEM_SPEC] + [HBM_SPEC] * len(arrived),
+        functools.partial(late_kernel, owned, width),
+        in_specs=[SMEM_SPEC] * 2 + [VMEM_SPEC] + [HBM_SPEC] * holders,
         out_specs=[VMEM_SPEC] * 2,
         out_shape=[out, out],
         scratch_shapes=[
             pltpu.VMEM((holders * rows * chunks, TILE), jnp.bfloat16),
-            pltpu.SemaphoreType.DMA((holders, chunks)),
+            pltpu.SemaphoreType.DMA((holders,)),
         ],
         compiler_params=pltpu.CompilerParams(vmem_limit_bytes=16 * 1024 * 1024),
         cost_estimate=pl.CostEstimate(
@@ -311,7 +314,7 @@
             bytes_accessed=2 * holders * rows * chunks * TILE,
             transcendentals=0,
         ),
-    )(spots, core, place, blocks, acc, *arrived)
+    )(spots, core, acc, *parts)
 
 
 def finish_kernel(slots_ref, core_ref, mine_ref, other_ref, choose_ref, terms_ref, out_ref, gram, stage, sems):
@@ -391,13 +394,14 @@
         return add(keep[bits, offsets, rows], came[bits, offsets, rows]).astype(jnp.bfloat16)
 
     every, top, rest = slice(None), slice(0, FIRST), slice(FIRST, None)
+    far_first = range(half - 1, 0, -1)
+    rest_far = [swap(both(every, j, rest), "pairs", 2 * j) for j in far_first]
     top_near = swap(both(1, every, top), "pairs", 1)
-    rest_far = [swap(both(every, j, rest), "pairs", 2 * j) for j in range(1, half)]
     top_sums = [
         add(keep[0, j, top], came[0, j, top], top_near[j]).astype(jnp.bfloat16)
         for j in range(half)
     ]
-    top_far = [swap(top_sums[j], "pairs", 2 * j) for j in range(1, half)]
+    top_far = [swap(top_sums[j], "pairs", 2 * j) for j in far_first]
     rest_sums = [
         add(keep[b, 0, rest], came[b, 0, rest], *(v[b] for v in rest_far)).astype(jnp.bfloat16)
         for b in range(2)
@@ -446,10 +450,11 @@
 
     cut = max(1, chunks - LATE)
     first, second = (0, cut), (cut, chunks)
-    early = exchange(column_parts(orders, first, True, wanted, place, core_id, stacked))
-    tied = len(early) // 2
+    early = exchange(column_parts(orders, first, False, wanted, place, core_id, stacked))
+    tied = 5
     early[tied], later = lax.optimization_barrier((early[tied], stacked))
-    late = exchange(column_parts(orders, second, False, wanted, place, core_id, later))
+    *late, own_early, own_late = column_parts(orders, second, True, wanted, place, core_id, later)
+    late = exchange(late)
     pairs_here = fock.shape[0]
     slots = lax.dynamic_slice_in_dim(pair_slots, core * pairs_here, pairs_here, axis=0)
     offsets = jnp.arange(width, dtype=jnp.int32)
@@ -457,8 +462,8 @@
     terms, choose = pair_terms(right_rows, fock, correlation, amplitudes)
     early, terms, choose, slots = lax.optimization_barrier((early, terms, choose, slots))
     order = (*range(0, holders, 2), *range(1, holders, 2))
-    acc, spots = early_grams(order, first, owned, wanted, place, slot, stacked, early)
-    keep, send = late_grams(second, owned, spots, core_id, place, stacked, acc, late)
+    acc, spots = early_grams(order, owned, width, wanted, place, slot, [own_early, *early])
+    keep, send = late_grams(owned, width, spots, core_id, acc, [own_late, *late])
     mine = to_owner(keep, swap(send, "aux", 1))
     other = swap(mine, "aux", 1)
     return finish(slots, core_id, mine, other, choose, terms)

time: 158 us -> 157 us (level)
  starting transfers between devices: 40.6 us -> 60.3 us
  waiting for transfers between devices: 85.3 us -> 67.3 us
  local copies, waits for them, and re-layouts: 2.76 us -> 0.28 us
    ppermute x14, waiting for transfers between devices: 69.4 us -> 49.9 us  [exchange(): arrived.append(lax.ppermute(part, ('pairs', 'aux'), moves))]
    ppermute x14, starting transfers between devices: 29.4 us -> 47.1 us  [exchange(): arrived.append(lax.ppermute(part, ('pairs', 'aux'), moves))]
    unnamed x14 -> x16, local copies, waits for them, and re-layouts: 2.51 us -> 0.03 us
    ppermute x10, starting transfers between devices: 11.2 us -> 13.2 us  [swap(): return lax.ppermute(value, axis, [(i, i ^ bit) for i in range(size)])]
  transfers between devices with their start and end apart: 24 -> 24, of which waited for: 12 -> 11; matrix products, arithmetic and copies ran while one was open for 1% -> 1% of each run, Pallas kernels for 11% -> 12%
where the time goes in v4:
time: 157 us; the launch traced here: 156 us
  waiting for transfers between devices  67.3 us (43%)
  starting transfers between devices  60.3 us (38%)
  Pallas kernels  27.1 us (17%)
    ppermute x14, waiting for transfers between devices, exchange(): arrived.append(lax.ppermute(part, ('pairs', 'aux'), moves))  49.9 us
    ppermute x14, starting transfers between devices, exchange(): arrived.append(lax.ppermute(part, ('pairs', 'aux'), moves))  47.1 us
    ppermute x10, waiting for transfers between devices, swap(): return lax.ppermute(value, axis, [(i, i ^ bit) for i in range(size)])  17.4 us
    ppermute x10, starting transfers between devices, swap(): return lax.ppermute(value, axis, [(i, i ^ bit) for i in range(size)])  13.2 us
    pallas_call x1, Pallas kernels, pair_terms(): pl.pallas_call(terms_kernel, grid=(pairs,), in_specs=[pl.BlockSpec((1, 1,...  8.36 us
    pallas_call x2, Pallas kernels, column_parts(): pl.pallas_call(functools.partial(split_kernel, orders, span, own), in_spe...  7.5 us
    pallas_call x1, Pallas kernels, early_grams(): pl.pallas_call(functools.partial(early_kernel, ks, owned, width), in_spec...  7.05 us
  transfers between devices with their start and end apart: 24, of which 11 were waited for; matrix products, arithmetic and copies ran while one was open for 1% of the time, Pallas kernels for 12%

profile of v4, /device:TPU:0, one launch (start us, length us, event | category | flops | bytes accessed | tf_op | source)
XLA Modules:
  0.0 156.3 jit_solution(7660674710294120599)
XLA Ops:
  0.0 3.8 %shard_map.73 = (bf16[1552,128]{1,0:T(8,128)(2,1)}, bf16[1552,128]{1,0:T(8,128)(2,1)}, bf16[1552,128]{1,0:T(8,128)(2,1)}, bf16[1552,128]{1,0:T(8,128)(2,1)}, bf1...) custom-call(s32[16]{0:T(128)} %wanted_ref.5, s32[1]{0:T(128)} %bitcast.place_ref, ...), custom_call_target="tpu_custom_call" | custom-call | tf_op jit(solution)/shard_map/pallas_call | solution.py:112
  3.8 4.1 %collective-permute-start = (bf16[1552,128]{1,0:T(8,128)(2,1)}, bf16[1552,128]{1,0:T(8,128)(2,1)S(1)}, u32[]{:S(2)}, u32[]{:S(2)}) collective-permute-start(bf16[1552,128]{1,0:T(8,128)(2,1)} %get-tuple-element.39), channel_id=1, source_target_pairs={{0,8},{1,3},{2,10},{3,1},{4,12},{5,7},{6,14},{7,5},{8,0},{9,11},{1... | collective-permute-start | bytes 1191944 | tf_op jit(solution)/shard_map/ppermute | solution.py:448
  7.9 2.3 %collective-permute-start.5 = (bf16[1552,128]{1,0:T(8,128)(2,1)}, bf16[1552,128]{1,0:T(8,128)(2,1)S(1)}, u32[]{:S(2)}, u32[]{:S(2)}) collective-permute-start(bf16[1552,128]{1,0:T(8,128)(2,1)} %get-tuple-element.44), channel_id=1, source_target_pairs={{0,14},{1,13},{2,12},{3,15},{4,10},{5,9},{6,8},{7,11},{8,6},{9,5},... | collective-permute-start | bytes 1191944 | tf_op jit(solution)/shard_map/ppermute | solution.py:448
  10.2 1.6 %collective-permute-start.1 = (bf16[1552,128]{1,0:T(8,128)(2,1)}, bf16[1552,128]{1,0:T(8,128)(2,1)S(1)}, u32[]{:S(2)}, u32[]{:S(2)}) collective-permute-start(bf16[1552,128]{1,0:T(8,128)(2,1)} %get-tuple-element.40), channel_id=1, source_target_pairs={{0,10},{1,9},{2,8},{3,11},{4,14},{5,13},{6,12},{7,15},{8,2},{9,1},... | collective-permute-start | bytes 1191944 | tf_op jit(solution)/shard_map/ppermute | solution.py:448
  11.9 1.5 collective-permute-start.2
  13.4 0.2 collective-permute-start.3
  13.6 33.9 %collective-permute-done.rest_1_ = bf16[1552,128]{1,0:T(8,128)(2,1)S(1)} collective-permute-done((bf16[1552,128]{1,0:T(8,128)(2,1)}, bf16[1552,128]{1,0:T(8,128)(2,1)S(1)}, u32[]{:S(2)}, u32[]{:S(2)}) %collective-permute-start) | collective-permute-done | bytes 397344 | tf_op jit(solution)/shard_map/ppermute | solution.py:448
  47.5 1.7 %collective-permute-start.4 = (bf16[1552,128]{1,0:T(8,128)(2,1)}, bf16[1552,128]{1,0:T(8,128)(2,1)S(1)}, u32[]{:S(2)}, u32[]{:S(2)}) collective-permute-start(bf16[1552,128]{1,0:T(8,128)(2,1)} %get-tuple-element.43), channel_id=1, source_target_pairs={{0,4},{1,7},{2,6},{3,5},{4,0},{5,3},{6,2},{7,1},{8,12},{9,15},{10,... | collective-permute-start | bytes 1191944 | tf_op jit(solution)/shard_map/ppermute | solution.py:448
  49.2 0.0 collective-permute-done.5.rest_6_
  49.2 13.8 %collective-permute-start.6 = (bf16[1552,128]{1,0:T(8,128)(2,1)}, bf16[1552,128]{1,0:T(8,128)(2,1)S(1)}, u32[]{:S(2)}, u32[]{:S(2)}) collective-permute-start(bf16[1552,128]{1,0:T(8,128)(2,1)} %get-tuple-element.46), channel_id=1, source_target_pairs={{0,6},{1,15},{2,4},{3,13},{4,2},{5,11},{6,0},{7,9},{8,14},{9,7},{1... | collective-permute-start | bytes 1191944 | tf_op jit(solution)/shard_map/ppermute | solution.py:448
  63.0 0.1 slice_multiply_fusion
  63.1 0.1 add.134
  63.2 0.1 add.131
  63.2 0.1 add.132
  63.3 3.7 %shard_map.75 = (bf16[1024,128]{1,0:T(8,128)(2,1)}, bf16[1024,128]{1,0:T(8,128)(2,1)}, bf16[1024,128]{1,0:T(8,128)(2,1)}, bf16[1024,128]{1,0:T(8,128)(2,1)}, bf1...) custom-call(s32[16]{0:T(128)} %wanted_ref.5, ...), custom_call_target="tpu_custom_call" | custom-call | tf_op jit(solution)/shard_map/pallas_call | solution.py:112
  67.0 6.4 %collective-permute-done.1.rest_2_ = bf16[1552,128]{1,0:T(8,128)(2,1)S(1)} collective-permute-done((bf16[1552,128]{1,0:T(8,128)(2,1)}, bf16[1552,128]{1,0:T(8,128)(2,1)S(1)}, u32[]{:S(2)}, u32[]{:S(2)}) %collective-permute-start.1) | collective-permute-done | bytes 397344 | tf_op jit(solution)/shard_map/ppermute | solution.py:448
  73.5 2.2 %collective-permute-start.8 = (bf16[1024,128]{1,0:T(8,128)(2,1)}, bf16[1024,128]{1,0:T(8,128)(2,1)S(1)}, u32[]{:S(2)}, u32[]{:S(2)}) collective-permute-start(bf16[1024,128]{1,0:T(8,128)(2,1)} %get-tuple-element.63), channel_id=1, source_target_pairs={{0,10},{1,9},{2,8},{3,11},{4,14},{5,13},{6,12},{7,15},{8,2},{9,1},... | collective-permute-start | bytes 786440 | tf_op jit(solution)/shard_map/ppermute | solution.py:448
  75.6 0.6 broadcast_add_fusion.right_ref
  76.3 8.4 %shard_map.74 = (f32[8,256,256]{2,1,0:T(8,128)}, bf16[8,512,256]{2,1,0:T(8,128)(2,1)}) custom-call(s32[8,1,256]{2,1,0:T(1,128)} %broadcast_add_fusion.right_ref, bf16[8,256,256]{2,1,0:T(8,128)(2,1)} %fock_ref.1, bf16[8,256,256]{2,1,0:T(8,128)(2,1)} %corr_ref.1, bf16[8,256,256]{2,1,0:T(8,128)(2,1)} %amp_ref.1), custom_call_target="tpu_custom_call" | custom-call | flops 1073741824 | bytes 7340032 | tf_op jit(solution)/shard_map/pallas_call | solution.py:39
  84.6 2.3 %collective-permute-start.9 = (bf16[1024,128]{1,0:T(8,128)(2,1)}, bf16[1024,128]{1,0:T(8,128)(2,1)S(1)}, u32[]{:S(2)}, u32[]{:S(2)}) collective-permute-start(bf16[1024,128]{1,0:T(8,128)(2,1)} %get-tuple-element.64), channel_id=1, source_target_pairs={{0,2},{1,5},{2,0},{3,7},{4,6},{5,1},{6,4},{7,3},{8,10},{9,13},{10,... | collective-permute-start | bytes 786440 | tf_op jit(solution)/shard_map/ppermute | solution.py:448
  86.9 3.7 %collective-permute-start.10 = (bf16[1024,128]{1,0:T(8,128)(2,1)}, bf16[1024,128]{1,0:T(8,128)(2,1)S(1)}, u32[]{:S(2)}, u32[]{:S(2)}) collective-permute-start(bf16[1024,128]{1,0:T(8,128)(2,1)} %get-tuple-element.65), channel_id=1, source_target_pairs={{0,12},{1,11},{2,14},{3,9},{4,8},{5,15},{6,10},{7,13},{8,4},{9,3},... | collective-permute-start | bytes 786440 | tf_op jit(solution)/shard_map/ppermute | solution.py:448
  90.6 3.7 %collective-permute-start.11 = (bf16[1024,128]{1,0:T(8,128)(2,1)}, bf16[1024,128]{1,0:T(8,128)(2,1)S(1)}, u32[]{:S(2)}, u32[]{:S(2)}) collective-permute-start(bf16[1024,128]{1,0:T(8,128)(2,1)} %get-tuple-element.66), channel_id=1, source_target_pairs={{0,4},{1,7},{2,6},{3,5},{4,0},{5,3},{6,2},{7,1},{8,12},{9,15},{10,... | collective-permute-start | bytes 786440 | tf_op jit(solution)/shard_map/ppermute | solution.py:448
  94.3 2.7 %collective-permute-done.7.rest_1_ = bf16[1024,128]{1,0:T(8,128)(2,1)S(1)} collective-permute-done((bf16[1024,128]{1,0:T(8,128)(2,1)}, bf16[1024,128]{1,0:T(8,128)(2,1)S(1)}, u32[]{:S(2)}, u32[]{:S(2)}) %collective-permute-start.7) | collective-permute-done | bytes 262176 | tf_op jit(solution)/shard_map/ppermute | solution.py:448
  97.0 9.1 %collective-permute-start.12 = (bf16[1024,128]{1,0:T(8,128)(2,1)}, bf16[1024,128]{1,0:T(8,128)(2,1)S(1)}, u32[]{:S(2)}, u32[]{:S(2)}) collective-permute-start(bf16[1024,128]{1,0:T(8,128)(2,1)} %get-tuple-element.67), channel_id=1, source_target_pairs={{0,14},{1,13},{2,12},{3,15},{4,10},{5,9},{6,8},{7,11},{8,6},{9,5},... | collective-permute-start | bytes 786440 | tf_op jit(solution)/shard_map/ppermute | solution.py:448
  106.0 6.8 %collective-permute-done.8.rest_2_ = bf16[1024,128]{1,0:T(8,128)(2,1)S(1)} collective-permute-done((bf16[1024,128]{1,0:T(8,128)(2,1)}, bf16[1024,128]{1,0:T(8,128)(2,1)S(1)}, u32[]{:S(2)}, u32[]{:S(2)}) %collective-permute-start.8) | collective-permute-done | bytes 262176 | tf_op jit(solution)/shard_map/ppermute | solution.py:448
  112.8 1.0 collective-permute-start.13
  113.9 7.0 %shard_map.76 = (f32[8,1088,128]{2,1,0:T(8,128)S(1)}, s32[8,16]{1,0:T(8,128)S(1)}) custom-call(s32[16]{0:T(128)S(1)} %copy-done.4, s32[1]{0:T(128)} %bitcast.place_ref, s32[8]{0:T(128)S(1)} %dynamic-slice_bitcast_fusion.slot_ref, bf16[1536,128]{1,0:T(8,128)(2,1)S(1)} %copy-done.5, bf16[1552,128]{1,0:T(8,128)(2,1)S(1)} %collective-permute-done.rest_1_, ...), custom_call_target="tpu_custom_call" | custom-call | flops 1610612736 | bytes 3145728 | tf_op jit(solution)/shard_map/pallas_call | solution.py:270
  121.0 2.0 %shard_map.77 = (bf16[8,544,128]{2,1,0:T(8,128)(2,1)S(1)}, bf16[8,544,128]{2,1,0:T(8,128)(2,1)S(1)}) custom-call(s32[8,16]{1,0:T(8,128)S(1)} %get-tuple-element.59.spots_ref, s32[1]{0:T(128)} %bitcast.1.core_ref, f32[8,1088,128]{2,1,0:T(8,128)S(1)} %get-tuple-element.60.acc_ref, bf16[1024,128]{1,0:T(8,128)(2,1)S(1)} %copy-done.3, ...), custom_call_target="tpu_custom_call" | custom-call | flops 1073741824 | bytes 2097152 | tf_op jit(solution)/shard_map/pallas_call | solution.py:302
  123.0 0.1 collective-permute-start.14
  123.1 2.7 %collective-permute-done.14 = bf16[8,544,128]{2,1,0:T(8,128)(2,1)S(1)} collective-permute-done((bf16[8,544,128]{2,1,0:T(8,128)(2,1)S(1)}, bf16[8,544,128]{2,1,0:T(8,128)(2,1)S(1)}, u32[]{:S(2)}, u32[]{:S(2)}) %collective-permute-start.14) | collective-permute-done | bytes 1114144 | tf_op jit(solution)/shard_map/ppermute | solution.py:382
  125.8 0.1 fusion
  125.9 0.6 collective-permute-start.15
  126.5 0.1 fusion.5
  126.5 2.8 %collective-permute-start.19 = (bf16[2,128,128]{2,1,0:T(8,128)(2,1)S(1)}, bf16[2,128,128]{2,1,0:T(8,128)(2,1)S(1)}, u32[]{:S(2)}, u32[]{:S(2)}) collective-permute-start(bf16[2,128,128]{2,1,0:T(8,128)(2,1)S(1)} %get-tuple-element.76), channel_id=1, source_target_pairs={{0,12},{2,14},{4,8},{6,10},{8,4},{10,6},{12,0},{14,2},{1,13},{3,15... | collective-permute-start | bytes 196616 | tf_op jit(solution)/shard_map/ppermute | solution.py:382
  129.4 4.8 %collective-permute-start.21 = (bf16[2,128,128]{2,1,0:T(8,128)(2,1)S(1)}, bf16[2,128,128]{2,1,0:T(8,128)(2,1)S(1)}, u32[]{:S(2)}, u32[]{:S(2)}) collective-permute-start(bf16[2,128,128]{2,1,0:T(8,128)(2,1)S(1)} %get-tuple-element.77), channel_id=1, source_target_pairs={{0,4},{2,6},{4,0},{6,2},{8,12},{10,14},{12,8},{14,10},{1,5},{3,7},... | collective-permute-start | bytes 196616 | tf_op jit(solution)/shard_map/ppermute | solution.py:382
  134.1 2.2 %collective-permute-done.21 = bf16[2,128,128]{2,1,0:T(8,128)(2,1)S(1)} collective-permute-done((bf16[2,128,128]{2,1,0:T(8,128)(2,1)S(1)}, bf16[2,128,128]{2,1,0:T(8,128)(2,1)S(1)}, u32[]{:S(2)}, u32[]{:S(2)}) %collective-permute-start.21) | collective-permute-done | bytes 65568 | tf_op jit(solution)/shard_map/ppermute | solution.py:382
  136.4 3.2 %collective-permute-done.20 = bf16[2,128,128]{2,1,0:T(8,128)(2,1)S(1)} collective-permute-done((bf16[2,128,128]{2,1,0:T(8,128)(2,1)S(1)}, bf16[2,128,128]{2,1,0:T(8,128)(2,1)S(1)}, u32[]{:S(2)}, u32[]{:S(2)}) %collective-permute-start.20) | collective-permute-done | bytes 65568 | tf_op jit(solution)/shard_map/ppermute | solution.py:382
  139.6 0.2 collective-permute-start.22
  139.9 0.1 fusion.3
  140.0 1.9 %collective-permute-start.16 = (bf16[416,128]{1,0:T(8,128)(2,1)S(1)}, bf16[416,128]{1,0:T(8,128)(2,1)S(1)}, u32[]{:S(2)}, u32[]{:S(2)}) collective-permute-start(bf16[416,128]{1,0:T(8,128)(2,1)S(1)} %get-tuple-element.73), channel_id=1, source_target_pairs={{0,12},{2,14},{4,8},{6,10},{8,4},{10,6},{12,0},{14,2},{1,13},{3,15... | collective-permute-start | bytes 319496 | tf_op jit(solution)/shard_map/ppermute | solution.py:382
  141.9 2.8 %collective-permute-start.18 = (bf16[416,128]{1,0:T(8,128)(2,1)S(1)}, bf16[416,128]{1,0:T(8,128)(2,1)S(1)}, u32[]{:S(2)}, u32[]{:S(2)}) collective-permute-start(bf16[416,128]{1,0:T(8,128)(2,1)S(1)} %get-tuple-element.74), channel_id=1, source_target_pairs={{0,4},{2,6},{4,0},{6,2},{8,12},{10,14},{12,8},{14,10},{1,5},{3,7},... | collective-permute-start | bytes 319496 | tf_op jit(solution)/shard_map/ppermute | solution.py:382
  144.7 2.9 %collective-permute-done.16 = bf16[416,128]{1,0:T(8,128)(2,1)S(1)} collective-permute-done((bf16[416,128]{1,0:T(8,128)(2,1)S(1)}, bf16[416,128]{1,0:T(8,128)(2,1)S(1)}, u32[]{:S(2)}, u32[]{:S(2)}) %collective-permute-start.16) | collective-permute-done | bytes 106528 | tf_op jit(solution)/shard_map/ppermute | solution.py:382
  147.6 0.9 collective-permute-done.18
  148.5 4.0 %collective-permute-done.17 = bf16[416,128]{1,0:T(8,128)(2,1)S(1)} collective-permute-done((bf16[416,128]{1,0:T(8,128)(2,1)S(1)}, bf16[416,128]{1,0:T(8,128)(2,1)S(1)}, u32[]{:S(2)}, u32[]{:S(2)}) %collective-permute-start.17) | collective-permute-done | bytes 106528 | tf_op jit(solution)/shard_map/ppermute | solution.py:382
  152.6 0.1 add_convert_fusion.1
  152.7 0.1 collective-permute-start.23
  152.8 1.3 collective-permute-done.23.other_ref
  154.1 2.2 %shard_map.78 = bf16[8,256,256]{2,1,0:T(8,128)(2,1)} custom-call(s32[8,16]{1,0:T(8,128)S(1)} %constant_dynamic-slice_fusion.slots_ref, s32[1]{0:T(128)} %bitcast.1.core_ref, bf16[544,128]{1,0:T(8,128)(2,1)S(1)} %pad_maximum_fusion.mine_ref, bf16[544,128]{1,0:T(8,128)(2,1)S(1)} %collective-permute-done.23.other_ref, bf16[8,512,256]{2,1,0:T(8,128)(2,1)S(1)} %copy-done.2, ...), custom_call_target="tpu_custom_call" | custom-call | flops 536870912 | bytes 5242880 | tf_op jit(solution)/shard_map/pallas_call | solution.py:361
  (37 shorter events, 0.1 us)
Async XLA Ops:
  0.0 13.6 %copy-start = (s32[16,16]{1,0:T(8,128)S(1)}, s32[16,16]{1,0:T(8,128)}, u32[]{:S(2)}) copy-start(s32[16,16]{1,0:T(8,128)} %param.9) | copy-start | bytes 3076
  3.8 43.7 %collective-permute-start = (bf16[1552,128]{1,0:T(8,128)(2,1)}, bf16[1552,128]{1,0:T(8,128)(2,1)S(1)}, u32[]{:S(2)}, u32[]{:S(2)}) collective-permute-start(bf16[1552,128]{1,0:T(8,128)(2,1)} %get-tuple-element.39), channel_id=1, source_target_pairs={{0,8},{1,3},{2,10},{3,1},{4,12},{5,7},{6,14},{7,5},{8,0},{9,11},{1... | collective-permute-start | bytes 1191944 | tf_op jit(solution)/shard_map/ppermute | solution.py:448
  7.9 41.3 %collective-permute-start.5 = (bf16[1552,128]{1,0:T(8,128)(2,1)}, bf16[1552,128]{1,0:T(8,128)(2,1)S(1)}, u32[]{:S(2)}, u32[]{:S(2)}) collective-permute-start(bf16[1552,128]{1,0:T(8,128)(2,1)} %get-tuple-element.44), channel_id=1, source_target_pairs={{0,14},{1,13},{2,12},{3,15},{4,10},{5,9},{6,8},{7,11},{8,6},{9,5},... | collective-permute-start | bytes 1191944 | tf_op jit(solution)/shard_map/ppermute | solution.py:448
  10.2 63.2 %collective-permute-start.1 = (bf16[1552,128]{1,0:T(8,128)(2,1)}, bf16[1552,128]{1,0:T(8,128)(2,1)S(1)}, u32[]{:S(2)}, u32[]{:S(2)}) collective-permute-start(bf16[1552,128]{1,0:T(8,128)(2,1)} %get-tuple-element.40), channel_id=1, source_target_pairs={{0,10},{1,9},{2,8},{3,11},{4,14},{5,13},{6,12},{7,15},{8,2},{9,1},... | collective-permute-start | bytes 1191944 | tf_op jit(solution)/shard_map/ppermute | solution.py:448
  11.9 61.6 %collective-permute-start.2 = (bf16[1552,128]{1,0:T(8,128)(2,1)}, bf16[1552,128]{1,0:T(8,128)(2,1)S(1)}, u32[]{:S(2)}, u32[]{:S(2)}) collective-permute-start(bf16[1552,128]{1,0:T(8,128)(2,1)} %get-tuple-element.41), channel_id=1, source_target_pairs={{0,2},{1,5},{2,0},{3,7},{4,6},{5,1},{6,4},{7,3},{8,10},{9,13},{10,... | collective-permute-start | bytes 1191944 | tf_op jit(solution)/shard_map/ppermute | solution.py:448
  13.4 71.2 %collective-permute-start.3 = (bf16[1552,128]{1,0:T(8,128)(2,1)}, bf16[1552,128]{1,0:T(8,128)(2,1)S(1)}, u32[]{:S(2)}, u32[]{:S(2)}) collective-permute-start(bf16[1552,128]{1,0:T(8,128)(2,1)} %get-tuple-element.42), channel_id=1, source_target_pairs={{0,12},{1,11},{2,14},{3,9},{4,8},{5,15},{6,10},{7,13},{8,4},{9,3},... | collective-permute-start | bytes 1191944 | tf_op jit(solution)/shard_map/ppermute | solution.py:448
  47.5 39.4 %collective-permute-start.4 = (bf16[1552,128]{1,0:T(8,128)(2,1)}, bf16[1552,128]{1,0:T(8,128)(2,1)S(1)}, u32[]{:S(2)}, u32[]{:S(2)}) collective-permute-start(bf16[1552,128]{1,0:T(8,128)(2,1)} %get-tuple-element.43), channel_id=1, source_target_pairs={{0,4},{1,7},{2,6},{3,5},{4,0},{5,3},{6,2},{7,1},{8,12},{9,15},{10,... | collective-permute-start | bytes 1191944 | tf_op jit(solution)/shard_map/ppermute | solution.py:448
  49.2 41.4 %collective-permute-start.6 = (bf16[1552,128]{1,0:T(8,128)(2,1)}, bf16[1552,128]{1,0:T(8,128)(2,1)S(1)}, u32[]{:S(2)}, u32[]{:S(2)}) collective-permute-start(bf16[1552,128]{1,0:T(8,128)(2,1)} %get-tuple-element.46), channel_id=1, source_target_pairs={{0,6},{1,15},{2,4},{3,13},{4,2},{5,11},{6,0},{7,9},{8,14},{9,7},{1... | collective-permute-start | bytes 1191944 | tf_op jit(solution)/shard_map/ppermute | solution.py:448
  73.4 23.5 %collective-permute-start.7 = (bf16[1024,128]{1,0:T(8,128)(2,1)}, bf16[1024,128]{1,0:T(8,128)(2,1)S(1)}, u32[]{:S(2)}, u32[]{:S(2)}) collective-permute-start(bf16[1024,128]{1,0:T(8,128)(2,1)} %get-tuple-element.62), channel_id=1, source_target_pairs={{0,8},{1,3},{2,10},{3,1},{4,12},{5,7},{6,14},{7,5},{8,0},{9,11},{1... | collective-permute-start | bytes 786440 | tf_op jit(solution)/shard_map/ppermute | solution.py:448
  73.5 39.4 %collective-permute-start.8 = (bf16[1024,128]{1,0:T(8,128)(2,1)}, bf16[1024,128]{1,0:T(8,128)(2,1)S(1)}, u32[]{:S(2)}, u32[]{:S(2)}) collective-permute-start(bf16[1024,128]{1,0:T(8,128)(2,1)} %get-tuple-element.63), channel_id=1, source_target_pairs={{0,10},{1,9},{2,8},{3,11},{4,14},{5,13},{6,12},{7,15},{8,2},{9,1},... | collective-permute-start | bytes 786440 | tf_op jit(solution)/shard_map/ppermute | solution.py:448
  76.2 36.6 %copy-start.6 = (bf16[1024,128]{1,0:T(8,128)(2,1)S(1)}, bf16[1024,128]{1,0:T(8,128)(2,1)}, u32[]{:S(2)}) copy-start(bf16[1024,128]{1,0:T(8,128)(2,1)} %get-tuple-element.68) | copy-start | bytes 786436
  76.2 37.6 %copy-start.7 = (s32[2,8]{1,0:T(2,128)S(1)}, s32[2,8]{1,0:T(2,128)}, u32[]{:S(2)}) copy-start(s32[2,8]{1,0:T(2,128)} %constant.30.clone) | copy-start | bytes 196
  76.2 37.6 %copy-start.4 = (s32[16]{0:T(128)S(1)}, s32[16]{0:T(128)}, u32[]{:S(2)}) copy-start(s32[16]{0:T(128)} %wanted_ref.5) | copy-start | bytes 196
  76.2 37.6 %copy-start.5 = (bf16[1536,128]{1,0:T(8,128)(2,1)S(1)}, bf16[1536,128]{1,0:T(8,128)(2,1)}, u32[]{:S(2)}) copy-start(bf16[1536,128]{1,0:T(8,128)(2,1)} %get-tuple-element.51.rest_0_) | copy-start | bytes 1179652
  84.6 36.3 %collective-permute-start.9 = (bf16[1024,128]{1,0:T(8,128)(2,1)}, bf16[1024,128]{1,0:T(8,128)(2,1)S(1)}, u32[]{:S(2)}, u32[]{:S(2)}) collective-permute-start(bf16[1024,128]{1,0:T(8,128)(2,1)} %get-tuple-element.64), channel_id=1, source_target_pairs={{0,2},{1,5},{2,0},{3,7},{4,6},{5,1},{6,4},{7,3},{8,10},{9,13},{10,... | collective-permute-start | bytes 786440 | tf_op jit(solution)/shard_map/ppermute | solution.py:448
  86.9 34.0 %collective-permute-start.10 = (bf16[1024,128]{1,0:T(8,128)(2,1)}, bf16[1024,128]{1,0:T(8,128)(2,1)S(1)}, u32[]{:S(2)}, u32[]{:S(2)}) collective-permute-start(bf16[1024,128]{1,0:T(8,128)(2,1)} %get-tuple-element.65), channel_id=1, source_target_pairs={{0,12},{1,11},{2,14},{3,9},{4,8},{5,15},{6,10},{7,13},{8,4},{9,3},... | collective-permute-start | bytes 786440 | tf_op jit(solution)/shard_map/ppermute | solution.py:448
  90.6 30.4 %collective-permute-start.11 = (bf16[1024,128]{1,0:T(8,128)(2,1)}, bf16[1024,128]{1,0:T(8,128)(2,1)S(1)}, u32[]{:S(2)}, u32[]{:S(2)}) collective-permute-start(bf16[1024,128]{1,0:T(8,128)(2,1)} %get-tuple-element.66), channel_id=1, source_target_pairs={{0,4},{1,7},{2,6},{3,5},{4,0},{5,3},{6,2},{7,1},{8,12},{9,15},{10,... | collective-permute-start | bytes 786440 | tf_op jit(solution)/shard_map/ppermute | solution.py:448
  97.0 24.0 %collective-permute-start.12 = (bf16[1024,128]{1,0:T(8,128)(2,1)}, bf16[1024,128]{1,0:T(8,128)(2,1)S(1)}, u32[]{:S(2)}, u32[]{:S(2)}) collective-permute-start(bf16[1024,128]{1,0:T(8,128)(2,1)} %get-tuple-element.67), channel_id=1, source_target_pairs={{0,14},{1,13},{2,12},{3,15},{4,10},{5,9},{6,8},{7,11},{8,6},{9,5},... | collective-permute-start | bytes 786440 | tf_op jit(solution)/shard_map/ppermute | solution.py:448
  112.8 8.1 %collective-permute-start.13 = (bf16[1024,128]{1,0:T(8,128)(2,1)S(1)}, bf16[1024,128]{1,0:T(8,128)(2,1)S(1)}, u32[]{:S(2)}, u32[]{:S(2)}) collective-permute-start(bf16[1024,128]{1,0:T(8,128)(2,1)S(1)} %copy-done.6), channel_id=1, source_target_pairs={{0,6},{1,15},{2,4},{3,13},{4,2},{5,11},{6,0},{7,9},{8,14},{9,7},{1... | collective-permute-start | bytes 786440 | tf_op jit(solution)/shard_map/ppermute | solution.py:448
  113.9 7.1 %copy-start.3 = (bf16[1024,128]{1,0:T(8,128)(2,1)S(1)}, bf16[1024,128]{1,0:T(8,128)(2,1)}, u32[]{:S(2)}) copy-start(bf16[1024,128]{1,0:T(8,128)(2,1)} %get-tuple-element.61.rest_0_) | copy-start | bytes 786436
  123.0 2.8 %collective-permute-start.14 = (bf16[8,544,128]{2,1,0:T(8,128)(2,1)S(1)}, bf16[8,544,128]{2,1,0:T(8,128)(2,1)S(1)}, u32[]{:S(2)}, u32[]{:S(2)}) collective-permute-start(bf16[8,544,128]{2,1,0:T(8,128)(2,1)S(1)} %get-tuple-element.70), channel_id=1, source_target_pairs={{0,1},{1,0},{2,3},{3,2},{4,5},{5,4},{6,7},{7,6},{8,9},{9,8},{10,11... | collective-permute-start | bytes 3342344 | tf_op jit(solution)/shard_map/ppermute | solution.py:382
  125.8 28.3 %copy-start.2 = (bf16[8,512,256]{2,1,0:T(8,128)(2,1)S(1)}, bf16[8,512,256]{2,1,0:T(8,128)(2,1)}, u32[]{:S(2)}) copy-start(bf16[8,512,256]{2,1,0:T(8,128)(2,1)} %get-tuple-element.71.choose_ref) | copy-start | bytes 6291460
  125.9 13.9 %collective-permute-start.15 = (bf16[4,416,128]{2,1,0:T(8,128)(2,1)S(1)}, bf16[4,416,128]{2,1,0:T(8,128)(2,1)S(1)}, u32[]{:S(2)}, u32[]{:S(2)}) collective-permute-start(bf16[4,416,128]{2,1,0:T(8,128)(2,1)S(1)} %fusion), channel_id=1, source_target_pairs={{0,2},{2,0},{4,6},{6,4},{8,10},{10,8},{12,14},{14,12},{1,3},{3,1},... | collective-permute-start | bytes 1277960 | tf_op jit(solution)/shard_map/ppermute | solution.py:382
  126.5 7.6 %collective-permute-start.19 = (bf16[2,128,128]{2,1,0:T(8,128)(2,1)S(1)}, bf16[2,128,128]{2,1,0:T(8,128)(2,1)S(1)}, u32[]{:S(2)}, u32[]{:S(2)}) collective-permute-start(bf16[2,128,128]{2,1,0:T(8,128)(2,1)S(1)} %get-tuple-element.76), channel_id=1, source_target_pairs={{0,12},{2,14},{4,8},{6,10},{8,4},{10,6},{12,0},{14,2},{1,13},{3,15... | collective-permute-start | bytes 196616 | tf_op jit(solution)/shard_map/ppermute | solution.py:382
  129.4 7.0 %collective-permute-start.21 = (bf16[2,128,128]{2,1,0:T(8,128)(2,1)S(1)}, bf16[2,128,128]{2,1,0:T(8,128)(2,1)S(1)}, u32[]{:S(2)}, u32[]{:S(2)}) collective-permute-start(bf16[2,128,128]{2,1,0:T(8,128)(2,1)S(1)} %get-tuple-element.77), channel_id=1, source_target_pairs={{0,4},{2,6},{4,0},{6,2},{8,12},{10,14},{12,8},{14,10},{1,5},{3,7},... | collective-permute-start | bytes 196616 | tf_op jit(solution)/shard_map/ppermute | solution.py:382
  134.1 5.5 %collective-permute-start.20 = (bf16[2,128,128]{2,1,0:T(8,128)(2,1)S(1)}, bf16[2,128,128]{2,1,0:T(8,128)(2,1)S(1)}, u32[]{:S(2)}, u32[]{:S(2)}) collective-permute-start(bf16[2,128,128]{2,1,0:T(8,128)(2,1)S(1)} %get-tuple-element.78), channel_id=1, source_target_pairs={{0,8},{2,10},{4,12},{6,14},{8,0},{10,2},{12,4},{14,6},{1,9},{3,11}... | collective-permute-start | bytes 196616 | tf_op jit(solution)/shard_map/ppermute | solution.py:382
  139.6 14.5 %copy-start.1 = (f32[8,256,256]{2,1,0:T(8,128)S(1)}, f32[8,256,256]{2,1,0:T(8,128)}, u32[]{:S(2)}) copy-start(f32[8,256,256]{2,1,0:T(8,128)} %get-tuple-element.72.terms_ref) | copy-start | bytes 6291460
  139.6 5.1 %collective-permute-start.22 = (bf16[128,128]{1,0:T(8,128)(2,1)S(1)}, bf16[128,128]{1,0:T(8,128)(2,1)S(1)}, u32[]{:S(2)}, u32[]{:S(2)}) collective-permute-start(bf16[128,128]{1,0:T(8,128)(2,1)S(1)} %fusion.8), channel_id=1, source_target_pairs={{0,2},{2,0},{4,6},{6,4},{8,10},{10,8},{12,14},{14,12},{1,3},{3,1},... | collective-permute-start | bytes 98312 | tf_op jit(solution)/shard_map/ppermute | solution.py:382
  140.0 7.6 %collective-permute-start.16 = (bf16[416,128]{1,0:T(8,128)(2,1)S(1)}, bf16[416,128]{1,0:T(8,128)(2,1)S(1)}, u32[]{:S(2)}, u32[]{:S(2)}) collective-permute-start(bf16[416,128]{1,0:T(8,128)(2,1)S(1)} %get-tuple-element.73), channel_id=1, source_target_pairs={{0,12},{2,14},{4,8},{6,10},{8,4},{10,6},{12,0},{14,2},{1,13},{3,15... | collective-permute-start | bytes 319496 | tf_op jit(solution)/shard_map/ppermute | solution.py:382
  141.9 6.6 %collective-permute-start.18 = (bf16[416,128]{1,0:T(8,128)(2,1)S(1)}, bf16[416,128]{1,0:T(8,128)(2,1)S(1)}, u32[]{:S(2)}, u32[]{:S(2)}) collective-permute-start(bf16[416,128]{1,0:T(8,128)(2,1)S(1)} %get-tuple-element.74), channel_id=1, source_target_pairs={{0,4},{2,6},{4,0},{6,2},{8,12},{10,14},{12,8},{14,10},{1,5},{3,7},... | collective-permute-start | bytes 319496 | tf_op jit(solution)/shard_map/ppermute | solution.py:382
  144.7 7.9 %collective-permute-start.17 = (bf16[416,128]{1,0:T(8,128)(2,1)S(1)}, bf16[416,128]{1,0:T(8,128)(2,1)S(1)}, u32[]{:S(2)}, u32[]{:S(2)}) collective-permute-start(bf16[416,128]{1,0:T(8,128)(2,1)S(1)} %get-tuple-element.75), channel_id=1, source_target_pairs={{0,8},{2,10},{4,12},{6,14},{8,0},{10,2},{12,4},{14,6},{1,9},{3,11}... | collective-permute-start | bytes 319496 | tf_op jit(solution)/shard_map/ppermute | solution.py:382
  152.7 1.4 collective-permute-start.23

commit v5 on v4

--- a/solution.py
+++ b/solution.py
@@ -12,11 +12,12 @@
 TILE = 128
 SIDE = 4
 LATE = 2
+
 STRIP = 256
 LIST_ROWS = 16
 VMEM_BYTES = 60 * 1024 * 1024
 LAST_VMEM = 24 * 1024 * 1024
-FIRST = 416
+FIRST = 384
 SMEM_SPEC = pl.BlockSpec(memory_space=pltpu.SMEM)
 VMEM_SPEC = pl.BlockSpec(memory_space=pltpu.VMEM)
 HBM_SPEC = pl.BlockSpec(memory_space=pltpu.HBM)
@@ -176,10 +177,14 @@
     )
 
 
-def pool_copies(refs, part, pool, sems):
+def pool_copies(refs, slots, part, pool, sems):
     return [
-        pltpu.make_async_copy(ref.at[pl.ds(0, part)], pool.at[pl.ds(k * part, part)], sems.at[k])
-        for k, ref in enumerate(refs)
+        pltpu.make_async_copy(
+            ref.at[pl.ds(0, part)],
+            pool.at[pl.ds(pl.multiple_of(slot * part, part), part)],
+            sems.at[k],
+        )
+        for k, (ref, slot) in enumerate(zip(refs, slots))
     ]
 
 
@@ -194,7 +199,7 @@
         pltpu.make_async_copy(ref.at[pl.ds(part, LIST_ROWS)], lists.at[k], list_sems.at[k])
         for k, ref in enumerate(refs[1:], 1)
     ]
-    copies = pool_copies(refs, part, pool, sems)
+    copies = pool_copies(refs, range(len(refs)), part, pool, sems)
     for copy in tails + copies:
         copy.start()
     for copy in tails:
@@ -227,7 +232,7 @@
             at += value.shape[0]
 
 
-def late_kernel(owned, width, spots_ref, core_ref, acc_ref, *rest):
+def late_kernel(slots, owned, width, spots_ref, core_ref, acc_ref, *rest):
     refs, rest = rest[:-4], rest[-4:]
     keep_ref, send_ref, pool, sems = rest
     rows = owned * width
@@ -236,7 +241,8 @@
     owners = acc_ref.shape[0]
     half = acc_ref.shape[1] // 2
     core = core_ref[0]
-    copies = pool_copies(refs, part, pool, sems)
+    targets = [jnp.where(core % 2 == 0, *pair) for pair in zip(*slots)]
+    copies = pool_copies(refs, targets, part, pool, sems)
     for copy in copies:
         copy.start()
     for copy in copies:
@@ -292,7 +298,7 @@
     )(wanted, place, slot, *parts)
 
 
-def late_grams(owned, width, spots, core, acc, parts):
+def late_grams(slots, owned, width, spots, core, acc, parts):
     holders = len(parts)
     rows = owned * width
     chunks = parts[0].shape[0] // rows
@@ -300,7 +306,7 @@
     out = jax.ShapeDtypeStruct((acc.shape[0], half, TILE), jnp.bfloat16)
     owners = acc.shape[0]
     return pl.pallas_call(
-        functools.partial(late_kernel, owned, width),
+        functools.partial(late_kernel, slots, owned, width),
         in_specs=[SMEM_SPEC] * 2 + [VMEM_SPEC] + [HBM_SPEC] * holders,
         out_specs=[VMEM_SPEC] * 2,
         out_shape=[out, out],
@@ -437,7 +443,7 @@
     chunks = depth // holders // TILE
     cores = lax.axis_size("aux")
 
-    def exchange(parts):
+    def exchange(parts, orders):
         arrived = []
         for n, part in enumerate(parts):
             moves = [
@@ -450,11 +456,13 @@
 
     cut = max(1, chunks - LATE)
     first, second = (0, cut), (cut, chunks)
-    early = exchange(column_parts(orders, first, False, wanted, place, core_id, stacked))
+    early = exchange(column_parts(orders, first, False, wanted, place, core_id, stacked), orders)
     tied = 5
     early[tied], later = lax.optimization_barrier((early[tied], stacked))
-    *late, own_early, own_late = column_parts(orders, second, True, wanted, place, core_id, later)
-    late = exchange(late)
+    late_orders = orders[::-1]
+    late_slots = [[0] + [t[k] for k in ks] for t, ks in zip(slot_tables, late_orders)]
+    *late, own_early, own_late = column_parts(late_orders, second, True, wanted, place, core_id, later)
+    late = exchange(late, late_orders)
     pairs_here = fock.shape[0]
     slots = lax.dynamic_slice_in_dim(pair_slots, core * pairs_here, pairs_here, axis=0)
     offsets = jnp.arange(width, dtype=jnp.int32)
@@ -463,7 +471,7 @@
     early, terms, choose, slots = lax.optimization_barrier((early, terms, choose, slots))
     order = (*range(0, holders, 2), *range(1, holders, 2))
     acc, spots = early_grams(order, owned, width, wanted, place, slot, [own_early, *early])
-    keep, send = late_grams(owned, width, spots, core_id, acc, [own_late, *late])
+    keep, send = late_grams(late_slots, owned, width, spots, core_id, acc, [own_late, *late])
     mine = to_owner(keep, swap(send, "aux", 1))
     other = swap(mine, "aux", 1)
     return finish(slots, core_id, mine, other, choose, terms)

time: 157 us -> 155 us (0.987)
  starting transfers between devices: 60.3 us -> 54.7 us
  waiting for transfers between devices: 67.3 us -> 70.8 us
    ppermute x14, starting transfers between devices: 47.1 us -> 42.6 us  [exchange(): arrived.append(lax.ppermute(part, ('pairs', 'aux'), moves))]
    ppermute x14, waiting for transfers between devices: 49.9 us -> 53.9 us  [exchange(): arrived.append(lax.ppermute(part, ('pairs', 'aux'), moves))]
  transfers between devices with their start and end apart: 24 -> 24, of which waited for: 11 -> 12; matrix products, arithmetic and copies ran while one was open for 1% -> 1% of each run, Pallas kernels for 12% -> 12%
where the time goes in v5:
time: 155 us; the launch traced here: 154 us
  waiting for transfers between devices  70.8 us (46%)
  starting transfers between devices  54.7 us (35%)
  Pallas kernels  27.1 us (17%)
    ppermute x14, waiting for transfers between devices, exchange(): arrived.append(lax.ppermute(part, ('pairs', 'aux'), moves))  53.9 us
    ppermute x14, starting transfers between devices, exchange(): arrived.append(lax.ppermute(part, ('pairs', 'aux'), moves))  42.6 us
    ppermute x10, waiting for transfers between devices, swap(): return lax.ppermute(value, axis, [(i, i ^ bit) for i in range(size)])  16.9 us
    ppermute x10, starting transfers between devices, swap(): return lax.ppermute(value, axis, [(i, i ^ bit) for i in range(size)])  12.1 us
    pallas_call x1, Pallas kernels, pair_terms(): pl.pallas_call(terms_kernel, grid=(pairs,), in_specs=[pl.BlockSpec((1, 1,...  8.36 us
    pallas_call x2, Pallas kernels, column_parts(): pl.pallas_call(functools.partial(split_kernel, orders, span, own), in_spe...  7.5 us
    pallas_call x1, Pallas kernels, early_grams(): pl.pallas_call(functools.partial(early_kernel, ks, owned, width), in_spec...  7.04 us
  transfers between devices with their start and end apart: 24, of which 12 were waited for; matrix products, arithmetic and copies ran while one was open for 1% of the time, Pallas kernels for 12%

profile of v5, /device:TPU:0, one launch (start us, length us, event | category | flops | bytes accessed | tf_op | source)
XLA Modules:
  0.0 154.3 jit_solution(3327917305544783386)
XLA Ops:
  0.0 3.8 %shard_map.73 = (bf16[1552,128]{1,0:T(8,128)(2,1)}, bf16[1552,128]{1,0:T(8,128)(2,1)}, bf16[1552,128]{1,0:T(8,128)(2,1)}, bf16[1552,128]{1,0:T(8,128)(2,1)}, bf1...) custom-call(s32[16]{0:T(128)} %wanted_ref.5, s32[1]{0:T(128)} %bitcast.place_ref, ...), custom_call_target="tpu_custom_call" | custom-call | tf_op jit(solution)/shard_map/pallas_call | solution.py:113
  3.8 4.1 %collective-permute-start = (bf16[1552,128]{1,0:T(8,128)(2,1)}, bf16[1552,128]{1,0:T(8,128)(2,1)S(1)}, u32[]{:S(2)}, u32[]{:S(2)}) collective-permute-start(bf16[1552,128]{1,0:T(8,128)(2,1)} %get-tuple-element.39), channel_id=1, source_target_pairs={{0,8},{1,3},{2,10},{3,1},{4,12},{5,7},{6,14},{7,5},{8,0},{9,11},{1... | collective-permute-start | bytes 1191944 | tf_op jit(solution)/shard_map/ppermute | solution.py:454
  7.9 2.3 %collective-permute-start.5 = (bf16[1552,128]{1,0:T(8,128)(2,1)}, bf16[1552,128]{1,0:T(8,128)(2,1)S(1)}, u32[]{:S(2)}, u32[]{:S(2)}) collective-permute-start(bf16[1552,128]{1,0:T(8,128)(2,1)} %get-tuple-element.44), channel_id=1, source_target_pairs={{0,14},{1,13},{2,12},{3,15},{4,10},{5,9},{6,8},{7,11},{8,6},{9,5},... | collective-permute-start | bytes 1191944 | tf_op jit(solution)/shard_map/ppermute | solution.py:454
  10.2 1.6 %collective-permute-start.1 = (bf16[1552,128]{1,0:T(8,128)(2,1)}, bf16[1552,128]{1,0:T(8,128)(2,1)S(1)}, u32[]{:S(2)}, u32[]{:S(2)}) collective-permute-start(bf16[1552,128]{1,0:T(8,128)(2,1)} %get-tuple-element.40), channel_id=1, source_target_pairs={{0,10},{1,9},{2,8},{3,11},{4,14},{5,13},{6,12},{7,15},{8,2},{9,1},... | collective-permute-start | bytes 1191944 | tf_op jit(solution)/shard_map/ppermute | solution.py:454
  11.9 1.5 collective-permute-start.2
  13.4 0.2 collective-permute-start.3
  13.6 33.9 %collective-permute-done.rest_1_ = bf16[1552,128]{1,0:T(8,128)(2,1)S(1)} collective-permute-done((bf16[1552,128]{1,0:T(8,128)(2,1)}, bf16[1552,128]{1,0:T(8,128)(2,1)S(1)}, u32[]{:S(2)}, u32[]{:S(2)}) %collective-permute-start) | collective-permute-done | bytes 397344 | tf_op jit(solution)/shard_map/ppermute | solution.py:454
  47.5 1.7 %collective-permute-start.4 = (bf16[1552,128]{1,0:T(8,128)(2,1)}, bf16[1552,128]{1,0:T(8,128)(2,1)S(1)}, u32[]{:S(2)}, u32[]{:S(2)}) collective-permute-start(bf16[1552,128]{1,0:T(8,128)(2,1)} %get-tuple-element.43), channel_id=1, source_target_pairs={{0,4},{1,7},{2,6},{3,5},{4,0},{5,3},{6,2},{7,1},{8,12},{9,15},{10,... | collective-permute-start | bytes 1191944 | tf_op jit(solution)/shard_map/ppermute | solution.py:454
  49.2 16.4 %collective-permute-start.6 = (bf16[1552,128]{1,0:T(8,128)(2,1)}, bf16[1552,128]{1,0:T(8,128)(2,1)S(1)}, u32[]{:S(2)}, u32[]{:S(2)}) collective-permute-start(bf16[1552,128]{1,0:T(8,128)(2,1)} %get-tuple-element.46), channel_id=1, source_target_pairs={{0,6},{1,15},{2,4},{3,13},{4,2},{5,11},{6,0},{7,9},{8,14},{9,7},{1... | collective-permute-start | bytes 1191944 | tf_op jit(solution)/shard_map/ppermute | solution.py:454
  65.7 0.1 slice_multiply_fusion
  65.7 0.1 add.134
  65.8 0.1 add.131
  65.9 0.1 add.132
  66.0 3.7 %shard_map.75 = (bf16[1024,128]{1,0:T(8,128)(2,1)}, bf16[1024,128]{1,0:T(8,128)(2,1)}, bf16[1024,128]{1,0:T(8,128)(2,1)}, bf16[1024,128]{1,0:T(8,128)(2,1)}, bf1...) custom-call(s32[16]{0:T(128)} %wanted_ref.5, ...), custom_call_target="tpu_custom_call" | custom-call | tf_op jit(solution)/shard_map/pallas_call | solution.py:113
  69.7 6.5 %collective-permute-done.1.rest_2_ = bf16[1552,128]{1,0:T(8,128)(2,1)S(1)} collective-permute-done((bf16[1552,128]{1,0:T(8,128)(2,1)}, bf16[1552,128]{1,0:T(8,128)(2,1)S(1)}, u32[]{:S(2)}, u32[]{:S(2)}) %collective-permute-start.1) | collective-permute-done | bytes 397344 | tf_op jit(solution)/shard_map/ppermute | solution.py:454
  76.2 0.2 collective-permute-start.8
  76.4 0.6 broadcast_add_fusion.right_ref
  77.0 8.4 %shard_map.74 = (f32[8,256,256]{2,1,0:T(8,128)}, bf16[8,512,256]{2,1,0:T(8,128)(2,1)}) custom-call(s32[8,1,256]{2,1,0:T(1,128)} %broadcast_add_fusion.right_ref, bf16[8,256,256]{2,1,0:T(8,128)(2,1)} %fock_ref.1, bf16[8,256,256]{2,1,0:T(8,128)(2,1)} %corr_ref.1, bf16[8,256,256]{2,1,0:T(8,128)(2,1)} %amp_ref.1), custom_call_target="tpu_custom_call" | custom-call | flops 1073741824 | bytes 7340032 | tf_op jit(solution)/shard_map/pallas_call | solution.py:40
  85.4 5.0 %collective-permute-start.9 = (bf16[1024,128]{1,0:T(8,128)(2,1)}, bf16[1024,128]{1,0:T(8,128)(2,1)S(1)}, u32[]{:S(2)}, u32[]{:S(2)}) collective-permute-start(bf16[1024,128]{1,0:T(8,128)(2,1)} %get-tuple-element.64), channel_id=1, source_target_pairs={{0,4},{1,3},{2,6},{3,1},{4,0},{5,7},{6,2},{7,5},{8,12},{9,11},{10,... | collective-permute-start | bytes 786440 | tf_op jit(solution)/shard_map/ppermute | solution.py:454
  90.3 2.8 %collective-permute-start.10 = (bf16[1024,128]{1,0:T(8,128)(2,1)}, bf16[1024,128]{1,0:T(8,128)(2,1)S(1)}, u32[]{:S(2)}, u32[]{:S(2)}) collective-permute-start(bf16[1024,128]{1,0:T(8,128)(2,1)} %get-tuple-element.65), channel_id=1, source_target_pairs={{0,10},{1,13},{2,8},{3,15},{4,14},{5,9},{6,12},{7,11},{8,2},{9,5},... | collective-permute-start | bytes 786440 | tf_op jit(solution)/shard_map/ppermute | solution.py:454
  93.1 2.0 %collective-permute-start.11 = (bf16[1024,128]{1,0:T(8,128)(2,1)}, bf16[1024,128]{1,0:T(8,128)(2,1)S(1)}, u32[]{:S(2)}, u32[]{:S(2)}) collective-permute-start(bf16[1024,128]{1,0:T(8,128)(2,1)} %get-tuple-element.66), channel_id=1, source_target_pairs={{0,6},{1,5},{2,4},{3,7},{4,2},{5,1},{6,0},{7,3},{8,14},{9,13},{10,... | collective-permute-start | bytes 786440 | tf_op jit(solution)/shard_map/ppermute | solution.py:454
  95.1 0.5 collective-permute-start.12
  95.6 4.2 %collective-permute-start.13 = (bf16[1024,128]{1,0:T(8,128)(2,1)S(1)}, bf16[1024,128]{1,0:T(8,128)(2,1)S(1)}, u32[]{:S(2)}, u32[]{:S(2)}) collective-permute-start(bf16[1024,128]{1,0:T(8,128)(2,1)S(1)} %copy-done.6), channel_id=1, source_target_pairs={{0,14},{1,7},{2,12},{3,5},{4,10},{5,3},{6,8},{7,1},{8,6},{9,15},{1... | collective-permute-start | bytes 786440 | tf_op jit(solution)/shard_map/ppermute | solution.py:454
  99.9 7.0 %shard_map.76 = (f32[8,1088,128]{2,1,0:T(8,128)S(1)}, s32[8,16]{1,0:T(8,128)S(1)}) custom-call(s32[16]{0:T(128)S(1)} %copy-done.4, s32[1]{0:T(128)} %bitcast.place_ref, s32[8]{0:T(128)S(1)} %dynamic-slice_bitcast_fusion.slot_ref, bf16[1536,128]{1,0:T(8,128)(2,1)S(1)} %copy-done.5, bf16[1552,128]{1,0:T(8,128)(2,1)S(1)} %collective-permute-done.rest_1_, ...), custom_call_target="tpu_custom_call" | custom-call | flops 1610612736 | bytes 3145728 | tf_op jit(solution)/shard_map/pallas_call | solution.py:276
  106.9 4.5 %collective-permute-done.9.rest_3_ = bf16[1024,128]{1,0:T(8,128)(2,1)S(1)} collective-permute-done((bf16[1024,128]{1,0:T(8,128)(2,1)}, bf16[1024,128]{1,0:T(8,128)(2,1)S(1)}, u32[]{:S(2)}, u32[]{:S(2)}) %collective-permute-start.9) | collective-permute-done | bytes 262176 | tf_op jit(solution)/shard_map/ppermute | solution.py:454
  111.5 9.0 %collective-permute-done.11.rest_5_ = bf16[1024,128]{1,0:T(8,128)(2,1)S(1)} collective-permute-done((bf16[1024,128]{1,0:T(8,128)(2,1)}, bf16[1024,128]{1,0:T(8,128)(2,1)S(1)}, u32[]{:S(2)}, u32[]{:S(2)}) %collective-permute-start.11) | collective-permute-done | bytes 262176 | tf_op jit(solution)/shard_map/ppermute | solution.py:454
  120.4 2.0 %shard_map.77 = (bf16[8,544,128]{2,1,0:T(8,128)(2,1)S(1)}, bf16[8,544,128]{2,1,0:T(8,128)(2,1)S(1)}) custom-call(s32[8,16]{1,0:T(8,128)S(1)} %get-tuple-element.59.spots_ref, s32[1]{0:T(128)} %bitcast.1.core_ref, f32[8,1088,128]{2,1,0:T(8,128)S(1)} %get-tuple-element.60.acc_ref, bf16[1024,128]{1,0:T(8,128)(2,1)S(1)} %copy-done.3, ...), custom_call_target="tpu_custom_call" | custom-call | flops 1073741824 | bytes 2097152 | tf_op jit(solution)/shard_map/pallas_call | solution.py:308
  122.5 0.1 collective-permute-start.14
  122.5 2.7 %collective-permute-done.14 = bf16[8,544,128]{2,1,0:T(8,128)(2,1)S(1)} collective-permute-done((bf16[8,544,128]{2,1,0:T(8,128)(2,1)S(1)}, bf16[8,544,128]{2,1,0:T(8,128)(2,1)S(1)}, u32[]{:S(2)}, u32[]{:S(2)}) %collective-permute-start.14) | collective-permute-done | bytes 1114144 | tf_op jit(solution)/shard_map/ppermute | solution.py:388
  125.3 0.1 fusion
  125.4 1.1 collective-permute-start.15
  126.6 2.5 %collective-permute-start.19 = (bf16[2,160,128]{2,1,0:T(8,128)(2,1)S(1)}, bf16[2,160,128]{2,1,0:T(8,128)(2,1)S(1)}, u32[]{:S(2)}, u32[]{:S(2)}) collective-permute-start(bf16[2,160,128]{2,1,0:T(8,128)(2,1)S(1)} %get-tuple-element.76), channel_id=1, source_target_pairs={{0,12},{2,14},{4,8},{6,10},{8,4},{10,6},{12,0},{14,2},{1,13},{3,15... | collective-permute-start | bytes 245768 | tf_op jit(solution)/shard_map/ppermute | solution.py:388
  129.1 3.1 %collective-permute-start.21 = (bf16[2,160,128]{2,1,0:T(8,128)(2,1)S(1)}, bf16[2,160,128]{2,1,0:T(8,128)(2,1)S(1)}, u32[]{:S(2)}, u32[]{:S(2)}) collective-permute-start(bf16[2,160,128]{2,1,0:T(8,128)(2,1)S(1)} %get-tuple-element.77), channel_id=1, source_target_pairs={{0,4},{2,6},{4,0},{6,2},{8,12},{10,14},{12,8},{14,10},{1,5},{3,7},... | collective-permute-start | bytes 245768 | tf_op jit(solution)/shard_map/ppermute | solution.py:388
  132.2 0.8 collective-permute-done.19
  133.0 1.6 %collective-permute-done.21 = bf16[2,160,128]{2,1,0:T(8,128)(2,1)S(1)} collective-permute-done((bf16[2,160,128]{2,1,0:T(8,128)(2,1)S(1)}, bf16[2,160,128]{2,1,0:T(8,128)(2,1)S(1)}, u32[]{:S(2)}, u32[]{:S(2)}) %collective-permute-start.21) | collective-permute-done | bytes 81952 | tf_op jit(solution)/shard_map/ppermute | solution.py:388
  134.7 3.7 %collective-permute-done.20 = bf16[2,160,128]{2,1,0:T(8,128)(2,1)S(1)} collective-permute-done((bf16[2,160,128]{2,1,0:T(8,128)(2,1)S(1)}, bf16[2,160,128]{2,1,0:T(8,128)(2,1)S(1)}, u32[]{:S(2)}, u32[]{:S(2)}) %collective-permute-start.20) | collective-permute-done | bytes 81952 | tf_op jit(solution)/shard_map/ppermute | solution.py:388
  138.4 0.8 collective-permute-start.22
  139.2 0.1 fusion.3
  139.3 2.4 %collective-permute-start.16 = (bf16[384,128]{1,0:T(8,128)(2,1)S(1)}, bf16[384,128]{1,0:T(8,128)(2,1)S(1)}, u32[]{:S(2)}, u32[]{:S(2)}) collective-permute-start(bf16[384,128]{1,0:T(8,128)(2,1)S(1)} %get-tuple-element.73), channel_id=1, source_target_pairs={{0,12},{2,14},{4,8},{6,10},{8,4},{10,6},{12,0},{14,2},{1,13},{3,15... | collective-permute-start | bytes 294920 | tf_op jit(solution)/shard_map/ppermute | solution.py:388
  141.7 0.5 collective-permute-start.18
  142.2 1.6 %collective-permute-start.17 = (bf16[384,128]{1,0:T(8,128)(2,1)S(1)}, bf16[384,128]{1,0:T(8,128)(2,1)S(1)}, u32[]{:S(2)}, u32[]{:S(2)}) collective-permute-start(bf16[384,128]{1,0:T(8,128)(2,1)S(1)} %get-tuple-element.75), channel_id=1, source_target_pairs={{0,8},{2,10},{4,12},{6,14},{8,0},{10,2},{12,4},{14,6},{1,9},{3,11}... | collective-permute-start | bytes 294920 | tf_op jit(solution)/shard_map/ppermute | solution.py:388
  143.8 3.2 %collective-permute-done.16 = bf16[384,128]{1,0:T(8,128)(2,1)S(1)} collective-permute-done((bf16[384,128]{1,0:T(8,128)(2,1)S(1)}, bf16[384,128]{1,0:T(8,128)(2,1)S(1)}, u32[]{:S(2)}, u32[]{:S(2)}) %collective-permute-start.16) | collective-permute-done | bytes 98336 | tf_op jit(solution)/shard_map/ppermute | solution.py:388
  147.0 1.2 collective-permute-done.18
  148.2 2.4 %collective-permute-done.17 = bf16[384,128]{1,0:T(8,128)(2,1)S(1)} collective-permute-done((bf16[384,128]{1,0:T(8,128)(2,1)S(1)}, bf16[384,128]{1,0:T(8,128)(2,1)S(1)}, u32[]{:S(2)}, u32[]{:S(2)}) %collective-permute-start.17) | collective-permute-done | bytes 98336 | tf_op jit(solution)/shard_map/ppermute | solution.py:388
  150.5 0.1 add_convert_fusion.1
  150.6 0.1 collective-permute-start.23
  150.7 1.3 collective-permute-done.23.other_ref
  152.1 2.2 %shard_map.78 = bf16[8,256,256]{2,1,0:T(8,128)(2,1)} custom-call(s32[8,16]{1,0:T(8,128)S(1)} %constant_dynamic-slice_fusion.slots_ref, s32[1]{0:T(128)} %bitcast.1.core_ref, bf16[544,128]{1,0:T(8,128)(2,1)S(1)} %pad_maximum_fusion.mine_ref, bf16[544,128]{1,0:T(8,128)(2,1)S(1)} %collective-permute-done.23.other_ref, bf16[8,512,256]{2,1,0:T(8,128)(2,1)S(1)} %copy-done.2, ...), custom_call_target="tpu_custom_call" | custom-call | flops 536870912 | bytes 5242880 | tf_op jit(solution)/shard_map/pallas_call | solution.py:367
  (37 shorter events, 0.2 us)
Async XLA Ops:
  0.0 13.6 %copy-start = (s32[16,16]{1,0:T(8,128)S(1)}, s32[16,16]{1,0:T(8,128)}, u32[]{:S(2)}) copy-start(s32[16,16]{1,0:T(8,128)} %param.9) | copy-start | bytes 3076
  3.8 43.7 %collective-permute-start = (bf16[1552,128]{1,0:T(8,128)(2,1)}, bf16[1552,128]{1,0:T(8,128)(2,1)S(1)}, u32[]{:S(2)}, u32[]{:S(2)}) collective-permute-start(bf16[1552,128]{1,0:T(8,128)(2,1)} %get-tuple-element.39), channel_id=1, source_target_pairs={{0,8},{1,3},{2,10},{3,1},{4,12},{5,7},{6,14},{7,5},{8,0},{9,11},{1... | collective-permute-start | bytes 1191944 | tf_op jit(solution)/shard_map/ppermute | solution.py:454
  7.9 41.3 %collective-permute-start.5 = (bf16[1552,128]{1,0:T(8,128)(2,1)}, bf16[1552,128]{1,0:T(8,128)(2,1)S(1)}, u32[]{:S(2)}, u32[]{:S(2)}) collective-permute-start(bf16[1552,128]{1,0:T(8,128)(2,1)} %get-tuple-element.44), channel_id=1, source_target_pairs={{0,14},{1,13},{2,12},{3,15},{4,10},{5,9},{6,8},{7,11},{8,6},{9,5},... | collective-permute-start | bytes 1191944 | tf_op jit(solution)/shard_map/ppermute | solution.py:454
  10.2 65.9 %collective-permute-start.1 = (bf16[1552,128]{1,0:T(8,128)(2,1)}, bf16[1552,128]{1,0:T(8,128)(2,1)S(1)}, u32[]{:S(2)}, u32[]{:S(2)}) collective-permute-start(bf16[1552,128]{1,0:T(8,128)(2,1)} %get-tuple-element.40), channel_id=1, source_target_pairs={{0,10},{1,9},{2,8},{3,11},{4,14},{5,13},{6,12},{7,15},{8,2},{9,1},... | collective-permute-start | bytes 1191944 | tf_op jit(solution)/shard_map/ppermute | solution.py:454
  11.9 64.3 %collective-permute-start.2 = (bf16[1552,128]{1,0:T(8,128)(2,1)}, bf16[1552,128]{1,0:T(8,128)(2,1)S(1)}, u32[]{:S(2)}, u32[]{:S(2)}) collective-permute-start(bf16[1552,128]{1,0:T(8,128)(2,1)} %get-tuple-element.41), channel_id=1, source_target_pairs={{0,2},{1,5},{2,0},{3,7},{4,6},{5,1},{6,4},{7,3},{8,10},{9,13},{10,... | collective-permute-start | bytes 1191944 | tf_op jit(solution)/shard_map/ppermute | solution.py:454
  13.4 72.0 %collective-permute-start.3 = (bf16[1552,128]{1,0:T(8,128)(2,1)}, bf16[1552,128]{1,0:T(8,128)(2,1)S(1)}, u32[]{:S(2)}, u32[]{:S(2)}) collective-permute-start(bf16[1552,128]{1,0:T(8,128)(2,1)} %get-tuple-element.42), channel_id=1, source_target_pairs={{0,12},{1,11},{2,14},{3,9},{4,8},{5,15},{6,10},{7,13},{8,4},{9,3},... | collective-permute-start | bytes 1191944 | tf_op jit(solution)/shard_map/ppermute | solution.py:454
  47.5 42.8 %collective-permute-start.4 = (bf16[1552,128]{1,0:T(8,128)(2,1)}, bf16[1552,128]{1,0:T(8,128)(2,1)S(1)}, u32[]{:S(2)}, u32[]{:S(2)}) collective-permute-start(bf16[1552,128]{1,0:T(8,128)(2,1)} %get-tuple-element.43), channel_id=1, source_target_pairs={{0,4},{1,7},{2,6},{3,5},{4,0},{5,3},{6,2},{7,1},{8,12},{9,15},{10,... | collective-permute-start | bytes 1191944 | tf_op jit(solution)/shard_map/ppermute | solution.py:454
  49.2 43.9 %collective-permute-start.6 = (bf16[1552,128]{1,0:T(8,128)(2,1)}, bf16[1552,128]{1,0:T(8,128)(2,1)S(1)}, u32[]{:S(2)}, u32[]{:S(2)}) collective-permute-start(bf16[1552,128]{1,0:T(8,128)(2,1)} %get-tuple-element.46), channel_id=1, source_target_pairs={{0,6},{1,15},{2,4},{3,13},{4,2},{5,11},{6,0},{7,9},{8,14},{9,7},{1... | collective-permute-start | bytes 1191944 | tf_op jit(solution)/shard_map/ppermute | solution.py:454
  76.2 18.9 %collective-permute-start.7 = (bf16[1024,128]{1,0:T(8,128)(2,1)}, bf16[1024,128]{1,0:T(8,128)(2,1)S(1)}, u32[]{:S(2)}, u32[]{:S(2)}) collective-permute-start(bf16[1024,128]{1,0:T(8,128)(2,1)} %get-tuple-element.62), channel_id=1, source_target_pairs={{0,2},{1,9},{2,0},{3,11},{4,6},{5,13},{6,4},{7,15},{8,10},{9,1},{1... | collective-permute-start | bytes 786440 | tf_op jit(solution)/shard_map/ppermute | solution.py:454
  76.2 19.4 %collective-permute-start.8 = (bf16[1024,128]{1,0:T(8,128)(2,1)}, bf16[1024,128]{1,0:T(8,128)(2,1)S(1)}, u32[]{:S(2)}, u32[]{:S(2)}) collective-permute-start(bf16[1024,128]{1,0:T(8,128)(2,1)} %get-tuple-element.63), channel_id=1, source_target_pairs={{0,8},{1,11},{2,10},{3,9},{4,12},{5,15},{6,14},{7,13},{8,0},{9,3},... | collective-permute-start | bytes 786440 | tf_op jit(solution)/shard_map/ppermute | solution.py:454
  77.0 18.6 %copy-start.6 = (bf16[1024,128]{1,0:T(8,128)(2,1)S(1)}, bf16[1024,128]{1,0:T(8,128)(2,1)}, u32[]{:S(2)}) copy-start(bf16[1024,128]{1,0:T(8,128)(2,1)} %get-tuple-element.68) | copy-start | bytes 786436
  77.0 22.9 %copy-start.7 = (s32[2,8]{1,0:T(2,128)S(1)}, s32[2,8]{1,0:T(2,128)}, u32[]{:S(2)}) copy-start(s32[2,8]{1,0:T(2,128)} %constant.30.clone) | copy-start | bytes 196
  77.0 22.9 %copy-start.4 = (s32[16]{0:T(128)S(1)}, s32[16]{0:T(128)}, u32[]{:S(2)}) copy-start(s32[16]{0:T(128)} %wanted_ref.5) | copy-start | bytes 196
  77.0 22.9 %copy-start.5 = (bf16[1536,128]{1,0:T(8,128)(2,1)S(1)}, bf16[1536,128]{1,0:T(8,128)(2,1)}, u32[]{:S(2)}) copy-start(bf16[1536,128]{1,0:T(8,128)(2,1)} %get-tuple-element.51.rest_0_) | copy-start | bytes 1179652
  85.4 26.1 %collective-permute-start.9 = (bf16[1024,128]{1,0:T(8,128)(2,1)}, bf16[1024,128]{1,0:T(8,128)(2,1)S(1)}, u32[]{:S(2)}, u32[]{:S(2)}) collective-permute-start(bf16[1024,128]{1,0:T(8,128)(2,1)} %get-tuple-element.64), channel_id=1, source_target_pairs={{0,4},{1,3},{2,6},{3,1},{4,0},{5,7},{6,2},{7,5},{8,12},{9,11},{10,... | collective-permute-start | bytes 786440 | tf_op jit(solution)/shard_map/ppermute | solution.py:454
  90.3 21.1 %collective-permute-start.10 = (bf16[1024,128]{1,0:T(8,128)(2,1)}, bf16[1024,128]{1,0:T(8,128)(2,1)S(1)}, u32[]{:S(2)}, u32[]{:S(2)}) collective-permute-start(bf16[1024,128]{1,0:T(8,128)(2,1)} %get-tuple-element.65), channel_id=1, source_target_pairs={{0,10},{1,13},{2,8},{3,15},{4,14},{5,9},{6,12},{7,11},{8,2},{9,5},... | collective-permute-start | bytes 786440 | tf_op jit(solution)/shard_map/ppermute | solution.py:454
  93.1 27.3 %collective-permute-start.11 = (bf16[1024,128]{1,0:T(8,128)(2,1)}, bf16[1024,128]{1,0:T(8,128)(2,1)S(1)}, u32[]{:S(2)}, u32[]{:S(2)}) collective-permute-start(bf16[1024,128]{1,0:T(8,128)(2,1)} %get-tuple-element.66), channel_id=1, source_target_pairs={{0,6},{1,5},{2,4},{3,7},{4,2},{5,1},{6,0},{7,3},{8,14},{9,13},{10,... | collective-permute-start | bytes 786440 | tf_op jit(solution)/shard_map/ppermute | solution.py:454
  95.1 25.4 %collective-permute-start.12 = (bf16[1024,128]{1,0:T(8,128)(2,1)}, bf16[1024,128]{1,0:T(8,128)(2,1)S(1)}, u32[]{:S(2)}, u32[]{:S(2)}) collective-permute-start(bf16[1024,128]{1,0:T(8,128)(2,1)} %get-tuple-element.67), channel_id=1, source_target_pairs={{0,12},{1,15},{2,14},{3,13},{4,8},{5,11},{6,10},{7,9},{8,4},{9,7},... | collective-permute-start | bytes 786440 | tf_op jit(solution)/shard_map/ppermute | solution.py:454
  95.6 24.8 %collective-permute-start.13 = (bf16[1024,128]{1,0:T(8,128)(2,1)S(1)}, bf16[1024,128]{1,0:T(8,128)(2,1)S(1)}, u32[]{:S(2)}, u32[]{:S(2)}) collective-permute-start(bf16[1024,128]{1,0:T(8,128)(2,1)S(1)} %copy-done.6), channel_id=1, source_target_pairs={{0,14},{1,7},{2,12},{3,5},{4,10},{5,3},{6,8},{7,1},{8,6},{9,15},{1... | collective-permute-start | bytes 786440 | tf_op jit(solution)/shard_map/ppermute | solution.py:454
  99.9 20.6 %copy-start.3 = (bf16[1024,128]{1,0:T(8,128)(2,1)S(1)}, bf16[1024,128]{1,0:T(8,128)(2,1)}, u32[]{:S(2)}) copy-start(bf16[1024,128]{1,0:T(8,128)(2,1)} %get-tuple-element.61.rest_0_) | copy-start | bytes 786436
  122.5 2.8 %collective-permute-start.14 = (bf16[8,544,128]{2,1,0:T(8,128)(2,1)S(1)}, bf16[8,544,128]{2,1,0:T(8,128)(2,1)S(1)}, u32[]{:S(2)}, u32[]{:S(2)}) collective-permute-start(bf16[8,544,128]{2,1,0:T(8,128)(2,1)S(1)} %get-tuple-element.70), channel_id=1, source_target_pairs={{0,1},{1,0},{2,3},{3,2},{4,5},{5,4},{6,7},{7,6},{8,9},{9,8},{10,11... | collective-permute-start | bytes 3342344 | tf_op jit(solution)/shard_map/ppermute | solution.py:388
  125.3 26.8 %copy-start.2 = (bf16[8,512,256]{2,1,0:T(8,128)(2,1)S(1)}, bf16[8,512,256]{2,1,0:T(8,128)(2,1)}, u32[]{:S(2)}) copy-start(bf16[8,512,256]{2,1,0:T(8,128)(2,1)} %get-tuple-element.71.choose_ref) | copy-start | bytes 6291460
  125.4 13.8 %collective-permute-start.15 = (bf16[4,384,128]{2,1,0:T(8,128)(2,1)S(1)}, bf16[4,384,128]{2,1,0:T(8,128)(2,1)S(1)}, u32[]{:S(2)}, u32[]{:S(2)}) collective-permute-start(bf16[4,384,128]{2,1,0:T(8,128)(2,1)S(1)} %fusion), channel_id=1, source_target_pairs={{0,2},{2,0},{4,6},{6,4},{8,10},{10,8},{12,14},{14,12},{1,3},{3,1},... | collective-permute-start | bytes 1179656 | tf_op jit(solution)/shard_map/ppermute | solution.py:388
  126.6 6.4 %collective-permute-start.19 = (bf16[2,160,128]{2,1,0:T(8,128)(2,1)S(1)}, bf16[2,160,128]{2,1,0:T(8,128)(2,1)S(1)}, u32[]{:S(2)}, u32[]{:S(2)}) collective-permute-start(bf16[2,160,128]{2,1,0:T(8,128)(2,1)S(1)} %get-tuple-element.76), channel_id=1, source_target_pairs={{0,12},{2,14},{4,8},{6,10},{8,4},{10,6},{12,0},{14,2},{1,13},{3,15... | collective-permute-start | bytes 245768 | tf_op jit(solution)/shard_map/ppermute | solution.py:388
  129.1 5.5 %collective-permute-start.21 = (bf16[2,160,128]{2,1,0:T(8,128)(2,1)S(1)}, bf16[2,160,128]{2,1,0:T(8,128)(2,1)S(1)}, u32[]{:S(2)}, u32[]{:S(2)}) collective-permute-start(bf16[2,160,128]{2,1,0:T(8,128)(2,1)S(1)} %get-tuple-element.77), channel_id=1, source_target_pairs={{0,4},{2,6},{4,0},{6,2},{8,12},{10,14},{12,8},{14,10},{1,5},{3,7},... | collective-permute-start | bytes 245768 | tf_op jit(solution)/shard_map/ppermute | solution.py:388
  132.2 6.2 %collective-permute-start.20 = (bf16[2,160,128]{2,1,0:T(8,128)(2,1)S(1)}, bf16[2,160,128]{2,1,0:T(8,128)(2,1)S(1)}, u32[]{:S(2)}, u32[]{:S(2)}) collective-permute-start(bf16[2,160,128]{2,1,0:T(8,128)(2,1)S(1)} %get-tuple-element.78), channel_id=1, source_target_pairs={{0,8},{2,10},{4,12},{6,14},{8,0},{10,2},{12,4},{14,6},{1,9},{3,11}... | collective-permute-start | bytes 245768 | tf_op jit(solution)/shard_map/ppermute | solution.py:388
  138.4 13.7 %copy-start.1 = (f32[8,256,256]{2,1,0:T(8,128)S(1)}, f32[8,256,256]{2,1,0:T(8,128)}, u32[]{:S(2)}) copy-start(f32[8,256,256]{2,1,0:T(8,128)} %get-tuple-element.72.terms_ref) | copy-start | bytes 6291460
  138.4 5.4 %collective-permute-start.22 = (bf16[160,128]{1,0:T(8,128)(2,1)S(1)}, bf16[160,128]{1,0:T(8,128)(2,1)S(1)}, u32[]{:S(2)}, u32[]{:S(2)}) collective-permute-start(bf16[160,128]{1,0:T(8,128)(2,1)S(1)} %fusion.8), channel_id=1, source_target_pairs={{0,2},{2,0},{4,6},{6,4},{8,10},{10,8},{12,14},{14,12},{1,3},{3,1},... | collective-permute-start | bytes 122888 | tf_op jit(solution)/shard_map/ppermute | solution.py:388
  139.3 7.7 %collective-permute-start.16 = (bf16[384,128]{1,0:T(8,128)(2,1)S(1)}, bf16[384,128]{1,0:T(8,128)(2,1)S(1)}, u32[]{:S(2)}, u32[]{:S(2)}) collective-permute-start(bf16[384,128]{1,0:T(8,128)(2,1)S(1)} %get-tuple-element.73), channel_id=1, source_target_pairs={{0,12},{2,14},{4,8},{6,10},{8,4},{10,6},{12,0},{14,2},{1,13},{3,15... | collective-permute-start | bytes 294920 | tf_op jit(solution)/shard_map/ppermute | solution.py:388
  141.7 6.4 %collective-permute-start.18 = (bf16[384,128]{1,0:T(8,128)(2,1)S(1)}, bf16[384,128]{1,0:T(8,128)(2,1)S(1)}, u32[]{:S(2)}, u32[]{:S(2)}) collective-permute-start(bf16[384,128]{1,0:T(8,128)(2,1)S(1)} %get-tuple-element.74), channel_id=1, source_target_pairs={{0,4},{2,6},{4,0},{6,2},{8,12},{10,14},{12,8},{14,10},{1,5},{3,7},... | collective-permute-start | bytes 294920 | tf_op jit(solution)/shard_map/ppermute | solution.py:388
  142.2 8.3 %collective-permute-start.17 = (bf16[384,128]{1,0:T(8,128)(2,1)S(1)}, bf16[384,128]{1,0:T(8,128)(2,1)S(1)}, u32[]{:S(2)}, u32[]{:S(2)}) collective-permute-start(bf16[384,128]{1,0:T(8,128)(2,1)S(1)} %get-tuple-element.75), channel_id=1, source_target_pairs={{0,8},{2,10},{4,12},{6,14},{8,0},{10,2},{12,4},{14,6},{1,9},{3,11}... | collective-permute-start | bytes 294920 | tf_op jit(solution)/shard_map/ppermute | solution.py:388
  150.6 1.4 collective-permute-start.23

commit v6 on v5

--- a/solution.py
+++ b/solution.py
@@ -56,7 +56,7 @@
 
 
 def split_kernel(orders, span, own, wanted_ref, place_ref, core_ref, blocks_ref, *rest):
-    outs, (bufs, own_buf, tail, in_sems, out_sems) = rest[:-5], rest[-5:]
+    outs, (bufs, own_buf, tail, ids_smem, in_sems, out_sems) = rest[:-6], rest[-6:]
     rows, depth = blocks_ref.shape
     columns = own_buf.shape[1]
     chunks = span[1] - span[0]
@@ -74,16 +74,20 @@
         stores.append(pltpu.make_async_copy(source, target, out_sems.at[n, c]))
         stores[-1].start()
 
+    lists = pltpu.make_async_copy(wanted_ref, ids_smem, in_sems.at[count])
+    if not own:
+        lists.start()
     for n, ks in enumerate(zip(*orders)):
         offset = jnp.where(core_ref[0] % 2 == 0, *ks)
         fetch(n, offset, span[0], bufs.at[n])
     if own:
         fetch(count, 0, 0, own_buf)
     else:
+        lists.wait()
         lane = lax.broadcasted_iota(jnp.int32, tail.shape, 1)
         ids = jnp.zeros(tail.shape, jnp.int32)
         for m in range(UNIQ):
-            ids = jnp.where(lane == m, wanted_ref[m], ids)
+            ids = jnp.where(lane == m, ids_smem[m], ids)
         tail[...] = ids.astype(jnp.float32).astype(jnp.bfloat16)
         for n in range(count):
             store(n, chunks, tail, outs[n], chunks * rows)
@@ -112,13 +116,14 @@
         heights += [span[0] * rows, chunks * rows]
     return pl.pallas_call(
         functools.partial(split_kernel, orders, span, own),
-        in_specs=[SMEM_SPEC] * 3 + [HBM_SPEC],
+        in_specs=[HBM_SPEC, SMEM_SPEC, SMEM_SPEC, HBM_SPEC],
         out_specs=[HBM_SPEC] * len(heights),
         out_shape=[jax.ShapeDtypeStruct((height, TILE), blocks.dtype) for height in heights],
         scratch_shapes=[
             pltpu.VMEM((count, rows, chunks * TILE), blocks.dtype),
             pltpu.VMEM((rows, columns), blocks.dtype),
             pltpu.VMEM((LIST_ROWS, TILE), blocks.dtype),
+            pltpu.SMEM(wanted.shape, wanted.dtype),
             pltpu.SemaphoreType.DMA((count + 1,)),
             pltpu.SemaphoreType.DMA((count + 1, columns // TILE + 1)),
         ],
@@ -232,9 +237,9 @@
             at += value.shape[0]
 
 
-def late_kernel(slots, owned, width, spots_ref, core_ref, acc_ref, *rest):
-    refs, rest = rest[:-4], rest[-4:]
-    keep_ref, send_ref, pool, sems = rest
+def late_kernel(slots, owned, width, spots_hbm, core_ref, acc_ref, *rest):
+    refs, rest = rest[:-6], rest[-6:]
+    keep_ref, send_ref, pool, spots_ref, spots_sem, sems = rest
     rows = owned * width
     part = refs[0].shape[0]
     chunks = part // rows
@@ -243,7 +248,8 @@
     core = core_ref[0]
     targets = [jnp.where(core % 2 == 0, *pair) for pair in zip(*slots)]
     copies = pool_copies(refs, targets, part, pool, sems)
-    for copy in copies:
+    copies.append(pltpu.make_async_copy(spots_hbm, spots_ref, spots_sem))
+    for copy in reversed(copies):
         copy.start()
     for copy in copies:
         copy.wait()
@@ -307,11 +313,13 @@
     owners = acc.shape[0]
     return pl.pallas_call(
         functools.partial(late_kernel, slots, owned, width),
-        in_specs=[SMEM_SPEC] * 2 + [VMEM_SPEC] + [HBM_SPEC] * holders,
+        in_specs=[HBM_SPEC, SMEM_SPEC, VMEM_SPEC] + [HBM_SPEC] * holders,
         out_specs=[VMEM_SPEC] * 2,
         out_shape=[out, out],
         scratch_shapes=[
             pltpu.VMEM((holders * rows * chunks, TILE), jnp.bfloat16),
+            pltpu.SMEM(spots.shape, spots.dtype),
+            pltpu.SemaphoreType.DMA,
             pltpu.SemaphoreType.DMA((holders,)),
         ],
         compiler_params=pltpu.CompilerParams(vmem_limit_bytes=16 * 1024 * 1024),
@@ -323,7 +331,10 @@
     )(spots, core, acc, *parts)
 
 
-def finish_kernel(slots_ref, core_ref, mine_ref, other_ref, choose_ref, terms_ref, out_ref, gram, stage, sems):
+def finish_kernel(slots_hbm, core_ref, mine_ref, other_ref, choose_ref, terms_ref, out_ref, *rest):
+    slots_ref, slots_sem, gram, stage, sems = rest
+    fetch = pltpu.make_async_copy(slots_hbm, slots_ref, slots_sem)
+    fetch.start()
     core = core_ref[0]
     width = gram.shape[0] // UNIQ
     pairs = out_ref.shape[0]
@@ -347,6 +358,8 @@
         lower = jnp.where(row > col, value, flipped)
         put(i + 1, i + 1, jnp.where(row == col, squares, lower))
 
+    fetch.wait()
+
     def result(pair):
         return pltpu.make_async_copy(stage.at[pair], out_ref.at[pair], sems.at[pair])
 
@@ -366,10 +379,12 @@
     gram_side = UNIQ * rows // DOM
     return pl.pallas_call(
         finish_kernel,
-        in_specs=[SMEM_SPEC] * 2 + [VMEM_SPEC] * 4,
+        in_specs=[HBM_SPEC, SMEM_SPEC] + [VMEM_SPEC] * 4,
         out_specs=HBM_SPEC,
         out_shape=jax.ShapeDtypeStruct(terms.shape, jnp.bfloat16),
         scratch_shapes=[
+            pltpu.SMEM(slots.shape, slots.dtype),
+            pltpu.SemaphoreType.DMA,
             pltpu.VMEM((gram_side, gram_side), jnp.bfloat16),
             pltpu.VMEM(terms.shape, jnp.bfloat16),
             pltpu.SemaphoreType.DMA((pairs,)),

time: 155 us -> 154 us (level)
  Pallas kernels: 27.1 us -> 25.4 us
where the time goes in v6:
time: 154 us; the launch traced here: 153 us
  waiting for transfers between devices  71.5 us (46%)
  starting transfers between devices  54.7 us (36%)
  Pallas kernels  25.4 us (16%)
    ppermute x14, waiting for transfers between devices, exchange(): arrived.append(lax.ppermute(part, ('pairs', 'aux'), moves))  54.6 us
    ppermute x14, starting transfers between devices, exchange(): arrived.append(lax.ppermute(part, ('pairs', 'aux'), moves))  42.6 us
    ppermute x10, waiting for transfers between devices, swap(): return lax.ppermute(value, axis, [(i, i ^ bit) for i in range(size)])  16.9 us
    ppermute x10, starting transfers between devices, swap(): return lax.ppermute(value, axis, [(i, i ^ bit) for i in range(size)])  12.1 us
    pallas_call x1, Pallas kernels, pair_terms(): pl.pallas_call(terms_kernel, grid=(pairs,), in_specs=[pl.BlockSpec((1, 1,...  8.36 us
    pallas_call x1, Pallas kernels, early_grams(): pl.pallas_call(functools.partial(early_kernel, ks, owned, width), in_spec...  7.05 us
    pallas_call x2, Pallas kernels, column_parts(): pl.pallas_call(functools.partial(split_kernel, orders, span, own), in_spe...  6.03 us
  transfers between devices with their start and end apart: 24, of which 12 were waited for; matrix products, arithmetic and copies ran while one was open for 1% of the time, Pallas kernels for 12%

profile of v6, /device:TPU:0, one launch (start us, length us, event | category | flops | bytes accessed | tf_op | source)
XLA Modules:
  0.0 153.2 jit_solution(1889201208763761316)
XLA Ops:
  0.0 3.0 %shard_map.73 = (bf16[1552,128]{1,0:T(8,128)(2,1)}, bf16[1552,128]{1,0:T(8,128)(2,1)}, bf16[1552,128]{1,0:T(8,128)(2,1)}, bf16[1552,128]{1,0:T(8,128)(2,1)}, bf1...) custom-call(s32[16]{0:T(128)} %wanted_ref.5, s32[1]{0:T(128)} %bitcast.place_ref, ...), custom_call_target="tpu_custom_call" | custom-call | tf_op jit(solution)/shard_map/pallas_call | solution.py:117
  3.0 4.1 %collective-permute-start = (bf16[1552,128]{1,0:T(8,128)(2,1)}, bf16[1552,128]{1,0:T(8,128)(2,1)S(1)}, u32[]{:S(2)}, u32[]{:S(2)}) collective-permute-start(bf16[1552,128]{1,0:T(8,128)(2,1)} %get-tuple-element.39), channel_id=1, source_target_pairs={{0,8},{1,3},{2,10},{3,1},{4,12},{5,7},{6,14},{7,5},{8,0},{9,11},{1... | collective-permute-start | bytes 1191944 | tf_op jit(solution)/shard_map/ppermute | solution.py:469
  7.1 2.3 %collective-permute-start.5 = (bf16[1552,128]{1,0:T(8,128)(2,1)}, bf16[1552,128]{1,0:T(8,128)(2,1)S(1)}, u32[]{:S(2)}, u32[]{:S(2)}) collective-permute-start(bf16[1552,128]{1,0:T(8,128)(2,1)} %get-tuple-element.44), channel_id=1, source_target_pairs={{0,14},{1,13},{2,12},{3,15},{4,10},{5,9},{6,8},{7,11},{8,6},{9,5},... | collective-permute-start | bytes 1191944 | tf_op jit(solution)/shard_map/ppermute | solution.py:469
  9.4 1.6 %collective-permute-start.1 = (bf16[1552,128]{1,0:T(8,128)(2,1)}, bf16[1552,128]{1,0:T(8,128)(2,1)S(1)}, u32[]{:S(2)}, u32[]{:S(2)}) collective-permute-start(bf16[1552,128]{1,0:T(8,128)(2,1)} %get-tuple-element.40), channel_id=1, source_target_pairs={{0,10},{1,9},{2,8},{3,11},{4,14},{5,13},{6,12},{7,15},{8,2},{9,1},... | collective-permute-start | bytes 1191944 | tf_op jit(solution)/shard_map/ppermute | solution.py:469
  11.1 1.5 collective-permute-start.2
  12.6 0.2 collective-permute-start.3
  12.8 33.9 %collective-permute-done.rest_1_ = bf16[1552,128]{1,0:T(8,128)(2,1)S(1)} collective-permute-done((bf16[1552,128]{1,0:T(8,128)(2,1)}, bf16[1552,128]{1,0:T(8,128)(2,1)S(1)}, u32[]{:S(2)}, u32[]{:S(2)}) %collective-permute-start) | collective-permute-done | bytes 397344 | tf_op jit(solution)/shard_map/ppermute | solution.py:469
  46.7 1.7 %collective-permute-start.4 = (bf16[1552,128]{1,0:T(8,128)(2,1)}, bf16[1552,128]{1,0:T(8,128)(2,1)S(1)}, u32[]{:S(2)}, u32[]{:S(2)}) collective-permute-start(bf16[1552,128]{1,0:T(8,128)(2,1)} %get-tuple-element.43), channel_id=1, source_target_pairs={{0,4},{1,7},{2,6},{3,5},{4,0},{5,3},{6,2},{7,1},{8,12},{9,15},{10,... | collective-permute-start | bytes 1191944 | tf_op jit(solution)/shard_map/ppermute | solution.py:469
  48.4 16.4 %collective-permute-start.6 = (bf16[1552,128]{1,0:T(8,128)(2,1)}, bf16[1552,128]{1,0:T(8,128)(2,1)S(1)}, u32[]{:S(2)}, u32[]{:S(2)}) collective-permute-start(bf16[1552,128]{1,0:T(8,128)(2,1)} %get-tuple-element.46), channel_id=1, source_target_pairs={{0,6},{1,15},{2,4},{3,13},{4,2},{5,11},{6,0},{7,9},{8,14},{9,7},{1... | collective-permute-start | bytes 1191944 | tf_op jit(solution)/shard_map/ppermute | solution.py:469
  64.9 0.1 slice_multiply_fusion
  64.9 0.1 add.134
  65.0 0.1 add.131
  65.1 0.1 add.132
  65.2 3.0 %shard_map.75 = (bf16[1024,128]{1,0:T(8,128)(2,1)}, bf16[1024,128]{1,0:T(8,128)(2,1)}, bf16[1024,128]{1,0:T(8,128)(2,1)}, bf16[1024,128]{1,0:T(8,128)(2,1)}, bf1...) custom-call(s32[16]{0:T(128)} %wanted_ref.5, ...), custom_call_target="tpu_custom_call" | custom-call | tf_op jit(solution)/shard_map/pallas_call | solution.py:117
  68.2 7.1 %collective-permute-done.1.rest_2_ = bf16[1552,128]{1,0:T(8,128)(2,1)S(1)} collective-permute-done((bf16[1552,128]{1,0:T(8,128)(2,1)}, bf16[1552,128]{1,0:T(8,128)(2,1)S(1)}, u32[]{:S(2)}, u32[]{:S(2)}) %collective-permute-start.1) | collective-permute-done | bytes 397344 | tf_op jit(solution)/shard_map/ppermute | solution.py:469
  75.4 0.2 collective-permute-start.8
  75.6 0.6 broadcast_add_fusion.right_ref
  76.2 8.4 %shard_map.74 = (f32[8,256,256]{2,1,0:T(8,128)}, bf16[8,512,256]{2,1,0:T(8,128)(2,1)}) custom-call(s32[8,1,256]{2,1,0:T(1,128)} %broadcast_add_fusion.right_ref, bf16[8,256,256]{2,1,0:T(8,128)(2,1)} %fock_ref.1, bf16[8,256,256]{2,1,0:T(8,128)(2,1)} %corr_ref.1, bf16[8,256,256]{2,1,0:T(8,128)(2,1)} %amp_ref.1), custom_call_target="tpu_custom_call" | custom-call | flops 1073741824 | bytes 7340032 | tf_op jit(solution)/shard_map/pallas_call | solution.py:40
  84.6 5.0 %collective-permute-start.9 = (bf16[1024,128]{1,0:T(8,128)(2,1)}, bf16[1024,128]{1,0:T(8,128)(2,1)S(1)}, u32[]{:S(2)}, u32[]{:S(2)}) collective-permute-start(bf16[1024,128]{1,0:T(8,128)(2,1)} %get-tuple-element.64), channel_id=1, source_target_pairs={{0,4},{1,3},{2,6},{3,1},{4,0},{5,7},{6,2},{7,5},{8,12},{9,11},{10,... | collective-permute-start | bytes 786440 | tf_op jit(solution)/shard_map/ppermute | solution.py:469
  89.5 2.8 %collective-permute-start.10 = (bf16[1024,128]{1,0:T(8,128)(2,1)}, bf16[1024,128]{1,0:T(8,128)(2,1)S(1)}, u32[]{:S(2)}, u32[]{:S(2)}) collective-permute-start(bf16[1024,128]{1,0:T(8,128)(2,1)} %get-tuple-element.65), channel_id=1, source_target_pairs={{0,10},{1,13},{2,8},{3,15},{4,14},{5,9},{6,12},{7,11},{8,2},{9,5},... | collective-permute-start | bytes 786440 | tf_op jit(solution)/shard_map/ppermute | solution.py:469
  92.3 2.0 %collective-permute-start.11 = (bf16[1024,128]{1,0:T(8,128)(2,1)}, bf16[1024,128]{1,0:T(8,128)(2,1)S(1)}, u32[]{:S(2)}, u32[]{:S(2)}) collective-permute-start(bf16[1024,128]{1,0:T(8,128)(2,1)} %get-tuple-element.66), channel_id=1, source_target_pairs={{0,6},{1,5},{2,4},{3,7},{4,2},{5,1},{6,0},{7,3},{8,14},{9,13},{10,... | collective-permute-start | bytes 786440 | tf_op jit(solution)/shard_map/ppermute | solution.py:469
  94.3 0.5 collective-permute-start.12
  94.8 4.2 %collective-permute-start.13 = (bf16[1024,128]{1,0:T(8,128)(2,1)S(1)}, bf16[1024,128]{1,0:T(8,128)(2,1)S(1)}, u32[]{:S(2)}, u32[]{:S(2)}) collective-permute-start(bf16[1024,128]{1,0:T(8,128)(2,1)S(1)} %copy-done.6), channel_id=1, source_target_pairs={{0,14},{1,7},{2,12},{3,5},{4,10},{5,3},{6,8},{7,1},{8,6},{9,15},{1... | collective-permute-start | bytes 786440 | tf_op jit(solution)/shard_map/ppermute | solution.py:469
  99.1 7.0 %shard_map.76 = (f32[8,1088,128]{2,1,0:T(8,128)S(1)}, s32[8,16]{1,0:T(8,128)S(1)}) custom-call(s32[16]{0:T(128)S(1)} %copy-done.4, s32[1]{0:T(128)} %bitcast.place_ref, s32[8]{0:T(128)S(1)} %dynamic-slice_bitcast_fusion.slot_ref, bf16[1536,128]{1,0:T(8,128)(2,1)S(1)} %copy-done.5, bf16[1552,128]{1,0:T(8,128)(2,1)S(1)} %collective-permute-done.rest_1_, ...), custom_call_target="tpu_custom_call" | custom-call | flops 1610612736 | bytes 3145728 | tf_op jit(solution)/shard_map/pallas_call | solution.py:282
  106.1 4.5 %collective-permute-done.9.rest_3_ = bf16[1024,128]{1,0:T(8,128)(2,1)S(1)} collective-permute-done((bf16[1024,128]{1,0:T(8,128)(2,1)}, bf16[1024,128]{1,0:T(8,128)(2,1)S(1)}, u32[]{:S(2)}, u32[]{:S(2)}) %collective-permute-start.9) | collective-permute-done | bytes 262176 | tf_op jit(solution)/shard_map/ppermute | solution.py:469
  110.6 9.0 %collective-permute-done.11.rest_5_ = bf16[1024,128]{1,0:T(8,128)(2,1)S(1)} collective-permute-done((bf16[1024,128]{1,0:T(8,128)(2,1)}, bf16[1024,128]{1,0:T(8,128)(2,1)S(1)}, u32[]{:S(2)}, u32[]{:S(2)}) %collective-permute-start.11) | collective-permute-done | bytes 262176 | tf_op jit(solution)/shard_map/ppermute | solution.py:469
  119.6 1.9 %shard_map.77 = (bf16[8,544,128]{2,1,0:T(8,128)(2,1)S(1)}, bf16[8,544,128]{2,1,0:T(8,128)(2,1)S(1)}) custom-call(s32[8,16]{1,0:T(8,128)S(1)} %get-tuple-element.59.spots_hbm, s32[1]{0:T(128)} %bitcast.1.core_ref, f32[8,1088,128]{2,1,0:T(8,128)S(1)} %get-tuple-element.60.acc_ref, bf16[1024,128]{1,0:T(8,128)(2,1)S(1)} %copy-done.3, ...), custom_call_target="tpu_custom_call" | custom-call | flops 1073741824 | bytes 2097152 | tf_op jit(solution)/shard_map/pallas_call | solution.py:314
  121.5 0.1 collective-permute-start.14
  121.6 2.7 %collective-permute-done.14 = bf16[8,544,128]{2,1,0:T(8,128)(2,1)S(1)} collective-permute-done((bf16[8,544,128]{2,1,0:T(8,128)(2,1)S(1)}, bf16[8,544,128]{2,1,0:T(8,128)(2,1)S(1)}, u32[]{:S(2)}, u32[]{:S(2)}) %collective-permute-start.14) | collective-permute-done | bytes 1114144 | tf_op jit(solution)/shard_map/ppermute | solution.py:403
  124.3 0.1 fusion
  124.5 1.1 collective-permute-start.15
  125.6 2.5 %collective-permute-start.19 = (bf16[2,160,128]{2,1,0:T(8,128)(2,1)S(1)}, bf16[2,160,128]{2,1,0:T(8,128)(2,1)S(1)}, u32[]{:S(2)}, u32[]{:S(2)}) collective-permute-start(bf16[2,160,128]{2,1,0:T(8,128)(2,1)S(1)} %get-tuple-element.76), channel_id=1, source_target_pairs={{0,12},{2,14},{4,8},{6,10},{8,4},{10,6},{12,0},{14,2},{1,13},{3,15... | collective-permute-start | bytes 245768 | tf_op jit(solution)/shard_map/ppermute | solution.py:403
  128.2 3.1 %collective-permute-start.21 = (bf16[2,160,128]{2,1,0:T(8,128)(2,1)S(1)}, bf16[2,160,128]{2,1,0:T(8,128)(2,1)S(1)}, u32[]{:S(2)}, u32[]{:S(2)}) collective-permute-start(bf16[2,160,128]{2,1,0:T(8,128)(2,1)S(1)} %get-tuple-element.77), channel_id=1, source_target_pairs={{0,4},{2,6},{4,0},{6,2},{8,12},{10,14},{12,8},{14,10},{1,5},{3,7},... | collective-permute-start | bytes 245768 | tf_op jit(solution)/shard_map/ppermute | solution.py:403
  131.3 0.8 collective-permute-done.19
  132.1 1.6 %collective-permute-done.21 = bf16[2,160,128]{2,1,0:T(8,128)(2,1)S(1)} collective-permute-done((bf16[2,160,128]{2,1,0:T(8,128)(2,1)S(1)}, bf16[2,160,128]{2,1,0:T(8,128)(2,1)S(1)}, u32[]{:S(2)}, u32[]{:S(2)}) %collective-permute-start.21) | collective-permute-done | bytes 81952 | tf_op jit(solution)/shard_map/ppermute | solution.py:403
  133.7 3.7 %collective-permute-done.20 = bf16[2,160,128]{2,1,0:T(8,128)(2,1)S(1)} collective-permute-done((bf16[2,160,128]{2,1,0:T(8,128)(2,1)S(1)}, bf16[2,160,128]{2,1,0:T(8,128)(2,1)S(1)}, u32[]{:S(2)}, u32[]{:S(2)}) %collective-permute-start.20) | collective-permute-done | bytes 81952 | tf_op jit(solution)/shard_map/ppermute | solution.py:403
  137.5 0.8 collective-permute-start.22
  138.3 0.1 fusion.3
  138.4 2.4 %collective-permute-start.16 = (bf16[384,128]{1,0:T(8,128)(2,1)S(1)}, bf16[384,128]{1,0:T(8,128)(2,1)S(1)}, u32[]{:S(2)}, u32[]{:S(2)}) collective-permute-start(bf16[384,128]{1,0:T(8,128)(2,1)S(1)} %get-tuple-element.73), channel_id=1, source_target_pairs={{0,12},{2,14},{4,8},{6,10},{8,4},{10,6},{12,0},{14,2},{1,13},{3,15... | collective-permute-start | bytes 294920 | tf_op jit(solution)/shard_map/ppermute | solution.py:403
  140.8 0.5 collective-permute-start.18
  141.3 1.6 %collective-permute-start.17 = (bf16[384,128]{1,0:T(8,128)(2,1)S(1)}, bf16[384,128]{1,0:T(8,128)(2,1)S(1)}, u32[]{:S(2)}, u32[]{:S(2)}) collective-permute-start(bf16[384,128]{1,0:T(8,128)(2,1)S(1)} %get-tuple-element.75), channel_id=1, source_target_pairs={{0,8},{2,10},{4,12},{6,14},{8,0},{10,2},{12,4},{14,6},{1,9},{3,11}... | collective-permute-start | bytes 294920 | tf_op jit(solution)/shard_map/ppermute | solution.py:403
  142.9 3.2 %collective-permute-done.16 = bf16[384,128]{1,0:T(8,128)(2,1)S(1)} collective-permute-done((bf16[384,128]{1,0:T(8,128)(2,1)S(1)}, bf16[384,128]{1,0:T(8,128)(2,1)S(1)}, u32[]{:S(2)}, u32[]{:S(2)}) %collective-permute-start.16) | collective-permute-done | bytes 98336 | tf_op jit(solution)/shard_map/ppermute | solution.py:403
  146.1 1.2 collective-permute-done.18
  147.3 2.3 %collective-permute-done.17 = bf16[384,128]{1,0:T(8,128)(2,1)S(1)} collective-permute-done((bf16[384,128]{1,0:T(8,128)(2,1)S(1)}, bf16[384,128]{1,0:T(8,128)(2,1)S(1)}, u32[]{:S(2)}, u32[]{:S(2)}) %collective-permute-start.17) | collective-permute-done | bytes 98336 | tf_op jit(solution)/shard_map/ppermute | solution.py:403
  149.6 0.1 add_convert_fusion.1
  149.7 0.1 collective-permute-start.23
  149.8 1.3 collective-permute-done.23.other_ref
  151.1 2.1 %shard_map.78 = bf16[8,256,256]{2,1,0:T(8,128)(2,1)} custom-call(s32[8,16]{1,0:T(8,128)S(1)} %constant_dynamic-slice_fusion.slots_hbm, s32[1]{0:T(128)} %bitcast.1.core_ref, bf16[544,128]{1,0:T(8,128)(2,1)S(1)} %pad_maximum_fusion.mine_ref, bf16[544,128]{1,0:T(8,128)(2,1)S(1)} %collective-permute-done.23.other_ref, bf16[8,512,256]{2,1,0:T(8,128)(2,1)S(1)} %copy-done.2, ...), custom_call_target="tpu_custom_call" | custom-call | flops 536870912 | bytes 5242880 | tf_op jit(solution)/shard_map/pallas_call | solution.py:380
  (37 shorter events, 0.2 us)
Async XLA Ops:
  0.0 12.8 %copy-start = (s32[16,16]{1,0:T(8,128)S(1)}, s32[16,16]{1,0:T(8,128)}, u32[]{:S(2)}) copy-start(s32[16,16]{1,0:T(8,128)} %param.9) | copy-start | bytes 3076
  3.0 43.7 %collective-permute-start = (bf16[1552,128]{1,0:T(8,128)(2,1)}, bf16[1552,128]{1,0:T(8,128)(2,1)S(1)}, u32[]{:S(2)}, u32[]{:S(2)}) collective-permute-start(bf16[1552,128]{1,0:T(8,128)(2,1)} %get-tuple-element.39), channel_id=1, source_target_pairs={{0,8},{1,3},{2,10},{3,1},{4,12},{5,7},{6,14},{7,5},{8,0},{9,11},{1... | collective-permute-start | bytes 1191944 | tf_op jit(solution)/shard_map/ppermute | solution.py:469
  7.1 41.3 %collective-permute-start.5 = (bf16[1552,128]{1,0:T(8,128)(2,1)}, bf16[1552,128]{1,0:T(8,128)(2,1)S(1)}, u32[]{:S(2)}, u32[]{:S(2)}) collective-permute-start(bf16[1552,128]{1,0:T(8,128)(2,1)} %get-tuple-element.44), channel_id=1, source_target_pairs={{0,14},{1,13},{2,12},{3,15},{4,10},{5,9},{6,8},{7,11},{8,6},{9,5},... | collective-permute-start | bytes 1191944 | tf_op jit(solution)/shard_map/ppermute | solution.py:469
  9.4 65.9 %collective-permute-start.1 = (bf16[1552,128]{1,0:T(8,128)(2,1)}, bf16[1552,128]{1,0:T(8,128)(2,1)S(1)}, u32[]{:S(2)}, u32[]{:S(2)}) collective-permute-start(bf16[1552,128]{1,0:T(8,128)(2,1)} %get-tuple-element.40), channel_id=1, source_target_pairs={{0,10},{1,9},{2,8},{3,11},{4,14},{5,13},{6,12},{7,15},{8,2},{9,1},... | collective-permute-start | bytes 1191944 | tf_op jit(solution)/shard_map/ppermute | solution.py:469
  11.1 64.3 %collective-permute-start.2 = (bf16[1552,128]{1,0:T(8,128)(2,1)}, bf16[1552,128]{1,0:T(8,128)(2,1)S(1)}, u32[]{:S(2)}, u32[]{:S(2)}) collective-permute-start(bf16[1552,128]{1,0:T(8,128)(2,1)} %get-tuple-element.41), channel_id=1, source_target_pairs={{0,2},{1,5},{2,0},{3,7},{4,6},{5,1},{6,4},{7,3},{8,10},{9,13},{10,... | collective-permute-start | bytes 1191944 | tf_op jit(solution)/shard_map/ppermute | solution.py:469
  12.6 72.0 %collective-permute-start.3 = (bf16[1552,128]{1,0:T(8,128)(2,1)}, bf16[1552,128]{1,0:T(8,128)(2,1)S(1)}, u32[]{:S(2)}, u32[]{:S(2)}) collective-permute-start(bf16[1552,128]{1,0:T(8,128)(2,1)} %get-tuple-element.42), channel_id=1, source_target_pairs={{0,12},{1,11},{2,14},{3,9},{4,8},{5,15},{6,10},{7,13},{8,4},{9,3},... | collective-permute-start | bytes 1191944 | tf_op jit(solution)/shard_map/ppermute | solution.py:469
  46.7 42.8 %collective-permute-start.4 = (bf16[1552,128]{1,0:T(8,128)(2,1)}, bf16[1552,128]{1,0:T(8,128)(2,1)S(1)}, u32[]{:S(2)}, u32[]{:S(2)}) collective-permute-start(bf16[1552,128]{1,0:T(8,128)(2,1)} %get-tuple-element.43), channel_id=1, source_target_pairs={{0,4},{1,7},{2,6},{3,5},{4,0},{5,3},{6,2},{7,1},{8,12},{9,15},{10,... | collective-permute-start | bytes 1191944 | tf_op jit(solution)/shard_map/ppermute | solution.py:469
  48.4 43.9 %collective-permute-start.6 = (bf16[1552,128]{1,0:T(8,128)(2,1)}, bf16[1552,128]{1,0:T(8,128)(2,1)S(1)}, u32[]{:S(2)}, u32[]{:S(2)}) collective-permute-start(bf16[1552,128]{1,0:T(8,128)(2,1)} %get-tuple-element.46), channel_id=1, source_target_pairs={{0,6},{1,15},{2,4},{3,13},{4,2},{5,11},{6,0},{7,9},{8,14},{9,7},{1... | collective-permute-start | bytes 1191944 | tf_op jit(solution)/shard_map/ppermute | solution.py:469
  75.4 18.9 %collective-permute-start.7 = (bf16[1024,128]{1,0:T(8,128)(2,1)}, bf16[1024,128]{1,0:T(8,128)(2,1)S(1)}, u32[]{:S(2)}, u32[]{:S(2)}) collective-permute-start(bf16[1024,128]{1,0:T(8,128)(2,1)} %get-tuple-element.62), channel_id=1, source_target_pairs={{0,2},{1,9},{2,0},{3,11},{4,6},{5,13},{6,4},{7,15},{8,10},{9,1},{1... | collective-permute-start | bytes 786440 | tf_op jit(solution)/shard_map/ppermute | solution.py:469
  75.4 19.4 %collective-permute-start.8 = (bf16[1024,128]{1,0:T(8,128)(2,1)}, bf16[1024,128]{1,0:T(8,128)(2,1)S(1)}, u32[]{:S(2)}, u32[]{:S(2)}) collective-permute-start(bf16[1024,128]{1,0:T(8,128)(2,1)} %get-tuple-element.63), channel_id=1, source_target_pairs={{0,8},{1,11},{2,10},{3,9},{4,12},{5,15},{6,14},{7,13},{8,0},{9,3},... | collective-permute-start | bytes 786440 | tf_op jit(solution)/shard_map/ppermute | solution.py:469
  76.2 18.6 %copy-start.6 = (bf16[1024,128]{1,0:T(8,128)(2,1)S(1)}, bf16[1024,128]{1,0:T(8,128)(2,1)}, u32[]{:S(2)}) copy-start(bf16[1024,128]{1,0:T(8,128)(2,1)} %get-tuple-element.68) | copy-start | bytes 786436
  76.2 22.9 %copy-start.7 = (s32[2,8]{1,0:T(2,128)S(1)}, s32[2,8]{1,0:T(2,128)}, u32[]{:S(2)}) copy-start(s32[2,8]{1,0:T(2,128)} %constant.30.clone) | copy-start | bytes 196
  76.2 22.9 %copy-start.4 = (s32[16]{0:T(128)S(1)}, s32[16]{0:T(128)}, u32[]{:S(2)}) copy-start(s32[16]{0:T(128)} %wanted_ref.5) | copy-start | bytes 196
  76.2 22.9 %copy-start.5 = (bf16[1536,128]{1,0:T(8,128)(2,1)S(1)}, bf16[1536,128]{1,0:T(8,128)(2,1)}, u32[]{:S(2)}) copy-start(bf16[1536,128]{1,0:T(8,128)(2,1)} %get-tuple-element.51.rest_0_) | copy-start | bytes 1179652
  84.6 26.1 %collective-permute-start.9 = (bf16[1024,128]{1,0:T(8,128)(2,1)}, bf16[1024,128]{1,0:T(8,128)(2,1)S(1)}, u32[]{:S(2)}, u32[]{:S(2)}) collective-permute-start(bf16[1024,128]{1,0:T(8,128)(2,1)} %get-tuple-element.64), channel_id=1, source_target_pairs={{0,4},{1,3},{2,6},{3,1},{4,0},{5,7},{6,2},{7,5},{8,12},{9,11},{10,... | collective-permute-start | bytes 786440 | tf_op jit(solution)/shard_map/ppermute | solution.py:469
  89.5 21.1 %collective-permute-start.10 = (bf16[1024,128]{1,0:T(8,128)(2,1)}, bf16[1024,128]{1,0:T(8,128)(2,1)S(1)}, u32[]{:S(2)}, u32[]{:S(2)}) collective-permute-start(bf16[1024,128]{1,0:T(8,128)(2,1)} %get-tuple-element.65), channel_id=1, source_target_pairs={{0,10},{1,13},{2,8},{3,15},{4,14},{5,9},{6,12},{7,11},{8,2},{9,5},... | collective-permute-start | bytes 786440 | tf_op jit(solution)/shard_map/ppermute | solution.py:469
  92.3 27.3 %collective-permute-start.11 = (bf16[1024,128]{1,0:T(8,128)(2,1)}, bf16[1024,128]{1,0:T(8,128)(2,1)S(1)}, u32[]{:S(2)}, u32[]{:S(2)}) collective-permute-start(bf16[1024,128]{1,0:T(8,128)(2,1)} %get-tuple-element.66), channel_id=1, source_target_pairs={{0,6},{1,5},{2,4},{3,7},{4,2},{5,1},{6,0},{7,3},{8,14},{9,13},{10,... | collective-permute-start | bytes 786440 | tf_op jit(solution)/shard_map/ppermute | solution.py:469
  94.3 25.4 %collective-permute-start.12 = (bf16[1024,128]{1,0:T(8,128)(2,1)}, bf16[1024,128]{1,0:T(8,128)(2,1)S(1)}, u32[]{:S(2)}, u32[]{:S(2)}) collective-permute-start(bf16[1024,128]{1,0:T(8,128)(2,1)} %get-tuple-element.67), channel_id=1, source_target_pairs={{0,12},{1,15},{2,14},{3,13},{4,8},{5,11},{6,10},{7,9},{8,4},{9,7},... | collective-permute-start | bytes 786440 | tf_op jit(solution)/shard_map/ppermute | solution.py:469
  94.8 24.8 %collective-permute-start.13 = (bf16[1024,128]{1,0:T(8,128)(2,1)S(1)}, bf16[1024,128]{1,0:T(8,128)(2,1)S(1)}, u32[]{:S(2)}, u32[]{:S(2)}) collective-permute-start(bf16[1024,128]{1,0:T(8,128)(2,1)S(1)} %copy-done.6), channel_id=1, source_target_pairs={{0,14},{1,7},{2,12},{3,5},{4,10},{5,3},{6,8},{7,1},{8,6},{9,15},{1... | collective-permute-start | bytes 786440 | tf_op jit(solution)/shard_map/ppermute | solution.py:469
  99.1 20.6 %copy-start.3 = (bf16[1024,128]{1,0:T(8,128)(2,1)S(1)}, bf16[1024,128]{1,0:T(8,128)(2,1)}, u32[]{:S(2)}) copy-start(bf16[1024,128]{1,0:T(8,128)(2,1)} %get-tuple-element.61.rest_0_) | copy-start | bytes 786436
  121.5 2.8 %collective-permute-start.14 = (bf16[8,544,128]{2,1,0:T(8,128)(2,1)S(1)}, bf16[8,544,128]{2,1,0:T(8,128)(2,1)S(1)}, u32[]{:S(2)}, u32[]{:S(2)}) collective-permute-start(bf16[8,544,128]{2,1,0:T(8,128)(2,1)S(1)} %get-tuple-element.70), channel_id=1, source_target_pairs={{0,1},{1,0},{2,3},{3,2},{4,5},{5,4},{6,7},{7,6},{8,9},{9,8},{10,11... | collective-permute-start | bytes 3342344 | tf_op jit(solution)/shard_map/ppermute | solution.py:403
  124.3 26.8 %copy-start.2 = (bf16[8,512,256]{2,1,0:T(8,128)(2,1)S(1)}, bf16[8,512,256]{2,1,0:T(8,128)(2,1)}, u32[]{:S(2)}) copy-start(bf16[8,512,256]{2,1,0:T(8,128)(2,1)} %get-tuple-element.71.choose_ref) | copy-start | bytes 6291460
  124.5 13.8 %collective-permute-start.15 = (bf16[4,384,128]{2,1,0:T(8,128)(2,1)S(1)}, bf16[4,384,128]{2,1,0:T(8,128)(2,1)S(1)}, u32[]{:S(2)}, u32[]{:S(2)}) collective-permute-start(bf16[4,384,128]{2,1,0:T(8,128)(2,1)S(1)} %fusion), channel_id=1, source_target_pairs={{0,2},{2,0},{4,6},{6,4},{8,10},{10,8},{12,14},{14,12},{1,3},{3,1},... | collective-permute-start | bytes 1179656 | tf_op jit(solution)/shard_map/ppermute | solution.py:403
  125.6 6.4 %collective-permute-start.19 = (bf16[2,160,128]{2,1,0:T(8,128)(2,1)S(1)}, bf16[2,160,128]{2,1,0:T(8,128)(2,1)S(1)}, u32[]{:S(2)}, u32[]{:S(2)}) collective-permute-start(bf16[2,160,128]{2,1,0:T(8,128)(2,1)S(1)} %get-tuple-element.76), channel_id=1, source_target_pairs={{0,12},{2,14},{4,8},{6,10},{8,4},{10,6},{12,0},{14,2},{1,13},{3,15... | collective-permute-start | bytes 245768 | tf_op jit(solution)/shard_map/ppermute | solution.py:403
  128.2 5.5 %collective-permute-start.21 = (bf16[2,160,128]{2,1,0:T(8,128)(2,1)S(1)}, bf16[2,160,128]{2,1,0:T(8,128)(2,1)S(1)}, u32[]{:S(2)}, u32[]{:S(2)}) collective-permute-start(bf16[2,160,128]{2,1,0:T(8,128)(2,1)S(1)} %get-tuple-element.77), channel_id=1, source_target_pairs={{0,4},{2,6},{4,0},{6,2},{8,12},{10,14},{12,8},{14,10},{1,5},{3,7},... | collective-permute-start | bytes 245768 | tf_op jit(solution)/shard_map/ppermute | solution.py:403
  131.3 6.2 %collective-permute-start.20 = (bf16[2,160,128]{2,1,0:T(8,128)(2,1)S(1)}, bf16[2,160,128]{2,1,0:T(8,128)(2,1)S(1)}, u32[]{:S(2)}, u32[]{:S(2)}) collective-permute-start(bf16[2,160,128]{2,1,0:T(8,128)(2,1)S(1)} %get-tuple-element.78), channel_id=1, source_target_pairs={{0,8},{2,10},{4,12},{6,14},{8,0},{10,2},{12,4},{14,6},{1,9},{3,11}... | collective-permute-start | bytes 245768 | tf_op jit(solution)/shard_map/ppermute | solution.py:403
  137.5 13.7 %copy-start.1 = (f32[8,256,256]{2,1,0:T(8,128)S(1)}, f32[8,256,256]{2,1,0:T(8,128)}, u32[]{:S(2)}) copy-start(f32[8,256,256]{2,1,0:T(8,128)} %get-tuple-element.72.terms_ref) | copy-start | bytes 6291460
  137.5 5.4 %collective-permute-start.22 = (bf16[160,128]{1,0:T(8,128)(2,1)S(1)}, bf16[160,128]{1,0:T(8,128)(2,1)S(1)}, u32[]{:S(2)}, u32[]{:S(2)}) collective-permute-start(bf16[160,128]{1,0:T(8,128)(2,1)S(1)} %fusion.8), channel_id=1, source_target_pairs={{0,2},{2,0},{4,6},{6,4},{8,10},{10,8},{12,14},{14,12},{1,3},{3,1},... | collective-permute-start | bytes 122888 | tf_op jit(solution)/shard_map/ppermute | solution.py:403
  138.4 7.7 %collective-permute-start.16 = (bf16[384,128]{1,0:T(8,128)(2,1)S(1)}, bf16[384,128]{1,0:T(8,128)(2,1)S(1)}, u32[]{:S(2)}, u32[]{:S(2)}) collective-permute-start(bf16[384,128]{1,0:T(8,128)(2,1)S(1)} %get-tuple-element.73), channel_id=1, source_target_pairs={{0,12},{2,14},{4,8},{6,10},{8,4},{10,6},{12,0},{14,2},{1,13},{3,15... | collective-permute-start | bytes 294920 | tf_op jit(solution)/shard_map/ppermute | solution.py:403
  140.8 6.5 %collective-permute-start.18 = (bf16[384,128]{1,0:T(8,128)(2,1)S(1)}, bf16[384,128]{1,0:T(8,128)(2,1)S(1)}, u32[]{:S(2)}, u32[]{:S(2)}) collective-permute-start(bf16[384,128]{1,0:T(8,128)(2,1)S(1)} %get-tuple-element.74), channel_id=1, source_target_pairs={{0,4},{2,6},{4,0},{6,2},{8,12},{10,14},{12,8},{14,10},{1,5},{3,7},... | collective-permute-start | bytes 294920 | tf_op jit(solution)/shard_map/ppermute | solution.py:403
  141.3 8.3 %collective-permute-start.17 = (bf16[384,128]{1,0:T(8,128)(2,1)S(1)}, bf16[384,128]{1,0:T(8,128)(2,1)S(1)}, u32[]{:S(2)}, u32[]{:S(2)}) collective-permute-start(bf16[384,128]{1,0:T(8,128)(2,1)S(1)} %get-tuple-element.75), channel_id=1, source_target_pairs={{0,8},{2,10},{4,12},{6,14},{8,0},{10,2},{12,4},{14,6},{1,9},{3,11}... | collective-permute-start | bytes 294920 | tf_op jit(solution)/shard_map/ppermute | solution.py:403
  149.7 1.4 collective-permute-start.23

commit v7 on v6

--- a/solution.py
+++ b/solution.py
@@ -17,7 +17,7 @@
 LIST_ROWS = 16
 VMEM_BYTES = 60 * 1024 * 1024
 LAST_VMEM = 24 * 1024 * 1024
-FIRST = 384
+FIRST = 416
 SMEM_SPEC = pl.BlockSpec(memory_space=pltpu.SMEM)
 VMEM_SPEC = pl.BlockSpec(memory_space=pltpu.VMEM)
 HBM_SPEC = pl.BlockSpec(memory_space=pltpu.HBM)
@@ -161,8 +161,8 @@
         return found
 
     both = [jnp.where(row <= col, tile[i, i], tile[i + 1, i + 1]) for i in (0, 2)]
-    first = [tile[0, 1], tile[0, 2], tile[0, 3], tile[1, 2], diagonal(tile[1, 1])]
-    second = [tile[1, 3], tile[2, 3], *both, diagonal(tile[3, 3])]
+    first = [diagonal(tile[1, 1]), tile[0, 1], tile[0, 2], tile[0, 3], tile[1, 2]]
+    second = [diagonal(tile[3, 3]), tile[1, 3], tile[2, 3], *both]
     return first, second
 
 
@@ -238,8 +238,8 @@
 
 
 def late_kernel(slots, owned, width, spots_hbm, core_ref, acc_ref, *rest):
-    refs, rest = rest[:-6], rest[-6:]
-    keep_ref, send_ref, pool, spots_ref, spots_sem, sems = rest
+    refs, rest = rest[:-8], rest[-8:]
+    keep_ref, near_ref, even_ref, odd_ref, pool, spots_ref, spots_sem, sems = rest
     rows = owned * width
     part = refs[0].shape[0]
     chunks = part // rows
@@ -267,7 +267,13 @@
             keep = jnp.where(core == 0, first, second)
             send = jnp.where(core == 0, second, first)
             keep_ref[n, at : at + height, :] = keep.astype(jnp.bfloat16)
-            send_ref[n, at : at + height, :] = send.astype(jnp.bfloat16)
+            if n < owners // 2:
+                even_ref[n, at : at + height, :] = send.astype(jnp.bfloat16)
+            elif at < FIRST:
+                near_ref[n - owners // 2, at : at + height, :] = send.astype(jnp.bfloat16)
+            else:
+                row = at - FIRST
+                odd_ref[n - owners // 2, row : row + height, :] = send.astype(jnp.bfloat16)
             at += height
 
 
@@ -309,13 +315,20 @@
     rows = owned * width
     chunks = parts[0].shape[0] // rows
     half = half_rows(width)
-    out = jax.ShapeDtypeStruct((acc.shape[0], half, TILE), jnp.bfloat16)
     owners = acc.shape[0]
     return pl.pallas_call(
         functools.partial(late_kernel, slots, owned, width),
         in_specs=[HBM_SPEC, SMEM_SPEC, VMEM_SPEC] + [HBM_SPEC] * holders,
-        out_specs=[VMEM_SPEC] * 2,
-        out_shape=[out, out],
+        out_specs=[VMEM_SPEC] * 4,
+        out_shape=[
+            jax.ShapeDtypeStruct((count, height, TILE), jnp.bfloat16)
+            for count, height in (
+                (owners, half),
+                (owners // 2, FIRST),
+                (owners // 2, half),
+                (owners // 2, half - FIRST),
+            )
+        ],
         scratch_shapes=[
             pltpu.VMEM((holders * rows * chunks, TILE), jnp.bfloat16),
             pltpu.SMEM(spots.shape, spots.dtype),
@@ -345,7 +358,11 @@
     mine, other = mine_ref[...], other_ref[...]
     first = jnp.where(core == 0, mine, other).astype(jnp.float32)
     second = jnp.where(core == 0, other, mine).astype(jnp.float32)
-    pieces = [v[t * TILE : (t + 1) * TILE] for v in (first, second) for t in range(SIDE)]
+    pieces = [
+        v[width + t * TILE : width + (t + 1) * TILE]
+        for v in (first, second)
+        for t in range(SIDE)
+    ]
     places = [(0, 1), (0, 2), (0, 3), (1, 2), (1, 3), (2, 3)]
     for (i, j), value in zip(places, pieces):
         put(i, j, value)
@@ -353,7 +370,7 @@
     row, col = block_order(width)
     for i, value, diagonal in zip((0, 2), pieces[6:], (first, second)):
         flipped = value.T
-        squares = jnp.concatenate([diagonal[SIDE * TILE :]] * (TILE // width), axis=0)
+        squares = jnp.concatenate([diagonal[:width]] * (TILE // width), axis=0)
         put(i, i, jnp.where(row <= col, value, flipped))
         lower = jnp.where(row > col, value, flipped)
         put(i + 1, i + 1, jnp.where(row == col, squares, lower))
@@ -407,24 +424,25 @@
     return sum(value.astype(jnp.float32) for value in values)
 
 
-def to_owner(keep, came):
+def to_owner(keep, came_near, came_even, came_odd):
     half = keep.shape[0] // 2
-    keep, came = (v.reshape(2, half, *v.shape[1:]) for v in (keep, came))
-
-    def both(bits, offsets, rows):
-        return add(keep[bits, offsets, rows], came[bits, offsets, rows]).astype(jnp.bfloat16)
-
-    every, top, rest = slice(None), slice(0, FIRST), slice(FIRST, None)
+    keep = keep.reshape(2, half, *keep.shape[1:])
+    top, rest = slice(0, FIRST), slice(FIRST, None)
+    top_near = swap(add(keep[1, :, top], came_near).astype(jnp.bfloat16), "pairs", 1)
+
+    def rest_sum(j):
+        even = add(keep[0, j, rest], came_even[j, rest])
+        return jnp.stack([even, add(keep[1, j, rest], came_odd[j])])
+
     far_first = range(half - 1, 0, -1)
-    rest_far = [swap(both(every, j, rest), "pairs", 2 * j) for j in far_first]
-    top_near = swap(both(1, every, top), "pairs", 1)
+    rest_far = [swap(rest_sum(j).astype(jnp.bfloat16), "pairs", 2 * j) for j in far_first]
     top_sums = [
-        add(keep[0, j, top], came[0, j, top], top_near[j]).astype(jnp.bfloat16)
+        add(keep[0, j, top], came_even[j, top], top_near[j]).astype(jnp.bfloat16)
         for j in range(half)
     ]
     top_far = [swap(top_sums[j], "pairs", 2 * j) for j in far_first]
     rest_sums = [
-        add(keep[b, 0, rest], came[b, 0, rest], *(v[b] for v in rest_far)).astype(jnp.bfloat16)
+        add(rest_sum(0)[b], *(v[b] for v in rest_far)).astype(jnp.bfloat16)
         for b in range(2)
     ]
     rest_near = swap(rest_sums[1], "pairs", 1)
@@ -472,7 +490,7 @@
     cut = max(1, chunks - LATE)
     first, second = (0, cut), (cut, chunks)
     early = exchange(column_parts(orders, first, False, wanted, place, core_id, stacked), orders)
-    tied = 5
+    tied = max(0, len(early) - 2)
     early[tied], later = lax.optimization_barrier((early[tied], stacked))
     late_orders = orders[::-1]
     late_slots = [[0] + [t[k] for k in ks] for t, ks in zip(slot_tables, late_orders)]
@@ -486,8 +504,8 @@
     early, terms, choose, slots = lax.optimization_barrier((early, terms, choose, slots))
     order = (*range(0, holders, 2), *range(1, holders, 2))
     acc, spots = early_grams(order, owned, width, wanted, place, slot, [own_early, *early])
-    keep, send = late_grams(late_slots, owned, width, spots, core_id, acc, [own_late, *late])
-    mine = to_owner(keep, swap(send, "aux", 1))
+    keep, *sent = late_grams(late_slots, owned, width, spots, core_id, acc, [own_late, *late])
+    mine = to_owner(keep, *(swap(value, "aux", 1) for value in sent))
     other = swap(mine, "aux", 1)
     return finish(slots, core_id, mine, other, choose, terms)
 

time: 154 us -> 153 us (level)
  waiting for transfers between devices: 71.5 us -> 69.5 us
  starting transfers between devices: 54.7 us -> 56.4 us
    ppermute x10 -> x12, waiting for transfers between devices: 16.9 us -> 14.9 us  [swap(): return lax.ppermute(value, axis, [(i, i ^ bit) for i in range(size)])]
    ppermute x10 -> x12, starting transfers between devices: 12.1 us -> 13.8 us  [swap(): return lax.ppermute(value, axis, [(i, i ^ bit) for i in range(size)])]
  transfers between devices with their start and end apart: 24 -> 26, of which waited for: 12 -> 12; matrix products, arithmetic and copies ran while one was open for 1% -> 1% of each run, Pallas kernels for 12% -> 12%
where the time goes in v7:
time: 153 us
  waiting for transfers between devices  69.5 us (45%)
  starting transfers between devices  56.4 us (37%)
  Pallas kernels  25.5 us (17%)
    ppermute x14, waiting for transfers between devices, exchange(): arrived.append(lax.ppermute(part, ('pairs', 'aux'), moves))  54.5 us
    ppermute x14, starting transfers between devices, exchange(): arrived.append(lax.ppermute(part, ('pairs', 'aux'), moves))  42.6 us
    ppermute x12, waiting for transfers between devices, swap(): return lax.ppermute(value, axis, [(i, i ^ bit) for i in range(size)])  14.9 us
    ppermute x12, starting transfers between devices, swap(): return lax.ppermute(value, axis, [(i, i ^ bit) for i in range(size)])  13.8 us
    pallas_call x1, Pallas kernels, pair_terms(): pl.pallas_call(terms_kernel, grid=(pairs,), in_specs=[pl.BlockSpec((1, 1,...  8.38 us
    pallas_call x1, Pallas kernels, early_grams(): pl.pallas_call(functools.partial(early_kernel, ks, owned, width), in_spec...  7.05 us
    pallas_call x2, Pallas kernels, column_parts(): pl.pallas_call(functools.partial(split_kernel, orders, span, own), in_spe...  6.05 us
  transfers between devices with their start and end apart: 26, of which 12 were waited for; matrix products, arithmetic and copies ran while one was open for 1% of the time, Pallas kernels for 12%

profile of v7, /device:TPU:0, one launch (start us, length us, event | category | flops | bytes accessed | tf_op | source)
XLA Modules:
  0.0 152.9 jit_solution(1320276105984456536)
XLA Ops:
  0.0 3.0 %shard_map.73 = (bf16[1552,128]{1,0:T(8,128)(2,1)}, bf16[1552,128]{1,0:T(8,128)(2,1)}, bf16[1552,128]{1,0:T(8,128)(2,1)}, bf16[1552,128]{1,0:T(8,128)(2,1)}, bf1...) custom-call(s32[16]{0:T(128)} %wanted_ref.5, s32[1]{0:T(128)} %bitcast.place_ref, ...), custom_call_target="tpu_custom_call" | custom-call | tf_op jit(solution)/shard_map/pallas_call | solution.py:117
  3.0 4.1 %collective-permute-start = (bf16[1552,128]{1,0:T(8,128)(2,1)}, bf16[1552,128]{1,0:T(8,128)(2,1)S(1)}, u32[]{:S(2)}, u32[]{:S(2)}) collective-permute-start(bf16[1552,128]{1,0:T(8,128)(2,1)} %get-tuple-element.41), channel_id=1, source_target_pairs={{0,8},{1,3},{2,10},{3,1},{4,12},{5,7},{6,14},{7,5},{8,0},{9,11},{1... | collective-permute-start | bytes 1191944 | tf_op jit(solution)/shard_map/ppermute | solution.py:487
  7.1 2.3 %collective-permute-start.5 = (bf16[1552,128]{1,0:T(8,128)(2,1)}, bf16[1552,128]{1,0:T(8,128)(2,1)S(1)}, u32[]{:S(2)}, u32[]{:S(2)}) collective-permute-start(bf16[1552,128]{1,0:T(8,128)(2,1)} %get-tuple-element.46), channel_id=1, source_target_pairs={{0,14},{1,13},{2,12},{3,15},{4,10},{5,9},{6,8},{7,11},{8,6},{9,5},... | collective-permute-start | bytes 1191944 | tf_op jit(solution)/shard_map/ppermute | solution.py:487
  9.4 1.6 %collective-permute-start.1 = (bf16[1552,128]{1,0:T(8,128)(2,1)}, bf16[1552,128]{1,0:T(8,128)(2,1)S(1)}, u32[]{:S(2)}, u32[]{:S(2)}) collective-permute-start(bf16[1552,128]{1,0:T(8,128)(2,1)} %get-tuple-element.42), channel_id=1, source_target_pairs={{0,10},{1,9},{2,8},{3,11},{4,14},{5,13},{6,12},{7,15},{8,2},{9,1},... | collective-permute-start | bytes 1191944 | tf_op jit(solution)/shard_map/ppermute | solution.py:487
  11.1 1.5 collective-permute-start.2
  12.6 0.2 collective-permute-start.3
  12.8 33.9 %collective-permute-done.rest_1_ = bf16[1552,128]{1,0:T(8,128)(2,1)S(1)} collective-permute-done((bf16[1552,128]{1,0:T(8,128)(2,1)}, bf16[1552,128]{1,0:T(8,128)(2,1)S(1)}, u32[]{:S(2)}, u32[]{:S(2)}) %collective-permute-start) | collective-permute-done | bytes 397344 | tf_op jit(solution)/shard_map/ppermute | solution.py:487
  46.7 1.7 %collective-permute-start.4 = (bf16[1552,128]{1,0:T(8,128)(2,1)}, bf16[1552,128]{1,0:T(8,128)(2,1)S(1)}, u32[]{:S(2)}, u32[]{:S(2)}) collective-permute-start(bf16[1552,128]{1,0:T(8,128)(2,1)} %get-tuple-element.45), channel_id=1, source_target_pairs={{0,4},{1,7},{2,6},{3,5},{4,0},{5,3},{6,2},{7,1},{8,12},{9,15},{10,... | collective-permute-start | bytes 1191944 | tf_op jit(solution)/shard_map/ppermute | solution.py:487
  48.4 16.4 %collective-permute-start.6 = (bf16[1552,128]{1,0:T(8,128)(2,1)}, bf16[1552,128]{1,0:T(8,128)(2,1)S(1)}, u32[]{:S(2)}, u32[]{:S(2)}) collective-permute-start(bf16[1552,128]{1,0:T(8,128)(2,1)} %get-tuple-element.48), channel_id=1, source_target_pairs={{0,6},{1,15},{2,4},{3,13},{4,2},{5,11},{6,0},{7,9},{8,14},{9,7},{1... | collective-permute-start | bytes 1191944 | tf_op jit(solution)/shard_map/ppermute | solution.py:487
  64.9 0.1 slice_multiply_fusion
  64.9 0.1 add.127
  65.0 0.1 add.124
  65.1 0.1 add.125
  65.2 3.0 %shard_map.75 = (bf16[1024,128]{1,0:T(8,128)(2,1)}, bf16[1024,128]{1,0:T(8,128)(2,1)}, bf16[1024,128]{1,0:T(8,128)(2,1)}, bf16[1024,128]{1,0:T(8,128)(2,1)}, bf1...) custom-call(s32[16]{0:T(128)} %wanted_ref.5, ...), custom_call_target="tpu_custom_call" | custom-call | tf_op jit(solution)/shard_map/pallas_call | solution.py:117
  68.2 7.1 %collective-permute-done.1.rest_2_ = bf16[1552,128]{1,0:T(8,128)(2,1)S(1)} collective-permute-done((bf16[1552,128]{1,0:T(8,128)(2,1)}, bf16[1552,128]{1,0:T(8,128)(2,1)S(1)}, u32[]{:S(2)}, u32[]{:S(2)}) %collective-permute-start.1) | collective-permute-done | bytes 397344 | tf_op jit(solution)/shard_map/ppermute | solution.py:487
  75.4 0.2 collective-permute-start.8
  75.6 0.6 broadcast_add_fusion.right_ref
  76.2 8.4 %shard_map.74 = (f32[8,256,256]{2,1,0:T(8,128)}, bf16[8,512,256]{2,1,0:T(8,128)(2,1)}) custom-call(s32[8,1,256]{2,1,0:T(1,128)} %broadcast_add_fusion.right_ref, bf16[8,256,256]{2,1,0:T(8,128)(2,1)} %fock_ref.1, bf16[8,256,256]{2,1,0:T(8,128)(2,1)} %corr_ref.1, bf16[8,256,256]{2,1,0:T(8,128)(2,1)} %amp_ref.1), custom_call_target="tpu_custom_call" | custom-call | flops 1073741824 | bytes 7340032 | tf_op jit(solution)/shard_map/pallas_call | solution.py:40
  84.6 4.9 %collective-permute-start.9 = (bf16[1024,128]{1,0:T(8,128)(2,1)}, bf16[1024,128]{1,0:T(8,128)(2,1)S(1)}, u32[]{:S(2)}, u32[]{:S(2)}) collective-permute-start(bf16[1024,128]{1,0:T(8,128)(2,1)} %get-tuple-element.66), channel_id=1, source_target_pairs={{0,4},{1,3},{2,6},{3,1},{4,0},{5,7},{6,2},{7,5},{8,12},{9,11},{10,... | collective-permute-start | bytes 786440 | tf_op jit(solution)/shard_map/ppermute | solution.py:487
  89.5 2.8 %collective-permute-start.10 = (bf16[1024,128]{1,0:T(8,128)(2,1)}, bf16[1024,128]{1,0:T(8,128)(2,1)S(1)}, u32[]{:S(2)}, u32[]{:S(2)}) collective-permute-start(bf16[1024,128]{1,0:T(8,128)(2,1)} %get-tuple-element.67), channel_id=1, source_target_pairs={{0,10},{1,13},{2,8},{3,15},{4,14},{5,9},{6,12},{7,11},{8,2},{9,5},... | collective-permute-start | bytes 786440 | tf_op jit(solution)/shard_map/ppermute | solution.py:487
  92.3 2.0 %collective-permute-start.11 = (bf16[1024,128]{1,0:T(8,128)(2,1)}, bf16[1024,128]{1,0:T(8,128)(2,1)S(1)}, u32[]{:S(2)}, u32[]{:S(2)}) collective-permute-start(bf16[1024,128]{1,0:T(8,128)(2,1)} %get-tuple-element.68), channel_id=1, source_target_pairs={{0,6},{1,5},{2,4},{3,7},{4,2},{5,1},{6,0},{7,3},{8,14},{9,13},{10,... | collective-permute-start | bytes 786440 | tf_op jit(solution)/shard_map/ppermute | solution.py:487
  94.3 0.5 collective-permute-start.12
  94.8 4.2 %collective-permute-start.13 = (bf16[1024,128]{1,0:T(8,128)(2,1)S(1)}, bf16[1024,128]{1,0:T(8,128)(2,1)S(1)}, u32[]{:S(2)}, u32[]{:S(2)}) collective-permute-start(bf16[1024,128]{1,0:T(8,128)(2,1)S(1)} %copy-done.6), channel_id=1, source_target_pairs={{0,14},{1,7},{2,12},{3,5},{4,10},{5,3},{6,8},{7,1},{8,6},{9,15},{1... | collective-permute-start | bytes 786440 | tf_op jit(solution)/shard_map/ppermute | solution.py:487
  99.1 7.0 %shard_map.76 = (f32[8,1088,128]{2,1,0:T(8,128)S(1)}, s32[8,16]{1,0:T(8,128)S(1)}) custom-call(s32[16]{0:T(128)S(1)} %copy-done.4, s32[1]{0:T(128)} %bitcast.place_ref, s32[8]{0:T(128)S(1)} %dynamic-slice_bitcast_fusion.slot_ref, bf16[1536,128]{1,0:T(8,128)(2,1)S(1)} %copy-done.5, bf16[1552,128]{1,0:T(8,128)(2,1)S(1)} %collective-permute-done.rest_1_, ...), custom_call_target="tpu_custom_call" | custom-call | flops 1610612736 | bytes 3145728 | tf_op jit(solution)/shard_map/pallas_call | solution.py:288
  106.1 4.5 %collective-permute-done.9.rest_3_ = bf16[1024,128]{1,0:T(8,128)(2,1)S(1)} collective-permute-done((bf16[1024,128]{1,0:T(8,128)(2,1)}, bf16[1024,128]{1,0:T(8,128)(2,1)S(1)}, u32[]{:S(2)}, u32[]{:S(2)}) %collective-permute-start.9) | collective-permute-done | bytes 262176 | tf_op jit(solution)/shard_map/ppermute | solution.py:487
  110.7 9.0 %collective-permute-done.11.rest_5_ = bf16[1024,128]{1,0:T(8,128)(2,1)S(1)} collective-permute-done((bf16[1024,128]{1,0:T(8,128)(2,1)}, bf16[1024,128]{1,0:T(8,128)(2,1)S(1)}, u32[]{:S(2)}, u32[]{:S(2)}) %collective-permute-start.11) | collective-permute-done | bytes 262176 | tf_op jit(solution)/shard_map/ppermute | solution.py:487
  119.6 1.9 %shard_map.77 = (bf16[8,544,128]{2,1,0:T(8,128)(2,1)S(1)}, bf16[4,416,128]{2,1,0:T(8,128)(2,1)S(1)}, bf16[4,544,128]{2,1,0:T(8,128)(2,1)S(1)}, bf16[4,128,128]{2,1,0:T(8,128)(2,1)S(1)}) custom-call(s32[8,16]{1,0:T(8,128)S(1)} %get-tuple-element.61.spots_hbm, s32[1]{0:T(128)} %bitcast.1.core_ref, f32[8,1088,128]{2,1,0:T(8,128)S(1)} %get-tuple-element.62.acc_ref, ...), custom_call_target="tpu_custom_call" | custom-call | flops 1073741824 | bytes 2097152 | tf_op jit(solution)/shard_map/pallas_call | solution.py:319
  121.6 0.5 collective-permute-start.14
  122.1 0.1 collective-permute-start.20
  122.2 1.2 collective-permute-done.15
  123.4 0.1 fusion
  123.5 1.1 collective-permute-start.16
  124.7 5.1 %collective-permute-start.22 = (bf16[2,128,128]{2,1,0:T(8,128)(2,1)S(1)}, bf16[2,128,128]{2,1,0:T(8,128)(2,1)S(1)}, u32[]{:S(2)}, u32[]{:S(2)}) collective-permute-start(bf16[2,128,128]{2,1,0:T(8,128)(2,1)S(1)} %pad_maximum_fusion.2), channel_id=1, source_target_pairs={{0,8},{2,10},{4,12},{6,14},{8,0},{10,2},{12,4},{14,6},{1,9},{3,11}... | collective-permute-start | bytes 196616 | tf_op jit(solution)/shard_map/ppermute | solution.py:420
  129.9 1.5 collective-permute-start.21
  131.4 1.9 %collective-permute-done.22 = bf16[2,128,128]{2,1,0:T(8,128)(2,1)S(1)} collective-permute-done((bf16[2,128,128]{2,1,0:T(8,128)(2,1)S(1)}, bf16[2,128,128]{2,1,0:T(8,128)(2,1)S(1)}, u32[]{:S(2)}, u32[]{:S(2)}) %collective-permute-start.22) | collective-permute-done | bytes 65568 | tf_op jit(solution)/shard_map/ppermute | solution.py:420
  133.3 1.5 collective-permute-done.23
  134.8 1.3 collective-permute-done.21
  136.2 0.8 collective-permute-start.24
  137.0 0.1 fusion.3
  137.1 2.5 %collective-permute-start.17 = (bf16[416,128]{1,0:T(8,128)(2,1)S(1)}, bf16[416,128]{1,0:T(8,128)(2,1)S(1)}, u32[]{:S(2)}, u32[]{:S(2)}) collective-permute-start(bf16[416,128]{1,0:T(8,128)(2,1)S(1)} %get-tuple-element.77), channel_id=1, source_target_pairs={{0,12},{2,14},{4,8},{6,10},{8,4},{10,6},{12,0},{14,2},{1,13},{3,15... | collective-permute-start | bytes 319496 | tf_op jit(solution)/shard_map/ppermute | solution.py:420
  139.6 1.3 collective-permute-start.19
  140.9 0.6 collective-permute-start.18
  141.6 3.2 %collective-permute-done.17 = bf16[416,128]{1,0:T(8,128)(2,1)S(1)} collective-permute-done((bf16[416,128]{1,0:T(8,128)(2,1)S(1)}, bf16[416,128]{1,0:T(8,128)(2,1)S(1)}, u32[]{:S(2)}, u32[]{:S(2)}) %collective-permute-start.17) | collective-permute-done | bytes 106528 | tf_op jit(solution)/shard_map/ppermute | solution.py:420
  144.8 0.5 collective-permute-done.19
  145.3 4.0 %collective-permute-done.18 = bf16[416,128]{1,0:T(8,128)(2,1)S(1)} collective-permute-done((bf16[416,128]{1,0:T(8,128)(2,1)S(1)}, bf16[416,128]{1,0:T(8,128)(2,1)S(1)}, u32[]{:S(2)}, u32[]{:S(2)}) %collective-permute-start.18) | collective-permute-done | bytes 106528 | tf_op jit(solution)/shard_map/ppermute | solution.py:420
  149.2 0.1 add_convert_fusion
  149.4 1.3 collective-permute-done.25.other_ref
  150.8 2.1 %shard_map.78 = bf16[8,256,256]{2,1,0:T(8,128)(2,1)} custom-call(s32[8,16]{1,0:T(8,128)S(1)} %constant_dynamic-slice_fusion.slots_hbm, s32[1]{0:T(128)} %bitcast.1.core_ref, bf16[544,128]{1,0:T(8,128)(2,1)S(1)} %pad_maximum_fusion.mine_ref, bf16[544,128]{1,0:T(8,128)(2,1)S(1)} %collective-permute-done.25.other_ref, bf16[8,512,256]{2,1,0:T(8,128)(2,1)S(1)} %copy-done.2, ...), custom_call_target="tpu_custom_call" | custom-call | flops 536870912 | bytes 5242880 | tf_op jit(solution)/shard_map/pallas_call | solution.py:397
  (44 shorter events, 0.4 us)
Async XLA Ops:
  0.0 12.8 %copy-start = (s32[16,16]{1,0:T(8,128)S(1)}, s32[16,16]{1,0:T(8,128)}, u32[]{:S(2)}) copy-start(s32[16,16]{1,0:T(8,128)} %param.9) | copy-start | bytes 3076
  3.0 43.7 %collective-permute-start = (bf16[1552,128]{1,0:T(8,128)(2,1)}, bf16[1552,128]{1,0:T(8,128)(2,1)S(1)}, u32[]{:S(2)}, u32[]{:S(2)}) collective-permute-start(bf16[1552,128]{1,0:T(8,128)(2,1)} %get-tuple-element.41), channel_id=1, source_target_pairs={{0,8},{1,3},{2,10},{3,1},{4,12},{5,7},{6,14},{7,5},{8,0},{9,11},{1... | collective-permute-start | bytes 1191944 | tf_op jit(solution)/shard_map/ppermute | solution.py:487
  7.1 41.3 %collective-permute-start.5 = (bf16[1552,128]{1,0:T(8,128)(2,1)}, bf16[1552,128]{1,0:T(8,128)(2,1)S(1)}, u32[]{:S(2)}, u32[]{:S(2)}) collective-permute-start(bf16[1552,128]{1,0:T(8,128)(2,1)} %get-tuple-element.46), channel_id=1, source_target_pairs={{0,14},{1,13},{2,12},{3,15},{4,10},{5,9},{6,8},{7,11},{8,6},{9,5},... | collective-permute-start | bytes 1191944 | tf_op jit(solution)/shard_map/ppermute | solution.py:487
  9.4 65.9 %collective-permute-start.1 = (bf16[1552,128]{1,0:T(8,128)(2,1)}, bf16[1552,128]{1,0:T(8,128)(2,1)S(1)}, u32[]{:S(2)}, u32[]{:S(2)}) collective-permute-start(bf16[1552,128]{1,0:T(8,128)(2,1)} %get-tuple-element.42), channel_id=1, source_target_pairs={{0,10},{1,9},{2,8},{3,11},{4,14},{5,13},{6,12},{7,15},{8,2},{9,1},... | collective-permute-start | bytes 1191944 | tf_op jit(solution)/shard_map/ppermute | solution.py:487
  11.1 64.3 %collective-permute-start.2 = (bf16[1552,128]{1,0:T(8,128)(2,1)}, bf16[1552,128]{1,0:T(8,128)(2,1)S(1)}, u32[]{:S(2)}, u32[]{:S(2)}) collective-permute-start(bf16[1552,128]{1,0:T(8,128)(2,1)} %get-tuple-element.43), channel_id=1, source_target_pairs={{0,2},{1,5},{2,0},{3,7},{4,6},{5,1},{6,4},{7,3},{8,10},{9,13},{10,... | collective-permute-start | bytes 1191944 | tf_op jit(solution)/shard_map/ppermute | solution.py:487
  12.6 72.0 %collective-permute-start.3 = (bf16[1552,128]{1,0:T(8,128)(2,1)}, bf16[1552,128]{1,0:T(8,128)(2,1)S(1)}, u32[]{:S(2)}, u32[]{:S(2)}) collective-permute-start(bf16[1552,128]{1,0:T(8,128)(2,1)} %get-tuple-element.44), channel_id=1, source_target_pairs={{0,12},{1,11},{2,14},{3,9},{4,8},{5,15},{6,10},{7,13},{8,4},{9,3},... | collective-permute-start | bytes 1191944 | tf_op jit(solution)/shard_map/ppermute | solution.py:487
  46.7 42.8 %collective-permute-start.4 = (bf16[1552,128]{1,0:T(8,128)(2,1)}, bf16[1552,128]{1,0:T(8,128)(2,1)S(1)}, u32[]{:S(2)}, u32[]{:S(2)}) collective-permute-start(bf16[1552,128]{1,0:T(8,128)(2,1)} %get-tuple-element.45), channel_id=1, source_target_pairs={{0,4},{1,7},{2,6},{3,5},{4,0},{5,3},{6,2},{7,1},{8,12},{9,15},{10,... | collective-permute-start | bytes 1191944 | tf_op jit(solution)/shard_map/ppermute | solution.py:487
  48.4 43.9 %collective-permute-start.6 = (bf16[1552,128]{1,0:T(8,128)(2,1)}, bf16[1552,128]{1,0:T(8,128)(2,1)S(1)}, u32[]{:S(2)}, u32[]{:S(2)}) collective-permute-start(bf16[1552,128]{1,0:T(8,128)(2,1)} %get-tuple-element.48), channel_id=1, source_target_pairs={{0,6},{1,15},{2,4},{3,13},{4,2},{5,11},{6,0},{7,9},{8,14},{9,7},{1... | collective-permute-start | bytes 1191944 | tf_op jit(solution)/shard_map/ppermute | solution.py:487
  75.4 18.9 %collective-permute-start.7 = (bf16[1024,128]{1,0:T(8,128)(2,1)}, bf16[1024,128]{1,0:T(8,128)(2,1)S(1)}, u32[]{:S(2)}, u32[]{:S(2)}) collective-permute-start(bf16[1024,128]{1,0:T(8,128)(2,1)} %get-tuple-element.64), channel_id=1, source_target_pairs={{0,2},{1,9},{2,0},{3,11},{4,6},{5,13},{6,4},{7,15},{8,10},{9,1},{1... | collective-permute-start | bytes 786440 | tf_op jit(solution)/shard_map/ppermute | solution.py:487
  75.4 19.4 %collective-permute-start.8 = (bf16[1024,128]{1,0:T(8,128)(2,1)}, bf16[1024,128]{1,0:T(8,128)(2,1)S(1)}, u32[]{:S(2)}, u32[]{:S(2)}) collective-permute-start(bf16[1024,128]{1,0:T(8,128)(2,1)} %get-tuple-element.65), channel_id=1, source_target_pairs={{0,8},{1,11},{2,10},{3,9},{4,12},{5,15},{6,14},{7,13},{8,0},{9,3},... | collective-permute-start | bytes 786440 | tf_op jit(solution)/shard_map/ppermute | solution.py:487
  76.2 18.6 %copy-start.6 = (bf16[1024,128]{1,0:T(8,128)(2,1)S(1)}, bf16[1024,128]{1,0:T(8,128)(2,1)}, u32[]{:S(2)}) copy-start(bf16[1024,128]{1,0:T(8,128)(2,1)} %get-tuple-element.70) | copy-start | bytes 786436
  76.2 22.9 %copy-start.7 = (s32[2,8]{1,0:T(2,128)S(1)}, s32[2,8]{1,0:T(2,128)}, u32[]{:S(2)}) copy-start(s32[2,8]{1,0:T(2,128)} %constant.30.clone) | copy-start | bytes 196
  76.2 22.9 %copy-start.4 = (s32[16]{0:T(128)S(1)}, s32[16]{0:T(128)}, u32[]{:S(2)}) copy-start(s32[16]{0:T(128)} %wanted_ref.5) | copy-start | bytes 196
  76.2 22.9 %copy-start.5 = (bf16[1536,128]{1,0:T(8,128)(2,1)S(1)}, bf16[1536,128]{1,0:T(8,128)(2,1)}, u32[]{:S(2)}) copy-start(bf16[1536,128]{1,0:T(8,128)(2,1)} %get-tuple-element.53.rest_0_) | copy-start | bytes 1179652
  84.6 26.1 %collective-permute-start.9 = (bf16[1024,128]{1,0:T(8,128)(2,1)}, bf16[1024,128]{1,0:T(8,128)(2,1)S(1)}, u32[]{:S(2)}, u32[]{:S(2)}) collective-permute-start(bf16[1024,128]{1,0:T(8,128)(2,1)} %get-tuple-element.66), channel_id=1, source_target_pairs={{0,4},{1,3},{2,6},{3,1},{4,0},{5,7},{6,2},{7,5},{8,12},{9,11},{10,... | collective-permute-start | bytes 786440 | tf_op jit(solution)/shard_map/ppermute | solution.py:487
  89.5 21.1 %collective-permute-start.10 = (bf16[1024,128]{1,0:T(8,128)(2,1)}, bf16[1024,128]{1,0:T(8,128)(2,1)S(1)}, u32[]{:S(2)}, u32[]{:S(2)}) collective-permute-start(bf16[1024,128]{1,0:T(8,128)(2,1)} %get-tuple-element.67), channel_id=1, source_target_pairs={{0,10},{1,13},{2,8},{3,15},{4,14},{5,9},{6,12},{7,11},{8,2},{9,5},... | collective-permute-start | bytes 786440 | tf_op jit(solution)/shard_map/ppermute | solution.py:487
  92.3 27.3 %collective-permute-start.11 = (bf16[1024,128]{1,0:T(8,128)(2,1)}, bf16[1024,128]{1,0:T(8,128)(2,1)S(1)}, u32[]{:S(2)}, u32[]{:S(2)}) collective-permute-start(bf16[1024,128]{1,0:T(8,128)(2,1)} %get-tuple-element.68), channel_id=1, source_target_pairs={{0,6},{1,5},{2,4},{3,7},{4,2},{5,1},{6,0},{7,3},{8,14},{9,13},{10,... | collective-permute-start | bytes 786440 | tf_op jit(solution)/shard_map/ppermute | solution.py:487
  94.3 25.4 %collective-permute-start.12 = (bf16[1024,128]{1,0:T(8,128)(2,1)}, bf16[1024,128]{1,0:T(8,128)(2,1)S(1)}, u32[]{:S(2)}, u32[]{:S(2)}) collective-permute-start(bf16[1024,128]{1,0:T(8,128)(2,1)} %get-tuple-element.69), channel_id=1, source_target_pairs={{0,12},{1,15},{2,14},{3,13},{4,8},{5,11},{6,10},{7,9},{8,4},{9,7},... | collective-permute-start | bytes 786440 | tf_op jit(solution)/shard_map/ppermute | solution.py:487
  94.8 24.8 %collective-permute-start.13 = (bf16[1024,128]{1,0:T(8,128)(2,1)S(1)}, bf16[1024,128]{1,0:T(8,128)(2,1)S(1)}, u32[]{:S(2)}, u32[]{:S(2)}) collective-permute-start(bf16[1024,128]{1,0:T(8,128)(2,1)S(1)} %copy-done.6), channel_id=1, source_target_pairs={{0,14},{1,7},{2,12},{3,5},{4,10},{5,3},{6,8},{7,1},{8,6},{9,15},{1... | collective-permute-start | bytes 786440 | tf_op jit(solution)/shard_map/ppermute | solution.py:487
  99.1 20.6 %copy-start.3 = (bf16[1024,128]{1,0:T(8,128)(2,1)S(1)}, bf16[1024,128]{1,0:T(8,128)(2,1)}, u32[]{:S(2)}) copy-start(bf16[1024,128]{1,0:T(8,128)(2,1)} %get-tuple-element.63.rest_0_) | copy-start | bytes 786436
  121.5 1.8 %collective-permute-start.15 = (bf16[4,416,128]{2,1,0:T(8,128)(2,1)S(1)}, bf16[4,416,128]{2,1,0:T(8,128)(2,1)S(1)}, u32[]{:S(2)}, u32[]{:S(2)}) collective-permute-start(bf16[4,416,128]{2,1,0:T(8,128)(2,1)S(1)} %get-tuple-element.73), channel_id=1, source_target_pairs={{0,1},{1,0},{2,3},{3,2},{4,5},{5,4},{6,7},{7,6},{8,9},{9,8},{10,11... | collective-permute-start | bytes 1277960 | tf_op jit(solution)/shard_map/ppermute | solution.py:420
  121.6 3.0 %collective-permute-start.14 = (bf16[4,544,128]{2,1,0:T(8,128)(2,1)S(1)}, bf16[4,544,128]{2,1,0:T(8,128)(2,1)S(1)}, u32[]{:S(2)}, u32[]{:S(2)}) collective-permute-start(bf16[4,544,128]{2,1,0:T(8,128)(2,1)S(1)} %get-tuple-element.72), channel_id=1, source_target_pairs={{0,1},{1,0},{2,3},{3,2},{4,5},{5,4},{6,7},{7,6},{8,9},{9,8},{10,11... | collective-permute-start | bytes 1671176 | tf_op jit(solution)/shard_map/ppermute | solution.py:420
  122.1 2.5 %collective-permute-start.20 = (bf16[4,128,128]{2,1,0:T(8,128)(2,1)S(1)}, bf16[4,128,128]{2,1,0:T(8,128)(2,1)S(1)}, u32[]{:S(2)}, u32[]{:S(2)}) collective-permute-start(bf16[4,128,128]{2,1,0:T(8,128)(2,1)S(1)} %get-tuple-element.74), channel_id=1, source_target_pairs={{0,1},{1,0},{2,3},{3,2},{4,5},{5,4},{6,7},{7,6},{8,9},{9,8},{10,11... | collective-permute-start | bytes 393224 | tf_op jit(solution)/shard_map/ppermute | solution.py:420
  123.4 27.4 %copy-start.2 = (bf16[8,512,256]{2,1,0:T(8,128)(2,1)S(1)}, bf16[8,512,256]{2,1,0:T(8,128)(2,1)}, u32[]{:S(2)}) copy-start(bf16[8,512,256]{2,1,0:T(8,128)(2,1)} %get-tuple-element.75.choose_ref) | copy-start | bytes 6291460
  123.5 13.5 %collective-permute-start.16 = (bf16[4,416,128]{2,1,0:T(8,128)(2,1)S(1)}, bf16[4,416,128]{2,1,0:T(8,128)(2,1)S(1)}, u32[]{:S(2)}, u32[]{:S(2)}) collective-permute-start(bf16[4,416,128]{2,1,0:T(8,128)(2,1)S(1)} %fusion), channel_id=1, source_target_pairs={{0,2},{2,0},{4,6},{6,4},{8,10},{10,8},{12,14},{14,12},{1,3},{3,1},... | collective-permute-start | bytes 1277960 | tf_op jit(solution)/shard_map/ppermute | solution.py:420
  124.7 8.6 %collective-permute-start.22 = (bf16[2,128,128]{2,1,0:T(8,128)(2,1)S(1)}, bf16[2,128,128]{2,1,0:T(8,128)(2,1)S(1)}, u32[]{:S(2)}, u32[]{:S(2)}) collective-permute-start(bf16[2,128,128]{2,1,0:T(8,128)(2,1)S(1)} %pad_maximum_fusion.2), channel_id=1, source_target_pairs={{0,8},{2,10},{4,12},{6,14},{8,0},{10,2},{12,4},{14,6},{1,9},{3,11}... | collective-permute-start | bytes 196616 | tf_op jit(solution)/shard_map/ppermute | solution.py:420
  129.8 5.0 %collective-permute-start.23 = (bf16[2,128,128]{2,1,0:T(8,128)(2,1)S(1)}, bf16[2,128,128]{2,1,0:T(8,128)(2,1)S(1)}, u32[]{:S(2)}, u32[]{:S(2)}) collective-permute-start(bf16[2,128,128]{2,1,0:T(8,128)(2,1)S(1)} %pad_maximum_fusion.3), channel_id=1, source_target_pairs={{0,4},{2,6},{4,0},{6,2},{8,12},{10,14},{12,8},{14,10},{1,5},{3,7},... | collective-permute-start | bytes 196616 | tf_op jit(solution)/shard_map/ppermute | solution.py:420
  129.9 6.2 %collective-permute-start.21 = (bf16[2,128,128]{2,1,0:T(8,128)(2,1)S(1)}, bf16[2,128,128]{2,1,0:T(8,128)(2,1)S(1)}, u32[]{:S(2)}, u32[]{:S(2)}) collective-permute-start(bf16[2,128,128]{2,1,0:T(8,128)(2,1)S(1)} %pad_maximum_fusion.1), channel_id=1, source_target_pairs={{0,12},{2,14},{4,8},{6,10},{8,4},{10,6},{12,0},{14,2},{1,13},{3,15... | collective-permute-start | bytes 196616 | tf_op jit(solution)/shard_map/ppermute | solution.py:420
  136.1 14.7 %copy-start.1 = (f32[8,256,256]{2,1,0:T(8,128)S(1)}, f32[8,256,256]{2,1,0:T(8,128)}, u32[]{:S(2)}) copy-start(f32[8,256,256]{2,1,0:T(8,128)} %get-tuple-element.76.terms_ref) | copy-start | bytes 6291460
  136.2 5.4 %collective-permute-start.24 = (bf16[128,128]{1,0:T(8,128)(2,1)S(1)}, bf16[128,128]{1,0:T(8,128)(2,1)S(1)}, u32[]{:S(2)}, u32[]{:S(2)}) collective-permute-start(bf16[128,128]{1,0:T(8,128)(2,1)S(1)} %fusion.5), channel_id=1, source_target_pairs={{0,2},{2,0},{4,6},{6,4},{8,10},{10,8},{12,14},{14,12},{1,3},{3,1},... | collective-permute-start | bytes 98312 | tf_op jit(solution)/shard_map/ppermute | solution.py:420
  137.1 7.7 %collective-permute-start.17 = (bf16[416,128]{1,0:T(8,128)(2,1)S(1)}, bf16[416,128]{1,0:T(8,128)(2,1)S(1)}, u32[]{:S(2)}, u32[]{:S(2)}) collective-permute-start(bf16[416,128]{1,0:T(8,128)(2,1)S(1)} %get-tuple-element.77), channel_id=1, source_target_pairs={{0,12},{2,14},{4,8},{6,10},{8,4},{10,6},{12,0},{14,2},{1,13},{3,15... | collective-permute-start | bytes 319496 | tf_op jit(solution)/shard_map/ppermute | solution.py:420
  139.6 5.6 %collective-permute-start.19 = (bf16[416,128]{1,0:T(8,128)(2,1)S(1)}, bf16[416,128]{1,0:T(8,128)(2,1)S(1)}, u32[]{:S(2)}, u32[]{:S(2)}) collective-permute-start(bf16[416,128]{1,0:T(8,128)(2,1)S(1)} %get-tuple-element.78), channel_id=1, source_target_pairs={{0,4},{2,6},{4,0},{6,2},{8,12},{10,14},{12,8},{14,10},{1,5},{3,7},... | collective-permute-start | bytes 319496 | tf_op jit(solution)/shard_map/ppermute | solution.py:420
  140.9 8.3 %collective-permute-start.18 = (bf16[416,128]{1,0:T(8,128)(2,1)S(1)}, bf16[416,128]{1,0:T(8,128)(2,1)S(1)}, u32[]{:S(2)}, u32[]{:S(2)}) collective-permute-start(bf16[416,128]{1,0:T(8,128)(2,1)S(1)} %get-tuple-element.79), channel_id=1, source_target_pairs={{0,8},{2,10},{4,12},{6,14},{8,0},{10,2},{12,4},{14,6},{1,9},{3,11}... | collective-permute-start | bytes 319496 | tf_op jit(solution)/shard_map/ppermute | solution.py:420
  149.4 1.4 collective-permute-start.25

commit v8 on v7

--- a/solution.py
+++ b/solution.py
@@ -344,7 +344,7 @@
     )(spots, core, acc, *parts)
 
 
-def finish_kernel(slots_hbm, core_ref, mine_ref, other_ref, choose_ref, terms_ref, out_ref, *rest):
+def finish_kernel(slots_hbm, core_ref, mine_top, mine_rest, other_top, other_rest, choose_ref, terms_ref, out_ref, *rest):
     slots_ref, slots_sem, gram, stage, sems = rest
     fetch = pltpu.make_async_copy(slots_hbm, slots_ref, slots_sem)
     fetch.start()
@@ -355,7 +355,8 @@
     def put(i, j, value):
         gram[i * TILE : (i + 1) * TILE, j * TILE : (j + 1) * TILE] = value.astype(jnp.bfloat16)
 
-    mine, other = mine_ref[...], other_ref[...]
+    mine = jnp.concatenate([mine_top[...], mine_rest[...]], axis=0)
+    other = jnp.concatenate([other_top[...], other_rest[...]], axis=0)
     first = jnp.where(core == 0, mine, other).astype(jnp.float32)
     second = jnp.where(core == 0, other, mine).astype(jnp.float32)
     pieces = [
@@ -396,7 +397,7 @@
     gram_side = UNIQ * rows // DOM
     return pl.pallas_call(
         finish_kernel,
-        in_specs=[HBM_SPEC, SMEM_SPEC] + [VMEM_SPEC] * 4,
+        in_specs=[HBM_SPEC, SMEM_SPEC] + [VMEM_SPEC] * 6,
         out_specs=HBM_SPEC,
         out_shape=jax.ShapeDtypeStruct(terms.shape, jnp.bfloat16),
         scratch_shapes=[
@@ -412,7 +413,7 @@
             bytes_accessed=10 * pairs * rows * cols,
             transcendentals=0,
         ),
-    )(slots, core, mine, other, choose, terms)
+    )(slots, core, *mine, *other, choose, terms)
 
 
 def swap(value, axis, bit):
@@ -448,7 +449,7 @@
     rest_near = swap(rest_sums[1], "pairs", 1)
     top_total = add(top_sums[0], *top_far).astype(jnp.bfloat16)
     rest_total = add(rest_sums[0], rest_near).astype(jnp.bfloat16)
-    return jnp.concatenate([top_total, rest_total], axis=0)
+    return top_total, rest_total
 
 
 def exchange_orders(holders):
@@ -506,7 +507,7 @@
     acc, spots = early_grams(order, owned, width, wanted, place, slot, [own_early, *early])
     keep, *sent = late_grams(late_slots, owned, width, spots, core_id, acc, [own_late, *late])
     mine = to_owner(keep, *(swap(value, "aux", 1) for value in sent))
-    other = swap(mine, "aux", 1)
+    other = [swap(value, "aux", 1) for value in mine]
     return finish(slots, core_id, mine, other, choose, terms)
 
 

time: 153 us -> 153 us (level)
  waiting for transfers between devices: 69.5 us -> 66.7 us
  starting transfers between devices: 56.4 us -> 58.4 us
    ppermute x12 -> x13, waiting for transfers between devices: 14.9 us -> 12.2 us  [swap(): return lax.ppermute(value, axis, [(i, i ^ bit) for i in range(size)])]
    ppermute x12 -> x13, starting transfers between devices: 13.8 us -> 15.8 us  [swap(): return lax.ppermute(value, axis, [(i, i ^ bit) for i in range(size)])]
  transfers between devices with their start and end apart: 26 -> 27, of which waited for: 12 -> 10; matrix products, arithmetic and copies ran while one was open for 1% -> 1% of each run, Pallas kernels for 12% -> 12%
where the time goes in v8:
time: 153 us; the launch traced here: 152 us
  waiting for transfers between devices  66.7 us (44%)
  starting transfers between devices  58.4 us (38%)
  Pallas kernels  25.4 us (17%)
    ppermute x14, waiting for transfers between devices, exchange(): arrived.append(lax.ppermute(part, ('pairs', 'aux'), moves))  54.6 us
    ppermute x14, starting transfers between devices, exchange(): arrived.append(lax.ppermute(part, ('pairs', 'aux'), moves))  42.6 us
    ppermute x13, starting transfers between devices, swap(): return lax.ppermute(value, axis, [(i, i ^ bit) for i in range(size)])  15.8 us
    ppermute x13, waiting for transfers between devices, swap(): return lax.ppermute(value, axis, [(i, i ^ bit) for i in range(size)])  12.2 us
    pallas_call x1, Pallas kernels, pair_terms(): pl.pallas_call(terms_kernel, grid=(pairs,), in_specs=[pl.BlockSpec((1, 1,...  8.34 us
    pallas_call x1, Pallas kernels, early_grams(): pl.pallas_call(functools.partial(early_kernel, ks, owned, width), in_spec...  7.05 us
    pallas_call x2, Pallas kernels, column_parts(): pl.pallas_call(functools.partial(split_kernel, orders, span, own), in_spe...  6.03 us
  transfers between devices with their start and end apart: 27, of which 10 were waited for; matrix products, arithmetic and copies ran while one was open for 1% of the time, Pallas kernels for 12%

profile of v8, /device:TPU:0, one launch (start us, length us, event | category | flops | bytes accessed | tf_op | source)
XLA Modules:
  0.0 152.2 jit_solution(14103438659759450234)
XLA Ops:
  0.0 3.0 %shard_map.73 = (bf16[1552,128]{1,0:T(8,128)(2,1)}, bf16[1552,128]{1,0:T(8,128)(2,1)}, bf16[1552,128]{1,0:T(8,128)(2,1)}, bf16[1552,128]{1,0:T(8,128)(2,1)}, bf1...) custom-call(s32[16]{0:T(128)} %wanted_ref.5, s32[1]{0:T(128)} %bitcast.place_ref, ...), custom_call_target="tpu_custom_call" | custom-call | tf_op jit(solution)/shard_map/pallas_call | solution.py:117
  3.0 4.1 %collective-permute-start = (bf16[1552,128]{1,0:T(8,128)(2,1)}, bf16[1552,128]{1,0:T(8,128)(2,1)S(1)}, u32[]{:S(2)}, u32[]{:S(2)}) collective-permute-start(bf16[1552,128]{1,0:T(8,128)(2,1)} %get-tuple-element.41), channel_id=1, source_target_pairs={{0,8},{1,3},{2,10},{3,1},{4,12},{5,7},{6,14},{7,5},{8,0},{9,11},{1... | collective-permute-start | bytes 1191944 | tf_op jit(solution)/shard_map/ppermute | solution.py:488
  7.1 2.3 %collective-permute-start.5 = (bf16[1552,128]{1,0:T(8,128)(2,1)}, bf16[1552,128]{1,0:T(8,128)(2,1)S(1)}, u32[]{:S(2)}, u32[]{:S(2)}) collective-permute-start(bf16[1552,128]{1,0:T(8,128)(2,1)} %get-tuple-element.46), channel_id=1, source_target_pairs={{0,14},{1,13},{2,12},{3,15},{4,10},{5,9},{6,8},{7,11},{8,6},{9,5},... | collective-permute-start | bytes 1191944 | tf_op jit(solution)/shard_map/ppermute | solution.py:488
  9.4 1.6 %collective-permute-start.1 = (bf16[1552,128]{1,0:T(8,128)(2,1)}, bf16[1552,128]{1,0:T(8,128)(2,1)S(1)}, u32[]{:S(2)}, u32[]{:S(2)}) collective-permute-start(bf16[1552,128]{1,0:T(8,128)(2,1)} %get-tuple-element.42), channel_id=1, source_target_pairs={{0,10},{1,9},{2,8},{3,11},{4,14},{5,13},{6,12},{7,15},{8,2},{9,1},... | collective-permute-start | bytes 1191944 | tf_op jit(solution)/shard_map/ppermute | solution.py:488
  11.1 1.5 %collective-permute-start.2 = (bf16[1552,128]{1,0:T(8,128)(2,1)}, bf16[1552,128]{1,0:T(8,128)(2,1)S(1)}, u32[]{:S(2)}, u32[]{:S(2)}) collective-permute-start(bf16[1552,128]{1,0:T(8,128)(2,1)} %get-tuple-element.43), channel_id=1, source_target_pairs={{0,2},{1,5},{2,0},{3,7},{4,6},{5,1},{6,4},{7,3},{8,10},{9,13},{10,... | collective-permute-start | bytes 1191944 | tf_op jit(solution)/shard_map/ppermute | solution.py:488
  12.6 0.2 collective-permute-start.3
  12.8 33.9 %collective-permute-done.rest_1_ = bf16[1552,128]{1,0:T(8,128)(2,1)S(1)} collective-permute-done((bf16[1552,128]{1,0:T(8,128)(2,1)}, bf16[1552,128]{1,0:T(8,128)(2,1)S(1)}, u32[]{:S(2)}, u32[]{:S(2)}) %collective-permute-start) | collective-permute-done | bytes 397344 | tf_op jit(solution)/shard_map/ppermute | solution.py:488
  46.7 1.7 %collective-permute-start.4 = (bf16[1552,128]{1,0:T(8,128)(2,1)}, bf16[1552,128]{1,0:T(8,128)(2,1)S(1)}, u32[]{:S(2)}, u32[]{:S(2)}) collective-permute-start(bf16[1552,128]{1,0:T(8,128)(2,1)} %get-tuple-element.45), channel_id=1, source_target_pairs={{0,4},{1,7},{2,6},{3,5},{4,0},{5,3},{6,2},{7,1},{8,12},{9,15},{10,... | collective-permute-start | bytes 1191944 | tf_op jit(solution)/shard_map/ppermute | solution.py:488
  48.4 16.4 %collective-permute-start.6 = (bf16[1552,128]{1,0:T(8,128)(2,1)}, bf16[1552,128]{1,0:T(8,128)(2,1)S(1)}, u32[]{:S(2)}, u32[]{:S(2)}) collective-permute-start(bf16[1552,128]{1,0:T(8,128)(2,1)} %get-tuple-element.48), channel_id=1, source_target_pairs={{0,6},{1,15},{2,4},{3,13},{4,2},{5,11},{6,0},{7,9},{8,14},{9,7},{1... | collective-permute-start | bytes 1191944 | tf_op jit(solution)/shard_map/ppermute | solution.py:488
  64.9 0.1 slice_multiply_fusion
  64.9 0.1 add.127
  65.0 0.1 add.124
  65.1 0.1 add.125
  65.2 3.0 %shard_map.75 = (bf16[1024,128]{1,0:T(8,128)(2,1)}, bf16[1024,128]{1,0:T(8,128)(2,1)}, bf16[1024,128]{1,0:T(8,128)(2,1)}, bf16[1024,128]{1,0:T(8,128)(2,1)}, bf1...) custom-call(s32[16]{0:T(128)} %wanted_ref.5, ...), custom_call_target="tpu_custom_call" | custom-call | tf_op jit(solution)/shard_map/pallas_call | solution.py:117
  68.2 7.1 %collective-permute-done.1.rest_2_ = bf16[1552,128]{1,0:T(8,128)(2,1)S(1)} collective-permute-done((bf16[1552,128]{1,0:T(8,128)(2,1)}, bf16[1552,128]{1,0:T(8,128)(2,1)S(1)}, u32[]{:S(2)}, u32[]{:S(2)}) %collective-permute-start.1) | collective-permute-done | bytes 397344 | tf_op jit(solution)/shard_map/ppermute | solution.py:488
  75.4 0.2 collective-permute-start.8
  75.6 0.6 broadcast_add_fusion.right_ref
  76.2 8.3 %shard_map.74 = (f32[8,256,256]{2,1,0:T(8,128)}, bf16[8,512,256]{2,1,0:T(8,128)(2,1)}) custom-call(s32[8,1,256]{2,1,0:T(1,128)} %broadcast_add_fusion.right_ref, bf16[8,256,256]{2,1,0:T(8,128)(2,1)} %fock_ref.1, bf16[8,256,256]{2,1,0:T(8,128)(2,1)} %corr_ref.1, bf16[8,256,256]{2,1,0:T(8,128)(2,1)} %amp_ref.1), custom_call_target="tpu_custom_call" | custom-call | flops 1073741824 | bytes 7340032 | tf_op jit(solution)/shard_map/pallas_call | solution.py:40
  84.5 5.0 %collective-permute-start.9 = (bf16[1024,128]{1,0:T(8,128)(2,1)}, bf16[1024,128]{1,0:T(8,128)(2,1)S(1)}, u32[]{:S(2)}, u32[]{:S(2)}) collective-permute-start(bf16[1024,128]{1,0:T(8,128)(2,1)} %get-tuple-element.66), channel_id=1, source_target_pairs={{0,4},{1,3},{2,6},{3,1},{4,0},{5,7},{6,2},{7,5},{8,12},{9,11},{10,... | collective-permute-start | bytes 786440 | tf_op jit(solution)/shard_map/ppermute | solution.py:488
  89.5 2.8 %collective-permute-start.10 = (bf16[1024,128]{1,0:T(8,128)(2,1)}, bf16[1024,128]{1,0:T(8,128)(2,1)S(1)}, u32[]{:S(2)}, u32[]{:S(2)}) collective-permute-start(bf16[1024,128]{1,0:T(8,128)(2,1)} %get-tuple-element.67), channel_id=1, source_target_pairs={{0,10},{1,13},{2,8},{3,15},{4,14},{5,9},{6,12},{7,11},{8,2},{9,5},... | collective-permute-start | bytes 786440 | tf_op jit(solution)/shard_map/ppermute | solution.py:488
  92.3 2.0 %collective-permute-start.11 = (bf16[1024,128]{1,0:T(8,128)(2,1)}, bf16[1024,128]{1,0:T(8,128)(2,1)S(1)}, u32[]{:S(2)}, u32[]{:S(2)}) collective-permute-start(bf16[1024,128]{1,0:T(8,128)(2,1)} %get-tuple-element.68), channel_id=1, source_target_pairs={{0,6},{1,5},{2,4},{3,7},{4,2},{5,1},{6,0},{7,3},{8,14},{9,13},{10,... | collective-permute-start | bytes 786440 | tf_op jit(solution)/shard_map/ppermute | solution.py:488
  94.3 0.5 collective-permute-start.12
  94.8 4.2 %collective-permute-start.13 = (bf16[1024,128]{1,0:T(8,128)(2,1)S(1)}, bf16[1024,128]{1,0:T(8,128)(2,1)S(1)}, u32[]{:S(2)}, u32[]{:S(2)}) collective-permute-start(bf16[1024,128]{1,0:T(8,128)(2,1)S(1)} %copy-done.6), channel_id=1, source_target_pairs={{0,14},{1,7},{2,12},{3,5},{4,10},{5,3},{6,8},{7,1},{8,6},{9,15},{1... | collective-permute-start | bytes 786440 | tf_op jit(solution)/shard_map/ppermute | solution.py:488
  99.1 7.0 %shard_map.76 = (f32[8,1088,128]{2,1,0:T(8,128)S(1)}, s32[8,16]{1,0:T(8,128)S(1)}) custom-call(s32[16]{0:T(128)S(1)} %copy-done.4, s32[1]{0:T(128)} %bitcast.place_ref, s32[8]{0:T(128)S(1)} %dynamic-slice_bitcast_fusion.slot_ref, bf16[1536,128]{1,0:T(8,128)(2,1)S(1)} %copy-done.5, bf16[1552,128]{1,0:T(8,128)(2,1)S(1)} %collective-permute-done.rest_1_, ...), custom_call_target="tpu_custom_call" | custom-call | flops 1610612736 | bytes 3145728 | tf_op jit(solution)/shard_map/pallas_call | solution.py:288
  106.1 4.5 %collective-permute-done.9.rest_3_ = bf16[1024,128]{1,0:T(8,128)(2,1)S(1)} collective-permute-done((bf16[1024,128]{1,0:T(8,128)(2,1)}, bf16[1024,128]{1,0:T(8,128)(2,1)S(1)}, u32[]{:S(2)}, u32[]{:S(2)}) %collective-permute-start.9) | collective-permute-done | bytes 262176 | tf_op jit(solution)/shard_map/ppermute | solution.py:488
  110.6 9.0 %collective-permute-done.11.rest_5_ = bf16[1024,128]{1,0:T(8,128)(2,1)S(1)} collective-permute-done((bf16[1024,128]{1,0:T(8,128)(2,1)}, bf16[1024,128]{1,0:T(8,128)(2,1)S(1)}, u32[]{:S(2)}, u32[]{:S(2)}) %collective-permute-start.11) | collective-permute-done | bytes 262176 | tf_op jit(solution)/shard_map/ppermute | solution.py:488
  119.6 1.9 %shard_map.77 = (bf16[8,544,128]{2,1,0:T(8,128)(2,1)S(1)}, bf16[4,416,128]{2,1,0:T(8,128)(2,1)S(1)}, bf16[4,544,128]{2,1,0:T(8,128)(2,1)S(1)}, bf16[4,128,128]{2,1,0:T(8,128)(2,1)S(1)}) custom-call(s32[8,16]{1,0:T(8,128)S(1)} %get-tuple-element.61.spots_hbm, s32[1]{0:T(128)} %bitcast.1.core_ref, f32[8,1088,128]{2,1,0:T(8,128)S(1)} %get-tuple-element.62.acc_ref, ...), custom_call_target="tpu_custom_call" | custom-call | flops 1073741824 | bytes 2097152 | tf_op jit(solution)/shard_map/pallas_call | solution.py:319
  121.5 0.1 collective-permute-start.15
  121.6 0.5 collective-permute-start.14
  122.1 0.1 collective-permute-start.20
  122.2 1.2 collective-permute-done.15
  123.4 0.1 fusion
  123.5 1.1 collective-permute-start.16
  124.7 5.1 %collective-permute-start.22 = (bf16[2,128,128]{2,1,0:T(8,128)(2,1)S(1)}, bf16[2,128,128]{2,1,0:T(8,128)(2,1)S(1)}, u32[]{:S(2)}, u32[]{:S(2)}) collective-permute-start(bf16[2,128,128]{2,1,0:T(8,128)(2,1)S(1)} %pad_maximum_fusion.1), channel_id=1, source_target_pairs={{0,8},{2,10},{4,12},{6,14},{8,0},{10,2},{12,4},{14,6},{1,9},{3,11}... | collective-permute-start | bytes 196616 | tf_op jit(solution)/shard_map/ppermute | solution.py:421
  129.9 1.5 %collective-permute-start.21 = (bf16[2,128,128]{2,1,0:T(8,128)(2,1)S(1)}, bf16[2,128,128]{2,1,0:T(8,128)(2,1)S(1)}, u32[]{:S(2)}, u32[]{:S(2)}) collective-permute-start(bf16[2,128,128]{2,1,0:T(8,128)(2,1)S(1)} %pad_maximum_fusion), channel_id=1, source_target_pairs={{0,12},{2,14},{4,8},{6,10},{8,4},{10,6},{12,0},{14,2},{1,13},{3,15... | collective-permute-start | bytes 196616 | tf_op jit(solution)/shard_map/ppermute | solution.py:421
  131.4 4.0 %collective-permute-done.16 = bf16[4,416,128]{2,1,0:T(8,128)(2,1)S(1)} collective-permute-done((bf16[4,416,128]{2,1,0:T(8,128)(2,1)S(1)}, bf16[4,416,128]{2,1,0:T(8,128)(2,1)S(1)}, u32[]{:S(2)}, u32[]{:S(2)}) %collective-permute-start.16) | collective-permute-done | bytes 426016 | tf_op jit(solution)/shard_map/ppermute | solution.py:421
  135.4 0.1 fusion.3
  135.5 2.4 %collective-permute-start.17 = (bf16[416,128]{1,0:T(8,128)(2,1)S(1)}, bf16[416,128]{1,0:T(8,128)(2,1)S(1)}, u32[]{:S(2)}, u32[]{:S(2)}) collective-permute-start(bf16[416,128]{1,0:T(8,128)(2,1)S(1)} %get-tuple-element.77), channel_id=1, source_target_pairs={{0,12},{2,14},{4,8},{6,10},{8,4},{10,6},{12,0},{14,2},{1,13},{3,15... | collective-permute-start | bytes 319496 | tf_op jit(solution)/shard_map/ppermute | solution.py:421
  137.9 2.7 %collective-permute-start.19 = (bf16[416,128]{1,0:T(8,128)(2,1)S(1)}, bf16[416,128]{1,0:T(8,128)(2,1)S(1)}, u32[]{:S(2)}, u32[]{:S(2)}) collective-permute-start(bf16[416,128]{1,0:T(8,128)(2,1)S(1)} %get-tuple-element.78), channel_id=1, source_target_pairs={{0,4},{2,6},{4,0},{6,2},{8,12},{10,14},{12,8},{14,10},{1,5},{3,7},... | collective-permute-start | bytes 319496 | tf_op jit(solution)/shard_map/ppermute | solution.py:421
  140.6 1.7 %collective-permute-start.24 = (bf16[128,128]{1,0:T(8,128)(2,1)S(1)}, bf16[128,128]{1,0:T(8,128)(2,1)S(1)}, u32[]{:S(2)}, u32[]{:S(2)}) collective-permute-start(bf16[128,128]{1,0:T(8,128)(2,1)S(1)} %fusion.5), channel_id=1, source_target_pairs={{0,2},{2,0},{4,6},{6,4},{8,10},{10,8},{12,14},{14,12},{1,3},{3,1},... | collective-permute-start | bytes 98312 | tf_op jit(solution)/shard_map/ppermute | solution.py:421
  142.3 0.4 collective-permute-done.17
  142.7 1.4 collective-permute-done.19
  144.1 4.3 %collective-permute-done.18 = bf16[416,128]{1,0:T(8,128)(2,1)S(1)} collective-permute-done((bf16[416,128]{1,0:T(8,128)(2,1)S(1)}, bf16[416,128]{1,0:T(8,128)(2,1)S(1)}, u32[]{:S(2)}, u32[]{:S(2)}) %collective-permute-start.18) | collective-permute-done | bytes 106528 | tf_op jit(solution)/shard_map/ppermute | solution.py:421
  148.4 0.1 add_convert_fusion.mine_top
  148.5 0.1 collective-permute-start.25
  148.7 0.5 collective-permute-start.26
  149.2 0.9 collective-permute-done.26.other_rest
  150.1 2.1 %shard_map.78 = bf16[8,256,256]{2,1,0:T(8,128)(2,1)} custom-call(s32[8,16]{1,0:T(8,128)S(1)} %constant_dynamic-slice_fusion.slots_hbm, s32[1]{0:T(128)} %bitcast.1.core_ref, bf16[416,128]{1,0:T(8,128)(2,1)S(1)} %add_convert_fusion.mine_top, bf16[128,128]{1,0:T(8,128)(2,1)S(1)} %add_convert_fusion.1.mine_rest, ...), custom_call_target="tpu_custom_call" | custom-call | flops 536870912 | bytes 5242880 | tf_op jit(solution)/shard_map/pallas_call | solution.py:398
  (45 shorter events, 0.3 us)
Async XLA Ops:
  0.0 12.8 %copy-start = (s32[16,16]{1,0:T(8,128)S(1)}, s32[16,16]{1,0:T(8,128)}, u32[]{:S(2)}) copy-start(s32[16,16]{1,0:T(8,128)} %param.9) | copy-start | bytes 3076
  3.0 43.7 %collective-permute-start = (bf16[1552,128]{1,0:T(8,128)(2,1)}, bf16[1552,128]{1,0:T(8,128)(2,1)S(1)}, u32[]{:S(2)}, u32[]{:S(2)}) collective-permute-start(bf16[1552,128]{1,0:T(8,128)(2,1)} %get-tuple-element.41), channel_id=1, source_target_pairs={{0,8},{1,3},{2,10},{3,1},{4,12},{5,7},{6,14},{7,5},{8,0},{9,11},{1... | collective-permute-start | bytes 1191944 | tf_op jit(solution)/shard_map/ppermute | solution.py:488
  7.1 41.3 %collective-permute-start.5 = (bf16[1552,128]{1,0:T(8,128)(2,1)}, bf16[1552,128]{1,0:T(8,128)(2,1)S(1)}, u32[]{:S(2)}, u32[]{:S(2)}) collective-permute-start(bf16[1552,128]{1,0:T(8,128)(2,1)} %get-tuple-element.46), channel_id=1, source_target_pairs={{0,14},{1,13},{2,12},{3,15},{4,10},{5,9},{6,8},{7,11},{8,6},{9,5},... | collective-permute-start | bytes 1191944 | tf_op jit(solution)/shard_map/ppermute | solution.py:488
  9.4 65.9 %collective-permute-start.1 = (bf16[1552,128]{1,0:T(8,128)(2,1)}, bf16[1552,128]{1,0:T(8,128)(2,1)S(1)}, u32[]{:S(2)}, u32[]{:S(2)}) collective-permute-start(bf16[1552,128]{1,0:T(8,128)(2,1)} %get-tuple-element.42), channel_id=1, source_target_pairs={{0,10},{1,9},{2,8},{3,11},{4,14},{5,13},{6,12},{7,15},{8,2},{9,1},... | collective-permute-start | bytes 1191944 | tf_op jit(solution)/shard_map/ppermute | solution.py:488
  11.1 64.3 %collective-permute-start.2 = (bf16[1552,128]{1,0:T(8,128)(2,1)}, bf16[1552,128]{1,0:T(8,128)(2,1)S(1)}, u32[]{:S(2)}, u32[]{:S(2)}) collective-permute-start(bf16[1552,128]{1,0:T(8,128)(2,1)} %get-tuple-element.43), channel_id=1, source_target_pairs={{0,2},{1,5},{2,0},{3,7},{4,6},{5,1},{6,4},{7,3},{8,10},{9,13},{10,... | collective-permute-start | bytes 1191944 | tf_op jit(solution)/shard_map/ppermute | solution.py:488
  12.6 71.9 %collective-permute-start.3 = (bf16[1552,128]{1,0:T(8,128)(2,1)}, bf16[1552,128]{1,0:T(8,128)(2,1)S(1)}, u32[]{:S(2)}, u32[]{:S(2)}) collective-permute-start(bf16[1552,128]{1,0:T(8,128)(2,1)} %get-tuple-element.44), channel_id=1, source_target_pairs={{0,12},{1,11},{2,14},{3,9},{4,8},{5,15},{6,10},{7,13},{8,4},{9,3},... | collective-permute-start | bytes 1191944 | tf_op jit(solution)/shard_map/ppermute | solution.py:488
  46.7 42.8 %collective-permute-start.4 = (bf16[1552,128]{1,0:T(8,128)(2,1)}, bf16[1552,128]{1,0:T(8,128)(2,1)S(1)}, u32[]{:S(2)}, u32[]{:S(2)}) collective-permute-start(bf16[1552,128]{1,0:T(8,128)(2,1)} %get-tuple-element.45), channel_id=1, source_target_pairs={{0,4},{1,7},{2,6},{3,5},{4,0},{5,3},{6,2},{7,1},{8,12},{9,15},{10,... | collective-permute-start | bytes 1191944 | tf_op jit(solution)/shard_map/ppermute | solution.py:488
  48.4 43.9 %collective-permute-start.6 = (bf16[1552,128]{1,0:T(8,128)(2,1)}, bf16[1552,128]{1,0:T(8,128)(2,1)S(1)}, u32[]{:S(2)}, u32[]{:S(2)}) collective-permute-start(bf16[1552,128]{1,0:T(8,128)(2,1)} %get-tuple-element.48), channel_id=1, source_target_pairs={{0,6},{1,15},{2,4},{3,13},{4,2},{5,11},{6,0},{7,9},{8,14},{9,7},{1... | collective-permute-start | bytes 1191944 | tf_op jit(solution)/shard_map/ppermute | solution.py:488
  75.3 18.9 %collective-permute-start.7 = (bf16[1024,128]{1,0:T(8,128)(2,1)}, bf16[1024,128]{1,0:T(8,128)(2,1)S(1)}, u32[]{:S(2)}, u32[]{:S(2)}) collective-permute-start(bf16[1024,128]{1,0:T(8,128)(2,1)} %get-tuple-element.64), channel_id=1, source_target_pairs={{0,2},{1,9},{2,0},{3,11},{4,6},{5,13},{6,4},{7,15},{8,10},{9,1},{1... | collective-permute-start | bytes 786440 | tf_op jit(solution)/shard_map/ppermute | solution.py:488
  75.4 19.4 %collective-permute-start.8 = (bf16[1024,128]{1,0:T(8,128)(2,1)}, bf16[1024,128]{1,0:T(8,128)(2,1)S(1)}, u32[]{:S(2)}, u32[]{:S(2)}) collective-permute-start(bf16[1024,128]{1,0:T(8,128)(2,1)} %get-tuple-element.65), channel_id=1, source_target_pairs={{0,8},{1,11},{2,10},{3,9},{4,12},{5,15},{6,14},{7,13},{8,0},{9,3},... | collective-permute-start | bytes 786440 | tf_op jit(solution)/shard_map/ppermute | solution.py:488
  76.2 18.6 %copy-start.6 = (bf16[1024,128]{1,0:T(8,128)(2,1)S(1)}, bf16[1024,128]{1,0:T(8,128)(2,1)}, u32[]{:S(2)}) copy-start(bf16[1024,128]{1,0:T(8,128)(2,1)} %get-tuple-element.70) | copy-start | bytes 786436
  76.2 22.9 %copy-start.7 = (s32[2,8]{1,0:T(2,128)S(1)}, s32[2,8]{1,0:T(2,128)}, u32[]{:S(2)}) copy-start(s32[2,8]{1,0:T(2,128)} %constant.30.clone) | copy-start | bytes 196
  76.2 22.9 %copy-start.4 = (s32[16]{0:T(128)S(1)}, s32[16]{0:T(128)}, u32[]{:S(2)}) copy-start(s32[16]{0:T(128)} %wanted_ref.5) | copy-start | bytes 196
  76.2 22.9 %copy-start.5 = (bf16[1536,128]{1,0:T(8,128)(2,1)S(1)}, bf16[1536,128]{1,0:T(8,128)(2,1)}, u32[]{:S(2)}) copy-start(bf16[1536,128]{1,0:T(8,128)(2,1)} %get-tuple-element.53.rest_0_) | copy-start | bytes 1179652
  84.5 26.1 %collective-permute-start.9 = (bf16[1024,128]{1,0:T(8,128)(2,1)}, bf16[1024,128]{1,0:T(8,128)(2,1)S(1)}, u32[]{:S(2)}, u32[]{:S(2)}) collective-permute-start(bf16[1024,128]{1,0:T(8,128)(2,1)} %get-tuple-element.66), channel_id=1, source_target_pairs={{0,4},{1,3},{2,6},{3,1},{4,0},{5,7},{6,2},{7,5},{8,12},{9,11},{10,... | collective-permute-start | bytes 786440 | tf_op jit(solution)/shard_map/ppermute | solution.py:488
  89.5 21.1 %collective-permute-start.10 = (bf16[1024,128]{1,0:T(8,128)(2,1)}, bf16[1024,128]{1,0:T(8,128)(2,1)S(1)}, u32[]{:S(2)}, u32[]{:S(2)}) collective-permute-start(bf16[1024,128]{1,0:T(8,128)(2,1)} %get-tuple-element.67), channel_id=1, source_target_pairs={{0,10},{1,13},{2,8},{3,15},{4,14},{5,9},{6,12},{7,11},{8,2},{9,5},... | collective-permute-start | bytes 786440 | tf_op jit(solution)/shard_map/ppermute | solution.py:488
  92.3 27.3 %collective-permute-start.11 = (bf16[1024,128]{1,0:T(8,128)(2,1)}, bf16[1024,128]{1,0:T(8,128)(2,1)S(1)}, u32[]{:S(2)}, u32[]{:S(2)}) collective-permute-start(bf16[1024,128]{1,0:T(8,128)(2,1)} %get-tuple-element.68), channel_id=1, source_target_pairs={{0,6},{1,5},{2,4},{3,7},{4,2},{5,1},{6,0},{7,3},{8,14},{9,13},{10,... | collective-permute-start | bytes 786440 | tf_op jit(solution)/shard_map/ppermute | solution.py:488
  94.3 25.4 %collective-permute-start.12 = (bf16[1024,128]{1,0:T(8,128)(2,1)}, bf16[1024,128]{1,0:T(8,128)(2,1)S(1)}, u32[]{:S(2)}, u32[]{:S(2)}) collective-permute-start(bf16[1024,128]{1,0:T(8,128)(2,1)} %get-tuple-element.69), channel_id=1, source_target_pairs={{0,12},{1,15},{2,14},{3,13},{4,8},{5,11},{6,10},{7,9},{8,4},{9,7},... | collective-permute-start | bytes 786440 | tf_op jit(solution)/shard_map/ppermute | solution.py:488
  94.8 24.8 %collective-permute-start.13 = (bf16[1024,128]{1,0:T(8,128)(2,1)S(1)}, bf16[1024,128]{1,0:T(8,128)(2,1)S(1)}, u32[]{:S(2)}, u32[]{:S(2)}) collective-permute-start(bf16[1024,128]{1,0:T(8,128)(2,1)S(1)} %copy-done.6), channel_id=1, source_target_pairs={{0,14},{1,7},{2,12},{3,5},{4,10},{5,3},{6,8},{7,1},{8,6},{9,15},{1... | collective-permute-start | bytes 786440 | tf_op jit(solution)/shard_map/ppermute | solution.py:488
  99.1 20.6 %copy-start.3 = (bf16[1024,128]{1,0:T(8,128)(2,1)S(1)}, bf16[1024,128]{1,0:T(8,128)(2,1)}, u32[]{:S(2)}) copy-start(bf16[1024,128]{1,0:T(8,128)(2,1)} %get-tuple-element.63.rest_0_) | copy-start | bytes 786436
  121.5 1.8 %collective-permute-start.15 = (bf16[4,416,128]{2,1,0:T(8,128)(2,1)S(1)}, bf16[4,416,128]{2,1,0:T(8,128)(2,1)S(1)}, u32[]{:S(2)}, u32[]{:S(2)}) collective-permute-start(bf16[4,416,128]{2,1,0:T(8,128)(2,1)S(1)} %get-tuple-element.73), channel_id=1, source_target_pairs={{0,1},{1,0},{2,3},{3,2},{4,5},{5,4},{6,7},{7,6},{8,9},{9,8},{10,11... | collective-permute-start | bytes 1277960 | tf_op jit(solution)/shard_map/ppermute | solution.py:421
  121.6 3.0 %collective-permute-start.14 = (bf16[4,544,128]{2,1,0:T(8,128)(2,1)S(1)}, bf16[4,544,128]{2,1,0:T(8,128)(2,1)S(1)}, u32[]{:S(2)}, u32[]{:S(2)}) collective-permute-start(bf16[4,544,128]{2,1,0:T(8,128)(2,1)S(1)} %get-tuple-element.72), channel_id=1, source_target_pairs={{0,1},{1,0},{2,3},{3,2},{4,5},{5,4},{6,7},{7,6},{8,9},{9,8},{10,11... | collective-permute-start | bytes 1671176 | tf_op jit(solution)/shard_map/ppermute | solution.py:421
  122.1 2.5 %collective-permute-start.20 = (bf16[4,128,128]{2,1,0:T(8,128)(2,1)S(1)}, bf16[4,128,128]{2,1,0:T(8,128)(2,1)S(1)}, u32[]{:S(2)}, u32[]{:S(2)}) collective-permute-start(bf16[4,128,128]{2,1,0:T(8,128)(2,1)S(1)} %get-tuple-element.74), channel_id=1, source_target_pairs={{0,1},{1,0},{2,3},{3,2},{4,5},{5,4},{6,7},{7,6},{8,9},{9,8},{10,11... | collective-permute-start | bytes 393224 | tf_op jit(solution)/shard_map/ppermute | solution.py:421
  123.4 26.7 %copy-start.2 = (bf16[8,512,256]{2,1,0:T(8,128)(2,1)S(1)}, bf16[8,512,256]{2,1,0:T(8,128)(2,1)}, u32[]{:S(2)}) copy-start(bf16[8,512,256]{2,1,0:T(8,128)(2,1)} %get-tuple-element.75.choose_ref) | copy-start | bytes 6291460
  123.5 11.9 %collective-permute-start.16 = (bf16[4,416,128]{2,1,0:T(8,128)(2,1)S(1)}, bf16[4,416,128]{2,1,0:T(8,128)(2,1)S(1)}, u32[]{:S(2)}, u32[]{:S(2)}) collective-permute-start(bf16[4,416,128]{2,1,0:T(8,128)(2,1)S(1)} %fusion), channel_id=1, source_target_pairs={{0,2},{2,0},{4,6},{6,4},{8,10},{10,8},{12,14},{14,12},{1,3},{3,1},... | collective-permute-start | bytes 1277960 | tf_op jit(solution)/shard_map/ppermute | solution.py:421
  124.7 15.9 %collective-permute-start.22 = (bf16[2,128,128]{2,1,0:T(8,128)(2,1)S(1)}, bf16[2,128,128]{2,1,0:T(8,128)(2,1)S(1)}, u32[]{:S(2)}, u32[]{:S(2)}) collective-permute-start(bf16[2,128,128]{2,1,0:T(8,128)(2,1)S(1)} %pad_maximum_fusion.1), channel_id=1, source_target_pairs={{0,8},{2,10},{4,12},{6,14},{8,0},{10,2},{12,4},{14,6},{1,9},{3,11}... | collective-permute-start | bytes 196616 | tf_op jit(solution)/shard_map/ppermute | solution.py:421
  129.8 10.8 %collective-permute-start.23 = (bf16[2,128,128]{2,1,0:T(8,128)(2,1)S(1)}, bf16[2,128,128]{2,1,0:T(8,128)(2,1)S(1)}, u32[]{:S(2)}, u32[]{:S(2)}) collective-permute-start(bf16[2,128,128]{2,1,0:T(8,128)(2,1)S(1)} %pad_maximum_fusion.2), channel_id=1, source_target_pairs={{0,4},{2,6},{4,0},{6,2},{8,12},{10,14},{12,8},{14,10},{1,5},{3,7},... | collective-permute-start | bytes 196616 | tf_op jit(solution)/shard_map/ppermute | solution.py:421
  129.8 20.2 %copy-start.1 = (f32[8,256,256]{2,1,0:T(8,128)S(1)}, f32[8,256,256]{2,1,0:T(8,128)}, u32[]{:S(2)}) copy-start(f32[8,256,256]{2,1,0:T(8,128)} %get-tuple-element.76.terms_ref) | copy-start | bytes 6291460
  129.9 10.7 %collective-permute-start.21 = (bf16[2,128,128]{2,1,0:T(8,128)(2,1)S(1)}, bf16[2,128,128]{2,1,0:T(8,128)(2,1)S(1)}, u32[]{:S(2)}, u32[]{:S(2)}) collective-permute-start(bf16[2,128,128]{2,1,0:T(8,128)(2,1)S(1)} %pad_maximum_fusion), channel_id=1, source_target_pairs={{0,12},{2,14},{4,8},{6,10},{8,4},{10,6},{12,0},{14,2},{1,13},{3,15... | collective-permute-start | bytes 196616 | tf_op jit(solution)/shard_map/ppermute | solution.py:421
  135.5 7.2 %collective-permute-start.17 = (bf16[416,128]{1,0:T(8,128)(2,1)S(1)}, bf16[416,128]{1,0:T(8,128)(2,1)S(1)}, u32[]{:S(2)}, u32[]{:S(2)}) collective-permute-start(bf16[416,128]{1,0:T(8,128)(2,1)S(1)} %get-tuple-element.77), channel_id=1, source_target_pairs={{0,12},{2,14},{4,8},{6,10},{8,4},{10,6},{12,0},{14,2},{1,13},{3,15... | collective-permute-start | bytes 319496 | tf_op jit(solution)/shard_map/ppermute | solution.py:421
  137.9 6.2 %collective-permute-start.19 = (bf16[416,128]{1,0:T(8,128)(2,1)S(1)}, bf16[416,128]{1,0:T(8,128)(2,1)S(1)}, u32[]{:S(2)}, u32[]{:S(2)}) collective-permute-start(bf16[416,128]{1,0:T(8,128)(2,1)S(1)} %get-tuple-element.78), channel_id=1, source_target_pairs={{0,4},{2,6},{4,0},{6,2},{8,12},{10,14},{12,8},{14,10},{1,5},{3,7},... | collective-permute-start | bytes 319496 | tf_op jit(solution)/shard_map/ppermute | solution.py:421
  140.6 7.9 %collective-permute-start.18 = (bf16[416,128]{1,0:T(8,128)(2,1)S(1)}, bf16[416,128]{1,0:T(8,128)(2,1)S(1)}, u32[]{:S(2)}, u32[]{:S(2)}) collective-permute-start(bf16[416,128]{1,0:T(8,128)(2,1)S(1)} %get-tuple-element.79), channel_id=1, source_target_pairs={{0,8},{2,10},{4,12},{6,14},{8,0},{10,2},{12,4},{14,6},{1,9},{3,11}... | collective-permute-start | bytes 319496 | tf_op jit(solution)/shard_map/ppermute | solution.py:421
  140.6 8.0 %collective-permute-start.24 = (bf16[128,128]{1,0:T(8,128)(2,1)S(1)}, bf16[128,128]{1,0:T(8,128)(2,1)S(1)}, u32[]{:S(2)}, u32[]{:S(2)}) collective-permute-start(bf16[128,128]{1,0:T(8,128)(2,1)S(1)} %fusion.5), channel_id=1, source_target_pairs={{0,2},{2,0},{4,6},{6,4},{8,10},{10,8},{12,14},{14,12},{1,3},{3,1},... | collective-permute-start | bytes 98312 | tf_op jit(solution)/shard_map/ppermute | solution.py:421
  148.5 1.5 %collective-permute-start.25 = (bf16[416,128]{1,0:T(8,128)(2,1)S(1)}, bf16[416,128]{1,0:T(8,128)(2,1)S(1)}, u32[]{:S(2)}, u32[]{:S(2)}) collective-permute-start(bf16[416,128]{1,0:T(8,128)(2,1)S(1)} %add_convert_fusion.mine_top), channel_id=1, source_target_pairs={{0,1},{1,0},{2,3},{3,2},{4,5},{5,4},{6,7},{7,6},{8,9},{9,8},{10,11... | collective-permute-start | bytes 319496 | tf_op jit(solution)/shard_map/ppermute | solution.py:421
  148.7 1.4 collective-permute-start.26

commit v9 on v8

--- a/solution.py
+++ b/solution.py
@@ -454,9 +454,10 @@
 
 def exchange_orders(holders):
     light, heavy = [*range(1, holders // 2)], [*range(holders // 2, holders)]
-    first = heavy[:1]
-    for pair in zip(heavy[1:], light):
+    first = []
+    for pair in zip(heavy, light):
         first += pair
+    first += heavy[-1:]
     second = [k for pair in zip(light, heavy) for k in pair] + heavy[-1:]
     return [first, second]
 

time: 153 us -> 152 us (level)
  waiting for transfers between devices: 66.7 us -> 48.7 us
  starting transfers between devices: 58.4 us -> 75.7 us
    ppermute x14, waiting for transfers between devices: 54.6 us -> 39.2 us  [exchange(): arrived.append(lax.ppermute(part, ('pairs', 'aux'), moves))]
    ppermute x14, starting transfers between devices: 42.6 us -> 55 us  [exchange(): arrived.append(lax.ppermute(part, ('pairs', 'aux'), moves))]
    ppermute x13, starting transfers between devices: 15.8 us -> 20.7 us  [swap(): return lax.ppermute(value, axis, [(i, i ^ bit) for i in range(size)])]
    ppermute x13, waiting for transfers between devices: 12.2 us -> 9.46 us  [swap(): return lax.ppermute(value, axis, [(i, i ^ bit) for i in range(size)])]
where the time goes in v9:
time: 152 us; the launch traced here: 151 us
  starting transfers between devices  75.7 us (50%)
  waiting for transfers between devices  48.7 us (32%)
  Pallas kernels  25.4 us (17%)
    ppermute x14, starting transfers between devices, exchange(): arrived.append(lax.ppermute(part, ('pairs', 'aux'), moves))  55 us
    ppermute x14, waiting for transfers between devices, exchange(): arrived.append(lax.ppermute(part, ('pairs', 'aux'), moves))  39.2 us
    ppermute x13, starting transfers between devices, swap(): return lax.ppermute(value, axis, [(i, i ^ bit) for i in range(size)])  20.7 us
    ppermute x13, waiting for transfers between devices, swap(): return lax.ppermute(value, axis, [(i, i ^ bit) for i in range(size)])  9.46 us
    pallas_call x1, Pallas kernels, pair_terms(): pl.pallas_call(terms_kernel, grid=(pairs,), in_specs=[pl.BlockSpec((1, 1,...  8.34 us
    pallas_call x1, Pallas kernels, early_grams(): pl.pallas_call(functools.partial(early_kernel, ks, owned, width), in_spec...  7.05 us
    pallas_call x2, Pallas kernels, column_parts(): pl.pallas_call(functools.partial(split_kernel, orders, span, own), in_spe...  6.04 us
  transfers between devices with their start and end apart: 27, of which 10 were waited for; matrix products, arithmetic and copies ran while one was open for 1% of the time, Pallas kernels for 12%

profile of v9, /device:TPU:0, one launch (start us, length us, event | category | flops | bytes accessed | tf_op | source)
XLA Modules:
  0.0 151.5 jit_solution(11937873176975634228)
XLA Ops:
  0.0 3.0 %shard_map.73 = (bf16[1552,128]{1,0:T(8,128)(2,1)}, bf16[1552,128]{1,0:T(8,128)(2,1)}, bf16[1552,128]{1,0:T(8,128)(2,1)}, bf16[1552,128]{1,0:T(8,128)(2,1)}, bf1...) custom-call(s32[16]{0:T(128)} %wanted_ref.5, s32[1]{0:T(128)} %bitcast.place_ref, ...), custom_call_target="tpu_custom_call" | custom-call | tf_op jit(solution)/shard_map/pallas_call | solution.py:117
  3.0 4.1 %collective-permute-start = (bf16[1552,128]{1,0:T(8,128)(2,1)}, bf16[1552,128]{1,0:T(8,128)(2,1)S(1)}, u32[]{:S(2)}, u32[]{:S(2)}) collective-permute-start(bf16[1552,128]{1,0:T(8,128)(2,1)} %get-tuple-element.41), channel_id=1, source_target_pairs={{0,8},{1,3},{2,10},{3,1},{4,12},{5,7},{6,14},{7,5},{8,0},{9,11},{1... | collective-permute-start | bytes 1191944 | tf_op jit(solution)/shard_map/ppermute | solution.py:489
  7.1 2.5 %collective-permute-start.5 = (bf16[1552,128]{1,0:T(8,128)(2,1)}, bf16[1552,128]{1,0:T(8,128)(2,1)S(1)}, u32[]{:S(2)}, u32[]{:S(2)}) collective-permute-start(bf16[1552,128]{1,0:T(8,128)(2,1)} %get-tuple-element.46), channel_id=1, source_target_pairs={{0,6},{1,13},{2,4},{3,15},{4,2},{5,9},{6,0},{7,11},{8,14},{9,5},{1... | collective-permute-start | bytes 1191944 | tf_op jit(solution)/shard_map/ppermute | solution.py:489
  9.7 0.5 collective-permute-start.1
  10.2 1.3 collective-permute-start.2
  11.5 0.4 collective-permute-start.3
  11.9 20.2 %collective-permute-done.rest_1_ = bf16[1552,128]{1,0:T(8,128)(2,1)S(1)} collective-permute-done((bf16[1552,128]{1,0:T(8,128)(2,1)}, bf16[1552,128]{1,0:T(8,128)(2,1)S(1)}, u32[]{:S(2)}, u32[]{:S(2)}) %collective-permute-start) | collective-permute-done | bytes 397344 | tf_op jit(solution)/shard_map/ppermute | solution.py:489
  32.1 6.3 %collective-permute-start.4 = (bf16[1552,128]{1,0:T(8,128)(2,1)}, bf16[1552,128]{1,0:T(8,128)(2,1)S(1)}, u32[]{:S(2)}, u32[]{:S(2)}) collective-permute-start(bf16[1552,128]{1,0:T(8,128)(2,1)} %get-tuple-element.45), channel_id=1, source_target_pairs={{0,12},{1,7},{2,14},{3,5},{4,8},{5,3},{6,10},{7,1},{8,4},{9,15},{1... | collective-permute-start | bytes 1191944 | tf_op jit(solution)/shard_map/ppermute | solution.py:489
  38.4 1.0 collective-permute-start.6
  39.4 0.1 slice_multiply_fusion
  39.5 0.1 add.127
  39.5 0.1 add.124
  39.6 0.1 add.125
  39.7 3.0 %shard_map.75 = (bf16[1024,128]{1,0:T(8,128)(2,1)}, bf16[1024,128]{1,0:T(8,128)(2,1)}, bf16[1024,128]{1,0:T(8,128)(2,1)}, bf16[1024,128]{1,0:T(8,128)(2,1)}, bf1...) custom-call(s32[16]{0:T(128)} %wanted_ref.5, ...), custom_call_target="tpu_custom_call" | custom-call | tf_op jit(solution)/shard_map/pallas_call | solution.py:117
  42.7 0.6 collective-permute-start.7
  43.4 8.2 %collective-permute-done.2.rest_3_ = bf16[1552,128]{1,0:T(8,128)(2,1)S(1)} collective-permute-done((bf16[1552,128]{1,0:T(8,128)(2,1)}, bf16[1552,128]{1,0:T(8,128)(2,1)S(1)}, u32[]{:S(2)}, u32[]{:S(2)}) %collective-permute-start.2) | collective-permute-done | bytes 397344 | tf_op jit(solution)/shard_map/ppermute | solution.py:489
  51.6 0.6 broadcast_add_fusion.right_ref
  52.2 8.3 %shard_map.74 = (f32[8,256,256]{2,1,0:T(8,128)}, bf16[8,512,256]{2,1,0:T(8,128)(2,1)}) custom-call(s32[8,1,256]{2,1,0:T(1,128)} %broadcast_add_fusion.right_ref, bf16[8,256,256]{2,1,0:T(8,128)(2,1)} %fock_ref.1, bf16[8,256,256]{2,1,0:T(8,128)(2,1)} %corr_ref.1, bf16[8,256,256]{2,1,0:T(8,128)(2,1)} %amp_ref.1), custom_call_target="tpu_custom_call" | custom-call | flops 1073741824 | bytes 7340032 | tf_op jit(solution)/shard_map/pallas_call | solution.py:40
  60.5 19.6 %collective-permute-start.9 = (bf16[1024,128]{1,0:T(8,128)(2,1)}, bf16[1024,128]{1,0:T(8,128)(2,1)S(1)}, u32[]{:S(2)}, u32[]{:S(2)}) collective-permute-start(bf16[1024,128]{1,0:T(8,128)(2,1)} %get-tuple-element.66), channel_id=1, source_target_pairs={{0,4},{1,11},{2,6},{3,9},{4,0},{5,15},{6,2},{7,13},{8,12},{9,3},{1... | collective-permute-start | bytes 786440 | tf_op jit(solution)/shard_map/ppermute | solution.py:489
  80.1 0.8 collective-permute-start.10
  80.9 12.3 %collective-permute-start.11 = (bf16[1024,128]{1,0:T(8,128)(2,1)}, bf16[1024,128]{1,0:T(8,128)(2,1)S(1)}, u32[]{:S(2)}, u32[]{:S(2)}) collective-permute-start(bf16[1024,128]{1,0:T(8,128)(2,1)} %get-tuple-element.68), channel_id=1, source_target_pairs={{0,6},{1,13},{2,4},{3,15},{4,2},{5,9},{6,0},{7,11},{8,14},{9,5},{1... | collective-permute-start | bytes 786440 | tf_op jit(solution)/shard_map/ppermute | solution.py:489
  93.3 2.9 %collective-permute-done.8.rest_2_ = bf16[1024,128]{1,0:T(8,128)(2,1)S(1)} collective-permute-done((bf16[1024,128]{1,0:T(8,128)(2,1)}, bf16[1024,128]{1,0:T(8,128)(2,1)S(1)}, u32[]{:S(2)}, u32[]{:S(2)}) %collective-permute-start.8) | collective-permute-done | bytes 262176 | tf_op jit(solution)/shard_map/ppermute | solution.py:489
  96.2 5.5 %collective-permute-start.13 = (bf16[1024,128]{1,0:T(8,128)(2,1)S(1)}, bf16[1024,128]{1,0:T(8,128)(2,1)S(1)}, u32[]{:S(2)}, u32[]{:S(2)}) collective-permute-start(bf16[1024,128]{1,0:T(8,128)(2,1)S(1)} %copy-done.6), channel_id=1, source_target_pairs={{0,14},{1,15},{2,12},{3,13},{4,10},{5,11},{6,8},{7,9},{8,6},{9,7},... | collective-permute-start | bytes 786440 | tf_op jit(solution)/shard_map/ppermute | solution.py:489
  101.7 7.0 %shard_map.76 = (f32[8,1088,128]{2,1,0:T(8,128)S(1)}, s32[8,16]{1,0:T(8,128)S(1)}) custom-call(s32[16]{0:T(128)S(1)} %copy-done.4, s32[1]{0:T(128)} %bitcast.place_ref, s32[8]{0:T(128)S(1)} %dynamic-slice_bitcast_fusion.slot_ref, bf16[1536,128]{1,0:T(8,128)(2,1)S(1)} %copy-done.5, bf16[1552,128]{1,0:T(8,128)(2,1)S(1)} %collective-permute-done.rest_1_, ...), custom_call_target="tpu_custom_call" | custom-call | flops 1610612736 | bytes 3145728 | tf_op jit(solution)/shard_map/pallas_call | solution.py:288
  108.8 7.9 %collective-permute-done.11.rest_5_ = bf16[1024,128]{1,0:T(8,128)(2,1)S(1)} collective-permute-done((bf16[1024,128]{1,0:T(8,128)(2,1)}, bf16[1024,128]{1,0:T(8,128)(2,1)S(1)}, u32[]{:S(2)}, u32[]{:S(2)}) %collective-permute-start.11) | collective-permute-done | bytes 262176 | tf_op jit(solution)/shard_map/ppermute | solution.py:489
  116.7 1.9 %shard_map.77 = (bf16[8,544,128]{2,1,0:T(8,128)(2,1)S(1)}, bf16[4,416,128]{2,1,0:T(8,128)(2,1)S(1)}, bf16[4,544,128]{2,1,0:T(8,128)(2,1)S(1)}, bf16[4,128,128]{2,1,0:T(8,128)(2,1)S(1)}) custom-call(s32[8,16]{1,0:T(8,128)S(1)} %get-tuple-element.61.spots_hbm, s32[1]{0:T(128)} %bitcast.1.core_ref, f32[8,1088,128]{2,1,0:T(8,128)S(1)} %get-tuple-element.62.acc_ref, ...), custom_call_target="tpu_custom_call" | custom-call | flops 1073741824 | bytes 2097152 | tf_op jit(solution)/shard_map/pallas_call | solution.py:319
  118.6 0.2 collective-permute-start.15
  118.8 0.4 collective-permute-start.14
  119.2 0.1 collective-permute-start.20
  119.3 1.2 collective-permute-done.15
  120.5 0.1 fusion
  120.6 0.1 collective-permute-start.16
  120.7 0.8 collective-permute-done.20
  121.5 8.1 %collective-permute-start.22 = (bf16[2,128,128]{2,1,0:T(8,128)(2,1)S(1)}, bf16[2,128,128]{2,1,0:T(8,128)(2,1)S(1)}, u32[]{:S(2)}, u32[]{:S(2)}) collective-permute-start(bf16[2,128,128]{2,1,0:T(8,128)(2,1)S(1)} %pad_maximum_fusion.1), channel_id=1, source_target_pairs={{0,8},{2,10},{4,12},{6,14},{8,0},{10,2},{12,4},{14,6},{1,9},{3,11}... | collective-permute-start | bytes 196616 | tf_op jit(solution)/shard_map/ppermute | solution.py:421
  129.7 0.1 collective-permute-start.23
  129.8 1.5 %collective-permute-start.21 = (bf16[2,128,128]{2,1,0:T(8,128)(2,1)S(1)}, bf16[2,128,128]{2,1,0:T(8,128)(2,1)S(1)}, u32[]{:S(2)}, u32[]{:S(2)}) collective-permute-start(bf16[2,128,128]{2,1,0:T(8,128)(2,1)S(1)} %pad_maximum_fusion), channel_id=1, source_target_pairs={{0,12},{2,14},{4,8},{6,10},{8,4},{10,6},{12,0},{14,2},{1,13},{3,15... | collective-permute-start | bytes 196616 | tf_op jit(solution)/shard_map/ppermute | solution.py:421
  131.3 1.2 collective-permute-done.16
  132.5 0.1 fusion.3
  132.6 2.4 %collective-permute-start.17 = (bf16[416,128]{1,0:T(8,128)(2,1)S(1)}, bf16[416,128]{1,0:T(8,128)(2,1)S(1)}, u32[]{:S(2)}, u32[]{:S(2)}) collective-permute-start(bf16[416,128]{1,0:T(8,128)(2,1)S(1)} %get-tuple-element.77), channel_id=1, source_target_pairs={{0,12},{2,14},{4,8},{6,10},{8,4},{10,6},{12,0},{14,2},{1,13},{3,15... | collective-permute-start | bytes 319496 | tf_op jit(solution)/shard_map/ppermute | solution.py:421
  135.0 5.6 %collective-permute-start.19 = (bf16[416,128]{1,0:T(8,128)(2,1)S(1)}, bf16[416,128]{1,0:T(8,128)(2,1)S(1)}, u32[]{:S(2)}, u32[]{:S(2)}) collective-permute-start(bf16[416,128]{1,0:T(8,128)(2,1)S(1)} %get-tuple-element.78), channel_id=1, source_target_pairs={{0,4},{2,6},{4,0},{6,2},{8,12},{10,14},{12,8},{14,10},{1,5},{3,7},... | collective-permute-start | bytes 319496 | tf_op jit(solution)/shard_map/ppermute | solution.py:421
  140.7 1.6 %collective-permute-start.24 = (bf16[128,128]{1,0:T(8,128)(2,1)S(1)}, bf16[128,128]{1,0:T(8,128)(2,1)S(1)}, u32[]{:S(2)}, u32[]{:S(2)}) collective-permute-start(bf16[128,128]{1,0:T(8,128)(2,1)S(1)} %fusion.5), channel_id=1, source_target_pairs={{0,2},{2,0},{4,6},{6,4},{8,10},{10,8},{12,14},{14,12},{1,3},{3,1},... | collective-permute-start | bytes 98312 | tf_op jit(solution)/shard_map/ppermute | solution.py:421
  142.3 1.0 collective-permute-done.19
  143.3 4.4 %collective-permute-done.18 = bf16[416,128]{1,0:T(8,128)(2,1)S(1)} collective-permute-done((bf16[416,128]{1,0:T(8,128)(2,1)S(1)}, bf16[416,128]{1,0:T(8,128)(2,1)S(1)}, u32[]{:S(2)}, u32[]{:S(2)}) %collective-permute-start.18) | collective-permute-done | bytes 106528 | tf_op jit(solution)/shard_map/ppermute | solution.py:421
  147.7 0.1 add_convert_fusion.mine_top
  147.8 0.1 collective-permute-start.25
  148.0 0.5 collective-permute-start.26
  148.5 0.9 collective-permute-done.26.other_rest
  149.4 2.1 %shard_map.78 = bf16[8,256,256]{2,1,0:T(8,128)(2,1)} custom-call(s32[8,16]{1,0:T(8,128)S(1)} %constant_dynamic-slice_fusion.slots_hbm, s32[1]{0:T(128)} %bitcast.1.core_ref, bf16[416,128]{1,0:T(8,128)(2,1)S(1)} %add_convert_fusion.mine_top, bf16[128,128]{1,0:T(8,128)(2,1)S(1)} %add_convert_fusion.1.mine_rest, ...), custom_call_target="tpu_custom_call" | custom-call | flops 536870912 | bytes 5242880 | tf_op jit(solution)/shard_map/pallas_call | solution.py:398
  (45 shorter events, 0.2 us)
Async XLA Ops:
  0.0 11.9 %copy-start = (s32[16,16]{1,0:T(8,128)S(1)}, s32[16,16]{1,0:T(8,128)}, u32[]{:S(2)}) copy-start(s32[16,16]{1,0:T(8,128)} %param.9) | copy-start | bytes 3076
  3.0 29.1 %collective-permute-start = (bf16[1552,128]{1,0:T(8,128)(2,1)}, bf16[1552,128]{1,0:T(8,128)(2,1)S(1)}, u32[]{:S(2)}, u32[]{:S(2)}) collective-permute-start(bf16[1552,128]{1,0:T(8,128)(2,1)} %get-tuple-element.41), channel_id=1, source_target_pairs={{0,8},{1,3},{2,10},{3,1},{4,12},{5,7},{6,14},{7,5},{8,0},{9,11},{1... | collective-permute-start | bytes 1191944 | tf_op jit(solution)/shard_map/ppermute | solution.py:489
  7.1 31.3 %collective-permute-start.5 = (bf16[1552,128]{1,0:T(8,128)(2,1)}, bf16[1552,128]{1,0:T(8,128)(2,1)S(1)}, u32[]{:S(2)}, u32[]{:S(2)}) collective-permute-start(bf16[1552,128]{1,0:T(8,128)(2,1)} %get-tuple-element.46), channel_id=1, source_target_pairs={{0,6},{1,13},{2,4},{3,15},{4,2},{5,9},{6,0},{7,11},{8,14},{9,5},{1... | collective-permute-start | bytes 1191944 | tf_op jit(solution)/shard_map/ppermute | solution.py:489
  9.7 33.1 %collective-permute-start.1 = (bf16[1552,128]{1,0:T(8,128)(2,1)}, bf16[1552,128]{1,0:T(8,128)(2,1)S(1)}, u32[]{:S(2)}, u32[]{:S(2)}) collective-permute-start(bf16[1552,128]{1,0:T(8,128)(2,1)} %get-tuple-element.42), channel_id=1, source_target_pairs={{0,2},{1,9},{2,0},{3,11},{4,6},{5,13},{6,4},{7,15},{8,10},{9,1},{1... | collective-permute-start | bytes 1191944 | tf_op jit(solution)/shard_map/ppermute | solution.py:489
  10.2 41.4 %collective-permute-start.2 = (bf16[1552,128]{1,0:T(8,128)(2,1)}, bf16[1552,128]{1,0:T(8,128)(2,1)S(1)}, u32[]{:S(2)}, u32[]{:S(2)}) collective-permute-start(bf16[1552,128]{1,0:T(8,128)(2,1)} %get-tuple-element.43), channel_id=1, source_target_pairs={{0,10},{1,5},{2,8},{3,7},{4,14},{5,1},{6,12},{7,3},{8,2},{9,13},{1... | collective-permute-start | bytes 1191944 | tf_op jit(solution)/shard_map/ppermute | solution.py:489
  11.5 49.1 %collective-permute-start.3 = (bf16[1552,128]{1,0:T(8,128)(2,1)}, bf16[1552,128]{1,0:T(8,128)(2,1)S(1)}, u32[]{:S(2)}, u32[]{:S(2)}) collective-permute-start(bf16[1552,128]{1,0:T(8,128)(2,1)} %get-tuple-element.44), channel_id=1, source_target_pairs={{0,4},{1,11},{2,6},{3,9},{4,0},{5,15},{6,2},{7,13},{8,12},{9,3},{1... | collective-permute-start | bytes 1191944 | tf_op jit(solution)/shard_map/ppermute | solution.py:489
  32.1 48.0 %collective-permute-start.4 = (bf16[1552,128]{1,0:T(8,128)(2,1)}, bf16[1552,128]{1,0:T(8,128)(2,1)S(1)}, u32[]{:S(2)}, u32[]{:S(2)}) collective-permute-start(bf16[1552,128]{1,0:T(8,128)(2,1)} %get-tuple-element.45), channel_id=1, source_target_pairs={{0,12},{1,7},{2,14},{3,5},{4,8},{5,3},{6,10},{7,1},{8,4},{9,15},{1... | collective-permute-start | bytes 1191944 | tf_op jit(solution)/shard_map/ppermute | solution.py:489
  38.4 42.5 %collective-permute-start.6 = (bf16[1552,128]{1,0:T(8,128)(2,1)}, bf16[1552,128]{1,0:T(8,128)(2,1)S(1)}, u32[]{:S(2)}, u32[]{:S(2)}) collective-permute-start(bf16[1552,128]{1,0:T(8,128)(2,1)} %get-tuple-element.48), channel_id=1, source_target_pairs={{0,14},{1,15},{2,12},{3,13},{4,10},{5,11},{6,8},{7,9},{8,6},{9,7},... | collective-permute-start | bytes 1191944 | tf_op jit(solution)/shard_map/ppermute | solution.py:489
  42.7 50.5 %collective-permute-start.7 = (bf16[1024,128]{1,0:T(8,128)(2,1)}, bf16[1024,128]{1,0:T(8,128)(2,1)S(1)}, u32[]{:S(2)}, u32[]{:S(2)}) collective-permute-start(bf16[1024,128]{1,0:T(8,128)(2,1)} %get-tuple-element.64), channel_id=1, source_target_pairs={{0,2},{1,9},{2,0},{3,11},{4,6},{5,13},{6,4},{7,15},{8,10},{9,1},{1... | collective-permute-start | bytes 786440 | tf_op jit(solution)/shard_map/ppermute | solution.py:489
  51.6 44.6 %collective-permute-start.8 = (bf16[1024,128]{1,0:T(8,128)(2,1)}, bf16[1024,128]{1,0:T(8,128)(2,1)S(1)}, u32[]{:S(2)}, u32[]{:S(2)}) collective-permute-start(bf16[1024,128]{1,0:T(8,128)(2,1)} %get-tuple-element.65), channel_id=1, source_target_pairs={{0,8},{1,3},{2,10},{3,1},{4,12},{5,7},{6,14},{7,5},{8,0},{9,11},{1... | collective-permute-start | bytes 786440 | tf_op jit(solution)/shard_map/ppermute | solution.py:489
  52.2 44.0 %copy-start.6 = (bf16[1024,128]{1,0:T(8,128)(2,1)S(1)}, bf16[1024,128]{1,0:T(8,128)(2,1)}, u32[]{:S(2)}) copy-start(bf16[1024,128]{1,0:T(8,128)(2,1)} %get-tuple-element.70) | copy-start | bytes 786436
  52.2 49.5 %copy-start.7 = (s32[2,8]{1,0:T(2,128)S(1)}, s32[2,8]{1,0:T(2,128)}, u32[]{:S(2)}) copy-start(s32[2,8]{1,0:T(2,128)} %constant.30.clone) | copy-start | bytes 196
  52.2 49.5 %copy-start.4 = (s32[16]{0:T(128)S(1)}, s32[16]{0:T(128)}, u32[]{:S(2)}) copy-start(s32[16]{0:T(128)} %wanted_ref.5) | copy-start | bytes 196
  52.2 49.5 %copy-start.5 = (bf16[1536,128]{1,0:T(8,128)(2,1)S(1)}, bf16[1536,128]{1,0:T(8,128)(2,1)}, u32[]{:S(2)}) copy-start(bf16[1536,128]{1,0:T(8,128)(2,1)} %get-tuple-element.53.rest_0_) | copy-start | bytes 1179652
  60.5 48.3 %collective-permute-start.9 = (bf16[1024,128]{1,0:T(8,128)(2,1)}, bf16[1024,128]{1,0:T(8,128)(2,1)S(1)}, u32[]{:S(2)}, u32[]{:S(2)}) collective-permute-start(bf16[1024,128]{1,0:T(8,128)(2,1)} %get-tuple-element.66), channel_id=1, source_target_pairs={{0,4},{1,11},{2,6},{3,9},{4,0},{5,15},{6,2},{7,13},{8,12},{9,3},{1... | collective-permute-start | bytes 786440 | tf_op jit(solution)/shard_map/ppermute | solution.py:489
  80.1 28.7 %collective-permute-start.10 = (bf16[1024,128]{1,0:T(8,128)(2,1)}, bf16[1024,128]{1,0:T(8,128)(2,1)S(1)}, u32[]{:S(2)}, u32[]{:S(2)}) collective-permute-start(bf16[1024,128]{1,0:T(8,128)(2,1)} %get-tuple-element.67), channel_id=1, source_target_pairs={{0,10},{1,5},{2,8},{3,7},{4,14},{5,1},{6,12},{7,3},{8,2},{9,13},{1... | collective-permute-start | bytes 786440 | tf_op jit(solution)/shard_map/ppermute | solution.py:489
  80.9 35.8 %collective-permute-start.11 = (bf16[1024,128]{1,0:T(8,128)(2,1)}, bf16[1024,128]{1,0:T(8,128)(2,1)S(1)}, u32[]{:S(2)}, u32[]{:S(2)}) collective-permute-start(bf16[1024,128]{1,0:T(8,128)(2,1)} %get-tuple-element.68), channel_id=1, source_target_pairs={{0,6},{1,13},{2,4},{3,15},{4,2},{5,9},{6,0},{7,11},{8,14},{9,5},{1... | collective-permute-start | bytes 786440 | tf_op jit(solution)/shard_map/ppermute | solution.py:489
  93.3 23.4 %collective-permute-start.12 = (bf16[1024,128]{1,0:T(8,128)(2,1)}, bf16[1024,128]{1,0:T(8,128)(2,1)S(1)}, u32[]{:S(2)}, u32[]{:S(2)}) collective-permute-start(bf16[1024,128]{1,0:T(8,128)(2,1)} %get-tuple-element.69), channel_id=1, source_target_pairs={{0,12},{1,7},{2,14},{3,5},{4,8},{5,3},{6,10},{7,1},{8,4},{9,15},{1... | collective-permute-start | bytes 786440 | tf_op jit(solution)/shard_map/ppermute | solution.py:489
  96.2 20.5 %collective-permute-start.13 = (bf16[1024,128]{1,0:T(8,128)(2,1)S(1)}, bf16[1024,128]{1,0:T(8,128)(2,1)S(1)}, u32[]{:S(2)}, u32[]{:S(2)}) collective-permute-start(bf16[1024,128]{1,0:T(8,128)(2,1)S(1)} %copy-done.6), channel_id=1, source_target_pairs={{0,14},{1,15},{2,12},{3,13},{4,10},{5,11},{6,8},{7,9},{8,6},{9,7},... | collective-permute-start | bytes 786440 | tf_op jit(solution)/shard_map/ppermute | solution.py:489
  101.7 15.0 %copy-start.3 = (bf16[1024,128]{1,0:T(8,128)(2,1)S(1)}, bf16[1024,128]{1,0:T(8,128)(2,1)}, u32[]{:S(2)}) copy-start(bf16[1024,128]{1,0:T(8,128)(2,1)} %get-tuple-element.63.rest_0_) | copy-start | bytes 786436
  118.6 1.8 %collective-permute-start.15 = (bf16[4,416,128]{2,1,0:T(8,128)(2,1)S(1)}, bf16[4,416,128]{2,1,0:T(8,128)(2,1)S(1)}, u32[]{:S(2)}, u32[]{:S(2)}) collective-permute-start(bf16[4,416,128]{2,1,0:T(8,128)(2,1)S(1)} %get-tuple-element.73), channel_id=1, source_target_pairs={{0,1},{1,0},{2,3},{3,2},{4,5},{5,4},{6,7},{7,6},{8,9},{9,8},{10,11... | collective-permute-start | bytes 1277960 | tf_op jit(solution)/shard_map/ppermute | solution.py:421
  118.8 2.6 %collective-permute-start.14 = (bf16[4,544,128]{2,1,0:T(8,128)(2,1)S(1)}, bf16[4,544,128]{2,1,0:T(8,128)(2,1)S(1)}, u32[]{:S(2)}, u32[]{:S(2)}) collective-permute-start(bf16[4,544,128]{2,1,0:T(8,128)(2,1)S(1)} %get-tuple-element.72), channel_id=1, source_target_pairs={{0,1},{1,0},{2,3},{3,2},{4,5},{5,4},{6,7},{7,6},{8,9},{9,8},{10,11... | collective-permute-start | bytes 1671176 | tf_op jit(solution)/shard_map/ppermute | solution.py:421
  119.2 2.2 %collective-permute-start.20 = (bf16[4,128,128]{2,1,0:T(8,128)(2,1)S(1)}, bf16[4,128,128]{2,1,0:T(8,128)(2,1)S(1)}, u32[]{:S(2)}, u32[]{:S(2)}) collective-permute-start(bf16[4,128,128]{2,1,0:T(8,128)(2,1)S(1)} %get-tuple-element.74), channel_id=1, source_target_pairs={{0,1},{1,0},{2,3},{3,2},{4,5},{5,4},{6,7},{7,6},{8,9},{9,8},{10,11... | collective-permute-start | bytes 393224 | tf_op jit(solution)/shard_map/ppermute | solution.py:421
  120.5 28.9 %copy-start.2 = (bf16[8,512,256]{2,1,0:T(8,128)(2,1)S(1)}, bf16[8,512,256]{2,1,0:T(8,128)(2,1)}, u32[]{:S(2)}) copy-start(bf16[8,512,256]{2,1,0:T(8,128)(2,1)} %get-tuple-element.75.choose_ref) | copy-start | bytes 6291460
  120.6 11.9 %collective-permute-start.16 = (bf16[4,416,128]{2,1,0:T(8,128)(2,1)S(1)}, bf16[4,416,128]{2,1,0:T(8,128)(2,1)S(1)}, u32[]{:S(2)}, u32[]{:S(2)}) collective-permute-start(bf16[4,416,128]{2,1,0:T(8,128)(2,1)S(1)} %fusion), channel_id=1, source_target_pairs={{0,2},{2,0},{4,6},{6,4},{8,10},{10,8},{12,14},{14,12},{1,3},{3,1},... | collective-permute-start | bytes 1277960 | tf_op jit(solution)/shard_map/ppermute | solution.py:421
  121.5 19.1 %collective-permute-start.22 = (bf16[2,128,128]{2,1,0:T(8,128)(2,1)S(1)}, bf16[2,128,128]{2,1,0:T(8,128)(2,1)S(1)}, u32[]{:S(2)}, u32[]{:S(2)}) collective-permute-start(bf16[2,128,128]{2,1,0:T(8,128)(2,1)S(1)} %pad_maximum_fusion.1), channel_id=1, source_target_pairs={{0,8},{2,10},{4,12},{6,14},{8,0},{10,2},{12,4},{14,6},{1,9},{3,11}... | collective-permute-start | bytes 196616 | tf_op jit(solution)/shard_map/ppermute | solution.py:421
  129.7 10.9 %collective-permute-start.23 = (bf16[2,128,128]{2,1,0:T(8,128)(2,1)S(1)}, bf16[2,128,128]{2,1,0:T(8,128)(2,1)S(1)}, u32[]{:S(2)}, u32[]{:S(2)}) collective-permute-start(bf16[2,128,128]{2,1,0:T(8,128)(2,1)S(1)} %pad_maximum_fusion.2), channel_id=1, source_target_pairs={{0,4},{2,6},{4,0},{6,2},{8,12},{10,14},{12,8},{14,10},{1,5},{3,7},... | collective-permute-start | bytes 196616 | tf_op jit(solution)/shard_map/ppermute | solution.py:421
  129.8 19.6 %copy-start.1 = (f32[8,256,256]{2,1,0:T(8,128)S(1)}, f32[8,256,256]{2,1,0:T(8,128)}, u32[]{:S(2)}) copy-start(f32[8,256,256]{2,1,0:T(8,128)} %get-tuple-element.76.terms_ref) | copy-start | bytes 6291460
  129.8 10.8 %collective-permute-start.21 = (bf16[2,128,128]{2,1,0:T(8,128)(2,1)S(1)}, bf16[2,128,128]{2,1,0:T(8,128)(2,1)S(1)}, u32[]{:S(2)}, u32[]{:S(2)}) collective-permute-start(bf16[2,128,128]{2,1,0:T(8,128)(2,1)S(1)} %pad_maximum_fusion), channel_id=1, source_target_pairs={{0,12},{2,14},{4,8},{6,10},{8,4},{10,6},{12,0},{14,2},{1,13},{3,15... | collective-permute-start | bytes 196616 | tf_op jit(solution)/shard_map/ppermute | solution.py:421
  132.6 9.6 %collective-permute-start.17 = (bf16[416,128]{1,0:T(8,128)(2,1)S(1)}, bf16[416,128]{1,0:T(8,128)(2,1)S(1)}, u32[]{:S(2)}, u32[]{:S(2)}) collective-permute-start(bf16[416,128]{1,0:T(8,128)(2,1)S(1)} %get-tuple-element.77), channel_id=1, source_target_pairs={{0,12},{2,14},{4,8},{6,10},{8,4},{10,6},{12,0},{14,2},{1,13},{3,15... | collective-permute-start | bytes 319496 | tf_op jit(solution)/shard_map/ppermute | solution.py:421
  135.0 8.3 %collective-permute-start.19 = (bf16[416,128]{1,0:T(8,128)(2,1)S(1)}, bf16[416,128]{1,0:T(8,128)(2,1)S(1)}, u32[]{:S(2)}, u32[]{:S(2)}) collective-permute-start(bf16[416,128]{1,0:T(8,128)(2,1)S(1)} %get-tuple-element.78), channel_id=1, source_target_pairs={{0,4},{2,6},{4,0},{6,2},{8,12},{10,14},{12,8},{14,10},{1,5},{3,7},... | collective-permute-start | bytes 319496 | tf_op jit(solution)/shard_map/ppermute | solution.py:421
  140.6 7.1 %collective-permute-start.18 = (bf16[416,128]{1,0:T(8,128)(2,1)S(1)}, bf16[416,128]{1,0:T(8,128)(2,1)S(1)}, u32[]{:S(2)}, u32[]{:S(2)}) collective-permute-start(bf16[416,128]{1,0:T(8,128)(2,1)S(1)} %get-tuple-element.79), channel_id=1, source_target_pairs={{0,8},{2,10},{4,12},{6,14},{8,0},{10,2},{12,4},{14,6},{1,9},{3,11}... | collective-permute-start | bytes 319496 | tf_op jit(solution)/shard_map/ppermute | solution.py:421
  140.7 7.3 %collective-permute-start.24 = (bf16[128,128]{1,0:T(8,128)(2,1)S(1)}, bf16[128,128]{1,0:T(8,128)(2,1)S(1)}, u32[]{:S(2)}, u32[]{:S(2)}) collective-permute-start(bf16[128,128]{1,0:T(8,128)(2,1)S(1)} %fusion.5), channel_id=1, source_target_pairs={{0,2},{2,0},{4,6},{6,4},{8,10},{10,8},{12,14},{14,12},{1,3},{3,1},... | collective-permute-start | bytes 98312 | tf_op jit(solution)/shard_map/ppermute | solution.py:421
  147.8 1.5 %collective-permute-start.25 = (bf16[416,128]{1,0:T(8,128)(2,1)S(1)}, bf16[416,128]{1,0:T(8,128)(2,1)S(1)}, u32[]{:S(2)}, u32[]{:S(2)}) collective-permute-start(bf16[416,128]{1,0:T(8,128)(2,1)S(1)} %add_convert_fusion.mine_top), channel_id=1, source_target_pairs={{0,1},{1,0},{2,3},{3,2},{4,5},{5,4},{6,7},{7,6},{8,9},{9,8},{10,11... | collective-permute-start | bytes 319496 | tf_op jit(solution)/shard_map/ppermute | solution.py:421
  148.0 1.4 collective-permute-start.26
